TPU v7x, 32 devices: a whole 2x2x4 slice. The times are simulated.
32 devices in a mesh: blk: 8 (over y, x, core), head: 4 (over z).
Axes of the slice: x: 2, y: 2, z: 4, core: 2. Of those that a mesh axis runs over, the one named last changes fastest.
Arguments:
- tokens: bfloat16 [2048, 2048], P('blk'), may hold values from -6 to 6
- gain_attn: bfloat16 [2048], replicated, may hold values from 0.25 to 1.75
- w_query: bfloat16 [2048, 256], P(None, 'head'), may hold values from -0.125 to 0.125
- w_key: bfloat16 [2048, 256], P(None, 'head'), may hold values from -0.125 to 0.125
- w_value: bfloat16 [2048, 2048], P(None, 'head'), may hold values from -0.125 to 0.125
- w_out: bfloat16 [2048, 2048], P('head'), may hold values from -1.5 to 1.5
- gain_mlp: bfloat16 [2048], replicated, may hold values from 0.25 to 1.75
- w_gate: bfloat16 [2048, 5504], P(None, 'head'), may hold values from -0.125 to 0.125
- w_up: bfloat16 [2048, 5504], P(None, 'head'), may hold values from -0.125 to 0.125
- w_down: bfloat16 [5504, 2048], P('head'), may hold values from -0.078125 to 0.078125
- doc_lengths: int32 [4], replicated, may hold values from 1 to 1920, 1984 in all
- cotangent: bfloat16 [2048, 2048], P('blk'), may hold values from -6 to 6
Outputs:
- output: bfloat16 [2048, 2048], P('blk')
- input_grad: float32 [2048, 2048], P('blk')
- gain_attn_grad: float32 [2048], replicated
- query_weight_grad: float32 [2048, 256], P(None, 'head')
- key_weight_grad: float32 [2048, 256], P(None, 'head')
- value_weight_grad: float32 [2048, 2048], P(None, 'head')
- out_weight_grad: float32 [2048, 2048], P('head')
- gain_mlp_grad: float32 [2048], replicated
- gate_weight_grad: float32 [2048, 5504], P(None, 'head')
- up_weight_grad: float32 [2048, 5504], P(None, 'head')
- down_weight_grad: float32 [5504, 2048], P('head')
Inputs may be any that keep to these rules, and one draw needn't show every extreme that they name: `doc_lengths`: the lengths are positive and sum to 1984; the documents lie end to end from position 0, the last 64 positions are padding, and the longest document has exactly 1920 tokens.
All inputs are finite; a program needn't handle non-finite values.
Results may differ from a plain program's by a relative error of at most 0.015.
Values sent between devices are 32-bit elements; how exact they have to be, the bound alone decides.
No kernel may reach another device: no remote copies, remote signals or barrier semaphores. Data moves between devices by JAX's collectives and lax.ppermute only.
A program may use at most 256 MiB of HBM per device.

v0:
```python
import math

import jax
import jax.numpy as jnp
from jax import lax
from jax.sharding import PartitionSpec as P

FEAT = 16
FMAP = 273
DV = 128


epsilon = 1e-05
highest = lax.Precision.HIGHEST
quad_scale = 1.0 / (4.0 * math.sqrt(2.0))


def carried_in(value, axis, join, neutral, backward):
    count, mine = (lax.axis_size(axis), lax.axis_index(axis))
    pieces = jax.tree.map(lambda part: lax.all_gather(part, axis), value)
    if backward:
        pieces = jax.tree.map(lambda part: part[::-1], pieces)
        mine = count - 1 - mine
    total = jax.tree.map(
        lambda part, zero: jnp.full_like(part, 0) + jnp.asarray(zero, part.dtype), value, neutral
    )

    def step(position, total):
        longer = join(total, jax.tree.map(lambda part: part[position], pieces))
        return jax.tree.map(lambda new, old: jnp.where(position < mine, new, old), longer, total)

    return lax.fori_loop(0, count - 1, step, total)


def feature_map(vectors):
    width = vectors.shape[-1]
    outer = (vectors[..., :, None] * vectors[..., None, :]).reshape(
        vectors.shape[:-1] + (width * width,)
    )
    ones_col = jnp.ones(vectors.shape[:-1] + (1,), vectors.dtype)
    return jnp.concatenate([ones_col, 0.5 * vectors, quad_scale * outer], axis=-1)


def doc_index(positions, ends):
    return jnp.sum((positions[:, None] >= ends[None, :-1]).astype(jnp.int32), axis=1)


def chain_combine(earlier, later):
    forget = 1.0 - later[2]
    return (
        later[0] + forget * earlier[0],
        later[1] + forget * earlier[1],
        jnp.maximum(earlier[2], later[2]),
    )


def norm_back(grad_out, values, inverse, gain):
    scaled = grad_out * gain
    return inverse * (
        scaled - values * inverse * inverse * jnp.mean(scaled * values, axis=-1, keepdims=True)
    )


def per_device(
    tokens,
    gain_attn,
    w_query,
    w_key,
    w_value,
    w_out,
    gain_mlp,
    w_gate,
    w_up,
    w_down,
    doc_lengths,
    cotangent,
):
    row_count = tokens.shape[0]
    head_count = w_query.shape[1] // FEAT
    blk_index = lax.axis_index("blk")
    blk_count = lax.axis_size("blk")
    ends = jnp.cumsum(doc_lengths)
    positions = blk_index * row_count + jnp.arange(row_count, dtype=jnp.int32)
    row_docs = doc_index(positions, ends)
    valid = (positions < ends[-1]).astype(jnp.float32)
    owners_all = jnp.arange(blk_count, dtype=jnp.int32)
    span_starts = owners_all * row_count
    start_docs = jnp.where(span_starts > 0, doc_index(span_starts - 1, ends), -1)
    end_docs = doc_index(span_starts + row_count - 1, ends)
    resets = (end_docs != start_docs).astype(jnp.float32)
    prev_doc = start_docs[blk_index]
    last_doc = end_docs[blk_index]
    my_reset = resets[blk_index]
    token_wide = tokens.astype(jnp.float32)
    gain_one = gain_attn.astype(jnp.float32)
    gain_two = gain_mlp.astype(jnp.float32)
    inv_in = lax.rsqrt(jnp.mean(token_wide * token_wide, axis=-1, keepdims=True) + epsilon)
    normed_in = (token_wide * inv_in * gain_one).astype(jnp.bfloat16)
    query_proj = jnp.dot(normed_in, w_query, preferred_element_type=jnp.float32)
    key_proj = jnp.dot(normed_in, w_key, preferred_element_type=jnp.float32)
    value_rows = jnp.dot(normed_in, w_value, preferred_element_type=jnp.float32).astype(
        jnp.bfloat16
    )
    query_heads = query_proj.reshape(row_count, head_count, FEAT).transpose(1, 0, 2)
    key_heads = key_proj.reshape(row_count, head_count, FEAT).transpose(1, 0, 2)
    query_feat = feature_map(query_heads).astype(jnp.bfloat16)
    key_feat = (feature_map(key_heads) * valid[None, :, None]).astype(jnp.bfloat16)
    value_heads = value_rows.reshape(row_count, head_count, DV).transpose(1, 0, 2)
    carried = (row_docs == prev_doc).astype(jnp.float32)
    keep_rows = (row_docs == last_doc).astype(jnp.float32)
    kept_keys = key_feat * keep_rows.astype(jnp.bfloat16)[None, :, None]
    local_state = jnp.einsum(
        "hsf,hsd->hfd", kept_keys, value_heads, preferred_element_type=jnp.float32
    )
    local_total = jnp.sum(kept_keys.astype(jnp.float32), axis=1)
    state_zero = jnp.zeros_like(local_state)
    total_zero = jnp.zeros_like(local_total)
    carry_state, carry_total, unused = carried_in(
        (local_state, local_total, my_reset[None]),
        "blk",
        chain_combine,
        (state_zero, total_zero, jnp.zeros((1,), jnp.float32)),
        False,
    )
    block_rows = min(512, row_count)
    block_count = row_count // block_rows
    block_starts = jnp.arange(block_count, dtype=jnp.int32) * block_rows
    key_index = jnp.arange(row_count, dtype=jnp.int32)

    def block_scores(start):
        block_pos = start + jnp.arange(block_rows, dtype=jnp.int32)
        allowed = (row_docs[:, None] == row_docs[None, :]) & (
            block_pos[:, None] >= key_index[None, :]
        )
        raw_scores = jnp.einsum(
            "htf,hsf->hts", query_feat, key_feat, preferred_element_type=jnp.float32
        )
        return (query_feat, allowed, jnp.where(allowed[None], raw_scores, 0.0).astype(jnp.bfloat16))

    def forward_block(start):
        query_block, allowed, scores = block_scores(start)
        query_wide = query_block.astype(jnp.float32)
        numerator = jnp.einsum(
            "hts,hsd->htd", scores, value_heads, preferred_element_type=jnp.float32
        )
        numerator = numerator + carried[None, :, None] * jnp.einsum(
            "htf,hfd->htd", query_wide, carry_state, precision=highest
        )
        denominator = jnp.sum(scores.astype(jnp.float32), axis=-1)
        denominator = denominator + carried[None, :] * jnp.einsum(
            "htf,hf->ht", query_wide, carry_total, precision=highest
        )
        return (numerator, denominator)

    numer_blocks, denom_blocks = lax.map(forward_block, block_starts)
    numerator = numer_blocks.transpose(1, 0, 2, 3).reshape(head_count, row_count, DV)
    denominator = denom_blocks.transpose(1, 0, 2).reshape(head_count, row_count)
    attended = (numerator / denominator[:, :, None] * valid[None, :, None]).astype(jnp.bfloat16)
    attended = attended.transpose(1, 0, 2).reshape(row_count, head_count * DV)
    attn_part = jnp.dot(attended, w_out, preferred_element_type=jnp.float32)
    resid_mid = token_wide + lax.psum(attn_part, "head")
    inv_mid = lax.rsqrt(jnp.mean(resid_mid * resid_mid, axis=-1, keepdims=True) + epsilon)
    normed_mid = (resid_mid * inv_mid * gain_two).astype(jnp.bfloat16)
    gate = jnp.dot(normed_mid, w_gate, preferred_element_type=jnp.float32)
    up_lin = jnp.dot(normed_mid, w_up, preferred_element_type=jnp.float32)
    sigmoid_gate = jax.nn.sigmoid(gate)
    silu_gate = gate * sigmoid_gate
    hidden = (silu_gate * up_lin).astype(jnp.bfloat16)
    mlp_part = jnp.dot(hidden, w_down, preferred_element_type=jnp.float32)
    output = (resid_mid + lax.psum(mlp_part, "head")).astype(jnp.bfloat16)
    cot_wide = cotangent.astype(jnp.float32)
    down_w_grad = jnp.einsum("tf,td->fd", hidden, cotangent, preferred_element_type=jnp.float32)
    hidden_grad = jnp.einsum("td,fd->tf", cotangent, w_down, preferred_element_type=jnp.float32)
    gate_lin_grad = (
        hidden_grad * up_lin * sigmoid_gate * (1.0 + gate * (1.0 - sigmoid_gate))
    ).astype(jnp.bfloat16)
    up_lin_grad = (hidden_grad * silu_gate).astype(jnp.bfloat16)
    gate_w_grad = jnp.einsum(
        "td,tf->df", normed_mid, gate_lin_grad, preferred_element_type=jnp.float32
    )
    up_w_grad = jnp.einsum("td,tf->df", normed_mid, up_lin_grad, preferred_element_type=jnp.float32)
    mid_part = jnp.einsum("tf,df->td", gate_lin_grad, w_gate, preferred_element_type=jnp.float32)
    mid_part = mid_part + jnp.einsum(
        "tf,df->td", up_lin_grad, w_up, preferred_element_type=jnp.float32
    )
    mid_grad = lax.psum(mid_part, "head")
    gain_mlp_grad = jnp.sum(mid_grad * resid_mid * inv_mid, axis=0)
    resid_grad = cot_wide + norm_back(mid_grad, resid_mid, inv_mid, gain_two)
    out_lin_grad = resid_grad.astype(jnp.bfloat16)
    out_w_grad = jnp.einsum("tc,td->cd", attended, out_lin_grad, preferred_element_type=jnp.float32)
    attended_grad = jnp.einsum("td,cd->tc", out_lin_grad, w_out, preferred_element_type=jnp.float32)
    attended_grad = attended_grad.reshape(row_count, head_count, DV).transpose(1, 0, 2)
    scale_rows = valid[None, :] / denominator
    numer_grad = (attended_grad * scale_rows[:, :, None]).astype(jnp.bfloat16)
    denom_grad = -jnp.sum(attended_grad * numerator, axis=-1) * scale_rows / denominator
    carry_query = query_feat * carried.astype(jnp.bfloat16)[None, :, None]
    state_grad_in = jnp.einsum(
        "htf,htd->hfd", carry_query, numer_grad, preferred_element_type=jnp.float32
    )
    total_grad_in = jnp.einsum(
        "htf,ht->hf", carry_query.astype(jnp.float32), denom_grad, precision=highest
    )
    later_state, later_total, unused = carried_in(
        (state_grad_in, total_grad_in, my_reset[None]),
        "blk",
        chain_combine,
        (state_zero, total_zero, jnp.zeros((1,), jnp.float32)),
        True,
    )

    def backward_block(sums, start):
        query_block, allowed, scores = block_scores(start)
        score_grad = (
            jnp.einsum("htd,hsd->hts", numer_grad, value_heads, preferred_element_type=jnp.float32)
            + denom_grad[:, :, None]
        )
        score_grad = jnp.where(allowed[None], score_grad, 0.0).astype(jnp.bfloat16)
        query_grad = jnp.einsum(
            "hts,hsf->htf", score_grad, key_feat, preferred_element_type=jnp.float32
        )
        far_part = jnp.einsum(
            "htd,hfd->htf", numer_grad.astype(jnp.float32), carry_state, precision=highest
        )
        far_part = far_part + denom_grad[:, :, None] * carry_total[:, None, :]
        query_grad = query_grad + carried[None, :, None] * far_part
        key_sum = sums[0] + jnp.einsum(
            "hts,htf->hsf", score_grad, query_block, preferred_element_type=jnp.float32
        )
        value_sum = sums[1] + jnp.einsum(
            "hts,htd->hsd", scores, numer_grad, preferred_element_type=jnp.float32
        )
        return ((key_sum, value_sum), query_grad)

    sums_zero = (
        jnp.zeros((head_count, row_count, FMAP), jnp.float32),
        jnp.zeros((head_count, row_count, DV), jnp.float32),
    )
    (key_feat_grad, value_head_grad), query_blocks = lax.scan(
        backward_block, sums_zero, block_starts
    )
    query_feat_grad = query_blocks.transpose(1, 0, 2, 3).reshape(head_count, row_count, FMAP)
    keep_wide = keep_rows[None, :, None]
    key_feat_grad = key_feat_grad + keep_wide * (
        jnp.einsum("hsd,hfd->hsf", value_heads.astype(jnp.float32), later_state, precision=highest)
        + later_total[:, None, :]
    )
    value_head_grad = value_head_grad + keep_wide * jnp.einsum(
        "hsf,hfd->hsd", key_feat.astype(jnp.float32), later_state, precision=highest
    )
    unused_query, query_pull = jax.vjp(feature_map, query_heads)
    unused_key, key_pull = jax.vjp(feature_map, key_heads)
    query_lin_grad = (
        query_pull(query_feat_grad)[0]
        .transpose(1, 0, 2)
        .reshape(row_count, head_count * FEAT)
        .astype(jnp.bfloat16)
    )
    key_lin_grad = (
        key_pull(key_feat_grad * valid[None, :, None])[0]
        .transpose(1, 0, 2)
        .reshape(row_count, head_count * FEAT)
        .astype(jnp.bfloat16)
    )
    value_grad = (
        value_head_grad.transpose(1, 0, 2).reshape(row_count, head_count * DV).astype(jnp.bfloat16)
    )
    query_w_grad = jnp.einsum(
        "td,tc->dc", normed_in, query_lin_grad, preferred_element_type=jnp.float32
    )
    key_w_grad = jnp.einsum(
        "td,tc->dc", normed_in, key_lin_grad, preferred_element_type=jnp.float32
    )
    value_w_grad = jnp.einsum(
        "td,tc->dc", normed_in, value_grad, preferred_element_type=jnp.float32
    )
    in_part = jnp.einsum("tc,dc->td", query_lin_grad, w_query, preferred_element_type=jnp.float32)
    in_part = in_part + jnp.einsum(
        "tc,dc->td", key_lin_grad, w_key, preferred_element_type=jnp.float32
    )
    in_part = in_part + jnp.einsum(
        "tc,dc->td", value_grad, w_value, preferred_element_type=jnp.float32
    )
    in_grad = lax.psum(in_part, "head")
    gain_attn_grad = jnp.sum(in_grad * token_wide * inv_in, axis=0)
    input_grad = resid_grad + norm_back(in_grad, token_wide, inv_in, gain_one)
    summed_grads = lax.psum(
        (
            gain_attn_grad,
            query_w_grad,
            key_w_grad,
            value_w_grad,
            out_w_grad,
            gain_mlp_grad,
            gate_w_grad,
            up_w_grad,
            down_w_grad,
        ),
        "blk",
    )
    return (
        output,
        input_grad,
        summed_grads[0],
        summed_grads[1],
        summed_grads[2],
        summed_grads[3],
        summed_grads[4],
        summed_grads[5],
        summed_grads[6],
        summed_grads[7],
        summed_grads[8],
    )


def solution(mesh):
    in_specs = (
        P("blk", None),
        P(),
        P(None, "head"),
        P(None, "head"),
        P(None, "head"),
        P("head", None),
        P(),
        P(None, "head"),
        P(None, "head"),
        P("head", None),
        P(),
        P("blk", None),
    )
    out_specs = (
        P("blk", None),
        P("blk", None),
        P(),
        P(None, "head"),
        P(None, "head"),
        P(None, "head"),
        P("head", None),
        P(),
        P(None, "head"),
        P(None, "head"),
        P("head", None),
    )
    return jax.shard_map(
        per_device, mesh=mesh, in_specs=in_specs, out_specs=out_specs, check_vma=False
    )
```

profile of v0, /device:TPU:0, one launch (start us, length us, event | category | flops | bytes accessed | tf_op | source)
XLA Modules:
  0.0 1104.7 jit_solution(6826603460394106047)
XLA Ops:
  9.5 1.5 fusion.11
  13.1 1.5 fusion.6
  16.0 1.9 fusion.63
  21.8 15.9 %all-reduce = f32[8]{0:T(128)} all-reduce(f32[8]{0:T(128)S(1)} %dynamic-slice_dynamic-update-slice_fusion), channel_id=3, replica_groups=mesh['blk'=8,'head'=4] {'blk'}, use_global_device_ids=true, to_apply=%add | all-reduce | flops 8 | bytes 64
  37.6 9.3 all-gather.5
  47.0 1.4 multiply_convert_fusion.6
  51.7 9.9 all-gather.10.cloned.1.call-done
  61.6 37.3 %while.20 = (s32[]{:T(128)}, f32[4,273,128]{2,1,0:T(8,128)}, f32[4,273]{1,0:T(4,128)S(1)}, s32[]{:T(128)}, f32[8,4,273,128]{3,2,1,0:T(8,128)}, /*index=5*/f32[8,...) while((s32[]{:T(128)}, f32[4,273,128]{2,1,0:T(8,128)}, f32[4,273]{1,0:T(4,128)S(1)}, ...), condition=%wide.region_7.8_spmd.clone, body=%wide.region_6.7_spmd.clone.sunk | while | flops 563477 | bytes 1690567 | solution.py:32
  62.9 1.4 fusion.146
  64.2 2.6 fusion.145
  68.0 1.4 fusion.146
  69.4 2.8 fusion.145
  74.7 2.8 fusion.145
  80.1 2.8 fusion.145
  85.5 2.8 fusion.145
  90.8 2.8 fusion.145
  96.2 2.8 fusion.145
  98.9 1.5 fusion.56
  102.4 3.1 fusion.30
  106.2 2.0 fusion.69
  110.1 84.8 %all-reduce.9.cloned.1.call-done = f32[256,2048]{1,0:T(8,128)} async-done(((f32[256,2048]{1,0:T(8,128)}), f32[256,2048]{1,0:T(8,128)}) %all-reduce.9.cloned.1.call-update) | async-done | bytes 2097168 | tf_op jit(solution)/shard_map/psum | solution.py:161
  194.9 2.2 multiply_reduce_fusion.2
  198.7 4.8 fusion.71
  203.6 1.7 fusion.70
  205.4 3.0 multiply_convert_fusion.1
  208.5 1.8 fusion.73
  210.3 3.1 convolution_add_fusion.2
  213.5 85.6 %all-reduce.11.cloned.1.call-done = f32[256,2048]{1,0:T(8,128)} async-done(((f32[256,2048]{1,0:T(8,128)}), f32[256,2048]{1,0:T(8,128)}) %all-reduce.11.cloned.1.call-update) | async-done | bytes 2097168 | tf_op jit(solution)/shard_map/psum | solution.py:186
  299.1 3.5 multiply_reduce_fusion
  302.6 2.0 multiply_add_fusion
  304.7 1.4 multiply_reduce_fusion.7
  308.4 5.8 fusion.72
  315.0 9.3 all-gather.6
  328.5 1.4 fusion.62
  329.9 1.8 fusion.75
  331.7 13.5 %all-gather.12.cloned.1.call-done = f32[32,273,128]{2,1,0:T(8,128)} async-done(((f32[4,273,128]{2,1,0:T(8,128)}), f32[32,273,128]{2,1,0:T(8,128)}) %all-gather.12.cloned.1.call-update) | async-done | bytes 4472848 | tf_op jit(solution)/shard_map/all_gather | solution.py:20
  345.1 4.8 rev.9
  349.9 29.0 %while.21 = (s32[]{:T(128)}, f32[4,273,128]{2,1,0:T(8,128)S(1)}, f32[4,273]{1,0:T(4,128)S(1)}, s32[]{:T(128)}, f32[8,4,273,128]{3,2,1,0:T(8,128)}, /*index=5*/f3...) while((s32[]{:T(128)}, f32[4,273,128]{2,1,0:T(8,128)S(1)}, ...), condition=%wide.region_18.19_spmd.clone, body=%wide.region_17.18_spmd.clone.sunk | while | flops 563477 | bytes 1690567 | solution.py:32
  351.8 2.2 fusion.148
  356.0 2.2 fusion.148
  360.1 2.2 fusion.148
  364.3 2.2 fusion.148
  368.4 2.2 fusion.148
  372.5 2.2 fusion.148
  376.7 2.2 fusion.148
  384.1 2.1 convolution_add_fusion
  387.2 7.4 fusion.78
  394.7 6.0 fusion.82
  400.7 6.0 fusion.81
  407.8 2.7 fusion.31
  411.6 2.8 fusion.77
  414.4 127.2 %all-reduce.15.cloned.1.call-done = (f32[256,2048]{1,0:T(8,128)}, f32[256,2048]{1,0:T(8,128)}) async-done(((f32[256,2048]{1,0:T(8,128)}, f32[256,2048]{1,0:T(8,128)}), (f32[256,2048]{1,0:T(8,128)}, f32[256,2048]{1,0:T(8,128)})) %all-reduce.15.cloned.1.call-update) | async-done | bytes 4194320 | tf_op jit(solution)/shard_map/psum | solution.py:170
  541.7 2.1 fusion.14
  543.8 25.9 %all-reduce.1 = (f32[2048]{0:T(1024)}, f32[2048]{0:T(1024)}) all-reduce(f32[2048]{0:T(1024)S(1)} %get-tuple-element.390, f32[2048]{0:T(1024)S(1)} %copy-done.50), channel_id=1, replica_groups=mesh['blk'=8,'head'=4] {'blk'}, use_global_device_ids=true, to_apply=%region_24.25 | all-reduce | flops 4096 | bytes 32768 | tf_op jit(solution)/shard_map/psum | solution.py:286
  569.7 3.0 add_convert_fusion
  572.7 2.0 fusion.10
  574.7 481.0 %all-reduce.13.cloned.1.call-done = (f32[2048,64]{0,1:T(8,128)}, f32[2048,64]{0,1:T(8,128)}, f32[2048,512]{1,0:T(8,128)}, f32[512,2048]{1,0:T(8,128)}, f32[2048,...) async-done(((f32[2048,64]{0,1:T(8,128)}, f32[2048,64]{0,1:T(8,128)}, f32[2048,512]{1,0:T(8,128)}, f32[512,2048]{1,0:T(8,128)}, f32[2048,1376]{0,1:T(8,128)}, ...) | async-done | bytes 43253776 | tf_op jit(solution)/shard_map/psum | solution.py:286
  1055.7 1.9 copy.127
  1057.6 1.9 copy.128
  1059.4 4.8 copy.129
  1064.3 2.0 copy.130
  1066.3 10.4 copy.131
  1076.7 10.4 copy.132
  1087.1 10.5 copy.133
  (255 shorter events, 63.5 us)
Async XLA Ops:
  7.2 99.0 %copy-start = (bf16[512,2048]{1,0:T(8,128)(2,1)S(1)}, bf16[512,2048]{1,0:T(8,128)(2,1)}, u32[]{:S(2)}) copy-start(bf16[512,2048]{1,0:T(8,128)(2,1)} %param.21) | copy-start | bytes 6291460
  7.2 7.4 copy-start.41
  7.2 54.4 %all-gather.10.cloned.1.call-start = ((), (), s32[]{:S(2)}) async-start(), calls=%async_computation.2 | async-start | bytes 5160960 | tf_op jit(solution)/shard_map/all_gather | solution.py:20
  9.5 8.4 copy-start.51
  11.0 2.1 copy-start.53
  11.2 3.9 copy-start.30
  16.0 4.4 copy-start.70
  20.3 174.6 %all-reduce.9.cloned.1.call-start = ((), (), s32[]{:S(2)}) async-start(), calls=%async_computation | async-start | bytes 4194304 | tf_op jit(solution)/shard_map/psum | solution.py:161
  37.6 11.0 copy-start.14
  37.6 12.2 %copy-start.62 = (bf16[273]{0:T(512)(128)(2,1)}, bf16[273]{0:T(512)(128)(2,1)S(1)}, u32[]{:S(2)}) copy-start(bf16[273]{0:T(512)(128)(2,1)S(1)} %pad.3.clone) | copy-start | bytes 1642
  47.0 2.8 copy-start.49
  108.3 190.8 %all-reduce.11.cloned.1.call-start = ((), (), s32[]{:S(2)}) async-start(), calls=%async_computation.1 | async-start | bytes 4194304 | tf_op jit(solution)/shard_map/psum | solution.py:186
  194.9 3.6 copy-start.44
  198.5 5.1 slice-start
  198.7 4.8 copy-start.10
  198.7 4.8 slice-start.1
  198.7 6.6 slice-start.2
  203.6 1.7 slice-start.3
  203.6 1.8 copy-start.26
  203.6 6.7 slice-start.4
  205.4 4.9 slice-start.5
  208.4 1.8 copy-start.19
  208.4 1.8 copy-start.23
  213.5 131.7 %all-gather.12.cloned.1.call-start = ((), (), s32[]{:S(2)}) async-start(), calls=%async_computation.3 | async-start | bytes 5160960 | tf_op jit(solution)/shard_map/all_gather | solution.py:20
  299.1 3.5 copy-start.3
  299.1 3.5 copy-start.17
  299.1 3.5 copy-start.45
  302.6 2.0 copy-start.43
  306.1 1.6 copy-start.68
  306.1 2.3 copy-start.21
  307.5 234.2 %all-reduce.15.cloned.1.call-start = ((), (), s32[]{:S(2)}) async-start(), calls=%async_computation.5 | async-start | bytes 8388608 | tf_op jit(solution)/shard_map/psum | solution.py:170
  308.4 5.9 copy-start.52
  308.4 5.9 copy-start.57
  308.4 5.9 copy-start.58
  308.4 5.9 copy-start.34
  308.4 5.9 copy-start.48
  308.4 5.9 copy-start.64
  308.4 5.9 copy-start.67
  314.3 11.8 %copy-start.15 = (bf16[4,256,273]{1,2,0:T(8,128)(2,1)S(1)}, bf16[4,256,273]{1,2,0:T(8,128)(2,1)}, u32[]{:S(2)}) copy-start(bf16[4,256,273]{1,2,0:T(8,128)(2,1)} %copy-done.13) | copy-start | bytes 1677316
  315.0 11.4 %copy-start.9 = (f32[4,273,128]{2,1,0:T(8,128)S(1)}, f32[4,273,128]{2,1,0:T(8,128)}, u32[]{:S(2)}) copy-start(f32[4,273,128]{2,1,0:T(8,128)} %get-tuple-element.336) | copy-start | bytes 1677316
  315.0 11.4 %copy-start.61 = (f32[256]{0:T(256)S(1)}, f32[256]{0:T(256)}, u32[]{:S(2)}) copy-start(f32[256]{0:T(256)} %get-tuple-element.438) | copy-start | bytes 3076
  327.7 2.2 copy-start.40
  345.1 4.8 copy-start.69
  349.9 29.0 %copy-start.60 = (f32[256]{0:T(256)S(1)}, f32[256]{0:T(256)}, u32[]{:S(2)}) copy-start(f32[256]{0:T(256)} %get-tuple-element.451) | copy-start | bytes 3076
  379.8 3.1 copy-start.28
  380.9 1.6 copy-start.18
  380.9 1.6 copy-start.42
  382.5 1.6 copy-start.31
  386.2 8.5 copy-start.11
  386.2 669.5 %all-reduce.13.cloned.1.call-start = ((), (), s32[]{:S(2)}) async-start(), calls=%async_computation.4 | async-start | bytes 86507520 | tf_op jit(solution)/shard_map/psum | solution.py:286
  387.2 7.5 copy-start.24
  394.7 6.0 copy-start.12
  394.7 6.0 copy-start.20
  400.7 7.1 copy-start.6
  400.7 7.1 copy-start.39
  407.8 3.8 copy-start.29
  414.4 127.3 %copy-start.8 = (bf16[256,2048]{1,0:T(8,128)(2,1)S(1)}, bf16[256,2048]{1,0:T(8,128)(2,1)}, u32[]{:S(2)}) copy-start(bf16[256,2048]{1,0:T(8,128)(2,1)} %param.16) | copy-start | bytes 3145732
  414.4 127.3 %copy-start.54 = (f32[256]{0:T(256)S(1)}, f32[256]{0:T(256)}, u32[]{:S(2)}) copy-start(f32[256]{0:T(256)} %copy-done.53) | copy-start | bytes 3076
  414.4 129.4 %copy-start.50 = (f32[2048]{0:T(1024)S(1)}, f32[2048]{0:T(1024)}, u32[]{:S(2)}) copy-start(f32[2048]{0:T(1024)} %get-tuple-element.388) | copy-start | bytes 24580
  414.4 155.2 %copy-start.4 = (f32[256,2048]{1,0:T(8,128)S(1)}, f32[256,2048]{1,0:T(8,128)}, u32[]{:S(2)}) copy-start(f32[256,2048]{1,0:T(8,128)} %copy-done.2) | copy-start | bytes 6291460
  569.7 3.0 copy-start.7
  569.7 3.0 copy-start.16
  1059.4 4.8 copy-start.27
  1087.1 10.5 copy-start.1
  (19 other events, 22.8 us)
Sparse Core Ops, SparseCore 0:
  20.4 41.1 all-gather.9
  108.4 86.4 all-reduce.8
  213.6 85.4 all-reduce.10
  307.6 37.4 all-gather.11
  386.3 155.3 all-reduce.14
  548.7 506.9 all-reduce.12
where the time goes:
time: 1110 us; the launch traced here: 1100 us
  waiting for transfers between devices  802 us (72%)
  other arithmetic  93.4 us (8%)
  matrix products  73.1 us (7%)
  blocking collectives  60.2 us (5%)
  local copies, waits for them, and re-layouts  59.3 us (5%)
  between operations  15.3 us (1%)
    psum x1, waiting for transfers between devices, per_device(): lax.psum((gain_attn_grad, query_w_grad, key_w_grad, value_w_grad, out_w_g...  481 us
    psum x1, waiting for transfers between devices, per_device(): output = (resid_mid + lax.psum(mlp_part, 'head')).astype(jnp.bfloat16)  127 us
    psum x1, waiting for transfers between devices, per_device(): mid_grad = lax.psum(mid_part, 'head')  85.6 us
    psum x1, waiting for transfers between devices, per_device(): resid_mid = token_wide + lax.psum(attn_part, 'head')  84.8 us
    select_n x28, other arithmetic, step(): jnp.where(position < mine, new, old)  53.4 us
    unnamed x165, local copies, waits for them, and re-layouts  52.1 us
    psum x1, blocking collectives, per_device(): lax.psum((gain_attn_grad, query_w_grad, key_w_grad, value_w_grad, out_w_g...  25.9 us
    all_gather x2, waiting for transfers between devices, carried_in(): pieces = jax.tree.map(lambda part: lax.all_gather(part, axis), value)  23.4 us
  transfers between devices with their start and end apart: 6, of which 6 were waited for; matrix products, arithmetic and copies ran while one was open for 5% of the time, Pallas kernels for 0%

commit v1 on v0

v1 whole, which is shorter than its diff:
```python
import functools

import jax
import jax.numpy as jnp
from jax import lax
from jax.experimental import pallas as pl
from jax.experimental.pallas import tpu as pltpu
from jax.sharding import PartitionSpec as P

FEAT = 16
DV = 128

epsilon = 1e-05
f32, bf16 = jnp.float32, jnp.bfloat16
VMEM_LIMIT = 56 * 1024 * 1024


def hop(value, axis, bit):
    count = lax.axis_size(axis)
    return lax.ppermute(value, axis, [(i, i ^ bit) for i in range(count)])


def gather_blk(value):
    count = lax.axis_size("blk")
    if count != 8:
        slots, bit = [value], 1
        while bit < count:
            slots = slots + [hop(slot, "blk", bit) for slot in slots]
            bit *= 2
        return slots
    half = value.shape[0] // 16 * 8
    from_x, from_y = hop(value, "blk", 2), hop(value, "blk", 4)
    far_low, far_high = hop(from_x[:half], "blk", 4), hop(from_y[half:], "blk", 2)
    own_pair, x_pair, y_pair = (hop(part, "blk", 1) for part in (value, from_x, from_y))
    far = jnp.concatenate([far_low, far_high])
    far_pair = jnp.concatenate([hop(far_low, "blk", 1), hop(far_high, "blk", 1)])
    return [value, own_pair, from_x, x_pair, from_y, y_pair, far, far_pair]


def fold(value, bit):
    low, high = jnp.split(value, 2)
    upper = (lax.axis_index("blk") & bit) != 0
    return jnp.where(upper, high, low) + hop(jnp.where(upper, low, high), "blk", bit)


def unfold(value, bit):
    other = hop(value, "blk", bit)
    upper = (lax.axis_index("blk") & bit) != 0
    return jnp.concatenate([jnp.where(upper, other, value), jnp.where(upper, value, other)])


def sum_blk(value):
    if lax.axis_size("blk") != 8:
        return lax.psum(value, "blk")
    one, two = jnp.split(fold(value, 1), 2)
    one, two = fold(one, 2), fold(two, 4)
    one, two = fold(one, 4), fold(two, 2)
    one, two = unfold(one, 4), unfold(two, 2)
    one, two = unfold(one, 2), unfold(two, 4)
    return unfold(jnp.concatenate([one, two]), 1)


def sum_head(value):
    return lax.psum(value, "head")


def dot_t(left, right):
    return lax.dot_general(left, right, (((1,), (1,)), ((), ())), preferred_element_type=f32)


def dot_n(left, right):
    return lax.dot_general(left, right, (((1,), (0,)), ((), ())), preferred_element_type=f32)


def two_parts(value):
    high = value.astype(bf16)
    return high, (value - high.astype(f32)).astype(bf16)


def quarter_dot(left, right):
    total = dot_t(left[0], right[0]) + (dot_t(left[0], right[1]) + dot_t(left[1], right[0]))
    return 0.25 * total


def head_lanes(rows, width, head):
    lanes = lax.broadcasted_iota(jnp.int32, (rows, width), 1)
    return (lanes >= head * FEAT) & (lanes < (head + 1) * FEAT)


def attend_kernel(heads, slots, col_ref, row_ref, *refs):
    slot_refs, (att_ref, mean_ref, inverse_ref) = refs[:slots], refs[slots:]
    rows = col_ref.shape[0]
    qk = heads * FEAT
    own_pos, own_doc = col_ref[:, 0:1], col_ref[:, 1:2]
    valid = col_ref[:, 2:3].astype(f32)
    query = slot_refs[0][:, :qk]
    numer = [jnp.zeros((rows, DV), f32) for _ in range(heads)]
    denom = [jnp.zeros((rows, 1), f32) for _ in range(heads)]
    queries = [
        two_parts(jnp.where(head_lanes(rows, qk, head), query, 0.0)) for head in range(heads)
    ]
    for slot in range(slots):
        allowed = (row_ref[slot : slot + 1, :] <= own_pos) & (
            row_ref[slots + slot : slots + slot + 1, :] == own_doc
        )
        keys = two_parts(slot_refs[slot][:, qk : 2 * qk])
        for head in range(heads):
            near = quarter_dot(queries[head], keys)
            score = jnp.where(allowed, 1.0 + near + 0.5 * near * near, 0.0).astype(bf16)
            first = 2 * qk + head * DV
            value = slot_refs[slot][:, first : first + DV].astype(bf16)
            numer[head] = numer[head] + dot_n(score, value)
            denom[head] = denom[head] + jnp.sum(score.astype(f32), axis=1, keepdims=True)
    for head in range(heads):
        span = slice(head * DV, (head + 1) * DV)
        mean = numer[head] / denom[head]
        att_ref[:, span] = (valid * mean).astype(bf16)
        mean_ref[:, span] = mean
        inverse_ref[:, span] = jnp.broadcast_to(valid / denom[head], (rows, DV))


def query_kernel(heads, slots, col_ref, row_ref, numer_ref, denom_ref, *refs):
    slot_refs, out_ref = refs[:slots], refs[slots]
    rows = col_ref.shape[0]
    qk = heads * FEAT
    own_pos, own_doc = col_ref[:, 0:1], col_ref[:, 1:2]
    query = slot_refs[0][:, :qk]
    queries = [
        two_parts(jnp.where(head_lanes(rows, qk, head), query, 0.0)) for head in range(heads)
    ]
    sums = [jnp.zeros((rows, qk), f32) for _ in range(heads)]
    for slot in range(slots):
        allowed = (row_ref[slot : slot + 1, :] <= own_pos) & (
            row_ref[slots + slot : slots + slot + 1, :] == own_doc
        )
        keys = two_parts(slot_refs[slot][:, qk : 2 * qk])
        for head in range(heads):
            near = quarter_dot(queries[head], keys)
            first = 2 * qk + head * DV
            value = slot_refs[slot][:, first : first + DV].astype(bf16)
            grad = dot_t(numer_ref[:, head * DV : (head + 1) * DV].astype(bf16), value)
            grad = grad + denom_ref[:, head * DV : head * DV + 1]
            grad = jnp.where(allowed, grad * (1.0 + near), 0.0).astype(bf16)
            sums[head] = sums[head] + dot_n(grad, keys[0])
    total = jnp.zeros((rows, qk), f32)
    for head in range(heads):
        total = jnp.where(head_lanes(rows, qk, head), 0.25 * sums[head], total)
    out_ref[...] = total.astype(bf16)


def key_kernel(heads, slots, col_ref, row_ref, *refs):
    slot_refs, grad_refs, out_ref = refs[:slots], refs[slots : 2 * slots], refs[2 * slots]
    rows = col_ref.shape[0]
    qk = heads * FEAT
    own_pos, own_doc = col_ref[:, 0:1], col_ref[:, 3:4]
    own = slot_refs[0]
    key = own[:, qk : 2 * qk]
    keys = [two_parts(jnp.where(head_lanes(rows, qk, head), key, 0.0)) for head in range(heads)]
    values = [
        own[:, 2 * qk + head * DV : 2 * qk + (head + 1) * DV].astype(bf16) for head in range(heads)
    ]
    key_sums = [jnp.zeros((rows, qk), f32) for _ in range(heads)]
    value_sums = [jnp.zeros((rows, DV), f32) for _ in range(heads)]
    for slot in range(slots):
        allowed = (row_ref[slot : slot + 1, :] >= own_pos) & (
            row_ref[2 * slots + slot : 2 * slots + slot + 1, :] == own_doc
        )
        queries = two_parts(slot_refs[slot][:, :qk])
        for head in range(heads):
            near = quarter_dot(keys[head], queries)
            numer = grad_refs[slot][:rows, head * DV : (head + 1) * DV].astype(bf16)
            lane = (head * rows) % (heads * DV)
            line = rows + (head * rows) // (heads * DV)
            grad = dot_t(values[head], numer) + grad_refs[slot][line : line + 1, lane : lane + rows]
            grad = jnp.where(allowed, grad * (1.0 + near), 0.0).astype(bf16)
            key_sums[head] = key_sums[head] + dot_n(grad, queries[0])
            score = jnp.where(allowed, 1.0 + near + 0.5 * near * near, 0.0).astype(bf16)
            value_sums[head] = value_sums[head] + dot_n(score, numer)
    total = jnp.zeros((rows, qk), f32)
    for head in range(heads):
        total = jnp.where(head_lanes(rows, qk, head), 0.25 * key_sums[head], total)
        out_ref[:, qk + head * DV : qk + (head + 1) * DV] = value_sums[head].astype(bf16)
    out_ref[:, :qk] = total.astype(bf16)


def whole_call(body, outs, *operands, flops=0):
    moved = sum(x.size * x.dtype.itemsize for x in (*operands, *outs))
    return pl.pallas_call(
        body,
        out_shape=outs,
        in_specs=[pl.BlockSpec(memory_space=pltpu.VMEM)] * len(operands),
        out_specs=jax.tree.map(lambda _: pl.BlockSpec(memory_space=pltpu.VMEM), outs),
        compiler_params=pltpu.CompilerParams(vmem_limit_bytes=VMEM_LIMIT),
        cost_estimate=pl.CostEstimate(flops=flops, bytes_accessed=moved, transcendentals=0),
    )(*operands)


def join_kernel(slots, *refs):
    step = pl.program_id(0)
    for slot in range(slots):

        @pl.when(step == slot)
        def _():
            refs[-1][...] = refs[slot][...].astype(bf16)


def join_rounded(parts):
    rows, width = parts[0].shape
    count = len(parts)
    cut = 512
    return pl.pallas_call(
        functools.partial(join_kernel, count),
        grid=(count, width // cut),
        out_shape=jax.ShapeDtypeStruct((count * rows, width), bf16),
        in_specs=[
            pl.BlockSpec(
                (rows, cut),
                functools.partial(
                    lambda slot, i, j: (
                        0,
                        jnp.where(i == slot, j, jnp.where(i < slot, 0, width // cut - 1)),
                    ),
                    slot,
                ),
            )
            for slot in range(count)
        ],
        out_specs=pl.BlockSpec((rows, cut), lambda i, j: (i, j)),
        compiler_params=pltpu.CompilerParams(vmem_limit_bytes=VMEM_LIMIT),
        cost_estimate=pl.CostEstimate(
            flops=0, bytes_accessed=6 * count * rows * width, transcendentals=0
        ),
    )(*parts)


def norm_back(grad_out, values, inverse, gain):
    scaled = grad_out * gain
    return inverse * (
        scaled - values * inverse * inverse * jnp.mean(scaled * values, axis=-1, keepdims=True)
    )


def mm(left, right):
    return jnp.dot(left, right, preferred_element_type=f32)


def mm_t(left, right):
    return jnp.einsum("ac,bc->ab", left, right, preferred_element_type=f32)


def t_mm(left, right):
    return jnp.einsum("ca,cb->ab", left, right, preferred_element_type=f32)


def gated(gate, up_lin, hidden_grad):
    sigmoid = jax.nn.sigmoid(gate)
    silu = gate * sigmoid
    return (
        (silu * up_lin).astype(bf16),
        (hidden_grad * up_lin * sigmoid * (1.0 + gate * (1.0 - sigmoid))).astype(bf16),
        (hidden_grad * silu).astype(bf16),
    )


def per_device(
    tokens,
    gain_attn,
    w_query,
    w_key,
    w_value,
    w_out,
    gain_mlp,
    w_gate,
    w_up,
    w_down,
    doc_lengths,
    cotangent,
):
    rows, width = tokens.shape
    heads = w_query.shape[1] // FEAT
    qk, vw = heads * FEAT, heads * DV
    blk_index, blk_count = lax.axis_index("blk"), lax.axis_size("blk")

    ends = [doc_lengths[0]]
    for doc in range(1, doc_lengths.shape[0]):
        ends.append(ends[-1] + doc_lengths[doc])

    def layout(positions):
        docs = sum((positions >= end).astype(jnp.int32) for end in ends[:-1])
        valid = positions < ends[-1]
        return docs, valid, jnp.where(valid, docs, -1)

    own_pos = blk_index * rows + jnp.arange(rows, dtype=jnp.int32)
    own_docs, own_valid, own_key_docs = layout(own_pos)
    columns = jnp.stack([own_pos, own_docs, own_valid.astype(jnp.int32), own_key_docs], axis=1)
    slot_blocks = blk_index ^ jnp.arange(blk_count, dtype=jnp.int32)
    slot_pos = slot_blocks[:, None] * rows + jnp.arange(rows, dtype=jnp.int32)[None, :]
    slot_docs, _, slot_key_docs = layout(slot_pos)
    lines = jnp.concatenate([slot_pos, slot_key_docs, slot_docs])

    gain_one, gain_two = gain_attn.astype(f32), gain_mlp.astype(f32)
    token_wide = tokens.astype(f32)
    inv_in = lax.rsqrt(jnp.mean(token_wide * token_wide, axis=-1, keepdims=True) + epsilon)
    normed_in = (token_wide * inv_in * gain_one).astype(bf16)
    w_qkv = jnp.concatenate([w_query, w_key, w_value], axis=1)
    qkv = gather_blk(mm(normed_in, w_qkv))

    cost = 16 * rows * rows * blk_count * vw
    attended, mean, inverse = whole_call(
        functools.partial(attend_kernel, heads, blk_count),
        (
            jax.ShapeDtypeStruct((rows, vw), bf16),
            jax.ShapeDtypeStruct((rows, vw), f32),
            jax.ShapeDtypeStruct((rows, vw), f32),
        ),
        columns,
        lines,
        *qkv,
        flops=cost,
    )
    resid_mid = token_wide + sum_head(mm(attended, w_out))
    inv_mid = lax.rsqrt(jnp.mean(resid_mid * resid_mid, axis=-1, keepdims=True) + epsilon)
    scaled_mid = resid_mid * inv_mid

    normed_mid = (scaled_mid * gain_two).astype(bf16)
    hidden, gate_lin_grad, up_lin_grad = gated(
        mm(normed_mid, w_gate), mm(normed_mid, w_up), mm_t(cotangent, w_down)
    )
    mid_part = mm_t(gate_lin_grad, w_gate) + mm_t(up_lin_grad, w_up)
    mlp_part = mm(hidden, w_down)
    mid_grad = sum_head(mid_part)
    output = (resid_mid + sum_head(mlp_part)).astype(bf16)

    all_cot = join_rounded(gather_blk(cotangent.astype(f32)))
    all_mid = join_rounded([part * gain_two for part in gather_blk(scaled_mid)])
    all_hidden, all_gate_grad, all_up_grad = gated(
        mm(all_mid, w_gate), mm(all_mid, w_up), mm_t(all_cot, w_down)
    )
    down_w_grad = t_mm(all_hidden, all_cot)
    gate_w_grad = t_mm(all_mid, all_gate_grad)
    up_w_grad = t_mm(all_mid, all_up_grad)

    resid_grad = cotangent.astype(f32) + norm_back(mid_grad, resid_mid, inv_mid, gain_two)
    out_lin_grad = resid_grad.astype(bf16)
    out_w_grad = sum_blk(t_mm(attended, out_lin_grad))
    attended_grad = mm_t(out_lin_grad, w_out)
    numer_grad = attended_grad * inverse
    denom_grad = -jnp.sum((numer_grad * mean).reshape(rows, heads, DV), axis=-1)
    denom_lines = denom_grad.T.reshape(rows // DV, vw)
    denom_lines = jnp.pad(denom_lines, ((0, -denom_lines.shape[0] % 8), (0, 0)))
    grads = gather_blk(jnp.concatenate([numer_grad, denom_lines]))
    (query_lin_grad,) = whole_call(
        functools.partial(query_kernel, heads, blk_count),
        (jax.ShapeDtypeStruct((rows, qk), bf16),),
        columns,
        lines,
        numer_grad,
        jnp.repeat(denom_grad, DV, axis=1),
        *qkv,
        flops=cost,
    )
    (key_value_grad,) = whole_call(
        functools.partial(key_kernel, heads, blk_count),
        (jax.ShapeDtypeStruct((rows, qk + vw), bf16),),
        columns,
        lines,
        *qkv,
        *grads,
        flops=2 * cost,
    )
    lin_grads = jnp.concatenate([query_lin_grad, key_value_grad], axis=1)
    in_part = mm_t(lin_grads, w_qkv)
    qkv_w_grad = sum_blk(t_mm(normed_in, lin_grads))
    in_grad = sum_head(in_part)
    input_grad = resid_grad + norm_back(in_grad, token_wide, inv_in, gain_one)
    gain_grads = lax.psum(
        jnp.stack(
            [
                jnp.sum(in_part * token_wide * inv_in, axis=0),
                jnp.sum(mid_part * scaled_mid, axis=0),
            ]
        ),
        ("blk", "head"),
    )
    return (
        output,
        input_grad,
        gain_grads[0],
        qkv_w_grad[:, :qk],
        qkv_w_grad[:, qk : 2 * qk],
        qkv_w_grad[:, 2 * qk :],
        out_w_grad,
        gain_grads[1],
        gate_w_grad,
        up_w_grad,
        down_w_grad,
    )


def solution(mesh):
    in_specs = (
        P("blk", None),
        P(),
        P(None, "head"),
        P(None, "head"),
        P(None, "head"),
        P("head", None),
        P(),
        P(None, "head"),
        P(None, "head"),
        P("head", None),
        P(),
        P("blk", None),
    )
    out_specs = (
        P("blk", None),
        P("blk", None),
        P(),
        P(None, "head"),
        P(None, "head"),
        P(None, "head"),
        P("head", None),
        P(),
        P(None, "head"),
        P(None, "head"),
        P("head", None),
    )
    return jax.shard_map(
        per_device, mesh=mesh, in_specs=in_specs, out_specs=out_specs, check_vma=False
    )
```

time: 1110 us -> 756 us (0.68)
  waiting for transfers between devices: 802 us -> 278 us
  matrix products: 73.1 us -> 167 us
  Pallas kernels: 0 us -> 87.6 us
  starting transfers between devices: 1.16 us -> 45.4 us
  local copies, waits for them, and re-layouts: 59.3 us -> 34.6 us
  blocking collectives: 60.2 us -> 39.3 us
  other arithmetic: 93.4 us -> 76.5 us
    psum x4 -> x3, waiting for transfers between devices: 779 us -> 156 us  [sum_head(): return lax.psum(value, 'head')]
    ppermute x0 -> x56, waiting for transfers between devices: none -> 122 us  [hop(): return lax.ppermute(value, axis, [(i, i ^ bit) for i in range(count)])]
    dot_general x35 -> x18, matrix products: 73.1 us -> 167 us  [the longest x5 77.7 us: t_mm(): return jnp.einsum('ca,cb->ab', left, right, preferred_element_type=f32)]
    pallas_call x0 -> x5, Pallas kernels: none -> 87.6 us  [the longest x2 46.5 us: join_rounded(): pl.pallas_call(functools.partial(join_kernel, count), grid=(count, width...]
    ppermute x0 -> x56, starting transfers between devices: none -> 44.9 us  [hop(): return lax.ppermute(value, axis, [(i, i ^ bit) for i in range(count)])]
    select_n x29 -> x19, other arithmetic: 53.4 us -> 12.5 us  [the longest x8 7.31 us: fold(): jnp.where(upper, low, high)]
    unnamed x165 -> x121, local copies, waits for them, and re-layouts: 52.1 us -> 15.6 us
    all_gather x2 -> x0, waiting for transfers between devices: 23.4 us -> none  [carried_in(): pieces = jax.tree.map(lambda part: lax.all_gather(part, axis), value)]
  transfers between devices with their start and end apart: 6 -> 59, of which waited for: 6 -> 21; matrix products, arithmetic and copies ran while one was open for 5% -> 31% of each run, Pallas kernels for 0% -> 12%
where the time goes in v1:
time: 756 us; the launch traced here: 746 us
  waiting for transfers between devices  278 us (37%)
  matrix products  167 us (22%)
  Pallas kernels  87.6 us (12%)
  other arithmetic  76.5 us (10%)
  starting transfers between devices  45.4 us (6%)
  blocking collectives  39.3 us (5%)
  local copies, waits for them, and re-layouts  34.6 us (5%)
  between operations  17.4 us (2%)
    psum x3, waiting for transfers between devices, sum_head(): return lax.psum(value, 'head')  156 us
    ppermute x56, waiting for transfers between devices, hop(): return lax.ppermute(value, axis, [(i, i ^ bit) for i in range(count)])  122 us
    dot_general x5, matrix products, t_mm(): return jnp.einsum('ca,cb->ab', left, right, preferred_element_type=f32)  77.7 us
    dot_general x7, matrix products, mm(): return jnp.dot(left, right, preferred_element_type=f32)  57.6 us
    pallas_call x2, Pallas kernels, join_rounded(): pl.pallas_call(functools.partial(join_kernel, count), grid=(count, width...  46.5 us
    ppermute x56, starting transfers between devices, hop(): return lax.ppermute(value, axis, [(i, i ^ bit) for i in range(count)])  44.9 us
    pallas_call x3, Pallas kernels, whole_call(): pl.pallas_call(body, out_shape=outs, in_specs=[pl.BlockSpec(memory_space=...  41.1 us
    psum x1, blocking collectives, per_device(): lax.psum(jnp.stack([jnp.sum(in_part * token_wide * inv_in, axis=0), jnp.s...  39.3 us
  transfers between devices with their start and end apart: 59, of which 21 were waited for; matrix products, arithmetic and copies ran while one was open for 31% of the time, Pallas kernels for 12%

profile of v1, /device:TPU:0, one launch (start us, length us, event | category | flops | bytes accessed | tf_op | source)
XLA Modules:
  0.0 745.9 jit_solution(472562794247461406)
XLA Ops:
  9.7 2.0 copy.28
  11.6 2.0 copy.29
  13.6 3.9 fusion.19.refs_0_
  17.5 2.9 collective-permute-start.1
  25.9 9.6 %collective-permute-done.1.refs_2_ = f32[256,640]{1,0:T(8,128)} collective-permute-done((f32[256,640]{1,0:T(8,128)}, f32[256,640]{1,0:T(8,128)}, u32[]{:S(2)}, u32[]{:S(2)}) %collective-permute-start.1) | collective-permute-done | bytes 655392 | tf_op jit(solution)/shard_map/ppermute | solution.py:20
  44.2 2.8 convert_element_type.120.refs_0_
  47.7 2.3 collective-permute-done.6
  54.2 14.4 %shard_map.203 = (bf16[256,512]{1,0:T(8,128)(2,1)}, f32[256,512]{1,0:T(8,128)}, f32[256,512]{1,0:T(8,128)}) custom-call(s32[256,4]{1,0:T(8,128)} %copy.30.col_ref, s32[24,256]{1,0:T(8,128)} %pad_add_fusion.row_ref, f32[256,640]{1,0:T(8,128)} %fusion.19.refs_0_, f32[256,640]{1,0:T(8,128)} %collective-permute-done.refs_1_, ...), custom_call_target="tpu_custom_call" | custom-call | flops 4294967296 | bytes 6582272 | tf_op jit(solution)/shard_map/pallas_call | solution.py:188
  68.7 3.0 fusion.57
  72.3 27.1 %collective-permute-done.50.refs_4_ = f32[256,2048]{1,0:T(8,128)} collective-permute-done((f32[256,2048]{1,0:T(8,128)}, f32[256,2048]{1,0:T(8,128)}, u32[]{:S(2)}, u32[]{:S(2)}) %collective-permute-start.50) | collective-permute-done | bytes 2097184 | tf_op jit(solution)/shard_map/ppermute | solution.py:20
  99.5 2.3 slice.83
  103.3 2.3 slice.82
  106.1 52.5 %all-reduce.6.cloned.1.call-done = f32[256,2048]{1,0:T(8,128)} async-done(((f32[256,2048]{1,0:T(8,128)}), f32[256,2048]{1,0:T(8,128)}) %all-reduce.6.cloned.1.call-update) | async-done | bytes 2097168 | tf_op jit(solution)/shard_map/psum | solution.py:64
  158.5 2.1 multiply_reduce_fusion.2
  160.7 2.4 broadcast_multiply_fusion.5
  166.1 4.6 fusion.58
  171.4 3.1 pad_maximum_fusion.5.refs_6_
  174.5 4.5 fusion.29
  179.0 4.9 fusion.27
  183.9 26.9 %collective-permute-done.39 = f32[256,2048]{1,0:T(8,128)} collective-permute-done((f32[256,2048]{1,0:T(8,128)}, f32[256,2048]{1,0:T(8,128)}, u32[]{:S(2)}, u32[]{:S(2)}) %collective-permute-start.39) | collective-permute-done | bytes 2097184 | tf_op jit(solution)/shard_map/ppermute | solution.py:20
  212.0 2.1 fusion.21
  214.2 2.3 slice.84
  216.5 2.3 slice.85
  221.1 3.2 convolution_add_fusion
  224.6 6.7 fusion.20
  231.3 3.1 pad_maximum_fusion.6.refs_7_
  234.4 22.7 %shard_map.207 = bf16[2048,2048]{1,0:T(8,128)(2,1)} custom-call(f32[256,2048]{1,0:T(8,128)} %convert_element_type.120.refs_0_, f32[256,2048]{1,0:T(8,128)} %collective-permute-done.47.refs_1_, f32[256,2048]{1,0:T(8,128)} %collective-permute-done.48.refs_2_, f32[256,2048]{1,0:T(8,128)} %collective-permute-done.49.refs_3_, ...), custom_call_target="tpu_custom_call" | custom-call | bytes 25165824 | tf_op jit(solution)/shard_map/pallas_call | solution.py:211
  258.1 18.5 %fusion.59 = f32[2048,1376]{0,1:T(8,128)} fusion(bf16[2048,2048]{1,0:T(8,128)(2,1)} %shard_map.207, bf16[1376,2048]{1,0:T(8,128)(2,1)} %param.21), kind=kOutput, calls=%fused_computation.160 | convolution fusion | flops 11542724608 | bytes 25296896 | tf_op jit(solution)/shard_map/ac,bc->ab/dot_general | solution.py:248
  276.6 32.4 %all-reduce.8.cloned.1.call-done = f32[256,2048]{1,0:T(8,128)} async-done(((f32[256,2048]{1,0:T(8,128)}), f32[256,2048]{1,0:T(8,128)}) %all-reduce.8.cloned.1.call-update) | async-done | bytes 2097168 | tf_op jit(solution)/shard_map/psum | solution.py:64
  309.0 2.8 multiply_reduce_fusion.1
  312.7 12.8 %multiply_reduce_fusion = (f32[2048]{0:T(1024)}, f32[256,2048]{1,0:T(8,128)S(1)}, f32[256,2048]{1,0:T(8,128)}, f32[256,2048]{1,0:T(8,128)}, f32[256,2048]{1,0:T(...) fusion(f32[256,2048]{1,0:T(8,128)S(1)} %copy-done.12, ...), kind=kLoop, calls=%fused_computation.37 | loop fusion | flops 9435136 | bytes 38815744 | tf_op jit(solution)/shard_map/reduce_sum | solution.py:380
  335.5 23.8 %shard_map.206 = bf16[2048,2048]{1,0:T(8,128)(2,1)} custom-call(f32[256,2048]{1,0:T(8,128)} %get-tuple-element.45.refs_0_, f32[256,2048]{1,0:T(8,128)} %get-tuple-element.93.refs_1_, f32[256,2048]{1,0:T(8,128)} %get-tuple-element.92.refs_2_, f32[256,2048]{1,0:T(8,128)} %get-tuple-element.91.refs_3_, f32[256,2048]{1,0:T(8,128)} %get-tuple-element.90.refs_4_, ...), custom_call_target="tpu_custom_call" | custom-call | bytes 25165824 | tf_op jit(solution)/shard_map/pallas_call | solution.py:211
  359.3 18.9 %fusion.61 = f32[2048,1376]{0,1:T(8,128)} fusion(bf16[2048,2048]{1,0:T(8,128)(2,1)} %shard_map.206, bf16[2048,1376]{0,1:T(8,128)(2,1)} %param.19), kind=kOutput, calls=%fused_computation.162 | convolution fusion | flops 11542724608 | bytes 25296896 | tf_op jit(solution)/shard_map/dot_general | solution.py:244
  378.3 15.8 %fusion.60 = f32[2048,1376]{0,1:T(8,128)} fusion(bf16[2048,2048]{1,0:T(8,128)(2,1)S(1)} %copy-done.10, bf16[2048,1376]{0,1:T(8,128)(2,1)} %param.20), kind=kOutput, calls=%fused_computation.161 | convolution fusion | flops 11542724608 | bytes 25296896 | tf_op jit(solution)/shard_map/dot_general | solution.py:244
  396.2 29.5 %fusion.3 = f32[2048,1376]{0,1:T(8,128)} fusion(bf16[2048,2048]{1,0:T(8,128)(2,1)} %shard_map.206, f32[2048,1376]{0,1:T(8,128)} %fusion.61, f32[2048,1376]{0,1:T(8,128)} %fusion.59, f32[2048,1376]{0,1:T(8,128)} %fusion.60), kind=kOutput, calls=%fused_computation.7 | convolution fusion | flops 11570905088 | bytes 53477376 | tf_op jit(solution)/shard_map/ca,cb->ab/dot_general | solution.py:252
  427.2 21.2 %fusion.2 = f32[1376,2048]{1,0:T(8,128)} fusion(bf16[2048,2048]{1,0:T(8,128)(2,1)} %shard_map.207, f32[2048,1376]{0,1:T(8,128)} %fusion.60, f32[2048,1376]{0,1:T(8,128)} %fusion.61), kind=kOutput, calls=%fused_computation.6 | convolution fusion | flops 11559632896 | bytes 42205184 | tf_op jit(solution)/shard_map/ca,cb->ab/dot_general | solution.py:252
  450.0 21.6 %fusion.1 = f32[2048,1376]{0,1:T(8,128)} fusion(bf16[2048,2048]{1,0:T(8,128)(2,1)} %shard_map.206, f32[2048,1376]{0,1:T(8,128)} %fusion.59, f32[2048,1376]{0,1:T(8,128)} %fusion.61), kind=kOutput, calls=%fused_computation.5 | convolution fusion | flops 11559632896 | bytes 42205184 | tf_op jit(solution)/shard_map/ca,cb->ab/dot_general | solution.py:252
  473.8 13.2 %shard_map.204 = bf16[256,64]{1,0:T(8,128)(2,1)} custom-call(s32[256,4]{1,0:T(8,128)} %copy.30.col_ref, s32[24,256]{1,0:T(8,128)} %pad_add_fusion.row_ref, f32[256,512]{1,0:T(8,128)} %copy-done.27, f32[256,512]{1,0:T(8,128)} %bitcast.37, f32[256,640]{1,0:T(8,128)} %fusion.19.refs_0_, f32[256,640]{1,0:T(8,128)} %collective-permute-done.refs_1_, ...), custom_call_target="tpu_custom_call" | custom-call | flops 4294967296 | bytes 6352896 | tf_op jit(solution)/shard_map/pallas_call | solution.py:188
  490.3 13.4 %shard_map.205 = bf16[256,576]{1,0:T(8,128)(2,1)} custom-call(s32[256,4]{1,0:T(8,128)} %copy.30.col_ref, s32[24,256]{1,0:T(8,128)} %pad_add_fusion.row_ref, f32[256,640]{1,0:T(8,128)} %fusion.19.refs_0_, f32[256,640]{1,0:T(8,128)} %collective-permute-done.refs_1_, f32[256,640]{1,0:T(8,128)} %collective-permute-done.1.refs_2_, ...), custom_call_target="tpu_custom_call" | custom-call | flops 8589934592 | bytes 9891840 | tf_op jit(solution)/shard_map/pallas_call | solution.py:188
  503.7 4.7 fusion.31
  508.4 2.3 select_add_fusion.1
  516.2 2.4 fusion.18
  518.6 4.3 slice_select_fusion
  522.9 4.3 collective-permute-done.29
  528.6 2.0 select_add_fusion.5
  533.3 4.6 collective-permute-done.34
  541.0 3.4 collective-permute-done.35
  544.4 2.1 select_add_fusion
  550.7 10.4 %collective-permute-done.19 = f32[256,640]{1,0:T(8,128)S(1)} collective-permute-done((f32[256,640]{1,0:T(8,128)S(1)}, f32[256,640]{1,0:T(8,128)S(1)}, u32[]{:S(2)}, u32[]{:S(2)}) %collective-permute-start.19) | collective-permute-done | bytes 655392 | tf_op jit(solution)/shard_map/ppermute | solution.py:20
  561.1 5.1 collective-permute-done.23
  570.2 7.0 collective-permute-done.24
  577.7 3.7 collective-permute-done.20
  583.0 4.4 collective-permute-done.25
  589.0 3.2 collective-permute-done.21
  594.4 7.5 collective-permute-done.26
  605.0 70.7 %all-reduce.10.cloned.1.call-done = (f32[256,2048]{1,0:T(8,128)}, f32[256,2048]{1,0:T(8,128)}) async-done(((f32[256,2048]{1,0:T(8,128)}, f32[256,2048]{1,0:T(8,128)}), (f32[256,2048]{1,0:T(8,128)}, f32[256,2048]{1,0:T(8,128)})) %all-reduce.10.cloned.1.call-update) | async-done | bytes 4194320 | tf_op jit(solution)/shard_map/psum | solution.py:64
  675.7 3.0 fusion.14
  678.7 39.3 %psum.39 = f32[2,2048]{1,0:T(2,128)S(1)} all-reduce(f32[2,2048]{1,0:T(2,128)S(1)} %pad_maximum_fusion.20), channel_id=1, replica_groups=mesh['blk'=8,'head'=4] {'blk','head'}, use_global_device_ids=true, to_apply=%region_11.12 | all-reduce | flops 4096 | bytes 32768 | tf_op jit(solution)/shard_map/psum | solution.py:376
  718.7 6.6 fusion.10
  725.3 1.9 broadcast_select_fusion.3
  727.3 2.4 pad_maximum_fusion.1
  729.7 2.1 broadcast_select_fusion.1
  733.1 2.6 pad_maximum_fusion
  735.7 2.3 copy.35
  (286 shorter events, 84.4 us)
Async XLA Ops:
  7.2 61.5 %copy-start = (bf16[512,2048]{1,0:T(8,128)(2,1)S(1)}, bf16[512,2048]{1,0:T(8,128)(2,1)}, u32[]{:S(2)}) copy-start(bf16[512,2048]{1,0:T(8,128)(2,1)} %param.17) | copy-start | bytes 6291460
  7.2 151.3 %all-reduce.6.cloned.1.call-start = ((), (), s32[]{:S(2)}) async-start(), calls=%async_computation | async-start | bytes 4194304 | tf_op jit(solution)/shard_map/psum | solution.py:64
  17.5 18.0 %collective-permute-start.1 = (f32[256,640]{1,0:T(8,128)}, f32[256,640]{1,0:T(8,128)}, u32[]{:S(2)}, u32[]{:S(2)}) collective-permute-start(f32[256,640]{1,0:T(8,128)} %fusion.19.refs_0_), channel_id=1, source_target_pairs={{0,8},{4,12},{8,0},{12,4},{16,24},{20,28},{24,16},{28,20},{1,9},{5... | collective-permute-start | bytes 1966088 | tf_op jit(solution)/shard_map/ppermute | solution.py:20
  20.4 19.2 %collective-permute-start.3 = (f32[256,640]{1,0:T(8,128)}, f32[256,640]{1,0:T(8,128)}, u32[]{:S(2)}, u32[]{:S(2)}) collective-permute-start(f32[256,640]{1,0:T(8,128)} %fusion.19.refs_0_), channel_id=1, source_target_pairs={{0,16},{4,20},{8,24},{12,28},{16,0},{20,4},{24,8},{28,12},{1,17},{... | collective-permute-start | bytes 1966088 | tf_op jit(solution)/shard_map/ppermute | solution.py:20
  22.0 31.4 %collective-permute-start = (f32[256,640]{1,0:T(8,128)}, f32[256,640]{1,0:T(8,128)}, u32[]{:S(2)}, u32[]{:S(2)}) collective-permute-start(f32[256,640]{1,0:T(8,128)} %fusion.19.refs_0_), channel_id=1, source_target_pairs={{0,4},{4,0},{8,12},{12,8},{16,20},{20,16},{24,28},{28,24},{1,5},{5... | collective-permute-start | bytes 1966088 | tf_op jit(solution)/shard_map/ppermute | solution.py:20
  37.2 9.8 %collective-permute-start.5 = (f32[128,640]{1,0:T(8,128)}, f32[128,640]{1,0:T(8,128)S(1)}, u32[]{:S(2)}, u32[]{:S(2)}) collective-permute-start(f32[128,640]{1,0:T(8,128)} %slice.76), channel_id=1, source_target_pairs={{0,16},{4,20},{8,24},{12,28},{16,0},{20,4},{24,8},{28,12},{1,17},{... | collective-permute-start | bytes 983048 | tf_op jit(solution)/shard_map/ppermute | solution.py:20
  41.4 8.6 %collective-permute-start.6 = (f32[128,640]{1,0:T(8,128)}, f32[128,640]{1,0:T(8,128)}, u32[]{:S(2)}, u32[]{:S(2)}) collective-permute-start(f32[128,640]{1,0:T(8,128)} %slice.77), channel_id=1, source_target_pairs={{0,8},{4,12},{8,0},{12,4},{16,24},{20,28},{24,16},{28,20},{1,9},{5... | collective-permute-start | bytes 983048 | tf_op jit(solution)/shard_map/ppermute | solution.py:20
  42.9 10.5 %collective-permute-start.4 = (f32[256,640]{1,0:T(8,128)}, f32[256,640]{1,0:T(8,128)}, u32[]{:S(2)}, u32[]{:S(2)}) collective-permute-start(f32[256,640]{1,0:T(8,128)} %collective-permute-done.3.refs_4_), channel_id=1, source_target_pairs={{0,4},{4,0},{8,12},{12,8},{16,20},{20,16},{24,28},{28,24},{1,5},{5... | collective-permute-start | bytes 1966088 | tf_op jit(solution)/shard_map/ppermute | solution.py:20
  42.9 10.5 %collective-permute-start.2 = (f32[256,640]{1,0:T(8,128)}, f32[256,640]{1,0:T(8,128)}, u32[]{:S(2)}, u32[]{:S(2)}) collective-permute-start(f32[256,640]{1,0:T(8,128)} %collective-permute-done.1.refs_2_), channel_id=1, source_target_pairs={{0,4},{4,0},{8,12},{12,8},{16,20},{20,16},{24,28},{28,24},{1,5},{5... | collective-permute-start | bytes 1966088 | tf_op jit(solution)/shard_map/ppermute | solution.py:20
  47.0 4.0 collective-permute-start.7
  50.0 1.8 collective-permute-start.8
  51.0 48.4 %collective-permute-start.50 = (f32[256,2048]{1,0:T(8,128)}, f32[256,2048]{1,0:T(8,128)}, u32[]{:S(2)}, u32[]{:S(2)}) collective-permute-start(f32[256,2048]{1,0:T(8,128)} %convert_element_type.120.refs_0_), channel_id=1, source_target_pairs={{0,16},{4,20},{8,24},{12,28},{16,0},{20,4},{24,8},{28,12},{1,17},{... | collective-permute-start | bytes 6291464 | tf_op jit(solution)/shard_map/ppermute | solution.py:20
  51.8 51.4 %collective-permute-start.48 = (f32[256,2048]{1,0:T(8,128)}, f32[256,2048]{1,0:T(8,128)}, u32[]{:S(2)}, u32[]{:S(2)}) collective-permute-start(f32[256,2048]{1,0:T(8,128)} %convert_element_type.120.refs_0_), channel_id=1, source_target_pairs={{0,8},{4,12},{8,0},{12,4},{16,24},{20,28},{24,16},{28,20},{1,9},{5... | collective-permute-start | bytes 6291464 | tf_op jit(solution)/shard_map/ppermute | solution.py:20
  71.7 237.3 %all-reduce.8.cloned.1.call-start = ((), (), s32[]{:S(2)}) async-start(), calls=%async_computation.1 | async-start | bytes 4194304 | tf_op jit(solution)/shard_map/psum | solution.py:64
  101.8 69.0 %collective-permute-start.53 = (f32[128,2048]{1,0:T(8,128)}, f32[128,2048]{1,0:T(8,128)}, u32[]{:S(2)}, u32[]{:S(2)}) collective-permute-start(f32[128,2048]{1,0:T(8,128)} %slice.83), channel_id=1, source_target_pairs={{0,8},{4,12},{8,0},{12,4},{16,24},{20,28},{24,16},{28,20},{1,9},{5... | collective-permute-start | bytes 3145736 | tf_op jit(solution)/shard_map/ppermute | solution.py:20
  105.6 65.8 %collective-permute-start.52 = (f32[128,2048]{1,0:T(8,128)}, f32[128,2048]{1,0:T(8,128)}, u32[]{:S(2)}, u32[]{:S(2)}) collective-permute-start(f32[128,2048]{1,0:T(8,128)} %slice.82), channel_id=1, source_target_pairs={{0,16},{4,20},{8,24},{12,28},{16,0},{20,4},{24,8},{28,12},{1,17},{... | collective-permute-start | bytes 3145736 | tf_op jit(solution)/shard_map/ppermute | solution.py:20
  163.2 47.7 %collective-permute-start.39 = (f32[256,2048]{1,0:T(8,128)}, f32[256,2048]{1,0:T(8,128)}, u32[]{:S(2)}, u32[]{:S(2)}) collective-permute-start(f32[256,2048]{1,0:T(8,128)} %get-tuple-element.46), channel_id=1, source_target_pairs={{0,8},{4,12},{8,0},{12,4},{16,24},{20,28},{24,16},{28,20},{1,9},{5... | collective-permute-start | bytes 6291464 | tf_op jit(solution)/shard_map/ppermute | solution.py:20
  164.6 47.4 %collective-permute-start.41 = (f32[256,2048]{1,0:T(8,128)}, f32[256,2048]{1,0:T(8,128)}, u32[]{:S(2)}, u32[]{:S(2)}) collective-permute-start(f32[256,2048]{1,0:T(8,128)} %get-tuple-element.46), channel_id=1, source_target_pairs={{0,16},{4,20},{8,24},{12,28},{16,0},{20,4},{24,8},{28,12},{1,17},{... | collective-permute-start | bytes 6291464 | tf_op jit(solution)/shard_map/ppermute | solution.py:20
  166.1 68.2 %collective-permute-start.47 = (f32[256,2048]{1,0:T(8,128)}, f32[256,2048]{1,0:T(8,128)}, u32[]{:S(2)}, u32[]{:S(2)}) collective-permute-start(f32[256,2048]{1,0:T(8,128)} %convert_element_type.120.refs_0_), channel_id=1, source_target_pairs={{0,4},{4,0},{8,12},{12,8},{16,20},{20,16},{24,28},{28,24},{1,5},{5... | collective-permute-start | bytes 6291464 | tf_op jit(solution)/shard_map/ppermute | solution.py:20
  170.8 48.0 %collective-permute-start.55 = (f32[128,2048]{1,0:T(8,128)}, f32[128,2048]{1,0:T(8,128)}, u32[]{:S(2)}, u32[]{:S(2)}) collective-permute-start(f32[128,2048]{1,0:T(8,128)} %collective-permute-done.53), channel_id=1, source_target_pairs={{0,4},{4,0},{8,12},{12,8},{16,20},{20,16},{24,28},{28,24},{1,5},{5... | collective-permute-start | bytes 3145736 | tf_op jit(solution)/shard_map/ppermute | solution.py:20
  171.3 48.9 %collective-permute-start.54 = (f32[128,2048]{1,0:T(8,128)}, f32[128,2048]{1,0:T(8,128)}, u32[]{:S(2)}, u32[]{:S(2)}) collective-permute-start(f32[128,2048]{1,0:T(8,128)} %collective-permute-done.52), channel_id=1, source_target_pairs={{0,4},{4,0},{8,12},{12,8},{16,20},{20,16},{24,28},{28,24},{1,5},{5... | collective-permute-start | bytes 3145736 | tf_op jit(solution)/shard_map/ppermute | solution.py:20
  174.5 37.5 %slice-start.2 = ((s8[5636096]{0:T(1024)(128)(4,1)}), s8[4194304]{0:T(1024)(128)(4,1)S(1)}, s32[]{:S(2)}) async-start(s8[5636096]{0:T(1024)(128)(4,1)} %bitcast.42), calls=%async_computation.5 | async-start | bytes 8388608
  179.0 42.1 %copy-start.49 = (f32[256,1376]{0,1:T(8,128)}, f32[256,1376]{0,1:T(8,128)S(1)}, u32[]{:S(2)}) copy-start(f32[256,1376]{0,1:T(8,128)S(1)} %fusion.29) | copy-start | bytes 4227076
  179.0 42.1 %slice-start.4 = ((s8[5636096]{0:T(1024)(128)(4,1)}), s8[4194304]{0:T(1024)(128)(4,1)S(1)}, s32[]{:S(2)}) async-start(s8[5636096]{0:T(1024)(128)(4,1)} %bitcast.44), calls=%async_computation.7 | async-start | bytes 8388608
  210.8 23.5 %collective-permute-start.51 = (f32[256,2048]{1,0:T(8,128)}, f32[256,2048]{1,0:T(8,128)}, u32[]{:S(2)}, u32[]{:S(2)}) collective-permute-start(f32[256,2048]{1,0:T(8,128)} %collective-permute-done.50.refs_4_), channel_id=1, source_target_pairs={{0,4},{4,0},{8,12},{12,8},{16,20},{20,16},{24,28},{28,24},{1,5},{5... | collective-permute-start | bytes 6291464 | tf_op jit(solution)/shard_map/ppermute | solution.py:20
  212.0 22.3 %collective-permute-start.49 = (f32[256,2048]{1,0:T(8,128)}, f32[256,2048]{1,0:T(8,128)}, u32[]{:S(2)}, u32[]{:S(2)}) collective-permute-start(f32[256,2048]{1,0:T(8,128)} %collective-permute-done.48.refs_2_), channel_id=1, source_target_pairs={{0,4},{4,0},{8,12},{12,8},{16,20},{20,16},{24,28},{28,24},{1,5},{5... | collective-permute-start | bytes 6291464 | tf_op jit(solution)/shard_map/ppermute | solution.py:20
  218.8 38.8 %collective-permute-start.43 = (f32[128,2048]{1,0:T(8,128)}, f32[128,2048]{1,0:T(8,128)}, u32[]{:S(2)}, u32[]{:S(2)}) collective-permute-start(f32[128,2048]{1,0:T(8,128)} %slice.84), channel_id=1, source_target_pairs={{0,16},{4,20},{8,24},{12,28},{16,0},{20,4},{24,8},{28,12},{1,17},{... | collective-permute-start | bytes 3145736 | tf_op jit(solution)/shard_map/ppermute | solution.py:20
  220.3 37.7 %collective-permute-start.44 = (f32[128,2048]{1,0:T(8,128)}, f32[128,2048]{1,0:T(8,128)}, u32[]{:S(2)}, u32[]{:S(2)}) collective-permute-start(f32[128,2048]{1,0:T(8,128)} %slice.85), channel_id=1, source_target_pairs={{0,8},{4,12},{8,0},{12,4},{16,24},{20,28},{24,16},{28,20},{1,9},{5... | collective-permute-start | bytes 3145736 | tf_op jit(solution)/shard_map/ppermute | solution.py:20
  224.3 451.4 %all-reduce.10.cloned.1.call-start = ((), (), s32[]{:S(2)}) async-start(), calls=%async_computation.2 | async-start | bytes 8388608 | tf_op jit(solution)/shard_map/psum | solution.py:64
  234.3 77.4 %collective-permute-start.38 = (f32[256,2048]{1,0:T(8,128)}, f32[256,2048]{1,0:T(8,128)}, u32[]{:S(2)}, u32[]{:S(2)}) collective-permute-start(f32[256,2048]{1,0:T(8,128)} %get-tuple-element.46), channel_id=1, source_target_pairs={{0,4},{4,0},{8,12},{12,8},{16,20},{20,16},{24,28},{28,24},{1,5},{5... | collective-permute-start | bytes 6291464 | tf_op jit(solution)/shard_map/ppermute | solution.py:20
  257.1 54.7 %collective-permute-start.40 = (f32[256,2048]{1,0:T(8,128)}, f32[256,2048]{1,0:T(8,128)}, u32[]{:S(2)}, u32[]{:S(2)}) collective-permute-start(f32[256,2048]{1,0:T(8,128)} %collective-permute-done.39), channel_id=1, source_target_pairs={{0,4},{4,0},{8,12},{12,8},{16,20},{20,16},{24,28},{28,24},{1,5},{5... | collective-permute-start | bytes 6291464 | tf_op jit(solution)/shard_map/ppermute | solution.py:20
  257.4 54.4 %collective-permute-start.42 = (f32[256,2048]{1,0:T(8,128)}, f32[256,2048]{1,0:T(8,128)}, u32[]{:S(2)}, u32[]{:S(2)}) collective-permute-start(f32[256,2048]{1,0:T(8,128)} %collective-permute-done.41), channel_id=1, source_target_pairs={{0,4},{4,0},{8,12},{12,8},{16,20},{20,16},{24,28},{28,24},{1,5},{5... | collective-permute-start | bytes 6291464 | tf_op jit(solution)/shard_map/ppermute | solution.py:20
  257.6 54.2 %collective-permute-start.45 = (f32[128,2048]{1,0:T(8,128)}, f32[128,2048]{1,0:T(8,128)}, u32[]{:S(2)}, u32[]{:S(2)}) collective-permute-start(f32[128,2048]{1,0:T(8,128)} %collective-permute-done.43), channel_id=1, source_target_pairs={{0,4},{4,0},{8,12},{12,8},{16,20},{20,16},{24,28},{28,24},{1,5},{5... | collective-permute-start | bytes 3145736 | tf_op jit(solution)/shard_map/ppermute | solution.py:20
  258.0 53.8 %collective-permute-start.46 = (f32[128,2048]{1,0:T(8,128)}, f32[128,2048]{1,0:T(8,128)}, u32[]{:S(2)}, u32[]{:S(2)}) collective-permute-start(f32[128,2048]{1,0:T(8,128)} %collective-permute-done.44), channel_id=1, source_target_pairs={{0,4},{4,0},{8,12},{12,8},{16,20},{20,16},{24,28},{28,24},{1,5},{5... | collective-permute-start | bytes 3145736 | tf_op jit(solution)/shard_map/ppermute | solution.py:20
  331.7 116.7 %collective-permute-start.12 = (f32[264,512]{1,0:T(8,128)}, f32[264,512]{1,0:T(8,128)}, u32[]{:S(2)}, u32[]{:S(2)}) collective-permute-start(f32[264,512]{1,0:T(8,128)} %select_maximum_fusion.refs_8_), channel_id=1, source_target_pairs={{0,16},{4,20},{8,24},{12,28},{16,0},{20,4},{24,8},{28,12},{1,17},{... | collective-permute-start | bytes 1622024 | tf_op jit(solution)/shard_map/ppermute | solution.py:20
  333.3 92.4 %collective-permute-start.10 = (f32[264,512]{1,0:T(8,128)}, f32[264,512]{1,0:T(8,128)}, u32[]{:S(2)}, u32[]{:S(2)}) collective-permute-start(f32[264,512]{1,0:T(8,128)} %select_maximum_fusion.refs_8_), channel_id=1, source_target_pairs={{0,8},{4,12},{8,0},{12,4},{16,24},{20,28},{24,16},{28,20},{1,9},{5... | collective-permute-start | bytes 1622024 | tf_op jit(solution)/shard_map/ppermute | solution.py:20
  334.7 153.9 %collective-permute-start.9 = (f32[264,512]{1,0:T(8,128)}, f32[264,512]{1,0:T(8,128)}, u32[]{:S(2)}, u32[]{:S(2)}) collective-permute-start(f32[264,512]{1,0:T(8,128)} %select_maximum_fusion.refs_8_), channel_id=1, source_target_pairs={{0,4},{4,0},{8,12},{12,8},{16,20},{20,16},{24,28},{28,24},{1,5},{5... | collective-permute-start | bytes 1622024 | tf_op jit(solution)/shard_map/ppermute | solution.py:20
  335.5 58.5 %copy-start.4 = (f32[512,2048]{1,0:T(8,128)}, f32[512,2048]{1,0:T(8,128)S(1)}, u32[]{:S(2)}) copy-start(f32[512,2048]{1,0:T(8,128)S(1)} %fusion.23) | copy-start | bytes 12582916
  395.7 112.7 %collective-permute-start.28 = (f32[256,2048]{1,0:T(8,128)}, f32[256,2048]{1,0:T(8,128)}, u32[]{:S(2)}, u32[]{:S(2)}) collective-permute-start(f32[256,2048]{1,0:T(8,128)} %slice_select_fusion.1), channel_id=1, source_target_pairs={{0,4},{4,0},{8,12},{12,8},{16,20},{20,16},{24,28},{28,24},{1,5},{5... | collective-permute-start | bytes 6291464 | tf_op jit(solution)/shard_map/ppermute | solution.py:20
  426.6 23.3 %collective-permute-start.14 = (f32[128,512]{1,0:T(8,128)S(1)}, f32[128,512]{1,0:T(8,128)S(1)}, u32[]{:S(2)}, u32[]{:S(2)}) collective-permute-start(f32[128,512]{1,0:T(8,128)S(1)} %slice.78), channel_id=1, source_target_pairs={{0,16},{4,20},{8,24},{12,28},{16,0},{20,4},{24,8},{28,12},{1,17},{... | collective-permute-start | bytes 786440 | tf_op jit(solution)/shard_map/ppermute | solution.py:20
  449.4 23.8 %collective-permute-start.15 = (f32[136,512]{1,0:T(8,128)S(1)}, f32[136,512]{1,0:T(8,128)S(1)}, u32[]{:S(2)}, u32[]{:S(2)}) collective-permute-start(f32[136,512]{1,0:T(8,128)S(1)} %slice.79), channel_id=1, source_target_pairs={{0,8},{4,12},{8,0},{12,4},{16,24},{20,28},{24,16},{28,20},{1,9},{5... | collective-permute-start | bytes 835592 | tf_op jit(solution)/shard_map/ppermute | solution.py:20
  450.0 23.3 %collective-permute-start.16 = (f32[128,512]{1,0:T(8,128)S(1)}, f32[128,512]{1,0:T(8,128)S(1)}, u32[]{:S(2)}, u32[]{:S(2)}) collective-permute-start(f32[128,512]{1,0:T(8,128)S(1)} %collective-permute-done.14), channel_id=1, source_target_pairs={{0,4},{4,0},{8,12},{12,8},{16,20},{20,16},{24,28},{28,24},{1,5},{5... | collective-permute-start | bytes 786440 | tf_op jit(solution)/shard_map/ppermute | solution.py:20
  472.7 15.9 %collective-permute-start.13 = (f32[264,512]{1,0:T(8,128)}, f32[264,512]{1,0:T(8,128)S(1)}, u32[]{:S(2)}, u32[]{:S(2)}) collective-permute-start(f32[264,512]{1,0:T(8,128)} %collective-permute-done.12.refs_12_), channel_id=1, source_target_pairs={{0,4},{4,0},{8,12},{12,8},{16,20},{20,16},{24,28},{28,24},{1,5},{5... | collective-permute-start | bytes 1622024 | tf_op jit(solution)/shard_map/ppermute | solution.py:20
  473.2 15.4 %collective-permute-start.11 = (f32[264,512]{1,0:T(8,128)}, f32[264,512]{1,0:T(8,128)S(1)}, u32[]{:S(2)}, u32[]{:S(2)}) collective-permute-start(f32[264,512]{1,0:T(8,128)} %collective-permute-done.10.refs_10_), channel_id=1, source_target_pairs={{0,4},{4,0},{8,12},{12,8},{16,20},{20,16},{24,28},{28,24},{1,5},{5... | collective-permute-start | bytes 1622024 | tf_op jit(solution)/shard_map/ppermute | solution.py:20
  473.3 14.5 %collective-permute-start.17 = (f32[136,512]{1,0:T(8,128)S(1)}, f32[136,512]{1,0:T(8,128)S(1)}, u32[]{:S(2)}, u32[]{:S(2)}) collective-permute-start(f32[136,512]{1,0:T(8,128)S(1)} %collective-permute-done.15), channel_id=1, source_target_pairs={{0,4},{4,0},{8,12},{12,8},{16,20},{20,16},{24,28},{28,24},{1,5},{5... | collective-permute-start | bytes 835592 | tf_op jit(solution)/shard_map/ppermute | solution.py:20
  513.1 14.1 %collective-permute-start.29 = (f32[64,2048]{1,0:T(8,128)}, f32[64,2048]{1,0:T(8,128)S(1)}, u32[]{:S(2)}, u32[]{:S(2)}) collective-permute-start(f32[64,2048]{1,0:T(8,128)} %get-tuple-element.61), channel_id=1, source_target_pairs={{0,8},{4,12},{8,0},{12,4},{16,24},{20,28},{24,16},{28,20},{1,9},{5... | collective-permute-start | bytes 1572872 | tf_op jit(solution)/shard_map/ppermute | solution.py:20
  514.7 13.9 %collective-permute-start.33 = (f32[64,2048]{1,0:T(8,128)}, f32[64,2048]{1,0:T(8,128)}, u32[]{:S(2)}, u32[]{:S(2)}) collective-permute-start(f32[64,2048]{1,0:T(8,128)} %get-tuple-element.62), channel_id=1, source_target_pairs={{0,16},{4,20},{8,24},{12,28},{16,0},{20,4},{24,8},{28,12},{1,17},{... | collective-permute-start | bytes 1572872 | tf_op jit(solution)/shard_map/ppermute | solution.py:20
  522.9 21.5 %collective-permute-start.18 = (f32[1024,640]{1,0:T(8,128)}, f32[1024,640]{1,0:T(8,128)}, u32[]{:S(2)}, u32[]{:S(2)}) collective-permute-start(f32[1024,640]{1,0:T(8,128)} %slice_select_fusion), channel_id=1, source_target_pairs={{0,4},{4,0},{8,12},{12,8},{16,20},{20,16},{24,28},{28,24},{1,5},{5... | collective-permute-start | bytes 7864328 | tf_op jit(solution)/shard_map/ppermute | solution.py:20
  530.7 7.2 collective-permute-start.34
  531.7 7.6 %collective-permute-start.30 = (f32[32,2048]{1,0:T(8,128)S(1)}, f32[32,2048]{1,0:T(8,128)S(1)}, u32[]{:S(2)}, u32[]{:S(2)}) collective-permute-start(f32[32,2048]{1,0:T(8,128)S(1)} %slice_select_fusion.9), channel_id=1, source_target_pairs={{0,16},{4,20},{8,24},{12,28},{16,0},{20,4},{24,8},{28,12},{1,17},{... | collective-permute-start | bytes 786440 | tf_op jit(solution)/shard_map/ppermute | solution.py:20
  537.9 6.5 collective-permute-start.35
  539.4 11.2 %collective-permute-start.31 = (f32[32,2048]{1,0:T(8,128)S(1)}, f32[32,2048]{1,0:T(8,128)S(1)}, u32[]{:S(2)}, u32[]{:S(2)}) collective-permute-start(f32[32,2048]{1,0:T(8,128)S(1)} %select_add_fusion.9), channel_id=1, source_target_pairs={{0,16},{4,20},{8,24},{12,28},{16,0},{20,4},{24,8},{28,12},{1,17},{... | collective-permute-start | bytes 786440 | tf_op jit(solution)/shard_map/ppermute | solution.py:20
  546.7 14.4 %collective-permute-start.19 = (f32[256,640]{1,0:T(8,128)S(1)}, f32[256,640]{1,0:T(8,128)S(1)}, u32[]{:S(2)}, u32[]{:S(2)}) collective-permute-start(f32[256,640]{1,0:T(8,128)S(1)} %get-tuple-element.57), channel_id=1, source_target_pairs={{0,8},{4,12},{8,0},{12,4},{16,24},{20,28},{24,16},{28,20},{1,9},{5... | collective-permute-start | bytes 1966088 | tf_op jit(solution)/shard_map/ppermute | solution.py:20
  548.5 17.7 %collective-permute-start.23 = (f32[256,640]{1,0:T(8,128)S(1)}, f32[256,640]{1,0:T(8,128)S(1)}, u32[]{:S(2)}, u32[]{:S(2)}) collective-permute-start(f32[256,640]{1,0:T(8,128)S(1)} %get-tuple-element.58), channel_id=1, source_target_pairs={{0,16},{4,20},{8,24},{12,28},{16,0},{20,4},{24,8},{28,12},{1,17},{... | collective-permute-start | bytes 1966088 | tf_op jit(solution)/shard_map/ppermute | solution.py:20
  550.0 27.6 %collective-permute-start.36 = (f32[64,2048]{1,0:T(8,128)S(1)}, f32[64,2048]{1,0:T(8,128)S(1)}, u32[]{:S(2)}, u32[]{:S(2)}) collective-permute-start(f32[64,2048]{1,0:T(8,128)S(1)} %pad_maximum_fusion.16), channel_id=1, source_target_pairs={{0,16},{4,20},{8,24},{12,28},{16,0},{20,4},{24,8},{28,12},{1,17},{... | collective-permute-start | bytes 1572872 | tf_op jit(solution)/shard_map/ppermute | solution.py:20
  566.5 10.7 %collective-permute-start.24 = (f32[128,640]{1,0:T(8,128)S(1)}, f32[128,640]{1,0:T(8,128)S(1)}, u32[]{:S(2)}, u32[]{:S(2)}) collective-permute-start(f32[128,640]{1,0:T(8,128)S(1)} %slice_select_fusion.6), channel_id=1, source_target_pairs={{0,8},{4,12},{8,0},{12,4},{16,24},{20,28},{24,16},{28,20},{1,9},{5... | collective-permute-start | bytes 983048 | tf_op jit(solution)/shard_map/ppermute | solution.py:20
  566.9 25.8 %collective-permute-start.32 = (f32[64,2048]{1,0:T(8,128)S(1)}, f32[64,2048]{1,0:T(8,128)S(1)}, u32[]{:S(2)}, u32[]{:S(2)}) collective-permute-start(f32[64,2048]{1,0:T(8,128)S(1)} %pad_maximum_fusion.15), channel_id=1, source_target_pairs={{0,8},{4,12},{8,0},{12,4},{16,24},{20,28},{24,16},{28,20},{1,9},{5... | collective-permute-start | bytes 1572872 | tf_op jit(solution)/shard_map/ppermute | solution.py:20
  568.7 12.7 %collective-permute-start.20 = (f32[128,640]{1,0:T(8,128)S(1)}, f32[128,640]{1,0:T(8,128)S(1)}, u32[]{:S(2)}, u32[]{:S(2)}) collective-permute-start(f32[128,640]{1,0:T(8,128)S(1)} %slice_select_fusion.7), channel_id=1, source_target_pairs={{0,16},{4,20},{8,24},{12,28},{16,0},{20,4},{24,8},{28,12},{1,17},{... | collective-permute-start | bytes 983048 | tf_op jit(solution)/shard_map/ppermute | solution.py:20
  577.2 10.2 %collective-permute-start.25 = (f32[128,640]{1,0:T(8,128)S(1)}, f32[128,640]{1,0:T(8,128)S(1)}, u32[]{:S(2)}, u32[]{:S(2)}) collective-permute-start(f32[128,640]{1,0:T(8,128)S(1)} %select_add_fusion.6), channel_id=1, source_target_pairs={{0,8},{4,12},{8,0},{12,4},{16,24},{20,28},{24,16},{28,20},{1,9},{5... | collective-permute-start | bytes 983048 | tf_op jit(solution)/shard_map/ppermute | solution.py:20
  581.5 10.7 %collective-permute-start.21 = (f32[128,640]{1,0:T(8,128)S(1)}, f32[128,640]{1,0:T(8,128)S(1)}, u32[]{:S(2)}, u32[]{:S(2)}) collective-permute-start(f32[128,640]{1,0:T(8,128)S(1)} %select_add_fusion.7), channel_id=1, source_target_pairs={{0,16},{4,20},{8,24},{12,28},{16,0},{20,4},{24,8},{28,12},{1,17},{... | collective-permute-start | bytes 983048 | tf_op jit(solution)/shard_map/ppermute | solution.py:20
  587.5 14.3 %collective-permute-start.26 = (f32[256,640]{1,0:T(8,128)S(1)}, f32[256,640]{1,0:T(8,128)S(1)}, u32[]{:S(2)}, u32[]{:S(2)}) collective-permute-start(f32[256,640]{1,0:T(8,128)S(1)} %pad_maximum_fusion.12), channel_id=1, source_target_pairs={{0,16},{4,20},{8,24},{12,28},{16,0},{20,4},{24,8},{28,12},{1,17},{... | collective-permute-start | bytes 1966088 | tf_op jit(solution)/shard_map/ppermute | solution.py:20
  592.3 10.7 %collective-permute-start.22 = (f32[256,640]{1,0:T(8,128)S(1)}, f32[256,640]{1,0:T(8,128)S(1)}, u32[]{:S(2)}, u32[]{:S(2)}) collective-permute-start(f32[256,640]{1,0:T(8,128)S(1)} %pad_maximum_fusion.11), channel_id=1, source_target_pairs={{0,8},{4,12},{8,0},{12,4},{16,24},{20,28},{24,16},{28,20},{1,9},{5... | collective-permute-start | bytes 1966088 | tf_op jit(solution)/shard_map/ppermute | solution.py:20
  594.4 130.9 %collective-permute-start.37 = (f32[256,2048]{1,0:T(8,128)}, f32[256,2048]{1,0:T(8,128)}, u32[]{:S(2)}, u32[]{:S(2)}) collective-permute-start(f32[256,2048]{1,0:T(8,128)} %pad_maximum_fusion.4), channel_id=1, source_target_pairs={{0,4},{4,0},{8,12},{12,8},{16,20},{20,16},{24,28},{28,24},{1,5},{5... | collective-permute-start | bytes 6291464 | tf_op jit(solution)/shard_map/ppermute | solution.py:20
  605.0 124.7 %collective-permute-start.27 = (f32[1024,640]{1,0:T(8,128)}, f32[1024,640]{1,0:T(8,128)}, u32[]{:S(2)}, u32[]{:S(2)}) collective-permute-start(f32[1024,640]{1,0:T(8,128)} %pad_maximum_fusion.3), channel_id=1, source_target_pairs={{0,4},{4,0},{8,12},{12,8},{16,20},{20,16},{24,28},{28,24},{1,5},{5... | collective-permute-start | bytes 7864328 | tf_op jit(solution)/shard_map/ppermute | solution.py:20
  (52 other events, 428.9 us)
Sparse Core Ops, SparseCore 0:
  71.8 86.6 all-reduce.5
  224.4 84.4 all-reduce.7
  523.1 152.5 all-reduce.9

commit v2 on v1

v2 whole, which is shorter than its diff:
```python
import functools

import jax
import jax.numpy as jnp
from jax import lax
from jax.experimental import pallas as pl
from jax.experimental.pallas import tpu as pltpu
from jax.sharding import PartitionSpec as P

FEAT = 16
DV = 128

epsilon = 1e-05
f32, bf16 = jnp.float32, jnp.bfloat16
VMEM_LIMIT = 56 * 1024 * 1024


def hop(value, axis, way):
    if isinstance(way, int):
        way = [(i, i ^ way) for i in range(lax.axis_size(axis))]
    return lax.ppermute(value, axis, way)


def after(value, *others):
    return lax.optimization_barrier((value, others))[0]


def gather_blk(value):
    count = lax.axis_size("blk")
    if count != 8:
        slots, bit = [value], 1
        while bit < count:
            slots = slots + [hop(slot, "blk", bit) for slot in slots]
            bit *= 2
        return [[slot] for slot in slots]
    half = value.shape[0] // 16 * 8
    low, high = value[:half], value[half:]
    x_low, y_high = hop(low, "blk", 2), hop(high, "blk", 4)
    x_high, y_low = hop(high, "blk", 2), hop(low, "blk", 4)
    own_pair = hop(value, "blk", 1)
    far_low, far_high = hop(x_low, "blk", 4), hop(y_high, "blk", 2)
    slots = [[value], [own_pair]]
    for slot in ([x_low, x_high], [y_low, y_high], [far_low, far_high]):
        slots += [slot, [hop(part, "blk", 1) for part in slot]]
    return slots


class Chain:
    def __init__(self, steps):
        self.steps, self.result = steps, None
        self.advance(None)

    def advance(self, values):
        try:
            self.due = self.steps.send(values)
        except StopIteration as end:
            self.due, self.result = [], end.value


class Convoy:
    def __init__(self):
        self.landed = ()

    def wave(self, chains, work=None, *operands):
        chains = [chain for chain in chains if chain.due]
        values = [after([value for value, _, _ in chain.due], self.landed) for chain in chains]
        flying = [
            [hop(value, axis, way) for value, (_, axis, way) in zip(sent, chain.due)]
            for sent, chain in zip(values, chains)
        ]
        result = None if work is None else work(*after(operands, values, self.landed))
        flying = after(flying, values if result is None else result)
        for chain, came in zip(chains, flying):
            chain.advance(came)
        self.landed = (flying, result)
        return result


def gather_steps(value, slots, even=False):
    count = lax.axis_size("blk")
    slots[0] = [value]
    if count != 8:
        bit = 1
        while bit < count:
            got = yield [(slots[slot][0], "blk", bit) for slot in range(bit)]
            slots.update({bit + slot: [part] for slot, part in enumerate(got)})
            bit *= 2
        return
    half = value.shape[0] // 16 * 8
    low, high = value[:half], value[half:]
    if even:
        x_low, y_high, own_pair = yield [(low, "blk", 2), (high, "blk", 4), (value, "blk", 1)]
        slots[1] = [own_pair]
        x_high, y_low = yield [(high, "blk", 2), (low, "blk", 4)]
        slots[2], slots[4] = [x_low, x_high], [y_low, y_high]
        slots[6] = yield [(x_low, "blk", 4), (y_high, "blk", 2)]
        first = yield [(x_low, "blk", 1), (y_high, "blk", 1)]
        second = yield [(x_high, "blk", 1), (y_low, "blk", 1)]
        slots[3], slots[5] = [first[0], second[0]], [second[1], first[1]]
    else:
        x_all, y_all, own_pair = yield [(value, "blk", way) for way in (2, 4, 1)]
        slots[1], slots[2], slots[4] = [own_pair], [x_all], [y_all]
        *slots[6], x_pair, y_pair = yield [
            (x_all[:half], "blk", 4),
            (y_all[half:], "blk", 2),
            (x_all, "blk", 1),
            (y_all, "blk", 1),
        ]
        slots[3], slots[5] = [x_pair], [y_pair]
    slots[7] = yield [(part, "blk", 1) for part in slots[6]]


def halves(value, bit):
    low, high = jnp.split(value, 2)
    upper = (lax.axis_index("blk") & bit) != 0
    return jnp.where(upper, high, low), jnp.where(upper, low, high)


def paired(value, other, bit):
    upper = (lax.axis_index("blk") & bit) != 0
    return jnp.concatenate([jnp.where(upper, other, value), jnp.where(upper, value, other)])


def sum_steps(value):
    count = lax.axis_size("blk")
    bits = [1 << place for place in range(count.bit_length() - 1)]
    for bit in bits:
        keep, send = halves(value, bit)
        (got,) = yield [(send, "blk", bit)]
        value = keep + got
    for bit in reversed(bits):
        (got,) = yield [(value, "blk", bit)]
        value = paired(value, got, bit)
    return value


def small_steps(value):
    for axis in ("head", "blk"):
        bit = 1
        while bit < lax.axis_size(axis):
            (got,) = yield [(value, axis, bit)]
            value = value + got
            bit *= 2
    return value


def head_steps(value):
    count, mine = lax.axis_size("head"), lax.axis_index("head")
    rows = value.shape[0] // count

    def share(step):
        return lax.dynamic_slice_in_dim(value, (mine ^ step) * rows, rows)

    got = yield [(share(step), "head", step) for step in range(1, count)]
    total = share(0)
    for part in got:
        total = total + part
    got = yield [(total, "head", step) for step in range(1, count)]
    whole = jnp.zeros_like(value)
    for step, part in enumerate([total, *got]):
        whole = lax.dynamic_update_slice_in_dim(whole, part, (mine ^ step) * rows, 0)
    return whole


def line_steps(value, pieces):
    if lax.axis_size("head") != 4:
        return (yield from head_steps(value))
    mine = lax.axis_index("head")
    inner = (mine == 1) | (mine == 2)
    parts = jnp.split(value, pieces)
    pairs, whole, done = {}, {}, {}
    for wave in range(pieces + 2):
        sends, takes = [], []
        if wave < pieces:
            sends.append((parts[wave], "head", [(0, 1), (3, 2)]))
            takes.append((pairs, wave, parts))
        if 0 <= wave - 1 < pieces:
            sends.append((pairs[wave - 1], "head", [(1, 2), (2, 1)]))
            takes.append((whole, wave - 1, pairs))
        if 0 <= wave - 2:
            sends.append((whole[wave - 2], "head", [(1, 0), (2, 3)]))
            takes.append((done, wave - 2, whole))
        got = yield sends
        for part, (into, piece, own) in zip(got, takes):
            if into is done:
                into[piece] = jnp.where(inner, own[piece], part)
            else:
                into[piece] = own[piece] + part
    return jnp.concatenate([done[piece] for piece in range(pieces)])


def sum_head(value):
    return lax.psum(value, "head")


def dot_t(left, right):
    return lax.dot_general(left, right, (((1,), (1,)), ((), ())), preferred_element_type=f32)


def dot_n(left, right):
    return lax.dot_general(left, right, (((1,), (0,)), ((), ())), preferred_element_type=f32)


def head_lanes(rows, width, first):
    lanes = lax.broadcasted_iota(jnp.int32, (rows, width), 1)
    return (lanes >= first) & (lanes < first + FEAT)


def read(slot, lines, lanes):
    parts = [ref[:, lanes] for ref in slot]
    whole = parts[0] if len(parts) == 1 else jnp.concatenate(parts)
    return whole if lines is None else whole[lines]


def split_refs(refs, shape):
    slots, at = [], 0
    for pieces in shape:
        slots.append(refs[at : at + pieces])
        at += pieces
    return slots, refs[at:]


def turned(tile, heads, use_key):
    rows, width = tile.shape
    moved = jnp.concatenate([tile[:, width // 2 :], tile[:, : width // 2]], axis=1)
    base = 0 if use_key else width // 2
    scaled = moved * 0.25
    return [
        jnp.where(head_lanes(rows, width, base + head * FEAT), scaled, 0.0).astype(bf16)
        for head in range(heads)
    ]


def attend_kernel(heads, shape, col_ref, row_ref, *refs):
    slots, (att_ref, mean_ref, inverse_ref) = split_refs(refs, shape)
    count = len(slots)
    rows = col_ref.shape[0]
    qk = heads * FEAT
    own_pos, own_doc = col_ref[:, 0:1], col_ref[:, 1:2]
    valid = col_ref[:, 2:3].astype(f32)
    numer = [jnp.zeros((rows, DV), f32) for _ in range(heads)]
    denom = [jnp.zeros((rows, 1), f32) for _ in range(heads)]
    queries = turned(read(slots[0], None, slice(0, 2 * qk)), heads, False)
    for slot in range(count):
        allowed = (row_ref[slot : slot + 1, :] <= own_pos) & (
            row_ref[count + slot : count + slot + 1, :] == own_doc
        )
        keys = read(slots[slot], None, slice(0, 2 * qk)).astype(bf16)
        for head in range(heads):
            near = 1.0 + dot_t(queries[head], keys)
            score = jnp.where(allowed, 0.5 * near * near + 0.5, 0.0)
            first = 2 * qk + head * DV
            value = read(slots[slot], None, slice(first, first + DV)).astype(bf16)
            numer[head] = numer[head] + dot_n(score.astype(bf16), value)
            denom[head] = denom[head] + jnp.sum(score, axis=1, keepdims=True)
    for head in range(heads):
        span = slice(head * DV, (head + 1) * DV)
        mean = numer[head] / denom[head]
        att_ref[:, span] = (valid * mean).astype(bf16)
        mean_ref[:, span] = mean
        inverse_ref[:, span] = jnp.broadcast_to(valid / denom[head], (rows, DV))


def query_kernel(heads, shape, col_ref, row_ref, numer_ref, denom_ref, *refs):
    slots, (out_ref,) = split_refs(refs, shape)
    count = len(slots)
    rows = col_ref.shape[0]
    qk = heads * FEAT
    own_pos, own_doc = col_ref[:, 0:1], col_ref[:, 1:2]
    queries = turned(read(slots[0], None, slice(0, 2 * qk)), heads, False)
    sums = [jnp.zeros((rows, 2 * qk), f32) for _ in range(heads)]
    for slot in range(count):
        allowed = (row_ref[slot : slot + 1, :] <= own_pos) & (
            row_ref[count + slot : count + slot + 1, :] == own_doc
        )
        keys = read(slots[slot], None, slice(0, 2 * qk)).astype(bf16)
        for head in range(heads):
            near = 1.0 + dot_t(queries[head], keys)
            first = 2 * qk + head * DV
            value = read(slots[slot], None, slice(first, first + DV)).astype(bf16)
            grad = dot_t(numer_ref[:, head * DV : (head + 1) * DV].astype(bf16), value)
            grad = grad + denom_ref[:, head * DV : head * DV + 1]
            grad = jnp.where(allowed, grad * near, 0.0).astype(bf16)
            sums[head] = sums[head] + dot_n(grad, keys)
    total = jnp.zeros((rows, 2 * qk), f32)
    for head in range(heads):
        total = jnp.where(head_lanes(rows, 2 * qk, qk + head * FEAT), 0.25 * sums[head], total)
    out_ref[...] = total[:, qk:].astype(bf16)


def key_kernel(heads, shape, grad_shape, col_ref, row_ref, *refs):
    slots, rest = split_refs(refs, shape)
    grads, (key_ref, value_ref) = split_refs(rest, grad_shape)
    count = len(slots)
    rows = col_ref.shape[0]
    qk, vw = heads * FEAT, heads * DV
    own_pos, own_doc = col_ref[:, 0:1], col_ref[:, 3:4]
    keys = turned(read(slots[0], None, slice(0, 2 * qk)), heads, True)
    values = [
        read(slots[0], None, slice(2 * qk + head * DV, 2 * qk + (head + 1) * DV)).astype(bf16)
        for head in range(heads)
    ]
    key_sums = [jnp.zeros((rows, 2 * qk), f32) for _ in range(heads)]
    value_sums = [jnp.zeros((rows, DV), f32) for _ in range(heads)]
    for slot in range(count):
        allowed = (row_ref[slot : slot + 1, :] >= own_pos) & (
            row_ref[2 * count + slot : 2 * count + slot + 1, :] == own_doc
        )
        queries = read(slots[slot], None, slice(0, 2 * qk)).astype(bf16)
        last = grads[slot][-1]
        extra = last.shape[0] - (rows - sum(ref.shape[0] for ref in grads[slot][:-1]))
        base = last.shape[0] - extra
        for head in range(heads):
            near = 1.0 + dot_t(keys[head], queries)
            span = slice(head * DV, (head + 1) * DV)
            numer = read(grads[slot], slice(0, rows), span).astype(bf16)
            line, lane = base + (head * rows) // vw, (head * rows) % vw
            grad = dot_t(values[head], numer) + last[line : line + 1, lane : lane + rows]
            grad = jnp.where(allowed, grad * near, 0.0).astype(bf16)
            key_sums[head] = key_sums[head] + dot_n(grad, queries)
            score = jnp.where(allowed, 0.5 * near * near + 0.5, 0.0).astype(bf16)
            value_sums[head] = value_sums[head] + dot_n(score, numer)
    total = jnp.zeros((rows, 2 * qk), f32)
    for head in range(heads):
        total = jnp.where(head_lanes(rows, 2 * qk, head * FEAT), 0.25 * key_sums[head], total)
        value_ref[:, head * DV : (head + 1) * DV] = value_sums[head].astype(bf16)
    key_ref[...] = total[:, :qk].astype(bf16)


def whole_call(body, outs, *operands, flops=0):
    moved = sum(x.size * x.dtype.itemsize for x in (*operands, *outs))
    return pl.pallas_call(
        body,
        out_shape=outs,
        in_specs=[pl.BlockSpec(memory_space=pltpu.VMEM)] * len(operands),
        out_specs=jax.tree.map(lambda _: pl.BlockSpec(memory_space=pltpu.VMEM), outs),
        compiler_params=pltpu.CompilerParams(vmem_limit_bytes=VMEM_LIMIT),
        cost_estimate=pl.CostEstimate(flops=flops, bytes_accessed=moved, transcendentals=0),
    )(*operands)


def join_kernel(shape, scale_ref, *refs):
    slots, (out_ref,) = split_refs(refs, shape)
    step = pl.program_id(0)
    for slot in range(len(slots)):

        @pl.when(step == slot)
        def _():
            at = 0
            for ref in slots[slot]:
                out_ref[at : at + ref.shape[0], :] = (ref[...] * scale_ref[...]).astype(bf16)
                at += ref.shape[0]


def join_rounded(slots, scale):
    parts = [part for slot in slots for part in slot]
    rows, width = sum(part.shape[0] for part in slots[0]), parts[0].shape[1]
    count = len(slots)
    return pl.pallas_call(
        functools.partial(join_kernel, tuple(len(slot) for slot in slots)),
        grid=(count,),
        out_shape=jax.ShapeDtypeStruct((count * rows, width), bf16),
        in_specs=[pl.BlockSpec((1, width), lambda i: (0, 0))]
        + [
            pl.BlockSpec(part.shape, lambda i: (0, 0), pipeline_mode=pl.Buffered(1))
            for part in parts
        ],
        out_specs=pl.BlockSpec((rows, width), lambda i: (i, 0)),
        compiler_params=pltpu.CompilerParams(vmem_limit_bytes=VMEM_LIMIT),
        cost_estimate=pl.CostEstimate(
            flops=0, bytes_accessed=6 * count * rows * width, transcendentals=0
        ),
    )(scale[None, :], *parts)


def norm_back(grad_out, values, inverse, gain):
    scaled = grad_out * gain
    return inverse * (
        scaled - values * inverse * inverse * jnp.mean(scaled * values, axis=-1, keepdims=True)
    )


def mm(left, right):
    return jnp.dot(left, right, preferred_element_type=f32)


def mm_t(left, right):
    return jnp.einsum("ac,bc->ab", left, right, preferred_element_type=f32)


def t_mm(left, right):
    return jnp.einsum("ca,cb->ab", left, right, preferred_element_type=f32)


def gated(gate, up_lin, hidden_grad):
    sigmoid = 0.5 + 0.5 * jnp.tanh(0.5 * gate)
    silu = gate * sigmoid
    return (
        (silu * up_lin).astype(bf16),
        (hidden_grad * up_lin * sigmoid * (1.0 + gate * (1.0 - sigmoid))).astype(bf16),
        (hidden_grad * silu).astype(bf16),
    )


def per_device(
    tokens,
    gain_attn,
    w_query,
    w_key,
    w_value,
    w_out,
    gain_mlp,
    w_gate,
    w_up,
    w_down,
    doc_lengths,
    cotangent,
):
    rows, width = tokens.shape
    heads = w_query.shape[1] // FEAT
    qk, vw = heads * FEAT, heads * DV
    blk_index, blk_count = lax.axis_index("blk"), lax.axis_size("blk")

    ends = [doc_lengths[0]]
    for doc in range(1, doc_lengths.shape[0]):
        ends.append(ends[-1] + doc_lengths[doc])

    def layout(positions):
        docs = sum((positions >= end).astype(jnp.int32) for end in ends[:-1])
        valid = positions < ends[-1]
        return docs, valid, jnp.where(valid, docs, -1)

    own_pos = blk_index * rows + jnp.arange(rows, dtype=jnp.int32)
    own_docs, own_valid, own_key_docs = layout(own_pos)
    columns = jnp.stack([own_pos, own_docs, own_valid.astype(jnp.int32), own_key_docs], axis=1)
    slot_blocks = blk_index ^ jnp.arange(blk_count, dtype=jnp.int32)
    slot_pos = slot_blocks[:, None] * rows + jnp.arange(rows, dtype=jnp.int32)[None, :]
    slot_docs, _, slot_key_docs = layout(slot_pos)
    lines = jnp.concatenate([slot_pos, slot_key_docs, slot_docs])

    gain_one, gain_two = gain_attn.astype(f32), gain_mlp.astype(f32)
    token_wide, cot_wide = tokens.astype(f32), cotangent.astype(f32)
    inv_in = lax.rsqrt(jnp.mean(token_wide * token_wide, axis=-1, keepdims=True) + epsilon)
    normed_in = (token_wide * inv_in * gain_one).astype(bf16)
    qkv_own = jnp.concatenate(
        [mm(normed_in, w_query), mm(normed_in, w_key), mm(normed_in, w_value)], axis=1
    )
    qkv = gather_blk(qkv_own)
    shape = tuple(len(slot) for slot in qkv)
    qkv_parts = [part for slot in qkv for part in slot]

    cost = 8 * rows * rows * blk_count * vw
    attended, mean, inverse = whole_call(
        functools.partial(attend_kernel, heads, shape),
        (
            jax.ShapeDtypeStruct((rows, vw), bf16),
            jax.ShapeDtypeStruct((rows, vw), f32),
            jax.ShapeDtypeStruct((rows, vw), f32),
        ),
        columns,
        lines,
        *qkv_parts,
        flops=cost,
    )
    attn_part = mm(attended, w_out)
    attn_sum = sum_head(attn_part)
    convoy = Convoy()
    cot_slots = {}
    cot = Chain(gather_steps(after(cot_wide, qkv[-2]), cot_slots))
    own_hidden_grad = convoy.wave(
        [cot], lambda left, _: mm_t(left, w_down), cotangent, attn_part
    )
    token_sum = after(token_wide, convoy.landed) + attn_sum

    def middle(resid_mid):
        inv_mid = lax.rsqrt(jnp.mean(resid_mid * resid_mid, axis=-1, keepdims=True) + epsilon)
        scaled_mid = resid_mid * inv_mid
        normed_mid = (scaled_mid * gain_two).astype(bf16)
        hidden, gate_lin_grad, up_lin_grad = gated(
            mm(normed_mid, w_gate), mm(normed_mid, w_up), own_hidden_grad
        )
        mid_part = mm_t(gate_lin_grad, w_gate) + mm_t(up_lin_grad, w_up)
        return resid_mid, inv_mid, scaled_mid, hidden, mid_part

    resid_mid, inv_mid, scaled_mid, hidden, mid_part = convoy.wave([cot], middle, token_sum)

    def ready(chain, slots, wanted):
        while not all(slot in slots for slot in wanted):
            convoy.wave([chain])
        return [slots[slot] for slot in wanted]

    order = [0, 1, 2, 4, 3, 5, 6, 7] if blk_count == 8 else list(range(blk_count))
    early, late = order[: blk_count // 2], order[blk_count // 2 :]
    ones = jnp.ones_like(gain_two)
    mid_slots = {}
    mid_sum = Chain(line_steps(mid_part, 2))
    mid = Chain(gather_steps(scaled_mid, mid_slots, even=True))
    cot_early, cot_late = ready(cot, cot_slots, early), ready(cot, cot_slots, late)

    def share_work(hidden, *slots):
        mlp_part = mm(hidden, w_down)
        cot_a = join_rounded(after(slots[: len(early)], mlp_part), ones)
        return mlp_part, cot_a, join_rounded(after(slots[len(early) :], cot_a), ones)

    mlp_part, cot_a, cot_b = convoy.wave([mid_sum, mid], share_work, hidden, *cot_early, *cot_late)
    hidden_grad_a, hidden_grad_b = convoy.wave(
        [mid_sum, mid], lambda a, b: (mm_t(a, w_down), mm_t(b, w_down)), cot_a, cot_b
    )
    mlp = Chain(line_steps(mlp_part, 2))

    def gate_work(*slots):
        rows_of = join_rounded(slots, gain_two)
        return rows_of, mm(rows_of, w_gate)

    def up_work(rows_of, gate, hidden_grad):
        return gated(gate, mm(rows_of, w_up), hidden_grad)

    mid_a, gate_a = convoy.wave([mid_sum, mid, mlp], gate_work, *ready(mid, mid_slots, early))
    hidden_a, gate_grad_a, up_grad_a = convoy.wave(
        [mid_sum, mid, mlp], up_work, mid_a, gate_a, hidden_grad_a
    )
    while mid_sum.due:
        convoy.wave([mid_sum])
    mid_grad = mid_sum.result

    resid_grad = cot_wide + norm_back(mid_grad, resid_mid, inv_mid, gain_two)
    out_lin_grad = resid_grad.astype(bf16)
    attended_grad = mm_t(out_lin_grad, w_out)
    numer_grad = attended_grad * inverse
    denom_grad = -jnp.sum((numer_grad * mean).reshape(rows, heads, DV), axis=-1)
    denom_lines = denom_grad.T.reshape(rows // DV, vw)
    denom_lines = jnp.pad(denom_lines, ((0, -denom_lines.shape[0] % 8), (0, 0)))
    grad_slots = {}
    grads = Chain(gather_steps(jnp.concatenate([numer_grad, denom_lines]), grad_slots))

    def query_work(numer_grad, denom_grad, out_lin_grad):
        (query_lin_grad,) = whole_call(
            functools.partial(query_kernel, heads, shape),
            (jax.ShapeDtypeStruct((rows, qk), bf16),),
            columns,
            lines,
            numer_grad,
            jnp.repeat(denom_grad, DV, axis=1),
            *qkv_parts,
            flops=cost,
        )
        return query_lin_grad, t_mm(attended, after(out_lin_grad, query_lin_grad))

    query_lin_grad, out_part = convoy.wave(
        [grads, mid], query_work, numer_grad, denom_grad, out_lin_grad
    )
    out = Chain(sum_steps(out_part))
    down_a = convoy.wave([grads, out], t_mm, hidden_a, cot_a)
    convoy.wave([grads, mid])
    grad_slots = ready(grads, grad_slots, range(blk_count))
    grad_shape = tuple(len(slot) for slot in grad_slots)

    def key_work(query_lin_grad, grad_parts):
        key_lin_grad, value_grad = whole_call(
            functools.partial(key_kernel, heads, shape, grad_shape),
            (jax.ShapeDtypeStruct((rows, qk), bf16), jax.ShapeDtypeStruct((rows, vw), bf16)),
            columns,
            lines,
            *qkv_parts,
            *grad_parts,
            flops=2 * cost,
        )
        in_part = mm_t(query_lin_grad, w_query) + mm_t(key_lin_grad, w_key)
        in_part = in_part + mm_t(value_grad, w_value)
        return in_part, query_lin_grad, key_lin_grad, value_grad

    grad_parts = [part for slot in grad_slots for part in slot]
    in_part, *lin_grads = convoy.wave([], key_work, query_lin_grad, grad_parts)
    late_in = after(normed_in, in_part)
    parts = [t_mm(late_in, grad) for grad in lin_grads]
    gain_parts = jnp.stack(
        [
            jnp.sum(after(in_part, parts) * token_wide * inv_in, axis=0),
            jnp.sum(mid_part * scaled_mid, axis=0),
        ]
    )
    qkv_w_grads = lax.psum(tuple(parts), "blk")
    gains = Chain(small_steps(gain_parts))

    in_sum = Chain(line_steps(in_part, 2))
    mid_late = ready(mid, mid_slots, late)

    def third_work(hidden_b, down_a, gate_grad_a):
        down_w_grad = down_a + t_mm(hidden_b, cot_b)
        return down_w_grad, t_mm(mid_a, after(gate_grad_a, down_w_grad))

    def second_work(mid_b, gate_b, hidden_grad_b, up_grad_a):
        parts = up_work(mid_b, gate_b, hidden_grad_b)
        return (*parts, t_mm(mid_a, after(up_grad_a, parts)))

    def last_work(gate_grad_b, gate_part, up_grad_b, up_part, mlp_sum):
        gate_w_grad = gate_part + t_mm(mid_b, gate_grad_b)
        output = (resid_mid + after(mlp_sum, gate_w_grad)).astype(bf16)
        late_grad = after(up_grad_b, gate_w_grad, output, qkv_w_grads)
        return gate_w_grad, up_part + t_mm(mid_b, late_grad), output

    chains = [in_sum, out, gains, mlp]
    mid_b, gate_b = convoy.wave(chains, gate_work, *after(mid_late, parts))
    hidden_b, gate_grad_b, up_grad_b, up_part = convoy.wave(
        chains, second_work, mid_b, gate_b, hidden_grad_b, up_grad_a
    )
    down_w_grad, gate_part = convoy.wave(chains, third_work, hidden_b, down_a, gate_grad_a)
    while mlp.due:
        convoy.wave([mlp])
    gate_w_grad, up_w_grad, output = convoy.wave(
        chains, last_work, gate_grad_b, gate_part, up_grad_b, up_part, mlp.result
    )
    while any(chain.due for chain in chains):
        convoy.wave(chains)
    in_grad, out_w_grad, gain_grads = (chain.result for chain in chains[:3])
    input_grad = resid_grad + norm_back(in_grad, token_wide, inv_in, gain_one)
    return (
        output,
        input_grad,
        gain_grads[0],
        *qkv_w_grads,
        out_w_grad,
        gain_grads[1],
        gate_w_grad,
        up_w_grad,
        down_w_grad,
    )


def solution(mesh):
    in_specs = (
        P("blk", None),
        P(),
        P(None, "head"),
        P(None, "head"),
        P(None, "head"),
        P("head", None),
        P(),
        P(None, "head"),
        P(None, "head"),
        P("head", None),
        P(),
        P("blk", None),
    )
    out_specs = (
        P("blk", None),
        P("blk", None),
        P(),
        P(None, "head"),
        P(None, "head"),
        P(None, "head"),
        P("head", None),
        P(),
        P(None, "head"),
        P(None, "head"),
        P("head", None),
    )
    return jax.shard_map(
        per_device, mesh=mesh, in_specs=in_specs, out_specs=out_specs, check_vma=False
    )
```

time: 756 us -> 542 us (0.72)
  waiting for transfers between devices: 278 us -> 120 us
  blocking collectives: 39.3 us -> 0 us
  Pallas kernels: 87.6 us -> 53 us
  starting transfers between devices: 45.4 us -> 75.8 us
  other arithmetic: 76.5 us -> 56.4 us
    psum x3 -> x1, waiting for transfers between devices: 156 us -> 44.9 us  [sum_head(): return lax.psum(value, 'head')]
    ppermute x56 -> x73, waiting for transfers between devices: 122 us -> 75.2 us  [hop(): return lax.ppermute(value, axis, way)]
    psum x1 -> x0, blocking collectives: 39.3 us -> none  [per_device(): lax.psum(jnp.stack([jnp.sum(in_part * token_wide * inv_in, axis=0), jnp.s...]
    ppermute x56 -> x73, starting transfers between devices: 44.9 us -> 75.1 us  [hop(): return lax.ppermute(value, axis, way)]
    pallas_call x2 -> x4, Pallas kernels: 46.5 us -> 24.4 us  [join_rounded(): pl.pallas_call(functools.partial(join_kernel, tuple((len(slot) for slot i...]
    reduce_sum x3 -> x2, other arithmetic: 17.8 us -> 0.55 us  [the longest x1 0.33 us: per_device(): jnp.sum(after(in_part, parts) * token_wide * inv_in, axis=0)]
    add x8 -> x21, other arithmetic: 6.85 us -> 21.8 us  [the longest x12 15.7 us: line_steps(): into[piece] = own[piece] + part]
    pallas_call x3, Pallas kernels: 41.1 us -> 28.7 us  [whole_call(): pl.pallas_call(body, out_shape=outs, in_specs=[pl.BlockSpec(memory_space=...]
  transfers between devices with their start and end apart: 59 -> 75, of which waited for: 21 -> 23; matrix products, arithmetic and copies ran while one was open for 31% -> 40% of each run, Pallas kernels for 12% -> 8%
where the time goes in v2:
time: 542 us; the launch traced here: 532 us
  matrix products  173 us (32%)
  waiting for transfers between devices  120 us (22%)
  starting transfers between devices  75.8 us (14%)
  other arithmetic  56.4 us (10%)
  Pallas kernels  53 us (10%)
  local copies, waits for them, and re-layouts  35.3 us (7%)
  between operations  18.4 us (3%)
    ppermute x73, waiting for transfers between devices, hop(): return lax.ppermute(value, axis, way)  75.2 us
    ppermute x73, starting transfers between devices, hop(): return lax.ppermute(value, axis, way)  75.1 us
    dot_general x10, matrix products, t_mm(): return jnp.einsum('ca,cb->ab', left, right, preferred_element_type=f32)  72.9 us
    dot_general x11, matrix products, mm(): return jnp.dot(left, right, preferred_element_type=f32)  69.7 us
    psum x1, waiting for transfers between devices, sum_head(): return lax.psum(value, 'head')  44.9 us
    dot_general x9, matrix products, mm_t(): return jnp.einsum('ac,bc->ab', left, right, preferred_element_type=f32)  30.4 us
    pallas_call x3, Pallas kernels, whole_call(): pl.pallas_call(body, out_shape=outs, in_specs=[pl.BlockSpec(memory_space=...  28.7 us
    pallas_call x4, Pallas kernels, join_rounded(): pl.pallas_call(functools.partial(join_kernel, tuple((len(slot) for slot i...  24.4 us
  transfers between devices with their start and end apart: 75, of which 23 were waited for; matrix products, arithmetic and copies ran while one was open for 40% of the time, Pallas kernels for 8%

profile of v2, /device:TPU:0, one launch (start us, length us, event | category | flops | bytes accessed | tf_op | source)
XLA Modules:
  0.0 532.1 jit_solution(1054723363511888578)
XLA Ops:
  8.1 1.6 multiply_reduce_fusion.5
  14.1 2.0 fusion.24
  16.0 2.9 collective-permute-start
  27.8 2.1 collective-permute-start.1
  29.9 4.1 collective-permute-done.8.refs_3_
  34.0 1.7 collective-permute-start.3
  36.9 5.6 %collective-permute-done.1.refs_10_ = f32[128,640]{1,0:T(8,128)} collective-permute-done((f32[128,640]{1,0:T(8,128)}, f32[128,640]{1,0:T(8,128)}, u32[]{:S(2)}, u32[]{:S(2)}) %collective-permute-start.1) | collective-permute-done | bytes 327712 | tf_op jit(solution)/shard_map/ppermute | solution.py:21
  49.7 7.9 %shard_map.203 = (bf16[256,512]{1,0:T(8,128)(2,1)}, f32[256,512]{1,0:T(8,128)}, f32[256,512]{1,0:T(8,128)}) custom-call(s32[256,4]{1,0:T(8,128)} %copy.31.col_ref, s32[24,256]{1,0:T(8,128)} %pad_add_fusion.row_ref, f32[256,640]{1,0:T(8,128)} %pad_maximum_fusion.4.refs_0_, f32[256,640]{1,0:T(8,128)} %collective-permute-done.7.refs_1_, ...), custom_call_target="tpu_custom_call" | custom-call | flops 2147483648 | bytes 6582272 | tf_op jit(solution)/shard_map/pallas_call | solution.py:332
  57.6 3.0 fusion.31
  61.2 2.9 convert_element_type.114
  64.1 5.8 %fusion.32 = f32[256,1376]{0,1:T(8,128)} fusion(bf16[256,2048]{1,0:T(8,128)(2,1)S(1)} %copy-done.19, bf16[1376,2048]{1,0:T(8,128)(2,1)} %param.21), kind=kOutput, calls=%fused_computation.113 | convolution fusion | flops 1442840576 | bytes 8093696 | tf_op jit(solution)/shard_map/ac,bc->ab/dot_general | solution.py:388
  69.9 23.6 %collective-permute-done.4.refs_2_ = f32[256,2048]{1,0:T(8,128)} collective-permute-done((f32[256,2048]{1,0:T(8,128)}, f32[256,2048]{1,0:T(8,128)}, u32[]{:S(2)}, u32[]{:S(2)}) %collective-permute-start.4) | collective-permute-done | bytes 2097184 | tf_op jit(solution)/shard_map/ppermute | solution.py:21
  94.6 2.3 slice.48
  96.9 2.3 slice.49
  101.7 44.9 %all-reduce.5.cloned.1.call-done = f32[256,2048]{1,0:T(8,128)} async-done(((f32[256,2048]{1,0:T(8,128)}), f32[256,2048]{1,0:T(8,128)}) %all-reduce.5.cloned.1.call-update) | async-done | bytes 2097168 | tf_op jit(solution)/shard_map/psum | solution.py:193
  146.7 2.5 add.233
  152.0 5.4 %fusion.7 = f32[256,1376]{0,1:T(8,128)S(1)} fusion(bf16[2048,1376]{0,1:T(8,128)(2,1)} %param.19, f32[256,2048]{1,0:T(8,128)} %broadcast_multiply_fusion.refs_0_, f32[2048]{0:T(1024)S(1)} %convert_element_type.125), kind=kOutput, calls=%fused_computation.64 | convolution fusion | flops 1443889152 | bytes 9150464 | tf_op jit(solution)/shard_map/dot_general | solution.py:384
  157.5 4.5 multiply_convert_fusion.8
  162.0 2.2 fusion.3
  164.2 1.9 convolution_add_fusion.5
  166.7 3.2 fusion.23
  171.9 3.1 collective-permute-start.22
  178.0 4.6 fusion.33
  184.5 6.0 %shard_map.204 = bf16[1024,2048]{1,0:T(8,128)(2,1)} custom-call(f32[1,2048]{1,0:T(1,128)} %broadcast_10_scale_ref.2.scale_ref, f32[256,2048]{1,0:T(8,128)} %convert_element_type.115.refs_0_, f32[256,2048]{1,0:T(8,128)} %collective-permute-done.6.refs_1_, f32[256,2048]{1,0:T(8,128)} %collective-permute-done.4.refs_2_, f32[256,2048]{1,0:T(8,128)} %collective-permute-done.5.refs_3_), custom_call_target="tpu_custom_call" | custom-call | bytes 12582912 | tf_op jit(solution)/shard_map/pallas_call | solution.py:359
  190.5 6.1 %shard_map.205 = bf16[1024,2048]{1,0:T(8,128)(2,1)} custom-call(f32[1,2048]{1,0:T(1,128)} %broadcast_10_scale_ref.2.scale_ref, f32[256,2048]{1,0:T(8,128)} %collective-permute-done.18.refs_0_, f32[256,2048]{1,0:T(8,128)} %collective-permute-done.19.refs_1_, f32[128,2048]{1,0:T(8,128)} %collective-permute-done.16.refs_2_, ...), custom_call_target="tpu_custom_call" | custom-call | bytes 12582912 | tf_op jit(solution)/shard_map/pallas_call | solution.py:359
  197.0 3.4 collective-permute-done.23.refs_2_
  203.2 1.6 collective-permute-start.26
  207.8 9.6 %fusion.34 = f32[1024,1376]{0,1:T(8,128)} fusion(bf16[1024,2048]{1,0:T(8,128)(2,1)S(1)} %copy-done.30, bf16[1376,2048]{1,0:T(8,128)(2,1)} %param.21), kind=kOutput, calls=%fused_computation.115 | convolution fusion | flops 5771362304 | bytes 15466496 | tf_op jit(solution)/shard_map/ac,bc->ab/dot_general | solution.py:388
  217.4 7.8 %fusion.35 = f32[1024,1376]{0,1:T(8,128)} fusion(bf16[1024,2048]{1,0:T(8,128)(2,1)S(1)} %copy-done.26, bf16[1376,2048]{1,0:T(8,128)(2,1)S(1)} %bitcast.73), kind=kOutput, calls=%fused_computation.116 | convolution fusion | flops 5771362304 | bytes 15466496 | tf_op jit(solution)/shard_map/ac,bc->ab/dot_general | solution.py:388
  226.4 3.4 collective-permute-done.28.refs_3_
  232.6 1.7 collective-permute-start.30
  238.4 6.7 %collective-permute-start.34 = (f32[128,2048]{1,0:T(8,128)}, f32[128,2048]{1,0:T(8,128)}, u32[]{:S(2)}, u32[]{:S(2)}) collective-permute-start(f32[128,2048]{1,0:T(8,128)} %split.50), channel_id=1, source_target_pairs={{0,1},{3,2},{4,5},{7,6},{8,9},{11,10},{12,13},{15,14},{16,17},{19,... | collective-permute-start | bytes 3145736 | tf_op jit(solution)/shard_map/ppermute | solution.py:21
  245.1 6.0 %shard_map.206 = bf16[1024,2048]{1,0:T(8,128)(2,1)} custom-call(f32[1,2048]{1,0:T(1,128)} %bitcast.82, f32[256,2048]{1,0:T(8,128)} %broadcast_multiply_fusion.refs_0_, f32[256,2048]{1,0:T(8,128)} %collective-permute-done.25.refs_1_, f32[128,2048]{1,0:T(8,128)} %collective-permute-done.23.refs_2_, f32[128,2048]{1,0:T(8,128)} %copy-done.51, ...), custom_call_target="tpu_custom_call" | custom-call | bytes 12582912 | tf_op jit(solution)/shard_map/pallas_call | solution.py:359
  251.1 10.8 %fusion.36 = f32[1024,1376]{0,1:T(8,128)} fusion(bf16[1024,2048]{1,0:T(8,128)(2,1)} %shard_map.206, bf16[2048,1376]{0,1:T(8,128)(2,1)} %param.19), kind=kOutput, calls=%fused_computation.117 | convolution fusion | flops 5771362304 | bytes 15466496 | tf_op jit(solution)/shard_map/dot_general | solution.py:384
  263.5 1.7 add.241
  268.6 4.7 collective-permute-start.38
  274.1 15.5 %multiply_convert_fusion.3 = (bf16[1024,1376]{0,1:T(8,128)(2,1)}, bf16[1024,1376]{0,1:T(8,128)(2,1)}, bf16[1024,1376]{0,1:T(8,128)(2,1)}) fusion(f32[1024,1376]{0,1:T(8,128)} %fusion.34, f32[1024,1376]{0,1:T(8,128)} %fusion.36, bf16[1024,2048]{1,0:T(8,128)(2,1)S(1)} %copy-done.28, bf16[2048,1376]{0,1:T(8,128)(2,1)} %param.20), kind=kOutput, calls=%fused_computation.8 | convolution fusion | flops 5792497664 | bytes 29556736 | tf_op jit(solution)/shard_map/dot_general | solution.py:384
  291.0 4.9 collective-permute-done.38
  297.9 2.5 fusion.21
  306.1 9.4 %shard_map.207 = bf16[256,64]{1,0:T(8,128)(2,1)} custom-call(s32[256,4]{1,0:T(8,128)} %copy.31.col_ref, s32[24,256]{1,0:T(8,128)} %pad_add_fusion.row_ref, f32[256,512]{1,0:T(8,128)} %copy-done.37, f32[256,512]{1,0:T(8,128)} %bitcast.81, f32[256,640]{1,0:T(8,128)} %pad_maximum_fusion.4.refs_0_, f32[256,640]{1,0:T(8,128)} %collective-permute-done.7.refs_1_, ...), custom_call_target="tpu_custom_call" | custom-call | flops 2147483648 | bytes 6352896 | tf_op jit(solution)/shard_map/pallas_call | solution.py:332
  317.4 2.5 copy-done.9
  325.5 9.0 %fusion.39 = f32[1376,2048]{1,0:T(8,128)} fusion(bf16[1024,1376]{0,1:T(8,128)(2,1)S(1)} %copy-done.84, bf16[1024,2048]{1,0:T(8,128)(2,1)S(1)} %copy-done.31), kind=kOutput, calls=%fused_computation.120 | convolution fusion | flops 5771362304 | bytes 18284544 | tf_op jit(solution)/shard_map/ca,cb->ab/dot_general | solution.py:392
  339.9 11.3 %shard_map.208 = (bf16[256,64]{1,0:T(8,128)(2,1)}, bf16[256,512]{1,0:T(8,128)(2,1)}) custom-call(s32[256,4]{1,0:T(8,128)} %copy.31.col_ref, s32[24,256]{1,0:T(8,128)} %pad_add_fusion.row_ref, f32[256,640]{1,0:T(8,128)} %pad_maximum_fusion.4.refs_0_, f32[256,640]{1,0:T(8,128)} %collective-permute-done.7.refs_1_, f32[128,640]{1,0:T(8,128)} %collective-permute-done.refs_2_, ...), custom_call_target="tpu_custom_call" | custom-call | flops 4294967296 | bytes 9891840 | tf_op jit(solution)/shard_map/pallas_call | solution.py:332
  357.2 2.8 fusion.43
  361.9 6.3 %collective-permute-start.54 = (f32[128,2048]{1,0:T(8,128)}, f32[128,2048]{1,0:T(8,128)}, u32[]{:S(2)}, u32[]{:S(2)}) collective-permute-start(f32[128,2048]{1,0:T(8,128)} %split.54), channel_id=1, source_target_pairs={{0,1},{3,2},{4,5},{7,6},{8,9},{11,10},{12,13},{15,14},{16,17},{19,... | collective-permute-start | bytes 3145736 | tf_op jit(solution)/shard_map/ppermute | solution.py:21
  369.2 1.7 collective-permute-start.57
  372.1 6.3 %shard_map.209 = bf16[1024,2048]{1,0:T(8,128)(2,1)} custom-call(f32[1,2048]{1,0:T(1,128)} %bitcast.83, f32[128,2048]{1,0:T(8,128)} %copy-done.49, f32[128,2048]{1,0:T(8,128)} %copy-done.53, f32[128,2048]{1,0:T(8,128)} %copy-done.54, f32[128,2048]{1,0:T(8,128)} %copy-done.50, f32[128,2048]{1,0:T(8,128)} %collective-permute-done.32.refs_4_, ...), custom_call_target="tpu_custom_call" | custom-call | bytes 12582912 | tf_op jit(solution)/shard_map/pallas_call | solution.py:359
  378.4 11.5 %fusion.44 = f32[1024,1376]{0,1:T(8,128)} fusion(bf16[1024,2048]{1,0:T(8,128)(2,1)} %shard_map.209, bf16[2048,1376]{0,1:T(8,128)(2,1)} %param.19), kind=kOutput, calls=%fused_computation.125 | convolution fusion | flops 5771362304 | bytes 15466496 | tf_op jit(solution)/shard_map/dot_general | solution.py:384
  390.5 16.3 %collective-permute-done.55 = f32[128,2048]{1,0:T(8,128)} collective-permute-done((f32[128,2048]{1,0:T(8,128)}, f32[128,2048]{1,0:T(8,128)}, u32[]{:S(2)}, u32[]{:S(2)}) %collective-permute-start.55) | collective-permute-done | bytes 1048608 | tf_op jit(solution)/shard_map/ppermute | solution.py:21
  410.0 1.9 add.254
  412.7 1.6 collective-permute-start.59
  414.3 1.7 collective-permute-start.60
  417.3 12.8 %multiply_convert_fusion = (bf16[1024,1376]{0,1:T(8,128)(2,1)}, bf16[1024,1376]{0,1:T(8,128)(2,1)}, bf16[1024,1376]{0,1:T(8,128)(2,1)}) fusion(f32[1024,1376]{0,1:T(8,128)} %fusion.35, f32[1024,1376]{0,1:T(8,128)} %fusion.44, bf16[1024,2048]{1,0:T(8,128)(2,1)S(1)} %copy-done.32, bf16[2048,1376]{0,1:T(8,128)(2,1)S(1)} %bitcast.77), kind=kOutput, calls=%fused_computation.3 | convolution fusion | flops 5792497664 | bytes 29556736 | tf_op jit(solution)/shard_map/dot_general | solution.py:384
  430.1 10.6 %fusion.45 = f32[2048,1376]{0,1:T(8,128)} fusion(bf16[1024,1376]{0,1:T(8,128)(2,1)} %get-tuple-element.400, bf16[1024,2048]{1,0:T(8,128)(2,1)S(1)} %copy-done.29), kind=kOutput, calls=%fused_computation.126 | convolution fusion | flops 5771362304 | bytes 18284544 | tf_op jit(solution)/shard_map/ca,cb->ab/dot_general | solution.py:392
  443.9 1.6 select_add_fusion.2
  447.5 2.0 collective-permute-start.66
  449.6 12.7 %convolution_add_fusion.2 = f32[1376,2048]{1,0:T(8,128)} fusion(f32[1376,2048]{1,0:T(8,128)} %fusion.39, bf16[1024,1376]{0,1:T(8,128)(2,1)} %get-tuple-element.412, bf16[1024,2048]{1,0:T(8,128)(2,1)S(1)} %copy-done.27), kind=kOutput, calls=%fused_computation.2 | convolution fusion | flops 5774180352 | bytes 29556736 | tf_op jit(solution)/shard_map/ca,cb->ab/dot_general | solution.py:392
  462.2 10.6 %fusion.46 = f32[2048,1376]{0,1:T(8,128)} fusion(bf16[1024,1376]{0,1:T(8,128)(2,1)} %get-tuple-element.413, bf16[1024,2048]{1,0:T(8,128)(2,1)S(1)} %copy-done.29), kind=kOutput, calls=%fused_computation.127 | convolution fusion | flops 5771362304 | bytes 18284544 | tf_op jit(solution)/shard_map/ca,cb->ab/dot_general | solution.py:392
  479.3 1.8 collective-permute-start.69
  481.4 11.5 %convolution_add_fusion.1 = f32[2048,1376]{0,1:T(8,128)} fusion(f32[2048,1376]{0,1:T(8,128)} %fusion.46, bf16[1024,1376]{0,1:T(8,128)(2,1)S(1)} %copy-done.85, bf16[1024,2048]{1,0:T(8,128)(2,1)S(1)} %copy-done.32), kind=kOutput, calls=%fused_computation.1 | convolution fusion | flops 5774180352 | bytes 29556736 | tf_op jit(solution)/shard_map/ca,cb->ab/dot_general | solution.py:392
  494.1 12.8 %convolution_add_fusion = f32[2048,1376]{0,1:T(8,128)} fusion(f32[2048,1376]{0,1:T(8,128)} %fusion.45, bf16[1024,1376]{0,1:T(8,128)(2,1)} %get-tuple-element.427, bf16[1024,2048]{1,0:T(8,128)(2,1)} %shard_map.209), kind=kOutput, calls=%fused_computation | convolution fusion | flops 5774180352 | bytes 29556736 | tf_op jit(solution)/shard_map/ca,cb->ab/dot_general | solution.py:392
  514.6 1.9 multiply_add_fusion.2
  517.7 2.6 pad_maximum_fusion
  522.0 2.1 copy.46
  (405 shorter events, 116.3 us)
Async XLA Ops:
  7.2 139.5 %all-reduce.5.cloned.1.call-start = ((), (), s32[]{:S(2)}) async-start(), calls=%async_computation | async-start | bytes 4194304 | tf_op jit(solution)/shard_map/psum | solution.py:193
  16.0 11.8 %collective-permute-start = (f32[128,640]{1,0:T(8,128)}, f32[128,640]{1,0:T(8,128)}, u32[]{:S(2)}, u32[]{:S(2)}) collective-permute-start(f32[128,640]{1,0:T(8,128)} %get-tuple-element.466), channel_id=1, source_target_pairs={{0,8},{4,12},{8,0},{12,4},{16,24},{20,28},{24,16},{28,20},{1,9},{5... | collective-permute-start | bytes 983048 | tf_op jit(solution)/shard_map/ppermute | solution.py:21
  19.0 11.0 %collective-permute-start.2 = (f32[128,640]{1,0:T(8,128)}, f32[128,640]{1,0:T(8,128)}, u32[]{:S(2)}, u32[]{:S(2)}) collective-permute-start(f32[128,640]{1,0:T(8,128)} %get-tuple-element.465), channel_id=1, source_target_pairs={{0,16},{4,20},{8,24},{12,28},{16,0},{20,4},{24,8},{28,12},{1,17},{... | collective-permute-start | bytes 983048 | tf_op jit(solution)/shard_map/ppermute | solution.py:21
  20.5 13.5 %collective-permute-start.8 = (f32[128,640]{1,0:T(8,128)}, f32[128,640]{1,0:T(8,128)}, u32[]{:S(2)}, u32[]{:S(2)}) collective-permute-start(f32[128,640]{1,0:T(8,128)} %get-tuple-element.465), channel_id=1, source_target_pairs={{0,8},{4,12},{8,0},{12,4},{16,24},{20,28},{24,16},{28,20},{1,9},{5... | collective-permute-start | bytes 983048 | tf_op jit(solution)/shard_map/ppermute | solution.py:21
  21.0 22.2 %collective-permute-start.7 = (f32[256,640]{1,0:T(8,128)}, f32[256,640]{1,0:T(8,128)}, u32[]{:S(2)}, u32[]{:S(2)}) collective-permute-start(f32[256,640]{1,0:T(8,128)} %pad_maximum_fusion.4.refs_0_), channel_id=1, source_target_pairs={{0,4},{4,0},{8,12},{12,8},{16,20},{20,16},{24,28},{28,24},{1,5},{5... | collective-permute-start | bytes 1966088 | tf_op jit(solution)/shard_map/ppermute | solution.py:21
  21.0 15.9 %collective-permute-start.11 = (f32[128,640]{1,0:T(8,128)}, f32[128,640]{1,0:T(8,128)}, u32[]{:S(2)}, u32[]{:S(2)}) collective-permute-start(f32[128,640]{1,0:T(8,128)} %get-tuple-element.466), channel_id=1, source_target_pairs={{0,16},{4,20},{8,24},{12,28},{16,0},{20,4},{24,8},{28,12},{1,17},{... | collective-permute-start | bytes 983048 | tf_op jit(solution)/shard_map/ppermute | solution.py:21
  27.8 14.7 %collective-permute-start.1 = (f32[128,640]{1,0:T(8,128)}, f32[128,640]{1,0:T(8,128)}, u32[]{:S(2)}, u32[]{:S(2)}) collective-permute-start(f32[128,640]{1,0:T(8,128)} %collective-permute-done.refs_2_), channel_id=1, source_target_pairs={{0,16},{4,20},{8,24},{12,28},{16,0},{20,4},{24,8},{28,12},{1,17},{... | collective-permute-start | bytes 983048 | tf_op jit(solution)/shard_map/ppermute | solution.py:21
  29.9 13.8 %collective-permute-start.9 = (f32[128,640]{1,0:T(8,128)}, f32[128,640]{1,0:T(8,128)}, u32[]{:S(2)}, u32[]{:S(2)}) collective-permute-start(f32[128,640]{1,0:T(8,128)} %collective-permute-done.refs_2_), channel_id=1, source_target_pairs={{0,4},{4,0},{8,12},{12,8},{16,20},{20,16},{24,28},{28,24},{1,5},{5... | collective-permute-start | bytes 983048 | tf_op jit(solution)/shard_map/ppermute | solution.py:21
  34.0 9.2 %collective-permute-start.3 = (f32[128,640]{1,0:T(8,128)}, f32[128,640]{1,0:T(8,128)}, u32[]{:S(2)}, u32[]{:S(2)}) collective-permute-start(f32[128,640]{1,0:T(8,128)} %collective-permute-done.2.refs_7_), channel_id=1, source_target_pairs={{0,8},{4,12},{8,0},{12,4},{16,24},{20,28},{24,16},{28,20},{1,9},{5... | collective-permute-start | bytes 983048 | tf_op jit(solution)/shard_map/ppermute | solution.py:21
  36.9 11.2 %collective-permute-start.13 = (f32[128,640]{1,0:T(8,128)}, f32[128,640]{1,0:T(8,128)S(1)}, u32[]{:S(2)}, u32[]{:S(2)}) collective-permute-start(f32[128,640]{1,0:T(8,128)} %collective-permute-done.2.refs_7_), channel_id=1, source_target_pairs={{0,4},{4,0},{8,12},{12,8},{16,20},{20,16},{24,28},{28,24},{1,5},{5... | collective-permute-start | bytes 983048 | tf_op jit(solution)/shard_map/ppermute | solution.py:21
  45.2 48.3 %collective-permute-start.4 = (f32[256,2048]{1,0:T(8,128)}, f32[256,2048]{1,0:T(8,128)}, u32[]{:S(2)}, u32[]{:S(2)}) collective-permute-start(f32[256,2048]{1,0:T(8,128)} %convert_element_type.115.refs_0_), channel_id=1, source_target_pairs={{0,8},{4,12},{8,0},{12,4},{16,24},{20,28},{24,16},{28,20},{1,9},{5... | collective-permute-start | bytes 6291464 | tf_op jit(solution)/shard_map/ppermute | solution.py:21
  46.6 48.0 %collective-permute-start.5 = (f32[256,2048]{1,0:T(8,128)}, f32[256,2048]{1,0:T(8,128)}, u32[]{:S(2)}, u32[]{:S(2)}) collective-permute-start(f32[256,2048]{1,0:T(8,128)} %convert_element_type.115.refs_0_), channel_id=1, source_target_pairs={{0,16},{4,20},{8,24},{12,28},{16,0},{20,4},{24,8},{28,12},{1,17},{... | collective-permute-start | bytes 6291464 | tf_op jit(solution)/shard_map/ppermute | solution.py:21
  48.1 46.5 %collective-permute-start.6 = (f32[256,2048]{1,0:T(8,128)}, f32[256,2048]{1,0:T(8,128)}, u32[]{:S(2)}, u32[]{:S(2)}) collective-permute-start(f32[256,2048]{1,0:T(8,128)} %convert_element_type.115.refs_0_), channel_id=1, source_target_pairs={{0,4},{4,0},{8,12},{12,8},{16,20},{20,16},{24,28},{28,24},{1,5},{5... | collective-permute-start | bytes 6291464 | tf_op jit(solution)/shard_map/ppermute | solution.py:21
  60.6 433.5 %all-reduce.7.cloned.1.call-start = ((), (), s32[]{:S(2)}) async-start(), calls=%async_computation.1 | async-start | bytes 10485760 | tf_op jit(solution)/shard_map/psum | solution.py:582
  99.2 66.9 %collective-permute-start.16 = (f32[128,2048]{1,0:T(8,128)}, f32[128,2048]{1,0:T(8,128)}, u32[]{:S(2)}, u32[]{:S(2)}) collective-permute-start(f32[128,2048]{1,0:T(8,128)} %slice.48), channel_id=1, source_target_pairs={{0,16},{4,20},{8,24},{12,28},{16,0},{20,4},{24,8},{28,12},{1,17},{... | collective-permute-start | bytes 3145736 | tf_op jit(solution)/shard_map/ppermute | solution.py:21
  100.7 65.4 %collective-permute-start.17 = (f32[128,2048]{1,0:T(8,128)}, f32[128,2048]{1,0:T(8,128)}, u32[]{:S(2)}, u32[]{:S(2)}) collective-permute-start(f32[128,2048]{1,0:T(8,128)} %slice.49), channel_id=1, source_target_pairs={{0,8},{4,12},{8,0},{12,4},{16,24},{20,28},{24,16},{28,20},{1,9},{5... | collective-permute-start | bytes 3145736 | tf_op jit(solution)/shard_map/ppermute | solution.py:21
  101.2 64.9 %collective-permute-start.18 = (f32[256,2048]{1,0:T(8,128)}, f32[256,2048]{1,0:T(8,128)}, u32[]{:S(2)}, u32[]{:S(2)}) collective-permute-start(f32[256,2048]{1,0:T(8,128)} %collective-permute-done.4.refs_2_), channel_id=1, source_target_pairs={{0,4},{4,0},{8,12},{12,8},{16,20},{20,16},{24,28},{28,24},{1,5},{5... | collective-permute-start | bytes 6291464 | tf_op jit(solution)/shard_map/ppermute | solution.py:21
  101.2 64.9 %collective-permute-start.19 = (f32[256,2048]{1,0:T(8,128)}, f32[256,2048]{1,0:T(8,128)}, u32[]{:S(2)}, u32[]{:S(2)}) collective-permute-start(f32[256,2048]{1,0:T(8,128)} %collective-permute-done.5.refs_3_), channel_id=1, source_target_pairs={{0,4},{4,0},{8,12},{12,8},{16,20},{20,16},{24,28},{28,24},{1,5},{5... | collective-permute-start | bytes 6291464 | tf_op jit(solution)/shard_map/ppermute | solution.py:21
  170.6 31.0 %collective-permute-start.25 = (f32[256,2048]{1,0:T(8,128)}, f32[256,2048]{1,0:T(8,128)}, u32[]{:S(2)}, u32[]{:S(2)}) collective-permute-start(f32[256,2048]{1,0:T(8,128)} %broadcast_multiply_fusion.refs_0_), channel_id=1, source_target_pairs={{0,4},{4,0},{8,12},{12,8},{16,20},{20,16},{24,28},{28,24},{1,5},{5... | collective-permute-start | bytes 6291464 | tf_op jit(solution)/shard_map/ppermute | solution.py:21
  171.9 25.1 %collective-permute-start.22 = (f32[128,2048]{1,0:T(8,128)}, f32[128,2048]{1,0:T(8,128)}, u32[]{:S(2)}, u32[]{:S(2)}) collective-permute-start(f32[128,2048]{1,0:T(8,128)} %split.49), channel_id=1, source_target_pairs={{0,1},{3,2},{4,5},{7,6},{8,9},{11,10},{12,13},{15,14},{16,17},{19,... | collective-permute-start | bytes 3145736 | tf_op jit(solution)/shard_map/ppermute | solution.py:21
  175.0 25.4 %collective-permute-start.23 = (f32[128,2048]{1,0:T(8,128)}, f32[128,2048]{1,0:T(8,128)}, u32[]{:S(2)}, u32[]{:S(2)}) collective-permute-start(f32[128,2048]{1,0:T(8,128)} %get-tuple-element.278), channel_id=1, source_target_pairs={{0,8},{4,12},{8,0},{12,4},{16,24},{20,28},{24,16},{28,20},{1,9},{5... | collective-permute-start | bytes 3145736 | tf_op jit(solution)/shard_map/ppermute | solution.py:21
  176.6 25.1 %collective-permute-start.24 = (f32[128,2048]{1,0:T(8,128)}, f32[128,2048]{1,0:T(8,128)}, u32[]{:S(2)}, u32[]{:S(2)}) collective-permute-start(f32[128,2048]{1,0:T(8,128)} %get-tuple-element.277), channel_id=1, source_target_pairs={{0,16},{4,20},{8,24},{12,28},{16,0},{20,4},{24,8},{28,12},{1,17},{... | collective-permute-start | bytes 3145736 | tf_op jit(solution)/shard_map/ppermute | solution.py:21
  203.2 23.2 %collective-permute-start.26 = (f32[128,2048]{1,0:T(8,128)S(1)}, f32[128,2048]{1,0:T(8,128)S(1)}, u32[]{:S(2)}, u32[]{:S(2)}) collective-permute-start(f32[128,2048]{1,0:T(8,128)S(1)} %get-tuple-element.275), channel_id=1, source_target_pairs={{0,1},{3,2},{4,5},{7,6},{8,9},{11,10},{12,13},{15,14},{16,17},{19,... | collective-permute-start | bytes 3145736 | tf_op jit(solution)/shard_map/ppermute | solution.py:21
  204.8 21.6 %collective-permute-start.27 = (f32[128,2048]{1,0:T(8,128)S(1)}, f32[128,2048]{1,0:T(8,128)S(1)}, u32[]{:S(2)}, u32[]{:S(2)}) collective-permute-start(f32[128,2048]{1,0:T(8,128)S(1)} %get-tuple-element.276), channel_id=1, source_target_pairs={{1,2},{2,1},{5,6},{6,5},{9,10},{10,9},{13,14},{14,13},{17,18},{18,... | collective-permute-start | bytes 3145736 | tf_op jit(solution)/shard_map/ppermute | solution.py:21
  205.7 24.1 %collective-permute-start.28 = (f32[128,2048]{1,0:T(8,128)}, f32[128,2048]{1,0:T(8,128)S(1)}, u32[]{:S(2)}, u32[]{:S(2)}) collective-permute-start(f32[128,2048]{1,0:T(8,128)} %get-tuple-element.277), channel_id=1, source_target_pairs={{0,8},{4,12},{8,0},{12,4},{16,24},{20,28},{24,16},{28,20},{1,9},{5... | collective-permute-start | bytes 3145736 | tf_op jit(solution)/shard_map/ppermute | solution.py:21
  206.3 23.8 %collective-permute-start.29 = (f32[128,2048]{1,0:T(8,128)}, f32[128,2048]{1,0:T(8,128)S(1)}, u32[]{:S(2)}, u32[]{:S(2)}) collective-permute-start(f32[128,2048]{1,0:T(8,128)} %get-tuple-element.278), channel_id=1, source_target_pairs={{0,16},{4,20},{8,24},{12,28},{16,0},{20,4},{24,8},{28,12},{1,17},{... | collective-permute-start | bytes 3145736 | tf_op jit(solution)/shard_map/ppermute | solution.py:21
  232.6 29.4 %collective-permute-start.30 = (f32[128,2048]{1,0:T(8,128)}, f32[128,2048]{1,0:T(8,128)}, u32[]{:S(2)}, u32[]{:S(2)}) collective-permute-start(f32[128,2048]{1,0:T(8,128)} %slice_add_fusion.5), channel_id=1, source_target_pairs={{1,2},{2,1},{5,6},{6,5},{9,10},{10,9},{13,14},{14,13},{17,18},{18,... | collective-permute-start | bytes 3145736 | tf_op jit(solution)/shard_map/ppermute | solution.py:21
  234.2 27.7 %collective-permute-start.31 = (f32[128,2048]{1,0:T(8,128)}, f32[128,2048]{1,0:T(8,128)}, u32[]{:S(2)}, u32[]{:S(2)}) collective-permute-start(f32[128,2048]{1,0:T(8,128)} %add.240), channel_id=1, source_target_pairs={{1,0},{2,3},{5,4},{6,7},{9,8},{10,11},{13,12},{14,15},{17,16},{18,... | collective-permute-start | bytes 3145736 | tf_op jit(solution)/shard_map/ppermute | solution.py:21
  235.5 26.4 %collective-permute-start.32 = (f32[128,2048]{1,0:T(8,128)}, f32[128,2048]{1,0:T(8,128)}, u32[]{:S(2)}, u32[]{:S(2)}) collective-permute-start(f32[128,2048]{1,0:T(8,128)} %collective-permute-done.23.refs_2_), channel_id=1, source_target_pairs={{0,16},{4,20},{8,24},{12,28},{16,0},{20,4},{24,8},{28,12},{1,17},{... | collective-permute-start | bytes 3145736 | tf_op jit(solution)/shard_map/ppermute | solution.py:21
  237.0 24.9 %collective-permute-start.33 = (f32[128,2048]{1,0:T(8,128)}, f32[128,2048]{1,0:T(8,128)}, u32[]{:S(2)}, u32[]{:S(2)}) collective-permute-start(f32[128,2048]{1,0:T(8,128)} %collective-permute-done.24.refs_5_), channel_id=1, source_target_pairs={{0,8},{4,12},{8,0},{12,4},{16,24},{20,28},{24,16},{28,20},{1,9},{5... | collective-permute-start | bytes 3145736 | tf_op jit(solution)/shard_map/ppermute | solution.py:21
  238.4 25.1 %collective-permute-start.34 = (f32[128,2048]{1,0:T(8,128)}, f32[128,2048]{1,0:T(8,128)}, u32[]{:S(2)}, u32[]{:S(2)}) collective-permute-start(f32[128,2048]{1,0:T(8,128)} %split.50), channel_id=1, source_target_pairs={{0,1},{3,2},{4,5},{7,6},{8,9},{11,10},{12,13},{15,14},{16,17},{19,... | collective-permute-start | bytes 3145736 | tf_op jit(solution)/shard_map/ppermute | solution.py:21
  266.8 24.2 %collective-permute-start.35 = (f32[128,2048]{1,0:T(8,128)S(1)}, f32[128,2048]{1,0:T(8,128)S(1)}, u32[]{:S(2)}, u32[]{:S(2)}) collective-permute-start(f32[128,2048]{1,0:T(8,128)S(1)} %add.241), channel_id=1, source_target_pairs={{1,0},{2,3},{5,4},{6,7},{9,8},{10,11},{13,12},{14,15},{17,16},{18,... | collective-permute-start | bytes 3145736 | tf_op jit(solution)/shard_map/ppermute | solution.py:21
  268.1 22.9 %collective-permute-start.36 = (f32[128,2048]{1,0:T(8,128)}, f32[128,2048]{1,0:T(8,128)S(1)}, u32[]{:S(2)}, u32[]{:S(2)}) collective-permute-start(f32[128,2048]{1,0:T(8,128)} %collective-permute-done.23.refs_2_), channel_id=1, source_target_pairs={{0,4},{4,0},{8,12},{12,8},{16,20},{20,16},{24,28},{28,24},{1,5},{5... | collective-permute-start | bytes 3145736 | tf_op jit(solution)/shard_map/ppermute | solution.py:21
  268.1 22.8 %collective-permute-start.37 = (f32[128,2048]{1,0:T(8,128)}, f32[128,2048]{1,0:T(8,128)S(1)}, u32[]{:S(2)}, u32[]{:S(2)}) collective-permute-start(f32[128,2048]{1,0:T(8,128)} %collective-permute-done.24.refs_5_), channel_id=1, source_target_pairs={{0,4},{4,0},{8,12},{12,8},{16,20},{20,16},{24,28},{28,24},{1,5},{5... | collective-permute-start | bytes 3145736 | tf_op jit(solution)/shard_map/ppermute | solution.py:21
  268.6 27.2 %collective-permute-start.38 = (f32[128,2048]{1,0:T(8,128)S(1)}, f32[128,2048]{1,0:T(8,128)S(1)}, u32[]{:S(2)}, u32[]{:S(2)}) collective-permute-start(f32[128,2048]{1,0:T(8,128)S(1)} %get-tuple-element.304), channel_id=1, source_target_pairs={{0,1},{3,2},{4,5},{7,6},{8,9},{11,10},{12,13},{15,14},{16,17},{19,... | collective-permute-start | bytes 3145736 | tf_op jit(solution)/shard_map/ppermute | solution.py:21
  273.3 22.6 %collective-permute-start.39 = (f32[128,2048]{1,0:T(8,128)S(1)}, f32[128,2048]{1,0:T(8,128)S(1)}, u32[]{:S(2)}, u32[]{:S(2)}) collective-permute-start(f32[128,2048]{1,0:T(8,128)S(1)} %get-tuple-element.305), channel_id=1, source_target_pairs={{1,2},{2,1},{5,6},{6,5},{9,10},{10,9},{13,14},{14,13},{17,18},{18,... | collective-permute-start | bytes 3145736 | tf_op jit(solution)/shard_map/ppermute | solution.py:21
  302.8 13.9 %collective-permute-start.40 = (f32[264,512]{1,0:T(8,128)S(1)}, f32[264,512]{1,0:T(8,128)S(1)}, u32[]{:S(2)}, u32[]{:S(2)}) collective-permute-start(f32[264,512]{1,0:T(8,128)S(1)} %select_maximum_fusion.refs_14_), channel_id=1, source_target_pairs={{0,8},{4,12},{8,0},{12,4},{16,24},{20,28},{24,16},{28,20},{1,9},{5... | collective-permute-start | bytes 1622024 | tf_op jit(solution)/shard_map/ppermute | solution.py:21
  303.8 13.1 %collective-permute-start.41 = (f32[264,512]{1,0:T(8,128)S(1)}, f32[264,512]{1,0:T(8,128)S(1)}, u32[]{:S(2)}, u32[]{:S(2)}) collective-permute-start(f32[264,512]{1,0:T(8,128)S(1)} %select_maximum_fusion.refs_14_), channel_id=1, source_target_pairs={{0,16},{4,20},{8,24},{12,28},{16,0},{20,4},{24,8},{28,12},{1,17},{... | collective-permute-start | bytes 1622024 | tf_op jit(solution)/shard_map/ppermute | solution.py:21
  304.4 12.6 %collective-permute-start.42 = (f32[264,512]{1,0:T(8,128)S(1)}, f32[264,512]{1,0:T(8,128)S(1)}, u32[]{:S(2)}, u32[]{:S(2)}) collective-permute-start(f32[264,512]{1,0:T(8,128)S(1)} %select_maximum_fusion.refs_14_), channel_id=1, source_target_pairs={{0,4},{4,0},{8,12},{12,8},{16,20},{20,16},{24,28},{28,24},{1,5},{5... | collective-permute-start | bytes 1622024 | tf_op jit(solution)/shard_map/ppermute | solution.py:21
  304.4 12.6 %collective-permute-start.43 = (f32[128,2048]{1,0:T(8,128)}, f32[128,2048]{1,0:T(8,128)S(1)}, u32[]{:S(2)}, u32[]{:S(2)}) collective-permute-start(f32[128,2048]{1,0:T(8,128)} %copy-done.51), channel_id=1, source_target_pairs={{0,4},{4,0},{8,12},{12,8},{16,20},{20,16},{24,28},{28,24},{1,5},{5... | collective-permute-start | bytes 3145736 | tf_op jit(solution)/shard_map/ppermute | solution.py:21
  304.9 12.1 %collective-permute-start.44 = (f32[128,2048]{1,0:T(8,128)}, f32[128,2048]{1,0:T(8,128)S(1)}, u32[]{:S(2)}, u32[]{:S(2)}) collective-permute-start(f32[128,2048]{1,0:T(8,128)} %copy-done.52), channel_id=1, source_target_pairs={{0,4},{4,0},{8,12},{12,8},{16,20},{20,16},{24,28},{28,24},{1,5},{5... | collective-permute-start | bytes 3145736 | tf_op jit(solution)/shard_map/ppermute | solution.py:21
  317.0 17.5 %collective-permute-start.49 = (f32[256,2048]{1,0:T(8,128)S(1)}, f32[256,2048]{1,0:T(8,128)S(1)}, u32[]{:S(2)}, u32[]{:S(2)}) collective-permute-start(f32[256,2048]{1,0:T(8,128)S(1)} %slice_select_fusion), channel_id=1, source_target_pairs={{0,4},{4,0},{8,12},{12,8},{16,20},{20,16},{24,28},{28,24},{1,5},{5... | collective-permute-start | bytes 6291464 | tf_op jit(solution)/shard_map/ppermute | solution.py:21
  322.4 12.1 %collective-permute-start.45 = (f32[128,512]{1,0:T(8,128)S(1)}, f32[128,512]{1,0:T(8,128)S(1)}, u32[]{:S(2)}, u32[]{:S(2)}) collective-permute-start(f32[128,512]{1,0:T(8,128)S(1)} %slice.52), channel_id=1, source_target_pairs={{0,16},{4,20},{8,24},{12,28},{16,0},{20,4},{24,8},{28,12},{1,17},{... | collective-permute-start | bytes 786440 | tf_op jit(solution)/shard_map/ppermute | solution.py:21
  323.9 10.5 %collective-permute-start.46 = (f32[136,512]{1,0:T(8,128)S(1)}, f32[136,512]{1,0:T(8,128)S(1)}, u32[]{:S(2)}, u32[]{:S(2)}) collective-permute-start(f32[136,512]{1,0:T(8,128)S(1)} %slice.53), channel_id=1, source_target_pairs={{0,8},{4,12},{8,0},{12,4},{16,24},{20,28},{24,16},{28,20},{1,9},{5... | collective-permute-start | bytes 835592 | tf_op jit(solution)/shard_map/ppermute | solution.py:21
  325.0 9.5 %collective-permute-start.47 = (f32[264,512]{1,0:T(8,128)S(1)}, f32[264,512]{1,0:T(8,128)S(1)}, u32[]{:S(2)}, u32[]{:S(2)}) collective-permute-start(f32[264,512]{1,0:T(8,128)S(1)} %collective-permute-done.40.refs_16_), channel_id=1, source_target_pairs={{0,4},{4,0},{8,12},{12,8},{16,20},{20,16},{24,28},{28,24},{1,5},{5... | collective-permute-start | bytes 1622024 | tf_op jit(solution)/shard_map/ppermute | solution.py:21
  325.0 9.5 %collective-permute-start.48 = (f32[264,512]{1,0:T(8,128)S(1)}, f32[264,512]{1,0:T(8,128)S(1)}, u32[]{:S(2)}, u32[]{:S(2)}) collective-permute-start(f32[264,512]{1,0:T(8,128)S(1)} %collective-permute-done.41.refs_18_), channel_id=1, source_target_pairs={{0,4},{4,0},{8,12},{12,8},{16,20},{20,16},{24,28},{28,24},{1,5},{5... | collective-permute-start | bytes 1622024 | tf_op jit(solution)/shard_map/ppermute | solution.py:21
  361.9 28.6 %collective-permute-start.54 = (f32[128,2048]{1,0:T(8,128)}, f32[128,2048]{1,0:T(8,128)}, u32[]{:S(2)}, u32[]{:S(2)}) collective-permute-start(f32[128,2048]{1,0:T(8,128)} %split.54), channel_id=1, source_target_pairs={{0,1},{3,2},{4,5},{7,6},{8,9},{11,10},{12,13},{15,14},{16,17},{19,... | collective-permute-start | bytes 3145736 | tf_op jit(solution)/shard_map/ppermute | solution.py:21
  368.2 38.6 %collective-permute-start.55 = (f32[128,2048]{1,0:T(8,128)}, f32[128,2048]{1,0:T(8,128)}, u32[]{:S(2)}, u32[]{:S(2)}) collective-permute-start(f32[128,2048]{1,0:T(8,128)} %slice_select_fusion.1), channel_id=1, source_target_pairs={{0,8},{4,12},{8,0},{12,4},{16,24},{20,28},{24,16},{28,20},{1,9},{5... | collective-permute-start | bytes 3145736 | tf_op jit(solution)/shard_map/ppermute | solution.py:21
  369.2 21.3 %collective-permute-start.56 = (f32[2,2048]{1,0:T(2,128)S(1)}, f32[2,2048]{1,0:T(2,128)S(1)}, u32[]{:S(2)}, u32[]{:S(2)}) collective-permute-start(f32[2,2048]{1,0:T(2,128)S(1)} %pad_maximum_fusion.5), channel_id=1, source_target_pairs={{0,1},{1,0},{2,3},{3,2},{4,5},{5,4},{6,7},{7,6},{8,9},{9,8},{10,11... | collective-permute-start | bytes 49160 | tf_op jit(solution)/shard_map/ppermute | solution.py:21
  369.2 37.6 %collective-permute-start.57 = (f32[128,2048]{1,0:T(8,128)}, f32[128,2048]{1,0:T(8,128)}, u32[]{:S(2)}, u32[]{:S(2)}) collective-permute-start(f32[128,2048]{1,0:T(8,128)} %slice_add_fusion.2), channel_id=1, source_target_pairs={{1,2},{2,1},{5,6},{6,5},{9,10},{10,9},{13,14},{14,13},{17,18},{18,... | collective-permute-start | bytes 3145736 | tf_op jit(solution)/shard_map/ppermute | solution.py:21
  370.8 36.0 %collective-permute-start.58 = (f32[128,2048]{1,0:T(8,128)}, f32[128,2048]{1,0:T(8,128)}, u32[]{:S(2)}, u32[]{:S(2)}) collective-permute-start(f32[128,2048]{1,0:T(8,128)} %add.250), channel_id=1, source_target_pairs={{1,0},{2,3},{5,4},{6,7},{9,8},{10,11},{13,12},{14,15},{17,16},{18,... | collective-permute-start | bytes 3145736 | tf_op jit(solution)/shard_map/ppermute | solution.py:21
  412.7 29.5 %collective-permute-start.59 = (f32[128,2048]{1,0:T(8,128)S(1)}, f32[128,2048]{1,0:T(8,128)S(1)}, u32[]{:S(2)}, u32[]{:S(2)}) collective-permute-start(f32[128,2048]{1,0:T(8,128)S(1)} %get-tuple-element.391), channel_id=1, source_target_pairs={{0,1},{3,2},{4,5},{7,6},{8,9},{11,10},{12,13},{15,14},{16,17},{19,... | collective-permute-start | bytes 3145736 | tf_op jit(solution)/shard_map/ppermute | solution.py:21
  414.3 27.9 %collective-permute-start.60 = (f32[128,2048]{1,0:T(8,128)S(1)}, f32[128,2048]{1,0:T(8,128)}, u32[]{:S(2)}, u32[]{:S(2)}) collective-permute-start(f32[128,2048]{1,0:T(8,128)S(1)} %get-tuple-element.392), channel_id=1, source_target_pairs={{1,2},{2,1},{5,6},{6,5},{9,10},{10,9},{13,14},{14,13},{17,18},{18,... | collective-permute-start | bytes 3145736 | tf_op jit(solution)/shard_map/ppermute | solution.py:21
  416.0 26.2 %collective-permute-start.61 = (f32[64,2048]{1,0:T(8,128)}, f32[64,2048]{1,0:T(8,128)}, u32[]{:S(2)}, u32[]{:S(2)}) collective-permute-start(f32[64,2048]{1,0:T(8,128)} %slice_select_fusion.2), channel_id=1, source_target_pairs={{0,16},{4,20},{8,24},{12,28},{16,0},{20,4},{24,8},{28,12},{1,17},{... | collective-permute-start | bytes 1572872 | tf_op jit(solution)/shard_map/ppermute | solution.py:21
  416.0 26.2 %collective-permute-start.62 = (f32[2,2048]{1,0:T(2,128)S(1)}, f32[2,2048]{1,0:T(2,128)S(1)}, u32[]{:S(2)}, u32[]{:S(2)}) collective-permute-start(f32[2,2048]{1,0:T(2,128)S(1)} %fusion.19), channel_id=1, source_target_pairs={{0,2},{1,3},{2,0},{3,1},{4,6},{5,7},{6,4},{7,5},{8,10},{9,11},{10,... | collective-permute-start | bytes 49160 | tf_op jit(solution)/shard_map/ppermute | solution.py:21
  416.0 26.2 %collective-permute-start.63 = (f32[128,2048]{1,0:T(8,128)S(1)}, f32[128,2048]{1,0:T(8,128)}, u32[]{:S(2)}, u32[]{:S(2)}) collective-permute-start(f32[128,2048]{1,0:T(8,128)S(1)} %add.254), channel_id=1, source_target_pairs={{1,0},{2,3},{5,4},{6,7},{9,8},{10,11},{13,12},{14,15},{17,16},{18,... | collective-permute-start | bytes 3145736 | tf_op jit(solution)/shard_map/ppermute | solution.py:21
  445.5 28.9 %collective-permute-start.64 = (f32[128,2048]{1,0:T(8,128)S(1)}, f32[128,2048]{1,0:T(8,128)S(1)}, u32[]{:S(2)}, u32[]{:S(2)}) collective-permute-start(f32[128,2048]{1,0:T(8,128)S(1)} %slice_add_fusion), channel_id=1, source_target_pairs={{1,2},{2,1},{5,6},{6,5},{9,10},{10,9},{13,14},{14,13},{17,18},{18,... | collective-permute-start | bytes 3145736 | tf_op jit(solution)/shard_map/ppermute | solution.py:21
  446.2 28.2 %collective-permute-start.65 = (f32[128,2048]{1,0:T(8,128)S(1)}, f32[128,2048]{1,0:T(8,128)S(1)}, u32[]{:S(2)}, u32[]{:S(2)}) collective-permute-start(f32[128,2048]{1,0:T(8,128)S(1)} %add.258), channel_id=1, source_target_pairs={{1,0},{2,3},{5,4},{6,7},{9,8},{10,11},{13,12},{14,15},{17,16},{18,... | collective-permute-start | bytes 3145736 | tf_op jit(solution)/shard_map/ppermute | solution.py:21
  447.5 26.9 %collective-permute-start.66 = (f32[64,2048]{1,0:T(8,128)S(1)}, f32[64,2048]{1,0:T(8,128)S(1)}, u32[]{:S(2)}, u32[]{:S(2)}) collective-permute-start(f32[64,2048]{1,0:T(8,128)S(1)} %select_add_fusion.2), channel_id=1, source_target_pairs={{0,16},{4,20},{8,24},{12,28},{16,0},{20,4},{24,8},{28,12},{1,17},{... | collective-permute-start | bytes 1572872 | tf_op jit(solution)/shard_map/ppermute | solution.py:21
  449.6 24.8 %collective-permute-start.67 = (f32[2,2048]{1,0:T(2,128)S(1)}, f32[2,2048]{1,0:T(2,128)S(1)}, u32[]{:S(2)}, u32[]{:S(2)}) collective-permute-start(f32[2,2048]{1,0:T(2,128)S(1)} %fusion.103), channel_id=1, source_target_pairs={{0,4},{4,0},{8,12},{12,8},{16,20},{20,16},{24,28},{28,24},{1,5},{5... | collective-permute-start | bytes 49160 | tf_op jit(solution)/shard_map/ppermute | solution.py:21
  477.9 30.6 %collective-permute-start.68 = (f32[128,2048]{1,0:T(8,128)}, f32[128,2048]{1,0:T(8,128)}, u32[]{:S(2)}, u32[]{:S(2)}) collective-permute-start(f32[128,2048]{1,0:T(8,128)} %add.262), channel_id=1, source_target_pairs={{1,0},{2,3},{5,4},{6,7},{9,8},{10,11},{13,12},{14,15},{17,16},{18,... | collective-permute-start | bytes 3145736 | tf_op jit(solution)/shard_map/ppermute | solution.py:21
  479.3 29.2 %collective-permute-start.69 = (f32[128,2048]{1,0:T(8,128)}, f32[128,2048]{1,0:T(8,128)}, u32[]{:S(2)}, u32[]{:S(2)}) collective-permute-start(f32[128,2048]{1,0:T(8,128)} %pad_maximum_fusion.3), channel_id=1, source_target_pairs={{0,8},{4,12},{8,0},{12,4},{16,24},{20,28},{24,16},{28,20},{1,9},{5... | collective-permute-start | bytes 3145736 | tf_op jit(solution)/shard_map/ppermute | solution.py:21
  481.1 25.8 %collective-permute-start.70 = (f32[2,2048]{1,0:T(2,128)S(1)}, f32[2,2048]{1,0:T(2,128)S(1)}, u32[]{:S(2)}, u32[]{:S(2)}) collective-permute-start(f32[2,2048]{1,0:T(2,128)S(1)} %add.263), channel_id=1, source_target_pairs={{0,8},{4,12},{8,0},{12,4},{16,24},{20,28},{24,16},{28,20},{1,9},{5... | collective-permute-start | bytes 49160 | tf_op jit(solution)/shard_map/ppermute | solution.py:21
  510.1 6.5 %collective-permute-start.71 = (f32[256,2048]{1,0:T(8,128)S(1)}, f32[256,2048]{1,0:T(8,128)S(1)}, u32[]{:S(2)}, u32[]{:S(2)}) collective-permute-start(f32[256,2048]{1,0:T(8,128)S(1)} %pad_maximum_fusion.2), channel_id=1, source_target_pairs={{0,4},{4,0},{8,12},{12,8},{16,20},{20,16},{24,28},{28,24},{1,5},{5... | collective-permute-start | bytes 6291464 | tf_op jit(solution)/shard_map/ppermute | solution.py:21
  (105 other events, 778.0 us)
Sparse Core Ops, SparseCore 0:
  60.7 85.9 all-reduce.4
  372.2 110.9 all-reduce.6

commit v3 on v2

--- a/solution.py
+++ b/solution.py
@@ -47,7 +47,7 @@
 
 class Chain:
     def __init__(self, steps):
-        self.steps, self.result = steps, None
+        self.steps, self.result, self.flying = steps, None, None
         self.advance(None)
 
     def advance(self, values):
@@ -59,24 +59,41 @@
 
 class Convoy:
     def __init__(self):
-        self.landed = ()
+        self.landed, self.sent, self.done = (), (), ()
+
+    def launch(self, *chains):
+        for chain in chains:
+            if chain.due:
+                values = after([value for value, _, _ in chain.due], self.landed, self.sent)
+                chain.flying = [
+                    hop(value, axis, way) for value, (_, axis, way) in zip(values, chain.due)
+                ]
+                self.sent = (self.sent, values)
+
+    def work(self, work, *operands):
+        self.done = work(*after(operands, self.sent, self.landed))
+        return self.done
+
+    def land(self, *chains):
+        chains = [chain for chain in chains if chain.flying is not None]
+        came = after([chain.flying for chain in chains], self.done)
+        self.landed, self.sent = (came, self.done), ()
+        for chain, values in zip(chains, came):
+            chain.flying = None
+            chain.advance(values)
 
     def wave(self, chains, work=None, *operands):
-        chains = [chain for chain in chains if chain.due]
-        values = [after([value for value, _, _ in chain.due], self.landed) for chain in chains]
-        flying = [
-            [hop(value, axis, way) for value, (_, axis, way) in zip(sent, chain.due)]
-            for sent, chain in zip(values, chains)
-        ]
-        result = None if work is None else work(*after(operands, values, self.landed))
-        flying = after(flying, values if result is None else result)
-        for chain, came in zip(chains, flying):
-            chain.advance(came)
-        self.landed = (flying, result)
+        self.launch(*chains)
+        result = None if work is None else self.work(work, *operands)
+        self.land(*chains)
         return result
 
-
-def gather_steps(value, slots, even=False):
+    def finish(self, chain):
+        while chain.due:
+            self.wave([chain])
+
+
+def gather_steps(value, slots):
     count = lax.axis_size("blk")
     slots[0] = [value]
     if count != 8:
@@ -87,78 +104,47 @@
             bit *= 2
         return
     half = value.shape[0] // 16 * 8
-    low, high = value[:half], value[half:]
-    if even:
-        x_low, y_high, own_pair = yield [(low, "blk", 2), (high, "blk", 4), (value, "blk", 1)]
-        slots[1] = [own_pair]
-        x_high, y_low = yield [(high, "blk", 2), (low, "blk", 4)]
-        slots[2], slots[4] = [x_low, x_high], [y_low, y_high]
-        slots[6] = yield [(x_low, "blk", 4), (y_high, "blk", 2)]
-        first = yield [(x_low, "blk", 1), (y_high, "blk", 1)]
-        second = yield [(x_high, "blk", 1), (y_low, "blk", 1)]
-        slots[3], slots[5] = [first[0], second[0]], [second[1], first[1]]
-    else:
-        x_all, y_all, own_pair = yield [(value, "blk", way) for way in (2, 4, 1)]
-        slots[1], slots[2], slots[4] = [own_pair], [x_all], [y_all]
-        *slots[6], x_pair, y_pair = yield [
-            (x_all[:half], "blk", 4),
-            (y_all[half:], "blk", 2),
-            (x_all, "blk", 1),
-            (y_all, "blk", 1),
-        ]
-        slots[3], slots[5] = [x_pair], [y_pair]
+    x_all, y_all, own_pair = yield [(value, "blk", way) for way in (2, 4, 1)]
+    slots[1], slots[2], slots[4] = [own_pair], [x_all], [y_all]
+    *slots[6], x_pair, y_pair = yield [
+        (x_all[:half], "blk", 4),
+        (y_all[half:], "blk", 2),
+        (x_all, "blk", 1),
+        (y_all, "blk", 1),
+    ]
+    slots[3], slots[5] = [x_pair], [y_pair]
     slots[7] = yield [(part, "blk", 1) for part in slots[6]]
-
-
-def halves(value, bit):
-    low, high = jnp.split(value, 2)
-    upper = (lax.axis_index("blk") & bit) != 0
-    return jnp.where(upper, high, low), jnp.where(upper, low, high)
-
-
-def paired(value, other, bit):
-    upper = (lax.axis_index("blk") & bit) != 0
-    return jnp.concatenate([jnp.where(upper, other, value), jnp.where(upper, value, other)])
-
-
-def sum_steps(value):
-    count = lax.axis_size("blk")
-    bits = [1 << place for place in range(count.bit_length() - 1)]
-    for bit in bits:
-        keep, send = halves(value, bit)
-        (got,) = yield [(send, "blk", bit)]
-        value = keep + got
-    for bit in reversed(bits):
-        (got,) = yield [(value, "blk", bit)]
-        value = paired(value, got, bit)
-    return value
 
 
 def small_steps(value):
     for axis in ("head", "blk"):
         bit = 1
         while bit < lax.axis_size(axis):
-            (got,) = yield [(value, axis, bit)]
-            value = value + got
-            bit *= 2
+            ways = [bit]
+            if axis == "blk" and bit == 2 and lax.axis_size(axis) == 8:
+                ways = [2, 4, 6]
+            for got in (yield [(value, axis, way) for way in ways]):
+                value = value + got
+            bit *= 2 * len(ways)
     return value
 
 
-def head_steps(value):
+def head_share(value, step=0):
+    rows = value.shape[0] // lax.axis_size("head")
+    return lax.dynamic_slice_in_dim(value, (lax.axis_index("head") ^ step) * rows, rows)
+
+
+def head_steps(value, finish=None):
     count, mine = lax.axis_size("head"), lax.axis_index("head")
-    rows = value.shape[0] // count
-
-    def share(step):
-        return lax.dynamic_slice_in_dim(value, (mine ^ step) * rows, rows)
-
-    got = yield [(share(step), "head", step) for step in range(1, count)]
-    total = share(0)
+    got = yield [(head_share(value, step), "head", step) for step in range(1, count)]
+    total = head_share(value)
     for part in got:
         total = total + part
+    total = total if finish is None else finish(total)
     got = yield [(total, "head", step) for step in range(1, count)]
     whole = jnp.zeros_like(value)
     for step, part in enumerate([total, *got]):
-        whole = lax.dynamic_update_slice_in_dim(whole, part, (mine ^ step) * rows, 0)
+        whole = lax.dynamic_update_slice_in_dim(whole, part, (mine ^ step) * part.shape[0], 0)
     return whole
 
 
@@ -464,64 +450,72 @@
     )
     attn_part = mm(attended, w_out)
     attn_sum = sum_head(attn_part)
+    order = [0, 1, 2, 4, 3, 5, 6, 7] if blk_count == 8 else list(range(blk_count))
+    early, late = order[: blk_count // 2], order[blk_count // 2 :]
+    ones = jnp.ones_like(gain_two)
     convoy = Convoy()
+
+    def ready(chain, slots, wanted):
+        while not all(slot in slots for slot in wanted):
+            convoy.wave([chain])
+        return [slots[slot] for slot in wanted]
+
+    def cot_work(*slots):
+        rows_of = join_rounded(slots, ones)
+        return rows_of, mm_t(rows_of, w_down)
+
+    def gate_work(*slots):
+        rows_of = join_rounded(slots, gain_two)
+        return rows_of, mm(rows_of, w_gate)
+
+    def up_work(rows_of, gate, hidden_grad):
+        return gated(gate, mm(rows_of, w_up), hidden_grad)
+
     cot_slots = {}
     cot = Chain(gather_steps(after(cot_wide, qkv[-2]), cot_slots))
     own_hidden_grad = convoy.wave(
         [cot], lambda left, _: mm_t(left, w_down), cotangent, attn_part
     )
-    token_sum = after(token_wide, convoy.landed) + attn_sum
-
-    def middle(resid_mid):
-        inv_mid = lax.rsqrt(jnp.mean(resid_mid * resid_mid, axis=-1, keepdims=True) + epsilon)
-        scaled_mid = resid_mid * inv_mid
+    cot_early = ready(cot, cot_slots, early)
+    convoy.launch(cot)
+    cot_a, hidden_grad_a = convoy.work(cot_work, *cot_early)
+    resid_mid = after(token_wide, convoy.done) + attn_sum
+    inv_mid = lax.rsqrt(jnp.mean(resid_mid * resid_mid, axis=-1, keepdims=True) + epsilon)
+    scaled_mid = resid_mid * inv_mid
+    convoy.done = scaled_mid
+    convoy.land(cot)
+    mid_slots = {}
+    mid = Chain(gather_steps(scaled_mid, mid_slots))
+
+    def middle(scaled_mid):
         normed_mid = (scaled_mid * gain_two).astype(bf16)
         hidden, gate_lin_grad, up_lin_grad = gated(
             mm(normed_mid, w_gate), mm(normed_mid, w_up), own_hidden_grad
         )
-        mid_part = mm_t(gate_lin_grad, w_gate) + mm_t(up_lin_grad, w_up)
-        return resid_mid, inv_mid, scaled_mid, hidden, mid_part
-
-    resid_mid, inv_mid, scaled_mid, hidden, mid_part = convoy.wave([cot], middle, token_sum)
-
-    def ready(chain, slots, wanted):
-        while not all(slot in slots for slot in wanted):
-            convoy.wave([chain])
-        return [slots[slot] for slot in wanted]
-
-    order = [0, 1, 2, 4, 3, 5, 6, 7] if blk_count == 8 else list(range(blk_count))
-    early, late = order[: blk_count // 2], order[blk_count // 2 :]
-    ones = jnp.ones_like(gain_two)
-    mid_slots = {}
-    mid_sum = Chain(line_steps(mid_part, 2))
-    mid = Chain(gather_steps(scaled_mid, mid_slots, even=True))
-    cot_early, cot_late = ready(cot, cot_slots, early), ready(cot, cot_slots, late)
+        return hidden, mm_t(gate_lin_grad, w_gate) + mm_t(up_lin_grad, w_up)
+
+    convoy.launch(mid, cot)
+    hidden, mid_part = convoy.work(middle, scaled_mid)
+    convoy.land(cot)
+    mid_sum = sum_head(mid_part)
 
     def share_work(hidden, *slots):
         mlp_part = mm(hidden, w_down)
-        cot_a = join_rounded(after(slots[: len(early)], mlp_part), ones)
-        return mlp_part, cot_a, join_rounded(after(slots[len(early) :], cot_a), ones)
-
-    mlp_part, cot_a, cot_b = convoy.wave([mid_sum, mid], share_work, hidden, *cot_early, *cot_late)
-    hidden_grad_a, hidden_grad_b = convoy.wave(
-        [mid_sum, mid], lambda a, b: (mm_t(a, w_down), mm_t(b, w_down)), cot_a, cot_b
+        return mlp_part, *cot_work(*after(slots, mlp_part))
+
+    mlp_part, cot_b, hidden_grad_b = convoy.work(
+        share_work, hidden, *ready(cot, cot_slots, late)
     )
     mlp = Chain(line_steps(mlp_part, 2))
-
-    def gate_work(*slots):
-        rows_of = join_rounded(slots, gain_two)
-        return rows_of, mm(rows_of, w_gate)
-
-    def up_work(rows_of, gate, hidden_grad):
-        return gated(gate, mm(rows_of, w_up), hidden_grad)
-
-    mid_a, gate_a = convoy.wave([mid_sum, mid, mlp], gate_work, *ready(mid, mid_slots, early))
-    hidden_a, gate_grad_a, up_grad_a = convoy.wave(
-        [mid_sum, mid, mlp], up_work, mid_a, gate_a, hidden_grad_a
-    )
-    while mid_sum.due:
-        convoy.wave([mid_sum])
-    mid_grad = mid_sum.result
+    convoy.land(mid)
+    mid_early = ready(mid, mid_slots, early)
+    convoy.launch(mid)
+    mid_a, gate_a = convoy.work(gate_work, *mid_early)
+    hidden_a, gate_grad_a, up_grad_a = convoy.work(
+        up_work, after(mid_a, convoy.done), gate_a, hidden_grad_a
+    )
+    down_a = convoy.work(t_mm, after(hidden_a, convoy.done), cot_a)
+    mid_grad = after(mid_sum, down_a)
 
     resid_grad = cot_wide + norm_back(mid_grad, resid_mid, inv_mid, gain_two)
     out_lin_grad = resid_grad.astype(bf16)
@@ -530,8 +524,11 @@
     denom_grad = -jnp.sum((numer_grad * mean).reshape(rows, heads, DV), axis=-1)
     denom_lines = denom_grad.T.reshape(rows // DV, vw)
     denom_lines = jnp.pad(denom_lines, ((0, -denom_lines.shape[0] % 8), (0, 0)))
+    sent = jnp.concatenate([numer_grad, denom_lines])
+    convoy.done = sent
+    convoy.land(mid)
     grad_slots = {}
-    grads = Chain(gather_steps(jnp.concatenate([numer_grad, denom_lines]), grad_slots))
+    grads = Chain(gather_steps(sent, grad_slots))
 
     def query_work(numer_grad, denom_grad, out_lin_grad):
         (query_lin_grad,) = whole_call(
@@ -546,13 +543,14 @@
         )
         return query_lin_grad, t_mm(attended, after(out_lin_grad, query_lin_grad))
 
-    query_lin_grad, out_part = convoy.wave(
-        [grads, mid], query_work, numer_grad, denom_grad, out_lin_grad
-    )
-    out = Chain(sum_steps(out_part))
-    down_a = convoy.wave([grads, out], t_mm, hidden_a, cot_a)
-    convoy.wave([grads, mid])
-    grad_slots = ready(grads, grad_slots, range(blk_count))
+    convoy.launch(grads, mlp)
+    query_lin_grad, out_part = convoy.work(query_work, numer_grad, denom_grad, out_lin_grad)
+    convoy.land(grads)
+    gate_part = convoy.wave([grads], t_mm, mid_a, gate_grad_a)
+    convoy.launch(grads)
+    convoy.land(grads, mlp)
+    convoy.finish(grads)
+    grad_slots = [grad_slots[slot] for slot in range(blk_count)]
     grad_shape = tuple(len(slot) for slot in grad_slots)
 
     def key_work(query_lin_grad, grad_parts):
@@ -570,8 +568,14 @@
         return in_part, query_lin_grad, key_lin_grad, value_grad
 
     grad_parts = [part for slot in grad_slots for part in slot]
-    in_part, *lin_grads = convoy.wave([], key_work, query_lin_grad, grad_parts)
-    late_in = after(normed_in, in_part)
+    convoy.launch(mid, mlp)
+    in_part, *lin_grads = convoy.work(key_work, query_lin_grad, grad_parts)
+    convoy.land(mid)
+    mid_late = ready(mid, mid_slots, late)
+
+    in_sum = Chain(line_steps(in_part, 2))
+    convoy.launch(in_sum)
+    late_in = after(normed_in, convoy.sent)
     parts = [t_mm(late_in, grad) for grad in lin_grads]
     gain_parts = jnp.stack(
         [
@@ -579,40 +583,38 @@
             jnp.sum(mid_part * scaled_mid, axis=0),
         ]
     )
-    qkv_w_grads = lax.psum(tuple(parts), "blk")
+    *qkv_w_grads, out_w_grad = lax.psum((*parts, out_part), "blk")
     gains = Chain(small_steps(gain_parts))
-
-    in_sum = Chain(line_steps(in_part, 2))
-    mid_late = ready(mid, mid_slots, late)
-
-    def third_work(hidden_b, down_a, gate_grad_a):
-        down_w_grad = down_a + t_mm(hidden_b, cot_b)
-        return down_w_grad, t_mm(mid_a, after(gate_grad_a, down_w_grad))
-
-    def second_work(mid_b, gate_b, hidden_grad_b, up_grad_a):
+    convoy.launch(gains)
+    chains = [in_sum, gains, mlp]
+    mid_b, gate_b = convoy.work(gate_work, *after(mid_late, gain_parts))
+    convoy.land(*chains)
+
+    def second_work(mid_b, gate_b, hidden_grad_b):
         parts = up_work(mid_b, gate_b, hidden_grad_b)
         return (*parts, t_mm(mid_a, after(up_grad_a, parts)))
 
-    def last_work(gate_grad_b, gate_part, up_grad_b, up_part, mlp_sum):
-        gate_w_grad = gate_part + t_mm(mid_b, gate_grad_b)
-        output = (resid_mid + after(mlp_sum, gate_w_grad)).astype(bf16)
-        late_grad = after(up_grad_b, gate_w_grad, output, qkv_w_grads)
-        return gate_w_grad, up_part + t_mm(mid_b, late_grad), output
-
-    chains = [in_sum, out, gains, mlp]
-    mid_b, gate_b = convoy.wave(chains, gate_work, *after(mid_late, parts))
     hidden_b, gate_grad_b, up_grad_b, up_part = convoy.wave(
-        chains, second_work, mid_b, gate_b, hidden_grad_b, up_grad_a
-    )
-    down_w_grad, gate_part = convoy.wave(chains, third_work, hidden_b, down_a, gate_grad_a)
-    while mlp.due:
-        convoy.wave([mlp])
-    gate_w_grad, up_w_grad, output = convoy.wave(
-        chains, last_work, gate_grad_b, gate_part, up_grad_b, up_part, mlp.result
-    )
+        chains, second_work, mid_b, gate_b, hidden_grad_b
+    )
+    down_w_grad = convoy.wave(chains, lambda x, y: down_a + t_mm(x, y), hidden_b, cot_b)
+    convoy.finish(mlp)
+
+    def gate_last(gate_grad_b, mlp_sum):
+        output = (resid_mid + mlp_sum).astype(bf16)
+        return gate_part + t_mm(mid_b, after(gate_grad_b, output)), output
+
+    chains = [in_sum, gains]
+    convoy.launch(*chains)
+    gate_w_grad, output = convoy.work(gate_last, gate_grad_b, mlp.result)
+    up_w_grad = convoy.work(
+        lambda x: up_part + t_mm(mid_b, x), after(up_grad_b, gate_w_grad)
+    )
+    convoy.land(*chains)
     while any(chain.due for chain in chains):
         convoy.wave(chains)
-    in_grad, out_w_grad, gain_grads = (chain.result for chain in chains[:3])
+    in_grad, gain_grads = (chain.result for chain in chains)
+    in_grad = after(in_grad, qkv_w_grads, out_w_grad)
     input_grad = resid_grad + norm_back(in_grad, token_wide, inv_in, gain_one)
     return (
         output,

time: 542 us -> 531 us (0.980)
  waiting for transfers between devices: 120 us -> 142 us
  starting transfers between devices: 75.8 us -> 58.1 us
  other arithmetic: 56.4 us -> 39.1 us
    ppermute x73 -> x58, waiting for transfers between devices: 75.2 us -> 94.2 us  [hop(): return lax.ppermute(value, axis, way)]
    ppermute x73 -> x58, starting transfers between devices: 75.1 us -> 58 us  [hop(): return lax.ppermute(value, axis, way)]
    add x12 -> x8, other arithmetic: 15.7 us -> 6.82 us  [line_steps(): into[piece] = own[piece] + part]
    add x4 -> x0, other arithmetic: 6.1 us -> none  [the longest x3 3.62 us: sum_steps(): value = keep + got]
    dot_general x9, matrix products: 30.4 us -> 36 us  [mm_t(): return jnp.einsum('ac,bc->ab', left, right, preferred_element_type=f32)]
    unnamed x192 -> x171, local copies, waits for them, and re-layouts: 18.9 us -> 22.4 us
    psum x1 -> x2, waiting for transfers between devices: 44.9 us -> 47.8 us  [sum_head(): return lax.psum(value, 'head')]
  transfers between devices with their start and end apart: 75 -> 61, of which waited for: 23 -> 16; matrix products, arithmetic and copies ran while one was open for 40% -> 41% of each run, Pallas kernels for 8% -> 10%
where the time goes in v3:
time: 531 us; the launch traced here: 522 us
  matrix products  173 us (33%)
  waiting for transfers between devices  142 us (27%)
  starting transfers between devices  58.1 us (11%)
  Pallas kernels  53.7 us (10%)
  other arithmetic  39.1 us (7%)
  local copies, waits for them, and re-layouts  38.3 us (7%)
  between operations  17.7 us (3%)
    ppermute x58, waiting for transfers between devices, hop(): return lax.ppermute(value, axis, way)  94.2 us
    dot_general x10, matrix products, t_mm(): return jnp.einsum('ca,cb->ab', left, right, preferred_element_type=f32)  69 us
    dot_general x11, matrix products, mm(): return jnp.dot(left, right, preferred_element_type=f32)  67.9 us
    ppermute x58, starting transfers between devices, hop(): return lax.ppermute(value, axis, way)  58 us
    psum x2, waiting for transfers between devices, sum_head(): return lax.psum(value, 'head')  47.8 us
    dot_general x9, matrix products, mm_t(): return jnp.einsum('ac,bc->ab', left, right, preferred_element_type=f32)  36 us
    pallas_call x3, Pallas kernels, whole_call(): pl.pallas_call(body, out_shape=outs, in_specs=[pl.BlockSpec(memory_space=...  28.6 us
    pallas_call x4, Pallas kernels, join_rounded(): pl.pallas_call(functools.partial(join_kernel, tuple((len(slot) for slot i...  25.1 us
  transfers between devices with their start and end apart: 61, of which 16 were waited for; matrix products, arithmetic and copies ran while one was open for 41% of the time, Pallas kernels for 10%

profile of v3, /device:TPU:0, one launch (start us, length us, event | category | flops | bytes accessed | tf_op | source)
XLA Modules:
  0.0 521.9 jit_solution(1024088769776376119)
XLA Ops:
  15.3 3.0 collective-permute-start
  19.8 6.2 %collective-permute-done.refs_2_ = f32[128,640]{1,0:T(8,128)S(1)} collective-permute-done((f32[128,640]{1,0:T(8,128)S(1)}, f32[128,640]{1,0:T(8,128)S(1)}, u32[]{:S(2)}, u32[]{:S(2)}) %collective-permute-start) | collective-permute-done | bytes 327712 | tf_op jit(solution)/shard_map/ppermute | solution.py:21
  26.0 1.8 collective-permute-start.1
  31.0 5.6 %collective-permute-done.1.refs_10_ = f32[128,640]{1,0:T(8,128)S(1)} collective-permute-done((f32[128,640]{1,0:T(8,128)S(1)}, f32[128,640]{1,0:T(8,128)S(1)}, u32[]{:S(2)}, u32[]{:S(2)}) %collective-permute-start.1) | collective-permute-done | bytes 327712 | tf_op jit(solution)/shard_map/ppermute | solution.py:21
  39.0 1.8 collective-permute-start.4
  40.8 3.1 collective-permute-done.8.refs_3_
  56.6 7.9 %shard_map.203 = (bf16[256,512]{1,0:T(8,128)(2,1)}, f32[256,512]{1,0:T(8,128)}, f32[256,512]{1,0:T(8,128)}) custom-call(s32[256,4]{1,0:T(8,128)} %copy.28.col_ref, s32[24,256]{1,0:T(8,128)} %pad_add_fusion.row_ref, f32[256,640]{1,0:T(8,128)} %pad_maximum_fusion.2.refs_0_, f32[256,640]{1,0:T(8,128)} %collective-permute-done.7.refs_1_, f32[128,640]{1,0:T(8,128)} %copy-done.60, ...), custom_call_target="tpu_custom_call" | custom-call | flops 2147483648 | bytes 6582272 | tf_op jit(solution)/shard_map/pallas_call | solution.py:318
  64.5 3.0 fusion.30
  67.6 5.7 %fusion.31 = f32[256,1376]{0,1:T(8,128)} fusion(bf16[256,2048]{1,0:T(8,128)(2,1)} %param.23, bf16[1376,2048]{1,0:T(8,128)(2,1)} %param.21), kind=kOutput, calls=%fused_computation.93 | convolution fusion | flops 1442840576 | bytes 8093696 | tf_op jit(solution)/shard_map/ac,bc->ab/dot_general | solution.py:374
  73.3 14.9 %collective-permute-done.4.refs_2_ = f32[256,2048]{1,0:T(8,128)} collective-permute-done((f32[256,2048]{1,0:T(8,128)}, f32[256,2048]{1,0:T(8,128)}, u32[]{:S(2)}, u32[]{:S(2)}) %collective-permute-start.4) | collective-permute-done | bytes 2097184 | tf_op jit(solution)/shard_map/ppermute | solution.py:21
  88.9 2.3 slice.48
  91.2 2.3 slice.49
  96.6 6.2 %shard_map.204 = bf16[1024,2048]{1,0:T(8,128)(2,1)} custom-call(f32[1,2048]{1,0:T(1,128)} %broadcast_12_scale_ref.2.scale_ref, f32[256,2048]{1,0:T(8,128)} %convert_element_type.115.refs_0_, f32[256,2048]{1,0:T(8,128)} %collective-permute-done.6.refs_1_, f32[256,2048]{1,0:T(8,128)} %collective-permute-done.4.refs_2_, f32[256,2048]{1,0:T(8,128)} %collective-permute-done.5.refs_3_), custom_call_target="tpu_custom_call" | custom-call | bytes 12582912 | tf_op jit(solution)/shard_map/pallas_call | solution.py:345
  102.9 10.9 %fusion.32 = f32[1024,1376]{0,1:T(8,128)} fusion(bf16[1024,2048]{1,0:T(8,128)(2,1)} %shard_map.204, bf16[1376,2048]{1,0:T(8,128)(2,1)} %param.21), kind=kOutput, calls=%fused_computation.94 | convolution fusion | flops 5771362304 | bytes 15466496 | tf_op jit(solution)/shard_map/ac,bc->ab/dot_general | solution.py:374
  113.8 41.4 %all-reduce.6.cloned.1.call-done = f32[256,2048]{1,0:T(8,128)} async-done(((f32[256,2048]{1,0:T(8,128)}), f32[256,2048]{1,0:T(8,128)}) %all-reduce.6.cloned.1.call-update) | async-done | bytes 2097168 | tf_op jit(solution)/shard_map/psum | solution.py:179
  155.1 2.5 multiply_reduce_fusion.4
  163.4 5.1 fusion.8
  168.5 4.5 multiply_convert_fusion.10
  173.0 2.2 fusion.3
  175.2 3.2 convolution_add_fusion.5
  178.5 4.7 fusion.33
  185.5 6.4 %shard_map.205 = bf16[1024,2048]{1,0:T(8,128)(2,1)} custom-call(f32[1,2048]{1,0:T(1,128)} %broadcast_12_scale_ref.2.scale_ref, f32[256,2048]{1,0:T(8,128)} %collective-permute-done.18.refs_0_, f32[256,2048]{1,0:T(8,128)} %collective-permute-done.19.refs_1_, f32[128,2048]{1,0:T(8,128)} %collective-permute-done.16.refs_2_, ...), custom_call_target="tpu_custom_call" | custom-call | bytes 12582912 | tf_op jit(solution)/shard_map/pallas_call | solution.py:345
  191.9 10.9 %fusion.34 = f32[1024,1376]{0,1:T(8,128)} fusion(bf16[1024,2048]{1,0:T(8,128)(2,1)} %shard_map.205, bf16[1376,2048]{1,0:T(8,128)(2,1)} %param.21), kind=kOutput, calls=%fused_computation.96 | convolution fusion | flops 5771362304 | bytes 15466496 | tf_op jit(solution)/shard_map/ac,bc->ab/dot_general | solution.py:374
  202.8 5.5 %collective-permute-done.20.refs_2_ = f32[256,2048]{1,0:T(8,128)} collective-permute-done((f32[256,2048]{1,0:T(8,128)}, f32[256,2048]{1,0:T(8,128)}, u32[]{:S(2)}, u32[]{:S(2)}) %collective-permute-start.20) | collective-permute-done | bytes 2097184 | tf_op jit(solution)/shard_map/ppermute | solution.py:21
  209.5 2.3 slice.50
  211.8 2.3 slice.51
  216.7 6.2 %shard_map.206 = bf16[1024,2048]{1,0:T(8,128)(2,1)} custom-call(f32[1,2048]{1,0:T(1,128)} %bitcast.81, f32[256,2048]{1,0:T(8,128)} %broadcast_multiply_fusion.refs_0_, f32[256,2048]{1,0:T(8,128)} %collective-permute-done.22.refs_1_, f32[256,2048]{1,0:T(8,128)} %collective-permute-done.20.refs_2_, f32[256,2048]{1,0:T(8,128)} %collective-permute-done.21.refs_3_), custom_call_target="tpu_custom_call" | custom-call | bytes 12582912 | tf_op jit(solution)/shard_map/pallas_call | solution.py:345
  222.9 11.3 %fusion.35 = f32[1024,1376]{0,1:T(8,128)} fusion(bf16[1024,2048]{1,0:T(8,128)(2,1)} %shard_map.206, bf16[2048,1376]{0,1:T(8,128)(2,1)} %param.19), kind=kOutput, calls=%fused_computation.97 | convolution fusion | flops 5771362304 | bytes 15466496 | tf_op jit(solution)/shard_map/dot_general | solution.py:370
  234.3 12.8 %multiply_convert_fusion.3 = (bf16[1024,1376]{0,1:T(8,128)(2,1)}, bf16[1024,1376]{0,1:T(8,128)(2,1)}, bf16[1024,1376]{0,1:T(8,128)(2,1)S(1)}) fusion(f32[1024,1376]{0,1:T(8,128)} %fusion.32, f32[1024,1376]{0,1:T(8,128)} %fusion.35, bf16[1024,2048]{1,0:T(8,128)(2,1)S(1)} %copy-done.21, bf16[2048,1376]{0,1:T(8,128)(2,1)S(1)} %bitcast.74), kind=kOutput, calls=%fused_computation.8 | convolution fusion | flops 5792497664 | bytes 29556736 | tf_op jit(solution)/shard_map/dot_general | solution.py:370
  247.0 8.9 %fusion.36 = f32[1376,2048]{1,0:T(8,128)} fusion(bf16[1024,1376]{0,1:T(8,128)(2,1)S(1)} %get-tuple-element.241, bf16[1024,2048]{1,0:T(8,128)(2,1)S(1)} %copy-done.25), kind=kOutput, calls=%fused_computation.98 | convolution fusion | flops 5771362304 | bytes 18284544 | tf_op jit(solution)/shard_map/ca,cb->ab/dot_general | solution.py:378
  256.0 6.5 %all-reduce.8.cloned.1.call-done = f32[256,2048]{1,0:T(8,128)} async-done(((f32[256,2048]{1,0:T(8,128)}), f32[256,2048]{1,0:T(8,128)}) %all-reduce.8.cloned.1.call-update) | async-done | bytes 2097168 | tf_op jit(solution)/shard_map/psum | solution.py:179
  262.4 2.7 multiply_reduce_fusion.3
  265.9 2.8 multiply_reduce_fusion.1
  274.3 2.9 collective-permute-start.38
  278.4 9.4 %shard_map.207 = bf16[256,64]{1,0:T(8,128)(2,1)} custom-call(s32[256,4]{1,0:T(8,128)} %copy.28.col_ref, s32[24,256]{1,0:T(8,128)} %pad_add_fusion.row_ref, f32[256,512]{1,0:T(8,128)} %copy-done.30, f32[256,512]{1,0:T(8,128)} %bitcast.80, f32[256,640]{1,0:T(8,128)} %pad_maximum_fusion.2.refs_0_, f32[256,640]{1,0:T(8,128)} %collective-permute-done.7.refs_1_, ...), custom_call_target="tpu_custom_call" | custom-call | flops 2147483648 | bytes 6352896 | tf_op jit(solution)/shard_map/pallas_call | solution.py:318
  287.9 2.9 fusion.38
  293.0 8.8 %fusion.44 = f32[2048,1376]{0,1:T(8,128)} fusion(bf16[1024,1376]{0,1:T(8,128)(2,1)S(1)} %copy-done.69, bf16[1024,2048]{1,0:T(8,128)(2,1)S(1)} %copy-done.22), kind=kOutput, calls=%fused_computation.106 | convolution fusion | flops 5771362304 | bytes 18284544 | tf_op jit(solution)/shard_map/ca,cb->ab/dot_general | solution.py:378
  303.7 1.6 collective-permute-done.36.refs_22_
  305.3 2.8 slice_add_fusion.3
  308.7 2.3 collective-permute-start.43
  311.0 1.8 collective-permute-start.44
  312.8 11.3 %shard_map.208 = (bf16[256,64]{1,0:T(8,128)(2,1)}, bf16[256,512]{1,0:T(8,128)(2,1)}) custom-call(s32[256,4]{1,0:T(8,128)} %copy.28.col_ref, s32[24,256]{1,0:T(8,128)} %pad_add_fusion.row_ref, f32[256,640]{1,0:T(8,128)} %pad_maximum_fusion.2.refs_0_, f32[256,640]{1,0:T(8,128)} %collective-permute-done.7.refs_1_, f32[128,640]{1,0:T(8,128)} %copy-done.60, ...), custom_call_target="tpu_custom_call" | custom-call | flops 4294967296 | bytes 9891840 | tf_op jit(solution)/shard_map/pallas_call | solution.py:318
  329.5 2.8 fusion.42
  334.5 1.9 multiply_reduce_fusion.2
  336.5 1.9 collective-permute-start.41
  338.5 6.2 %shard_map.209 = bf16[1024,2048]{1,0:T(8,128)(2,1)} custom-call(f32[1,2048]{1,0:T(1,128)} %bitcast.82, f32[256,2048]{1,0:T(8,128)} %collective-permute-done.27.refs_0_, f32[256,2048]{1,0:T(8,128)} %collective-permute-done.28.refs_1_, f32[128,2048]{1,0:T(8,128)} %collective-permute-done.25.refs_2_, f32[128,2048]{1,0:T(8,128)} %collective-permute-done.26.refs_3_, ...), custom_call_target="tpu_custom_call" | custom-call | bytes 12582912 | tf_op jit(solution)/shard_map/pallas_call | solution.py:345
  344.7 11.0 %fusion.43 = f32[1024,1376]{0,1:T(8,128)} fusion(bf16[1024,2048]{1,0:T(8,128)(2,1)} %shard_map.209, bf16[2048,1376]{0,1:T(8,128)(2,1)} %param.19), kind=kOutput, calls=%fused_computation.105 | convolution fusion | flops 5771362304 | bytes 15466496 | tf_op jit(solution)/shard_map/dot_general | solution.py:370
  355.7 5.5 %collective-permute-done.42 = f32[2,2048]{1,0:T(2,128)S(1)} collective-permute-done((f32[2,2048]{1,0:T(2,128)S(1)}, f32[2,2048]{1,0:T(2,128)S(1)}, u32[]{:S(2)}, u32[]{:S(2)}) %collective-permute-start.42) | collective-permute-done | bytes 16416 | tf_op jit(solution)/shard_map/ppermute | solution.py:21
  362.2 1.7 add.228
  368.9 7.5 %collective-permute-start.45 = (f32[128,2048]{1,0:T(8,128)S(1)}, f32[128,2048]{1,0:T(8,128)S(1)}, u32[]{:S(2)}, u32[]{:S(2)}) collective-permute-start(f32[128,2048]{1,0:T(8,128)S(1)} %get-tuple-element.315), channel_id=1, source_target_pairs={{0,1},{3,2},{4,5},{7,6},{8,9},{11,10},{12,13},{15,14},{16,17},{19,... | collective-permute-start | bytes 3145736 | tf_op jit(solution)/shard_map/ppermute | solution.py:21
  377.1 2.0 collective-permute-start.47
  379.2 14.1 %multiply_convert_fusion = (bf16[1024,1376]{0,1:T(8,128)(2,1)}, bf16[1024,1376]{0,1:T(8,128)(2,1)}, bf16[1024,1376]{0,1:T(8,128)(2,1)}) fusion(f32[1024,1376]{0,1:T(8,128)} %fusion.34, f32[1024,1376]{0,1:T(8,128)} %fusion.43, bf16[1024,2048]{1,0:T(8,128)(2,1)} %shard_map.209, bf16[2048,1376]{0,1:T(8,128)(2,1)S(1)} %bitcast.76), kind=kOutput, calls=%fused_computation.3 | convolution fusion | flops 5792497664 | bytes 29556736 | tf_op jit(solution)/shard_map/dot_general | solution.py:370
  393.3 10.5 %fusion.45 = f32[2048,1376]{0,1:T(8,128)} fusion(bf16[1024,1376]{0,1:T(8,128)(2,1)} %get-tuple-element.323, bf16[1024,2048]{1,0:T(8,128)(2,1)S(1)} %copy-done.23), kind=kOutput, calls=%fused_computation.107 | convolution fusion | flops 5771362304 | bytes 18284544 | tf_op jit(solution)/shard_map/ca,cb->ab/dot_general | solution.py:378
  403.8 15.2 %collective-permute-done.47 = f32[2,2048]{1,0:T(2,128)S(1)} collective-permute-done((f32[2,2048]{1,0:T(2,128)S(1)}, f32[2,2048]{1,0:T(2,128)S(1)}, u32[]{:S(2)}, u32[]{:S(2)}) %collective-permute-start.47) | collective-permute-done | bytes 16416 | tf_op jit(solution)/shard_map/ppermute | solution.py:21
  423.3 11.4 %convolution_add_fusion.2 = f32[1376,2048]{1,0:T(8,128)} fusion(f32[1376,2048]{1,0:T(8,128)} %fusion.36, bf16[1024,1376]{0,1:T(8,128)(2,1)S(1)} %copy-done.71, bf16[1024,2048]{1,0:T(8,128)(2,1)S(1)} %copy-done.20), kind=kOutput, calls=%fused_computation.2 | convolution fusion | flops 5774180352 | bytes 29556736 | tf_op jit(solution)/shard_map/ca,cb->ab/dot_general | solution.py:378
  434.9 12.8 %collective-permute-done.53 = f32[128,2048]{1,0:T(8,128)S(1)} collective-permute-done((f32[128,2048]{1,0:T(8,128)S(1)}, f32[128,2048]{1,0:T(8,128)S(1)}, u32[]{:S(2)}, u32[]{:S(2)}) %collective-permute-start.53) | collective-permute-done | bytes 1048608 | tf_op jit(solution)/shard_map/ppermute | solution.py:21
  447.7 20.2 %collective-permute-done.51 = f32[128,2048]{1,0:T(8,128)S(1)} collective-permute-done((f32[128,2048]{1,0:T(8,128)S(1)}, f32[128,2048]{1,0:T(8,128)S(1)}, u32[]{:S(2)}, u32[]{:S(2)}) %collective-permute-start.51) | collective-permute-done | bytes 1048608 | tf_op jit(solution)/shard_map/ppermute | solution.py:21
  470.0 2.1 collective-permute-start.56
  475.9 12.4 %convolution_add_fusion.1 = f32[2048,1376]{0,1:T(8,128)} fusion(f32[2048,1376]{0,1:T(8,128)} %fusion.44, bf16[1024,1376]{0,1:T(8,128)(2,1)} %get-tuple-element.345, bf16[1024,2048]{1,0:T(8,128)(2,1)S(1)} %copy-done.24), kind=kOutput, calls=%fused_computation.1 | convolution fusion | flops 5774180352 | bytes 29556736 | tf_op jit(solution)/shard_map/ca,cb->ab/dot_general | solution.py:378
  488.3 9.1 %convolution_add_fusion = f32[2048,1376]{0,1:T(8,128)} fusion(f32[2048,1376]{0,1:T(8,128)S(1)} %bitcast.92, bf16[1024,1376]{0,1:T(8,128)(2,1)S(1)} %copy-done.70, bf16[1024,2048]{1,0:T(8,128)(2,1)S(1)} %copy-done.24), kind=kOutput, calls=%fused_computation | convolution fusion | flops 5774180352 | bytes 29556736 | tf_op jit(solution)/shard_map/ca,cb->ab/dot_general | solution.py:378
  499.9 2.1 multiply_reduce_fusion
  502.3 4.4 multiply_add_fusion.2
  508.4 2.1 copy.45
  512.1 2.1 copy.46
  (339 shorter events, 84.3 us)
Async XLA Ops:
  7.2 57.3 %copy-start = (bf16[512,2048]{1,0:T(8,128)(2,1)S(1)}, bf16[512,2048]{1,0:T(8,128)(2,1)}, u32[]{:S(2)}) copy-start(bf16[512,2048]{1,0:T(8,128)(2,1)} %param.17) | copy-start | bytes 6291460
  7.2 147.9 %all-reduce.6.cloned.1.call-start = ((), (), s32[]{:S(2)}) async-start(), calls=%async_computation | async-start | bytes 4194304 | tf_op jit(solution)/shard_map/psum | solution.py:179
  15.3 10.7 %collective-permute-start = (f32[128,640]{1,0:T(8,128)S(1)}, f32[128,640]{1,0:T(8,128)S(1)}, u32[]{:S(2)}, u32[]{:S(2)}) collective-permute-start(f32[128,640]{1,0:T(8,128)S(1)} %get-tuple-element.376), channel_id=1, source_target_pairs={{0,8},{4,12},{8,0},{12,4},{16,24},{20,28},{24,16},{28,20},{1,9},{5... | collective-permute-start | bytes 983048 | tf_op jit(solution)/shard_map/ppermute | solution.py:21
  18.3 9.5 %collective-permute-start.2 = (f32[128,640]{1,0:T(8,128)S(1)}, f32[128,640]{1,0:T(8,128)S(1)}, u32[]{:S(2)}, u32[]{:S(2)}) collective-permute-start(f32[128,640]{1,0:T(8,128)S(1)} %get-tuple-element.375), channel_id=1, source_target_pairs={{0,16},{4,20},{8,24},{12,28},{16,0},{20,4},{24,8},{28,12},{1,17},{... | collective-permute-start | bytes 983048 | tf_op jit(solution)/shard_map/ppermute | solution.py:21
  26.0 10.6 %collective-permute-start.1 = (f32[128,640]{1,0:T(8,128)S(1)}, f32[128,640]{1,0:T(8,128)S(1)}, u32[]{:S(2)}, u32[]{:S(2)}) collective-permute-start(f32[128,640]{1,0:T(8,128)S(1)} %collective-permute-done.refs_2_), channel_id=1, source_target_pairs={{0,16},{4,20},{8,24},{12,28},{16,0},{20,4},{24,8},{28,12},{1,17},{... | collective-permute-start | bytes 983048 | tf_op jit(solution)/shard_map/ppermute | solution.py:21
  27.8 11.2 %collective-permute-start.3 = (f32[128,640]{1,0:T(8,128)S(1)}, f32[128,640]{1,0:T(8,128)S(1)}, u32[]{:S(2)}, u32[]{:S(2)}) collective-permute-start(f32[128,640]{1,0:T(8,128)S(1)} %collective-permute-done.2.refs_7_), channel_id=1, source_target_pairs={{0,8},{4,12},{8,0},{12,4},{16,24},{20,28},{24,16},{28,20},{1,9},{5... | collective-permute-start | bytes 983048 | tf_op jit(solution)/shard_map/ppermute | solution.py:21
  29.3 14.6 %collective-permute-start.8 = (f32[128,640]{1,0:T(8,128)S(1)}, f32[128,640]{1,0:T(8,128)}, u32[]{:S(2)}, u32[]{:S(2)}) collective-permute-start(f32[128,640]{1,0:T(8,128)S(1)} %get-tuple-element.375), channel_id=1, source_target_pairs={{0,8},{4,12},{8,0},{12,4},{16,24},{20,28},{24,16},{28,20},{1,9},{5... | collective-permute-start | bytes 983048 | tf_op jit(solution)/shard_map/ppermute | solution.py:21
  29.8 14.6 %collective-permute-start.11 = (f32[128,640]{1,0:T(8,128)S(1)}, f32[128,640]{1,0:T(8,128)S(1)}, u32[]{:S(2)}, u32[]{:S(2)}) collective-permute-start(f32[128,640]{1,0:T(8,128)S(1)} %get-tuple-element.376), channel_id=1, source_target_pairs={{0,16},{4,20},{8,24},{12,28},{16,0},{20,4},{24,8},{28,12},{1,17},{... | collective-permute-start | bytes 983048 | tf_op jit(solution)/shard_map/ppermute | solution.py:21
  31.0 13.5 %collective-permute-start.13 = (f32[128,640]{1,0:T(8,128)S(1)}, f32[128,640]{1,0:T(8,128)S(1)}, u32[]{:S(2)}, u32[]{:S(2)}) collective-permute-start(f32[128,640]{1,0:T(8,128)S(1)} %collective-permute-done.2.refs_7_), channel_id=1, source_target_pairs={{0,4},{4,0},{8,12},{12,8},{16,20},{20,16},{24,28},{28,24},{1,5},{5... | collective-permute-start | bytes 983048 | tf_op jit(solution)/shard_map/ppermute | solution.py:21
  37.4 7.7 %collective-permute-start.9 = (f32[128,640]{1,0:T(8,128)S(1)}, f32[128,640]{1,0:T(8,128)S(1)}, u32[]{:S(2)}, u32[]{:S(2)}) collective-permute-start(f32[128,640]{1,0:T(8,128)S(1)} %collective-permute-done.refs_2_), channel_id=1, source_target_pairs={{0,4},{4,0},{8,12},{12,8},{16,20},{20,16},{24,28},{28,24},{1,5},{5... | collective-permute-start | bytes 983048 | tf_op jit(solution)/shard_map/ppermute | solution.py:21
  39.0 49.2 %collective-permute-start.4 = (f32[256,2048]{1,0:T(8,128)}, f32[256,2048]{1,0:T(8,128)}, u32[]{:S(2)}, u32[]{:S(2)}) collective-permute-start(f32[256,2048]{1,0:T(8,128)} %convert_element_type.115.refs_0_), channel_id=1, source_target_pairs={{0,8},{4,12},{8,0},{12,4},{16,24},{20,28},{24,16},{28,20},{1,9},{5... | collective-permute-start | bytes 6291464 | tf_op jit(solution)/shard_map/ppermute | solution.py:21
  43.9 44.9 %collective-permute-start.5 = (f32[256,2048]{1,0:T(8,128)}, f32[256,2048]{1,0:T(8,128)}, u32[]{:S(2)}, u32[]{:S(2)}) collective-permute-start(f32[256,2048]{1,0:T(8,128)} %convert_element_type.115.refs_0_), channel_id=1, source_target_pairs={{0,16},{4,20},{8,24},{12,28},{16,0},{20,4},{24,8},{28,12},{1,17},{... | collective-permute-start | bytes 6291464 | tf_op jit(solution)/shard_map/ppermute | solution.py:21
  44.5 44.4 %collective-permute-start.6 = (f32[256,2048]{1,0:T(8,128)}, f32[256,2048]{1,0:T(8,128)}, u32[]{:S(2)}, u32[]{:S(2)}) collective-permute-start(f32[256,2048]{1,0:T(8,128)} %convert_element_type.115.refs_0_), channel_id=1, source_target_pairs={{0,4},{4,0},{8,12},{12,8},{16,20},{20,16},{24,28},{28,24},{1,5},{5... | collective-permute-start | bytes 6291464 | tf_op jit(solution)/shard_map/ppermute | solution.py:21
  44.6 6.7 %collective-permute-start.10 = (f32[128,640]{1,0:T(8,128)}, f32[128,640]{1,0:T(8,128)}, u32[]{:S(2)}, u32[]{:S(2)}) collective-permute-start(f32[128,640]{1,0:T(8,128)} %collective-permute-done.8.refs_3_), channel_id=1, source_target_pairs={{0,4},{4,0},{8,12},{12,8},{16,20},{20,16},{24,28},{28,24},{1,5},{5... | collective-permute-start | bytes 983048 | tf_op jit(solution)/shard_map/ppermute | solution.py:21
  45.1 8.4 %collective-permute-start.7 = (f32[256,640]{1,0:T(8,128)}, f32[256,640]{1,0:T(8,128)}, u32[]{:S(2)}, u32[]{:S(2)}) collective-permute-start(f32[256,640]{1,0:T(8,128)} %pad_maximum_fusion.2.refs_0_), channel_id=1, source_target_pairs={{0,4},{4,0},{8,12},{12,8},{16,20},{20,16},{24,28},{28,24},{1,5},{5... | collective-permute-start | bytes 1966088 | tf_op jit(solution)/shard_map/ppermute | solution.py:21
  51.2 2.0 collective-permute-start.12
  52.3 116.2 %copy-start.46 = (f32[2048]{0:T(1024)}, f32[2048]{0:T(1024)S(1)}, u32[]{:S(2)}) copy-start(f32[2048]{0:T(1024)S(1)} %convert_element_type.125) | copy-start | bytes 24580
  53.3 1.8 collective-permute-start.14
  53.4 2.2 collective-permute-start.15
  67.5 194.9 %all-reduce.8.cloned.1.call-start = ((), (), s32[]{:S(2)}) async-start(), calls=%async_computation.1 | async-start | bytes 4194304 | tf_op jit(solution)/shard_map/psum | solution.py:179
  93.5 66.3 %collective-permute-start.18 = (f32[256,2048]{1,0:T(8,128)}, f32[256,2048]{1,0:T(8,128)}, u32[]{:S(2)}, u32[]{:S(2)}) collective-permute-start(f32[256,2048]{1,0:T(8,128)} %collective-permute-done.4.refs_2_), channel_id=1, source_target_pairs={{0,4},{4,0},{8,12},{12,8},{16,20},{20,16},{24,28},{28,24},{1,5},{5... | collective-permute-start | bytes 6291464 | tf_op jit(solution)/shard_map/ppermute | solution.py:21
  93.5 66.3 %collective-permute-start.19 = (f32[256,2048]{1,0:T(8,128)}, f32[256,2048]{1,0:T(8,128)}, u32[]{:S(2)}, u32[]{:S(2)}) collective-permute-start(f32[256,2048]{1,0:T(8,128)} %collective-permute-done.5.refs_3_), channel_id=1, source_target_pairs={{0,4},{4,0},{8,12},{12,8},{16,20},{20,16},{24,28},{28,24},{1,5},{5... | collective-permute-start | bytes 6291464 | tf_op jit(solution)/shard_map/ppermute | solution.py:21
  94.0 65.8 %collective-permute-start.16 = (f32[128,2048]{1,0:T(8,128)}, f32[128,2048]{1,0:T(8,128)}, u32[]{:S(2)}, u32[]{:S(2)}) collective-permute-start(f32[128,2048]{1,0:T(8,128)} %slice.48), channel_id=1, source_target_pairs={{0,16},{4,20},{8,24},{12,28},{16,0},{20,4},{24,8},{28,12},{1,17},{... | collective-permute-start | bytes 3145736 | tf_op jit(solution)/shard_map/ppermute | solution.py:21
  95.5 64.3 %collective-permute-start.17 = (f32[128,2048]{1,0:T(8,128)}, f32[128,2048]{1,0:T(8,128)}, u32[]{:S(2)}, u32[]{:S(2)}) collective-permute-start(f32[128,2048]{1,0:T(8,128)} %slice.49), channel_id=1, source_target_pairs={{0,8},{4,12},{8,0},{12,4},{16,24},{20,28},{24,16},{28,20},{1,9},{5... | collective-permute-start | bytes 3145736 | tf_op jit(solution)/shard_map/ppermute | solution.py:21
  159.8 18.7 %collective-permute-start.23 = (f32[128,2048]{1,0:T(8,128)}, f32[128,2048]{1,0:T(8,128)}, u32[]{:S(2)}, u32[]{:S(2)}) collective-permute-start(f32[128,2048]{1,0:T(8,128)} %collective-permute-done.16.refs_2_), channel_id=1, source_target_pairs={{0,4},{4,0},{8,12},{12,8},{16,20},{20,16},{24,28},{28,24},{1,5},{5... | collective-permute-start | bytes 3145736 | tf_op jit(solution)/shard_map/ppermute | solution.py:21
  159.9 18.6 %collective-permute-start.24 = (f32[128,2048]{1,0:T(8,128)}, f32[128,2048]{1,0:T(8,128)}, u32[]{:S(2)}, u32[]{:S(2)}) collective-permute-start(f32[128,2048]{1,0:T(8,128)} %collective-permute-done.17.refs_3_), channel_id=1, source_target_pairs={{0,4},{4,0},{8,12},{12,8},{16,20},{20,16},{24,28},{28,24},{1,5},{5... | collective-permute-start | bytes 3145736 | tf_op jit(solution)/shard_map/ppermute | solution.py:21
  160.4 47.9 %collective-permute-start.20 = (f32[256,2048]{1,0:T(8,128)}, f32[256,2048]{1,0:T(8,128)}, u32[]{:S(2)}, u32[]{:S(2)}) collective-permute-start(f32[256,2048]{1,0:T(8,128)} %broadcast_multiply_fusion.refs_0_), channel_id=1, source_target_pairs={{0,8},{4,12},{8,0},{12,4},{16,24},{20,28},{24,16},{28,20},{1,9},{5... | collective-permute-start | bytes 6291464 | tf_op jit(solution)/shard_map/ppermute | solution.py:21
  161.9 47.6 %collective-permute-start.21 = (f32[256,2048]{1,0:T(8,128)}, f32[256,2048]{1,0:T(8,128)}, u32[]{:S(2)}, u32[]{:S(2)}) collective-permute-start(f32[256,2048]{1,0:T(8,128)} %broadcast_multiply_fusion.refs_0_), channel_id=1, source_target_pairs={{0,16},{4,20},{8,24},{12,28},{16,0},{20,4},{24,8},{28,12},{1,17},{... | collective-permute-start | bytes 6291464 | tf_op jit(solution)/shard_map/ppermute | solution.py:21
  163.4 46.2 %collective-permute-start.22 = (f32[256,2048]{1,0:T(8,128)}, f32[256,2048]{1,0:T(8,128)}, u32[]{:S(2)}, u32[]{:S(2)}) collective-permute-start(f32[256,2048]{1,0:T(8,128)} %broadcast_multiply_fusion.refs_0_), channel_id=1, source_target_pairs={{0,4},{4,0},{8,12},{12,8},{16,20},{20,16},{24,28},{28,24},{1,5},{5... | collective-permute-start | bytes 6291464 | tf_op jit(solution)/shard_map/ppermute | solution.py:21
  178.4 321.4 %all-reduce.10.cloned.1.call-start = ((), (), s32[]{:S(2)}) async-start(), calls=%async_computation.2 | async-start | bytes 18874368 | tf_op jit(solution)/shard_map/psum | solution.py:586
  214.1 57.1 %collective-permute-start.27 = (f32[256,2048]{1,0:T(8,128)}, f32[256,2048]{1,0:T(8,128)}, u32[]{:S(2)}, u32[]{:S(2)}) collective-permute-start(f32[256,2048]{1,0:T(8,128)} %collective-permute-done.20.refs_2_), channel_id=1, source_target_pairs={{0,4},{4,0},{8,12},{12,8},{16,20},{20,16},{24,28},{28,24},{1,5},{5... | collective-permute-start | bytes 6291464 | tf_op jit(solution)/shard_map/ppermute | solution.py:21
  214.2 57.1 %collective-permute-start.28 = (f32[256,2048]{1,0:T(8,128)}, f32[256,2048]{1,0:T(8,128)}, u32[]{:S(2)}, u32[]{:S(2)}) collective-permute-start(f32[256,2048]{1,0:T(8,128)} %collective-permute-done.21.refs_3_), channel_id=1, source_target_pairs={{0,4},{4,0},{8,12},{12,8},{16,20},{20,16},{24,28},{28,24},{1,5},{5... | collective-permute-start | bytes 6291464 | tf_op jit(solution)/shard_map/ppermute | solution.py:21
  214.7 56.6 %collective-permute-start.25 = (f32[128,2048]{1,0:T(8,128)}, f32[128,2048]{1,0:T(8,128)}, u32[]{:S(2)}, u32[]{:S(2)}) collective-permute-start(f32[128,2048]{1,0:T(8,128)} %slice.50), channel_id=1, source_target_pairs={{0,16},{4,20},{8,24},{12,28},{16,0},{20,4},{24,8},{28,12},{1,17},{... | collective-permute-start | bytes 3145736 | tf_op jit(solution)/shard_map/ppermute | solution.py:21
  216.1 55.1 %collective-permute-start.26 = (f32[128,2048]{1,0:T(8,128)}, f32[128,2048]{1,0:T(8,128)}, u32[]{:S(2)}, u32[]{:S(2)}) collective-permute-start(f32[128,2048]{1,0:T(8,128)} %slice.51), channel_id=1, source_target_pairs={{0,8},{4,12},{8,0},{12,4},{16,24},{20,28},{24,16},{28,20},{1,9},{5... | collective-permute-start | bytes 3145736 | tf_op jit(solution)/shard_map/ppermute | solution.py:21
  271.3 19.4 %collective-permute-start.29 = (f32[264,512]{1,0:T(8,128)S(1)}, f32[264,512]{1,0:T(8,128)S(1)}, u32[]{:S(2)}, u32[]{:S(2)}) collective-permute-start(f32[264,512]{1,0:T(8,128)S(1)} %select_maximum_fusion.refs_14_), channel_id=1, source_target_pairs={{0,8},{4,12},{8,0},{12,4},{16,24},{20,28},{24,16},{28,20},{1,9},{5... | collective-permute-start | bytes 1622024 | tf_op jit(solution)/shard_map/ppermute | solution.py:21
  272.9 17.9 %collective-permute-start.30 = (f32[264,512]{1,0:T(8,128)S(1)}, f32[264,512]{1,0:T(8,128)S(1)}, u32[]{:S(2)}, u32[]{:S(2)}) collective-permute-start(f32[264,512]{1,0:T(8,128)S(1)} %select_maximum_fusion.refs_14_), channel_id=1, source_target_pairs={{0,16},{4,20},{8,24},{12,28},{16,0},{20,4},{24,8},{28,12},{1,17},{... | collective-permute-start | bytes 1622024 | tf_op jit(solution)/shard_map/ppermute | solution.py:21
  274.3 16.5 %collective-permute-start.31 = (f32[264,512]{1,0:T(8,128)S(1)}, f32[264,512]{1,0:T(8,128)S(1)}, u32[]{:S(2)}, u32[]{:S(2)}) collective-permute-start(f32[264,512]{1,0:T(8,128)S(1)} %select_maximum_fusion.refs_14_), channel_id=1, source_target_pairs={{0,4},{4,0},{8,12},{12,8},{16,20},{20,16},{24,28},{28,24},{1,5},{5... | collective-permute-start | bytes 1622024 | tf_op jit(solution)/shard_map/ppermute | solution.py:21
  274.3 29.4 %collective-permute-start.38 = (f32[128,2048]{1,0:T(8,128)}, f32[128,2048]{1,0:T(8,128)}, u32[]{:S(2)}, u32[]{:S(2)}) collective-permute-start(f32[128,2048]{1,0:T(8,128)} %split.16), channel_id=1, source_target_pairs={{0,1},{3,2},{4,5},{7,6},{8,9},{11,10},{12,13},{15,14},{16,17},{19,... | collective-permute-start | bytes 3145736 | tf_op jit(solution)/shard_map/ppermute | solution.py:21
  290.9 11.0 %collective-permute-start.34 = (f32[264,512]{1,0:T(8,128)S(1)}, f32[264,512]{1,0:T(8,128)S(1)}, u32[]{:S(2)}, u32[]{:S(2)}) collective-permute-start(f32[264,512]{1,0:T(8,128)S(1)} %collective-permute-done.29.refs_16_), channel_id=1, source_target_pairs={{0,4},{4,0},{8,12},{12,8},{16,20},{20,16},{24,28},{28,24},{1,5},{5... | collective-permute-start | bytes 1622024 | tf_op jit(solution)/shard_map/ppermute | solution.py:21
  291.1 10.7 %collective-permute-start.35 = (f32[264,512]{1,0:T(8,128)S(1)}, f32[264,512]{1,0:T(8,128)S(1)}, u32[]{:S(2)}, u32[]{:S(2)}) collective-permute-start(f32[264,512]{1,0:T(8,128)S(1)} %collective-permute-done.30.refs_18_), channel_id=1, source_target_pairs={{0,4},{4,0},{8,12},{12,8},{16,20},{20,16},{24,28},{28,24},{1,5},{5... | collective-permute-start | bytes 1622024 | tf_op jit(solution)/shard_map/ppermute | solution.py:21
  291.4 10.4 %collective-permute-start.33 = (f32[136,512]{1,0:T(8,128)S(1)}, f32[136,512]{1,0:T(8,128)}, u32[]{:S(2)}, u32[]{:S(2)}) collective-permute-start(f32[136,512]{1,0:T(8,128)S(1)} %slice.53), channel_id=1, source_target_pairs={{0,8},{4,12},{8,0},{12,4},{16,24},{20,28},{24,16},{28,20},{1,9},{5... | collective-permute-start | bytes 835592 | tf_op jit(solution)/shard_map/ppermute | solution.py:21
  292.0 9.8 %collective-permute-start.32 = (f32[128,512]{1,0:T(8,128)S(1)}, f32[128,512]{1,0:T(8,128)}, u32[]{:S(2)}, u32[]{:S(2)}) collective-permute-start(f32[128,512]{1,0:T(8,128)S(1)} %slice.52), channel_id=1, source_target_pairs={{0,16},{4,20},{8,24},{12,28},{16,0},{20,4},{24,8},{28,12},{1,17},{... | collective-permute-start | bytes 786440 | tf_op jit(solution)/shard_map/ppermute | solution.py:21
  302.7 2.7 collective-permute-start.37
  303.5 1.9 collective-permute-start.36
  308.1 20.9 %collective-permute-start.39 = (f32[128,2048]{1,0:T(8,128)}, f32[128,2048]{1,0:T(8,128)S(1)}, u32[]{:S(2)}, u32[]{:S(2)}) collective-permute-start(f32[128,2048]{1,0:T(8,128)} %collective-permute-done.25.refs_2_), channel_id=1, source_target_pairs={{0,4},{4,0},{8,12},{12,8},{16,20},{20,16},{24,28},{28,24},{1,5},{5... | collective-permute-start | bytes 3145736 | tf_op jit(solution)/shard_map/ppermute | solution.py:21
  308.4 20.7 %collective-permute-start.40 = (f32[128,2048]{1,0:T(8,128)}, f32[128,2048]{1,0:T(8,128)S(1)}, u32[]{:S(2)}, u32[]{:S(2)}) collective-permute-start(f32[128,2048]{1,0:T(8,128)} %collective-permute-done.26.refs_3_), channel_id=1, source_target_pairs={{0,4},{4,0},{8,12},{12,8},{16,20},{20,16},{24,28},{28,24},{1,5},{5... | collective-permute-start | bytes 3145736 | tf_op jit(solution)/shard_map/ppermute | solution.py:21
  308.7 47.0 %collective-permute-start.43 = (f32[128,2048]{1,0:T(8,128)}, f32[128,2048]{1,0:T(8,128)}, u32[]{:S(2)}, u32[]{:S(2)}) collective-permute-start(f32[128,2048]{1,0:T(8,128)} %get-tuple-element.278), channel_id=1, source_target_pairs={{0,1},{3,2},{4,5},{7,6},{8,9},{11,10},{12,13},{15,14},{16,17},{19,... | collective-permute-start | bytes 3145736 | tf_op jit(solution)/shard_map/ppermute | solution.py:21
  311.0 44.7 %collective-permute-start.44 = (f32[128,2048]{1,0:T(8,128)}, f32[128,2048]{1,0:T(8,128)}, u32[]{:S(2)}, u32[]{:S(2)}) collective-permute-start(f32[128,2048]{1,0:T(8,128)} %get-tuple-element.279), channel_id=1, source_target_pairs={{1,2},{2,1},{5,6},{6,5},{9,10},{10,9},{13,14},{14,13},{17,18},{18,... | collective-permute-start | bytes 3145736 | tf_op jit(solution)/shard_map/ppermute | solution.py:21
  336.5 24.7 %collective-permute-start.41 = (f32[128,2048]{1,0:T(8,128)S(1)}, f32[128,2048]{1,0:T(8,128)S(1)}, u32[]{:S(2)}, u32[]{:S(2)}) collective-permute-start(f32[128,2048]{1,0:T(8,128)S(1)} %copy-done.35), channel_id=1, source_target_pairs={{0,1},{3,2},{4,5},{7,6},{8,9},{11,10},{12,13},{15,14},{16,17},{19,... | collective-permute-start | bytes 3145736 | tf_op jit(solution)/shard_map/ppermute | solution.py:21
  338.4 22.7 %collective-permute-start.42 = (f32[2,2048]{1,0:T(2,128)S(1)}, f32[2,2048]{1,0:T(2,128)S(1)}, u32[]{:S(2)}, u32[]{:S(2)}) collective-permute-start(f32[2,2048]{1,0:T(2,128)S(1)} %pad_maximum_fusion.3), channel_id=1, source_target_pairs={{0,1},{1,0},{2,3},{3,2},{4,5},{5,4},{6,7},{7,6},{8,9},{9,8},{10,11... | collective-permute-start | bytes 49160 | tf_op jit(solution)/shard_map/ppermute | solution.py:21
  338.5 40.7 %slice-start.4 = ((s8[5636096]{0:T(1024)(128)(4,1)}), s8[1441792]{0:T(1024)(128)(4,1)S(1)}, s32[]{:S(2)}) async-start(s8[5636096]{0:T(1024)(128)(4,1)} %bitcast.75), calls=%async_computation.7 | async-start | bytes 2883584
  366.6 52.3 %collective-permute-start.48 = (f32[128,2048]{1,0:T(8,128)S(1)}, f32[128,2048]{1,0:T(8,128)S(1)}, u32[]{:S(2)}, u32[]{:S(2)}) collective-permute-start(f32[128,2048]{1,0:T(8,128)S(1)} %slice_add_fusion.2), channel_id=1, source_target_pairs={{1,2},{2,1},{5,6},{6,5},{9,10},{10,9},{13,14},{14,13},{17,18},{18,... | collective-permute-start | bytes 3145736 | tf_op jit(solution)/shard_map/ppermute | solution.py:21
  367.5 51.5 %collective-permute-start.49 = (f32[128,2048]{1,0:T(8,128)S(1)}, f32[128,2048]{1,0:T(8,128)S(1)}, u32[]{:S(2)}, u32[]{:S(2)}) collective-permute-start(f32[128,2048]{1,0:T(8,128)S(1)} %add.228), channel_id=1, source_target_pairs={{1,0},{2,3},{5,4},{6,7},{9,8},{10,11},{13,12},{14,15},{17,16},{18,... | collective-permute-start | bytes 3145736 | tf_op jit(solution)/shard_map/ppermute | solution.py:21
  368.9 50.0 %collective-permute-start.45 = (f32[128,2048]{1,0:T(8,128)S(1)}, f32[128,2048]{1,0:T(8,128)S(1)}, u32[]{:S(2)}, u32[]{:S(2)}) collective-permute-start(f32[128,2048]{1,0:T(8,128)S(1)} %get-tuple-element.315), channel_id=1, source_target_pairs={{0,1},{3,2},{4,5},{7,6},{8,9},{11,10},{12,13},{15,14},{16,17},{19,... | collective-permute-start | bytes 3145736 | tf_op jit(solution)/shard_map/ppermute | solution.py:21
  376.4 42.5 %collective-permute-start.46 = (f32[128,2048]{1,0:T(8,128)S(1)}, f32[128,2048]{1,0:T(8,128)S(1)}, u32[]{:S(2)}, u32[]{:S(2)}) collective-permute-start(f32[128,2048]{1,0:T(8,128)S(1)} %get-tuple-element.316), channel_id=1, source_target_pairs={{1,2},{2,1},{5,6},{6,5},{9,10},{10,9},{13,14},{14,13},{17,18},{18,... | collective-permute-start | bytes 3145736 | tf_op jit(solution)/shard_map/ppermute | solution.py:21
  377.1 41.8 %collective-permute-start.47 = (f32[2,2048]{1,0:T(2,128)S(1)}, f32[2,2048]{1,0:T(2,128)S(1)}, u32[]{:S(2)}, u32[]{:S(2)}) collective-permute-start(f32[2,2048]{1,0:T(2,128)S(1)} %fusion.19), channel_id=1, source_target_pairs={{0,2},{1,3},{2,0},{3,1},{4,6},{5,7},{6,4},{7,5},{8,10},{9,11},{10,... | collective-permute-start | bytes 49160 | tf_op jit(solution)/shard_map/ppermute | solution.py:21
  419.4 28.3 %collective-permute-start.53 = (f32[128,2048]{1,0:T(8,128)S(1)}, f32[128,2048]{1,0:T(8,128)S(1)}, u32[]{:S(2)}, u32[]{:S(2)}) collective-permute-start(f32[128,2048]{1,0:T(8,128)S(1)} %add.231), channel_id=1, source_target_pairs={{1,0},{2,3},{5,4},{6,7},{9,8},{10,11},{13,12},{14,15},{17,16},{18,... | collective-permute-start | bytes 3145736 | tf_op jit(solution)/shard_map/ppermute | solution.py:21
  421.0 13.9 %collective-permute-start.52 = (f32[2,2048]{1,0:T(2,128)S(1)}, f32[2,2048]{1,0:T(2,128)S(1)}, u32[]{:S(2)}, u32[]{:S(2)}) collective-permute-start(f32[2,2048]{1,0:T(2,128)S(1)} %fusion.102), channel_id=1, source_target_pairs={{0,4},{4,0},{8,12},{12,8},{16,20},{20,16},{24,28},{28,24},{1,5},{5... | collective-permute-start | bytes 49160 | tf_op jit(solution)/shard_map/ppermute | solution.py:21
  421.1 26.6 %collective-permute-start.50 = (f32[128,2048]{1,0:T(8,128)S(1)}, f32[128,2048]{1,0:T(8,128)S(1)}, u32[]{:S(2)}, u32[]{:S(2)}) collective-permute-start(f32[128,2048]{1,0:T(8,128)S(1)} %slice_add_fusion), channel_id=1, source_target_pairs={{1,2},{2,1},{5,6},{6,5},{9,10},{10,9},{13,14},{14,13},{17,18},{18,... | collective-permute-start | bytes 3145736 | tf_op jit(solution)/shard_map/ppermute | solution.py:21
  421.8 46.0 %collective-permute-start.51 = (f32[128,2048]{1,0:T(8,128)S(1)}, f32[128,2048]{1,0:T(8,128)S(1)}, u32[]{:S(2)}, u32[]{:S(2)}) collective-permute-start(f32[128,2048]{1,0:T(8,128)S(1)} %add.233), channel_id=1, source_target_pairs={{1,0},{2,3},{5,4},{6,7},{9,8},{10,11},{13,12},{14,15},{17,16},{18,... | collective-permute-start | bytes 3145736 | tf_op jit(solution)/shard_map/ppermute | solution.py:21
  468.1 29.4 %collective-permute-start.54 = (f32[128,2048]{1,0:T(8,128)S(1)}, f32[128,2048]{1,0:T(8,128)S(1)}, u32[]{:S(2)}, u32[]{:S(2)}) collective-permute-start(f32[128,2048]{1,0:T(8,128)S(1)} %add.236), channel_id=1, source_target_pairs={{1,0},{2,3},{5,4},{6,7},{9,8},{10,11},{13,12},{14,15},{17,16},{18,... | collective-permute-start | bytes 3145736 | tf_op jit(solution)/shard_map/ppermute | solution.py:21
  469.6 28.0 %collective-permute-start.55 = (f32[2,2048]{1,0:T(2,128)S(1)}, f32[2,2048]{1,0:T(2,128)S(1)}, u32[]{:S(2)}, u32[]{:S(2)}) collective-permute-start(f32[2,2048]{1,0:T(2,128)S(1)} %add.237), channel_id=1, source_target_pairs={{0,8},{4,12},{8,0},{12,4},{16,24},{20,28},{24,16},{28,20},{1,9},{5... | collective-permute-start | bytes 49160 | tf_op jit(solution)/shard_map/ppermute | solution.py:21
  470.0 27.5 %collective-permute-start.56 = (f32[2,2048]{1,0:T(2,128)S(1)}, f32[2,2048]{1,0:T(2,128)S(1)}, u32[]{:S(2)}, u32[]{:S(2)}) collective-permute-start(f32[2,2048]{1,0:T(2,128)S(1)} %add.237), channel_id=1, source_target_pairs={{0,16},{4,20},{8,24},{12,28},{16,0},{20,4},{24,8},{28,12},{1,17},{... | collective-permute-start | bytes 49160 | tf_op jit(solution)/shard_map/ppermute | solution.py:21
  472.1 25.4 %collective-permute-start.57 = (f32[2,2048]{1,0:T(2,128)S(1)}, f32[2,2048]{1,0:T(2,128)S(1)}, u32[]{:S(2)}, u32[]{:S(2)}) collective-permute-start(f32[2,2048]{1,0:T(2,128)S(1)} %add.237), channel_id=1, source_target_pairs={{0,24},{4,28},{8,16},{12,20},{16,8},{20,12},{24,0},{28,4},{1,25},{... | collective-permute-start | bytes 49160 | tf_op jit(solution)/shard_map/ppermute | solution.py:21
  (80 other events, 558.1 us)
Sparse Core Ops, SparseCore 0:
  67.6 87.4 all-reduce.5
  178.6 83.8 all-reduce.7
  338.6 139.2 all-reduce.9

commit v4 on v3

--- a/solution.py
+++ b/solution.py
@@ -575,19 +575,24 @@
 
     in_sum = Chain(line_steps(in_part, 2))
     convoy.launch(in_sum)
-    late_in = after(normed_in, convoy.sent)
-    parts = [t_mm(late_in, grad) for grad in lin_grads]
+
+    def parts_work(normed_in, *lin_grads):
+        return [t_mm(normed_in, grad) for grad in lin_grads]
+
+    parts = convoy.work(parts_work, normed_in, *lin_grads)
+    *qkv_w_grads, out_w_grad = lax.psum((*parts, out_part), "blk")
     gain_parts = jnp.stack(
         [
             jnp.sum(after(in_part, parts) * token_wide * inv_in, axis=0),
             jnp.sum(mid_part * scaled_mid, axis=0),
         ]
     )
-    *qkv_w_grads, out_w_grad = lax.psum((*parts, out_part), "blk")
+    convoy.done = gain_parts
+    convoy.land(mlp)
     gains = Chain(small_steps(gain_parts))
-    convoy.launch(gains)
+    convoy.launch(mlp, gains)
     chains = [in_sum, gains, mlp]
-    mid_b, gate_b = convoy.work(gate_work, *after(mid_late, gain_parts))
+    mid_b, gate_b = convoy.work(gate_work, *mid_late)
     convoy.land(*chains)
 
     def second_work(mid_b, gate_b, hidden_grad_b):

time: 531 us -> 520 us (0.979)
  waiting for transfers between devices: 142 us -> 123 us
  other arithmetic: 39.1 us -> 45.4 us
    ppermute x58, waiting for transfers between devices: 94.2 us -> 57.5 us  [hop(): return lax.ppermute(value, axis, way)]
    psum x1, waiting for transfers between devices: 0.01 us -> 17.9 us  [per_device(): *qkv_w_grads, out_w_grad = lax.psum((*parts, out_part), 'blk')]
    unnamed x171 -> x161, local copies, waits for them, and re-layouts: 22.4 us -> 18.9 us
  transfers between devices with their start and end apart: 61 -> 61, of which waited for: 16 -> 16; matrix products, arithmetic and copies ran while one was open for 41% -> 42% of each run, Pallas kernels for 10% -> 11%
where the time goes in v4:
time: 520 us; the launch traced here: 512 us
  matrix products  174 us (33%)
  waiting for transfers between devices  123 us (24%)
  starting transfers between devices  62.2 us (12%)
  Pallas kernels  53.8 us (10%)
  other arithmetic  45.4 us (9%)
  local copies, waits for them, and re-layouts  34.9 us (7%)
  between operations  17.7 us (3%)
    dot_general x10, matrix products, t_mm(): return jnp.einsum('ca,cb->ab', left, right, preferred_element_type=f32)  71.4 us
    dot_general x11, matrix products, mm(): return jnp.dot(left, right, preferred_element_type=f32)  67 us
    ppermute x58, starting transfers between devices, hop(): return lax.ppermute(value, axis, way)  62.1 us
    ppermute x58, waiting for transfers between devices, hop(): return lax.ppermute(value, axis, way)  57.5 us
    psum x2, waiting for transfers between devices, sum_head(): return lax.psum(value, 'head')  47.7 us
    dot_general x9, matrix products, mm_t(): return jnp.einsum('ac,bc->ab', left, right, preferred_element_type=f32)  36.1 us
    pallas_call x3, Pallas kernels, whole_call(): pl.pallas_call(body, out_shape=outs, in_specs=[pl.BlockSpec(memory_space=...  28.7 us
    pallas_call x4, Pallas kernels, join_rounded(): pl.pallas_call(functools.partial(join_kernel, tuple((len(slot) for slot i...  25.1 us
  transfers between devices with their start and end apart: 61, of which 16 were waited for; matrix products, arithmetic and copies ran while one was open for 42% of the time, Pallas kernels for 11%

profile of v4, /device:TPU:0, one launch (start us, length us, event | category | flops | bytes accessed | tf_op | source)
XLA Modules:
  0.0 511.6 jit_solution(11900843053948231263)
XLA Ops:
  15.3 3.0 collective-permute-start
  19.8 6.2 %collective-permute-done.refs_2_ = f32[128,640]{1,0:T(8,128)S(1)} collective-permute-done((f32[128,640]{1,0:T(8,128)S(1)}, f32[128,640]{1,0:T(8,128)S(1)}, u32[]{:S(2)}, u32[]{:S(2)}) %collective-permute-start) | collective-permute-done | bytes 327712 | tf_op jit(solution)/shard_map/ppermute | solution.py:21
  26.0 1.8 collective-permute-start.1
  31.0 5.6 %collective-permute-done.1.refs_10_ = f32[128,640]{1,0:T(8,128)S(1)} collective-permute-done((f32[128,640]{1,0:T(8,128)S(1)}, f32[128,640]{1,0:T(8,128)S(1)}, u32[]{:S(2)}, u32[]{:S(2)}) %collective-permute-start.1) | collective-permute-done | bytes 327712 | tf_op jit(solution)/shard_map/ppermute | solution.py:21
  39.0 1.8 collective-permute-start.4
  40.8 3.2 collective-permute-done.8.refs_3_
  56.6 7.9 %shard_map.203 = (bf16[256,512]{1,0:T(8,128)(2,1)}, f32[256,512]{1,0:T(8,128)}, f32[256,512]{1,0:T(8,128)}) custom-call(s32[256,4]{1,0:T(8,128)} %copy.28.col_ref, s32[24,256]{1,0:T(8,128)} %pad_add_fusion.row_ref, f32[256,640]{1,0:T(8,128)} %pad_maximum_fusion.2.refs_0_, f32[256,640]{1,0:T(8,128)} %collective-permute-done.7.refs_1_, f32[128,640]{1,0:T(8,128)} %copy-done.57, ...), custom_call_target="tpu_custom_call" | custom-call | flops 2147483648 | bytes 6582272 | tf_op jit(solution)/shard_map/pallas_call | solution.py:318
  64.5 3.0 fusion.30
  67.5 5.7 %fusion.31 = f32[256,1376]{0,1:T(8,128)} fusion(bf16[256,2048]{1,0:T(8,128)(2,1)} %param.23, bf16[1376,2048]{1,0:T(8,128)(2,1)} %param.21), kind=kOutput, calls=%fused_computation.93 | convolution fusion | flops 1442840576 | bytes 8093696 | tf_op jit(solution)/shard_map/ac,bc->ab/dot_general | solution.py:374
  73.2 14.9 %collective-permute-done.4.refs_2_ = f32[256,2048]{1,0:T(8,128)} collective-permute-done((f32[256,2048]{1,0:T(8,128)}, f32[256,2048]{1,0:T(8,128)}, u32[]{:S(2)}, u32[]{:S(2)}) %collective-permute-start.4) | collective-permute-done | bytes 2097184 | tf_op jit(solution)/shard_map/ppermute | solution.py:21
  88.9 2.3 slice.48
  91.2 2.3 slice.49
  96.6 6.2 %shard_map.204 = bf16[1024,2048]{1,0:T(8,128)(2,1)} custom-call(f32[1,2048]{1,0:T(1,128)} %broadcast_12_scale_ref.2.scale_ref, f32[256,2048]{1,0:T(8,128)} %convert_element_type.115.refs_0_, f32[256,2048]{1,0:T(8,128)} %collective-permute-done.6.refs_1_, f32[256,2048]{1,0:T(8,128)} %collective-permute-done.4.refs_2_, f32[256,2048]{1,0:T(8,128)} %collective-permute-done.5.refs_3_), custom_call_target="tpu_custom_call" | custom-call | bytes 12582912 | tf_op jit(solution)/shard_map/pallas_call | solution.py:345
  102.9 10.9 %fusion.32 = f32[1024,1376]{0,1:T(8,128)} fusion(bf16[1024,2048]{1,0:T(8,128)(2,1)} %shard_map.204, bf16[1376,2048]{1,0:T(8,128)(2,1)} %param.21), kind=kOutput, calls=%fused_computation.94 | convolution fusion | flops 5771362304 | bytes 15466496 | tf_op jit(solution)/shard_map/ac,bc->ab/dot_general | solution.py:374
  113.7 41.4 %all-reduce.6.cloned.1.call-done = f32[256,2048]{1,0:T(8,128)} async-done(((f32[256,2048]{1,0:T(8,128)}), f32[256,2048]{1,0:T(8,128)}) %all-reduce.6.cloned.1.call-update) | async-done | bytes 2097168 | tf_op jit(solution)/shard_map/psum | solution.py:179
  155.1 2.5 multiply_reduce_fusion.4
  163.3 5.1 fusion.8
  168.5 4.5 multiply_convert_fusion.10
  173.0 2.2 fusion.3
  175.2 3.2 convolution_add_fusion.5
  178.5 4.7 fusion.33
  185.6 6.4 %shard_map.205 = bf16[1024,2048]{1,0:T(8,128)(2,1)} custom-call(f32[1,2048]{1,0:T(1,128)} %broadcast_12_scale_ref.2.scale_ref, f32[256,2048]{1,0:T(8,128)} %collective-permute-done.18.refs_0_, f32[256,2048]{1,0:T(8,128)} %collective-permute-done.19.refs_1_, f32[128,2048]{1,0:T(8,128)} %collective-permute-done.16.refs_2_, ...), custom_call_target="tpu_custom_call" | custom-call | bytes 12582912 | tf_op jit(solution)/shard_map/pallas_call | solution.py:345
  192.0 10.9 %fusion.34 = f32[1024,1376]{0,1:T(8,128)} fusion(bf16[1024,2048]{1,0:T(8,128)(2,1)} %shard_map.205, bf16[1376,2048]{1,0:T(8,128)(2,1)} %param.21), kind=kOutput, calls=%fused_computation.96 | convolution fusion | flops 5771362304 | bytes 15466496 | tf_op jit(solution)/shard_map/ac,bc->ab/dot_general | solution.py:374
  202.9 5.4 %collective-permute-done.20.refs_2_ = f32[256,2048]{1,0:T(8,128)} collective-permute-done((f32[256,2048]{1,0:T(8,128)}, f32[256,2048]{1,0:T(8,128)}, u32[]{:S(2)}, u32[]{:S(2)}) %collective-permute-start.20) | collective-permute-done | bytes 2097184 | tf_op jit(solution)/shard_map/ppermute | solution.py:21
  209.5 2.3 slice.50
  211.8 2.4 slice.51
  216.7 6.3 %shard_map.206 = bf16[1024,2048]{1,0:T(8,128)(2,1)} custom-call(f32[1,2048]{1,0:T(1,128)} %bitcast.81, f32[256,2048]{1,0:T(8,128)} %broadcast_multiply_fusion.refs_0_, f32[256,2048]{1,0:T(8,128)} %collective-permute-done.22.refs_1_, f32[256,2048]{1,0:T(8,128)} %collective-permute-done.20.refs_2_, f32[256,2048]{1,0:T(8,128)} %collective-permute-done.21.refs_3_), custom_call_target="tpu_custom_call" | custom-call | bytes 12582912 | tf_op jit(solution)/shard_map/pallas_call | solution.py:345
  223.0 11.3 %fusion.35 = f32[1024,1376]{0,1:T(8,128)} fusion(bf16[1024,2048]{1,0:T(8,128)(2,1)} %shard_map.206, bf16[2048,1376]{0,1:T(8,128)(2,1)} %param.19), kind=kOutput, calls=%fused_computation.97 | convolution fusion | flops 5771362304 | bytes 15466496 | tf_op jit(solution)/shard_map/dot_general | solution.py:370
  234.4 12.8 %multiply_convert_fusion.3 = (bf16[1024,1376]{0,1:T(8,128)(2,1)}, bf16[1024,1376]{0,1:T(8,128)(2,1)}, bf16[1024,1376]{0,1:T(8,128)(2,1)S(1)}) fusion(f32[1024,1376]{0,1:T(8,128)} %fusion.32, f32[1024,1376]{0,1:T(8,128)} %fusion.35, bf16[1024,2048]{1,0:T(8,128)(2,1)S(1)} %copy-done.21, bf16[2048,1376]{0,1:T(8,128)(2,1)S(1)} %bitcast.74), kind=kOutput, calls=%fused_computation.8 | convolution fusion | flops 5792497664 | bytes 29556736 | tf_op jit(solution)/shard_map/dot_general | solution.py:370
  247.1 8.9 %fusion.36 = f32[1376,2048]{1,0:T(8,128)} fusion(bf16[1024,1376]{0,1:T(8,128)(2,1)S(1)} %get-tuple-element.238, bf16[1024,2048]{1,0:T(8,128)(2,1)S(1)} %copy-done.25), kind=kOutput, calls=%fused_computation.98 | convolution fusion | flops 5771362304 | bytes 18284544 | tf_op jit(solution)/shard_map/ca,cb->ab/dot_general | solution.py:378
  256.1 6.4 %all-reduce.8.cloned.1.call-done = f32[256,2048]{1,0:T(8,128)} async-done(((f32[256,2048]{1,0:T(8,128)}), f32[256,2048]{1,0:T(8,128)}) %all-reduce.8.cloned.1.call-update) | async-done | bytes 2097168 | tf_op jit(solution)/shard_map/psum | solution.py:179
  262.4 2.7 multiply_reduce_fusion.3
  265.9 2.8 multiply_reduce_fusion.1
  274.3 3.0 collective-permute-start.38
  278.5 9.4 %shard_map.207 = bf16[256,64]{1,0:T(8,128)(2,1)} custom-call(s32[256,4]{1,0:T(8,128)} %copy.28.col_ref, s32[24,256]{1,0:T(8,128)} %pad_add_fusion.row_ref, f32[256,512]{1,0:T(8,128)} %copy-done.30, f32[256,512]{1,0:T(8,128)} %bitcast.80, f32[256,640]{1,0:T(8,128)} %pad_maximum_fusion.2.refs_0_, f32[256,640]{1,0:T(8,128)} %collective-permute-done.7.refs_1_, ...), custom_call_target="tpu_custom_call" | custom-call | flops 2147483648 | bytes 6352896 | tf_op jit(solution)/shard_map/pallas_call | solution.py:318
  287.9 2.9 fusion.38
  293.1 8.8 %fusion.44 = f32[2048,1376]{0,1:T(8,128)} fusion(bf16[1024,1376]{0,1:T(8,128)(2,1)S(1)} %copy-done.66, bf16[1024,2048]{1,0:T(8,128)(2,1)S(1)} %copy-done.22), kind=kOutput, calls=%fused_computation.106 | convolution fusion | flops 5771362304 | bytes 18284544 | tf_op jit(solution)/shard_map/ca,cb->ab/dot_general | solution.py:378
  305.4 2.8 slice_add_fusion.3
  308.8 2.3 collective-permute-start.41
  311.0 1.9 collective-permute-start.42
  312.9 11.4 %shard_map.208 = (bf16[256,64]{1,0:T(8,128)(2,1)}, bf16[256,512]{1,0:T(8,128)(2,1)}) custom-call(s32[256,4]{1,0:T(8,128)} %copy.28.col_ref, s32[24,256]{1,0:T(8,128)} %pad_add_fusion.row_ref, f32[256,640]{1,0:T(8,128)} %pad_maximum_fusion.2.refs_0_, f32[256,640]{1,0:T(8,128)} %collective-permute-done.7.refs_1_, f32[128,640]{1,0:T(8,128)} %copy-done.57, ...), custom_call_target="tpu_custom_call" | custom-call | flops 4294967296 | bytes 9891840 | tf_op jit(solution)/shard_map/pallas_call | solution.py:318
  331.8 2.8 fusion.42
  334.6 1.9 multiply_reduce_fusion.2
  336.5 2.8 add.226
  343.6 3.7 collective-permute-start.44
  347.3 3.3 collective-permute-start.43
  350.6 6.2 %shard_map.209 = bf16[1024,2048]{1,0:T(8,128)(2,1)} custom-call(f32[1,2048]{1,0:T(1,128)} %bitcast.82, f32[256,2048]{1,0:T(8,128)} %collective-permute-done.27.refs_0_, f32[256,2048]{1,0:T(8,128)} %collective-permute-done.28.refs_1_, f32[128,2048]{1,0:T(8,128)} %collective-permute-done.25.refs_2_, f32[128,2048]{1,0:T(8,128)} %collective-permute-done.26.refs_3_, ...), custom_call_target="tpu_custom_call" | custom-call | bytes 12582912 | tf_op jit(solution)/shard_map/pallas_call | solution.py:345
  356.8 11.0 %fusion.43 = f32[1024,1376]{0,1:T(8,128)} fusion(bf16[1024,2048]{1,0:T(8,128)(2,1)} %shard_map.209, bf16[2048,1376]{0,1:T(8,128)(2,1)} %param.19), kind=kOutput, calls=%fused_computation.105 | convolution fusion | flops 5771362304 | bytes 15466496 | tf_op jit(solution)/shard_map/dot_general | solution.py:370
  367.8 2.3 collective-permute-done.44
  370.1 1.9 collective-permute-done.43
  373.4 1.8 slice_add_fusion.1
  376.8 5.7 %collective-permute-start.47 = (f32[128,2048]{1,0:T(8,128)S(1)}, f32[128,2048]{1,0:T(8,128)S(1)}, u32[]{:S(2)}, u32[]{:S(2)}) collective-permute-start(f32[128,2048]{1,0:T(8,128)S(1)} %get-tuple-element.313), channel_id=1, source_target_pairs={{0,1},{3,2},{4,5},{7,6},{8,9},{11,10},{12,13},{15,14},{16,17},{19,... | collective-permute-start | bytes 3145736 | tf_op jit(solution)/shard_map/ppermute | solution.py:21
  383.3 2.0 collective-permute-start.49
  385.3 13.1 %multiply_convert_fusion = (bf16[1024,1376]{0,1:T(8,128)(2,1)}, bf16[1024,1376]{0,1:T(8,128)(2,1)}, bf16[1024,1376]{0,1:T(8,128)(2,1)}) fusion(f32[1024,1376]{0,1:T(8,128)} %fusion.34, f32[1024,1376]{0,1:T(8,128)} %fusion.43, bf16[1024,2048]{1,0:T(8,128)(2,1)S(1)} %copy-done.24, bf16[2048,1376]{0,1:T(8,128)(2,1)S(1)} %bitcast.76), kind=kOutput, calls=%fused_computation.3 | convolution fusion | flops 5792497664 | bytes 29556736 | tf_op jit(solution)/shard_map/dot_general | solution.py:370
  398.4 10.5 %fusion.45 = f32[2048,1376]{0,1:T(8,128)} fusion(bf16[1024,1376]{0,1:T(8,128)(2,1)} %get-tuple-element.320, bf16[1024,2048]{1,0:T(8,128)(2,1)S(1)} %copy-done.23), kind=kOutput, calls=%fused_computation.107 | convolution fusion | flops 5771362304 | bytes 18284544 | tf_op jit(solution)/shard_map/ca,cb->ab/dot_general | solution.py:378
  413.2 11.4 %convolution_add_fusion.2 = f32[1376,2048]{1,0:T(8,128)} fusion(f32[1376,2048]{1,0:T(8,128)} %fusion.36, bf16[1024,1376]{0,1:T(8,128)(2,1)S(1)} %copy-done.69, bf16[1024,2048]{1,0:T(8,128)(2,1)S(1)} %copy-done.20), kind=kOutput, calls=%fused_computation.2 | convolution fusion | flops 5774180352 | bytes 29556736 | tf_op jit(solution)/shard_map/ca,cb->ab/dot_general | solution.py:378
  426.3 12.8 %collective-permute-done.52 = f32[128,2048]{1,0:T(8,128)S(1)} collective-permute-done((f32[128,2048]{1,0:T(8,128)S(1)}, f32[128,2048]{1,0:T(8,128)S(1)}, u32[]{:S(2)}, u32[]{:S(2)}) %collective-permute-start.52) | collective-permute-done | bytes 1048608 | tf_op jit(solution)/shard_map/ppermute | solution.py:21
  445.7 12.0 %convolution_add_fusion.1 = f32[2048,1376]{0,1:T(8,128)} fusion(f32[2048,1376]{0,1:T(8,128)} %fusion.44, bf16[1024,1376]{0,1:T(8,128)(2,1)S(1)} %copy-done.68, bf16[1024,2048]{1,0:T(8,128)(2,1)S(1)} %copy-done.24), kind=kOutput, calls=%fused_computation.1 | convolution fusion | flops 5774180352 | bytes 29556736 | tf_op jit(solution)/shard_map/ca,cb->ab/dot_general | solution.py:378
  457.7 11.5 %convolution_add_fusion = f32[2048,1376]{0,1:T(8,128)} fusion(f32[2048,1376]{0,1:T(8,128)} %fusion.45, bf16[1024,1376]{0,1:T(8,128)(2,1)S(1)} %copy-done.67, bf16[1024,2048]{1,0:T(8,128)(2,1)S(1)} %copy-done.24), kind=kOutput, calls=%fused_computation | convolution fusion | flops 5774180352 | bytes 29556736 | tf_op jit(solution)/shard_map/ca,cb->ab/dot_general | solution.py:378
  471.7 17.9 %all-reduce.10.cloned.1.call-done = (f32[2048,64]{0,1:T(8,128)}, f32[2048,64]{0,1:T(8,128)}, f32[2048,512]{1,0:T(8,128)}, f32[512,2048]{1,0:T(8,128)}) async-done(((f32[2048,64]{0,1:T(8,128)}, f32[2048,64]{0,1:T(8,128)}, f32[2048,512]{1,0:T(8,128)}, f32[512,2048]{1,0:T(8,128)}), (f32[2048,64]{0,1:T(8,128)}, f32[2048,64]{0,1:T(8,128)}, f32[2048,512]{1,0:T(8,128)}, ...) | async-done | bytes 9437200 | tf_op jit(solution)/shard_map/psum | solution.py:583
  489.6 2.1 multiply_reduce_fusion
  492.0 4.4 multiply_add_fusion.2
  498.1 2.1 copy.45
  501.8 2.1 copy.46
  (328 shorter events, 89.2 us)
Async XLA Ops:
  7.2 57.3 %copy-start = (bf16[512,2048]{1,0:T(8,128)(2,1)S(1)}, bf16[512,2048]{1,0:T(8,128)(2,1)}, u32[]{:S(2)}) copy-start(bf16[512,2048]{1,0:T(8,128)(2,1)} %param.17) | copy-start | bytes 6291460
  7.2 147.9 %all-reduce.6.cloned.1.call-start = ((), (), s32[]{:S(2)}) async-start(), calls=%async_computation | async-start | bytes 4194304 | tf_op jit(solution)/shard_map/psum | solution.py:179
  15.3 10.7 %collective-permute-start = (f32[128,640]{1,0:T(8,128)S(1)}, f32[128,640]{1,0:T(8,128)S(1)}, u32[]{:S(2)}, u32[]{:S(2)}) collective-permute-start(f32[128,640]{1,0:T(8,128)S(1)} %get-tuple-element.370), channel_id=1, source_target_pairs={{0,8},{4,12},{8,0},{12,4},{16,24},{20,28},{24,16},{28,20},{1,9},{5... | collective-permute-start | bytes 983048 | tf_op jit(solution)/shard_map/ppermute | solution.py:21
  18.3 9.5 %collective-permute-start.2 = (f32[128,640]{1,0:T(8,128)S(1)}, f32[128,640]{1,0:T(8,128)S(1)}, u32[]{:S(2)}, u32[]{:S(2)}) collective-permute-start(f32[128,640]{1,0:T(8,128)S(1)} %get-tuple-element.369), channel_id=1, source_target_pairs={{0,16},{4,20},{8,24},{12,28},{16,0},{20,4},{24,8},{28,12},{1,17},{... | collective-permute-start | bytes 983048 | tf_op jit(solution)/shard_map/ppermute | solution.py:21
  26.0 10.6 %collective-permute-start.1 = (f32[128,640]{1,0:T(8,128)S(1)}, f32[128,640]{1,0:T(8,128)S(1)}, u32[]{:S(2)}, u32[]{:S(2)}) collective-permute-start(f32[128,640]{1,0:T(8,128)S(1)} %collective-permute-done.refs_2_), channel_id=1, source_target_pairs={{0,16},{4,20},{8,24},{12,28},{16,0},{20,4},{24,8},{28,12},{1,17},{... | collective-permute-start | bytes 983048 | tf_op jit(solution)/shard_map/ppermute | solution.py:21
  27.8 11.2 %collective-permute-start.3 = (f32[128,640]{1,0:T(8,128)S(1)}, f32[128,640]{1,0:T(8,128)S(1)}, u32[]{:S(2)}, u32[]{:S(2)}) collective-permute-start(f32[128,640]{1,0:T(8,128)S(1)} %collective-permute-done.2.refs_7_), channel_id=1, source_target_pairs={{0,8},{4,12},{8,0},{12,4},{16,24},{20,28},{24,16},{28,20},{1,9},{5... | collective-permute-start | bytes 983048 | tf_op jit(solution)/shard_map/ppermute | solution.py:21
  29.3 14.6 %collective-permute-start.8 = (f32[128,640]{1,0:T(8,128)S(1)}, f32[128,640]{1,0:T(8,128)}, u32[]{:S(2)}, u32[]{:S(2)}) collective-permute-start(f32[128,640]{1,0:T(8,128)S(1)} %get-tuple-element.369), channel_id=1, source_target_pairs={{0,8},{4,12},{8,0},{12,4},{16,24},{20,28},{24,16},{28,20},{1,9},{5... | collective-permute-start | bytes 983048 | tf_op jit(solution)/shard_map/ppermute | solution.py:21
  29.8 14.7 %collective-permute-start.11 = (f32[128,640]{1,0:T(8,128)S(1)}, f32[128,640]{1,0:T(8,128)S(1)}, u32[]{:S(2)}, u32[]{:S(2)}) collective-permute-start(f32[128,640]{1,0:T(8,128)S(1)} %get-tuple-element.370), channel_id=1, source_target_pairs={{0,16},{4,20},{8,24},{12,28},{16,0},{20,4},{24,8},{28,12},{1,17},{... | collective-permute-start | bytes 983048 | tf_op jit(solution)/shard_map/ppermute | solution.py:21
  31.0 13.5 %collective-permute-start.13 = (f32[128,640]{1,0:T(8,128)S(1)}, f32[128,640]{1,0:T(8,128)S(1)}, u32[]{:S(2)}, u32[]{:S(2)}) collective-permute-start(f32[128,640]{1,0:T(8,128)S(1)} %collective-permute-done.2.refs_7_), channel_id=1, source_target_pairs={{0,4},{4,0},{8,12},{12,8},{16,20},{20,16},{24,28},{28,24},{1,5},{5... | collective-permute-start | bytes 983048 | tf_op jit(solution)/shard_map/ppermute | solution.py:21
  37.4 7.7 %collective-permute-start.9 = (f32[128,640]{1,0:T(8,128)S(1)}, f32[128,640]{1,0:T(8,128)S(1)}, u32[]{:S(2)}, u32[]{:S(2)}) collective-permute-start(f32[128,640]{1,0:T(8,128)S(1)} %collective-permute-done.refs_2_), channel_id=1, source_target_pairs={{0,4},{4,0},{8,12},{12,8},{16,20},{20,16},{24,28},{28,24},{1,5},{5... | collective-permute-start | bytes 983048 | tf_op jit(solution)/shard_map/ppermute | solution.py:21
  39.0 49.2 %collective-permute-start.4 = (f32[256,2048]{1,0:T(8,128)}, f32[256,2048]{1,0:T(8,128)}, u32[]{:S(2)}, u32[]{:S(2)}) collective-permute-start(f32[256,2048]{1,0:T(8,128)} %convert_element_type.115.refs_0_), channel_id=1, source_target_pairs={{0,8},{4,12},{8,0},{12,4},{16,24},{20,28},{24,16},{28,20},{1,9},{5... | collective-permute-start | bytes 6291464 | tf_op jit(solution)/shard_map/ppermute | solution.py:21
  43.9 44.9 %collective-permute-start.5 = (f32[256,2048]{1,0:T(8,128)}, f32[256,2048]{1,0:T(8,128)}, u32[]{:S(2)}, u32[]{:S(2)}) collective-permute-start(f32[256,2048]{1,0:T(8,128)} %convert_element_type.115.refs_0_), channel_id=1, source_target_pairs={{0,16},{4,20},{8,24},{12,28},{16,0},{20,4},{24,8},{28,12},{1,17},{... | collective-permute-start | bytes 6291464 | tf_op jit(solution)/shard_map/ppermute | solution.py:21
  44.5 44.4 %collective-permute-start.6 = (f32[256,2048]{1,0:T(8,128)}, f32[256,2048]{1,0:T(8,128)}, u32[]{:S(2)}, u32[]{:S(2)}) collective-permute-start(f32[256,2048]{1,0:T(8,128)} %convert_element_type.115.refs_0_), channel_id=1, source_target_pairs={{0,4},{4,0},{8,12},{12,8},{16,20},{20,16},{24,28},{28,24},{1,5},{5... | collective-permute-start | bytes 6291464 | tf_op jit(solution)/shard_map/ppermute | solution.py:21
  44.6 6.6 %collective-permute-start.10 = (f32[128,640]{1,0:T(8,128)}, f32[128,640]{1,0:T(8,128)}, u32[]{:S(2)}, u32[]{:S(2)}) collective-permute-start(f32[128,640]{1,0:T(8,128)} %collective-permute-done.8.refs_3_), channel_id=1, source_target_pairs={{0,4},{4,0},{8,12},{12,8},{16,20},{20,16},{24,28},{28,24},{1,5},{5... | collective-permute-start | bytes 983048 | tf_op jit(solution)/shard_map/ppermute | solution.py:21
  45.1 8.3 %collective-permute-start.7 = (f32[256,640]{1,0:T(8,128)}, f32[256,640]{1,0:T(8,128)}, u32[]{:S(2)}, u32[]{:S(2)}) collective-permute-start(f32[256,640]{1,0:T(8,128)} %pad_maximum_fusion.2.refs_0_), channel_id=1, source_target_pairs={{0,4},{4,0},{8,12},{12,8},{16,20},{20,16},{24,28},{28,24},{1,5},{5... | collective-permute-start | bytes 1966088 | tf_op jit(solution)/shard_map/ppermute | solution.py:21
  51.2 2.0 collective-permute-start.12
  52.2 116.2 %copy-start.43 = (f32[2048]{0:T(1024)}, f32[2048]{0:T(1024)S(1)}, u32[]{:S(2)}) copy-start(f32[2048]{0:T(1024)S(1)} %convert_element_type.125) | copy-start | bytes 24580
  53.3 1.9 collective-permute-start.14
  53.4 2.2 collective-permute-start.15
  67.5 194.9 %all-reduce.8.cloned.1.call-start = ((), (), s32[]{:S(2)}) async-start(), calls=%async_computation.1 | async-start | bytes 4194304 | tf_op jit(solution)/shard_map/psum | solution.py:179
  93.5 66.3 %collective-permute-start.18 = (f32[256,2048]{1,0:T(8,128)}, f32[256,2048]{1,0:T(8,128)}, u32[]{:S(2)}, u32[]{:S(2)}) collective-permute-start(f32[256,2048]{1,0:T(8,128)} %collective-permute-done.4.refs_2_), channel_id=1, source_target_pairs={{0,4},{4,0},{8,12},{12,8},{16,20},{20,16},{24,28},{28,24},{1,5},{5... | collective-permute-start | bytes 6291464 | tf_op jit(solution)/shard_map/ppermute | solution.py:21
  93.5 66.3 %collective-permute-start.19 = (f32[256,2048]{1,0:T(8,128)}, f32[256,2048]{1,0:T(8,128)}, u32[]{:S(2)}, u32[]{:S(2)}) collective-permute-start(f32[256,2048]{1,0:T(8,128)} %collective-permute-done.5.refs_3_), channel_id=1, source_target_pairs={{0,4},{4,0},{8,12},{12,8},{16,20},{20,16},{24,28},{28,24},{1,5},{5... | collective-permute-start | bytes 6291464 | tf_op jit(solution)/shard_map/ppermute | solution.py:21
  94.0 65.8 %collective-permute-start.16 = (f32[128,2048]{1,0:T(8,128)}, f32[128,2048]{1,0:T(8,128)}, u32[]{:S(2)}, u32[]{:S(2)}) collective-permute-start(f32[128,2048]{1,0:T(8,128)} %slice.48), channel_id=1, source_target_pairs={{0,16},{4,20},{8,24},{12,28},{16,0},{20,4},{24,8},{28,12},{1,17},{... | collective-permute-start | bytes 3145736 | tf_op jit(solution)/shard_map/ppermute | solution.py:21
  95.5 64.3 %collective-permute-start.17 = (f32[128,2048]{1,0:T(8,128)}, f32[128,2048]{1,0:T(8,128)}, u32[]{:S(2)}, u32[]{:S(2)}) collective-permute-start(f32[128,2048]{1,0:T(8,128)} %slice.49), channel_id=1, source_target_pairs={{0,8},{4,12},{8,0},{12,4},{16,24},{20,28},{24,16},{28,20},{1,9},{5... | collective-permute-start | bytes 3145736 | tf_op jit(solution)/shard_map/ppermute | solution.py:21
  159.8 18.7 %collective-permute-start.23 = (f32[128,2048]{1,0:T(8,128)}, f32[128,2048]{1,0:T(8,128)}, u32[]{:S(2)}, u32[]{:S(2)}) collective-permute-start(f32[128,2048]{1,0:T(8,128)} %collective-permute-done.16.refs_2_), channel_id=1, source_target_pairs={{0,4},{4,0},{8,12},{12,8},{16,20},{20,16},{24,28},{28,24},{1,5},{5... | collective-permute-start | bytes 3145736 | tf_op jit(solution)/shard_map/ppermute | solution.py:21
  159.9 18.6 %collective-permute-start.24 = (f32[128,2048]{1,0:T(8,128)}, f32[128,2048]{1,0:T(8,128)}, u32[]{:S(2)}, u32[]{:S(2)}) collective-permute-start(f32[128,2048]{1,0:T(8,128)} %collective-permute-done.17.refs_3_), channel_id=1, source_target_pairs={{0,4},{4,0},{8,12},{12,8},{16,20},{20,16},{24,28},{28,24},{1,5},{5... | collective-permute-start | bytes 3145736 | tf_op jit(solution)/shard_map/ppermute | solution.py:21
  160.4 47.9 %collective-permute-start.20 = (f32[256,2048]{1,0:T(8,128)}, f32[256,2048]{1,0:T(8,128)}, u32[]{:S(2)}, u32[]{:S(2)}) collective-permute-start(f32[256,2048]{1,0:T(8,128)} %broadcast_multiply_fusion.refs_0_), channel_id=1, source_target_pairs={{0,8},{4,12},{8,0},{12,4},{16,24},{20,28},{24,16},{28,20},{1,9},{5... | collective-permute-start | bytes 6291464 | tf_op jit(solution)/shard_map/ppermute | solution.py:21
  161.9 47.6 %collective-permute-start.21 = (f32[256,2048]{1,0:T(8,128)}, f32[256,2048]{1,0:T(8,128)}, u32[]{:S(2)}, u32[]{:S(2)}) collective-permute-start(f32[256,2048]{1,0:T(8,128)} %broadcast_multiply_fusion.refs_0_), channel_id=1, source_target_pairs={{0,16},{4,20},{8,24},{12,28},{16,0},{20,4},{24,8},{28,12},{1,17},{... | collective-permute-start | bytes 6291464 | tf_op jit(solution)/shard_map/ppermute | solution.py:21
  163.3 46.2 %collective-permute-start.22 = (f32[256,2048]{1,0:T(8,128)}, f32[256,2048]{1,0:T(8,128)}, u32[]{:S(2)}, u32[]{:S(2)}) collective-permute-start(f32[256,2048]{1,0:T(8,128)} %broadcast_multiply_fusion.refs_0_), channel_id=1, source_target_pairs={{0,4},{4,0},{8,12},{12,8},{16,20},{20,16},{24,28},{28,24},{1,5},{5... | collective-permute-start | bytes 6291464 | tf_op jit(solution)/shard_map/ppermute | solution.py:21
  178.5 311.1 %all-reduce.10.cloned.1.call-start = ((), (), s32[]{:S(2)}) async-start(), calls=%async_computation.2 | async-start | bytes 18874368 | tf_op jit(solution)/shard_map/psum | solution.py:583
  214.2 57.1 %collective-permute-start.27 = (f32[256,2048]{1,0:T(8,128)}, f32[256,2048]{1,0:T(8,128)}, u32[]{:S(2)}, u32[]{:S(2)}) collective-permute-start(f32[256,2048]{1,0:T(8,128)} %collective-permute-done.20.refs_2_), channel_id=1, source_target_pairs={{0,4},{4,0},{8,12},{12,8},{16,20},{20,16},{24,28},{28,24},{1,5},{5... | collective-permute-start | bytes 6291464 | tf_op jit(solution)/shard_map/ppermute | solution.py:21
  214.2 57.1 %collective-permute-start.28 = (f32[256,2048]{1,0:T(8,128)}, f32[256,2048]{1,0:T(8,128)}, u32[]{:S(2)}, u32[]{:S(2)}) collective-permute-start(f32[256,2048]{1,0:T(8,128)} %collective-permute-done.21.refs_3_), channel_id=1, source_target_pairs={{0,4},{4,0},{8,12},{12,8},{16,20},{20,16},{24,28},{28,24},{1,5},{5... | collective-permute-start | bytes 6291464 | tf_op jit(solution)/shard_map/ppermute | solution.py:21
  214.7 56.5 %collective-permute-start.25 = (f32[128,2048]{1,0:T(8,128)}, f32[128,2048]{1,0:T(8,128)}, u32[]{:S(2)}, u32[]{:S(2)}) collective-permute-start(f32[128,2048]{1,0:T(8,128)} %slice.50), channel_id=1, source_target_pairs={{0,16},{4,20},{8,24},{12,28},{16,0},{20,4},{24,8},{28,12},{1,17},{... | collective-permute-start | bytes 3145736 | tf_op jit(solution)/shard_map/ppermute | solution.py:21
  216.2 55.1 %collective-permute-start.26 = (f32[128,2048]{1,0:T(8,128)}, f32[128,2048]{1,0:T(8,128)}, u32[]{:S(2)}, u32[]{:S(2)}) collective-permute-start(f32[128,2048]{1,0:T(8,128)} %slice.51), channel_id=1, source_target_pairs={{0,8},{4,12},{8,0},{12,4},{16,24},{20,28},{24,16},{28,20},{1,9},{5... | collective-permute-start | bytes 3145736 | tf_op jit(solution)/shard_map/ppermute | solution.py:21
  271.3 19.5 %collective-permute-start.29 = (f32[264,512]{1,0:T(8,128)S(1)}, f32[264,512]{1,0:T(8,128)S(1)}, u32[]{:S(2)}, u32[]{:S(2)}) collective-permute-start(f32[264,512]{1,0:T(8,128)S(1)} %select_maximum_fusion.refs_14_), channel_id=1, source_target_pairs={{0,8},{4,12},{8,0},{12,4},{16,24},{20,28},{24,16},{28,20},{1,9},{5... | collective-permute-start | bytes 1622024 | tf_op jit(solution)/shard_map/ppermute | solution.py:21
  272.8 18.0 %collective-permute-start.30 = (f32[264,512]{1,0:T(8,128)S(1)}, f32[264,512]{1,0:T(8,128)S(1)}, u32[]{:S(2)}, u32[]{:S(2)}) collective-permute-start(f32[264,512]{1,0:T(8,128)S(1)} %select_maximum_fusion.refs_14_), channel_id=1, source_target_pairs={{0,16},{4,20},{8,24},{12,28},{16,0},{20,4},{24,8},{28,12},{1,17},{... | collective-permute-start | bytes 1622024 | tf_op jit(solution)/shard_map/ppermute | solution.py:21
  274.3 16.5 %collective-permute-start.31 = (f32[264,512]{1,0:T(8,128)S(1)}, f32[264,512]{1,0:T(8,128)S(1)}, u32[]{:S(2)}, u32[]{:S(2)}) collective-permute-start(f32[264,512]{1,0:T(8,128)S(1)} %select_maximum_fusion.refs_14_), channel_id=1, source_target_pairs={{0,4},{4,0},{8,12},{12,8},{16,20},{20,16},{24,28},{28,24},{1,5},{5... | collective-permute-start | bytes 1622024 | tf_op jit(solution)/shard_map/ppermute | solution.py:21
  274.3 29.5 %collective-permute-start.38 = (f32[128,2048]{1,0:T(8,128)}, f32[128,2048]{1,0:T(8,128)}, u32[]{:S(2)}, u32[]{:S(2)}) collective-permute-start(f32[128,2048]{1,0:T(8,128)} %split.16), channel_id=1, source_target_pairs={{0,1},{3,2},{4,5},{7,6},{8,9},{11,10},{12,13},{15,14},{16,17},{19,... | collective-permute-start | bytes 3145736 | tf_op jit(solution)/shard_map/ppermute | solution.py:21
  290.9 11.0 %collective-permute-start.34 = (f32[264,512]{1,0:T(8,128)S(1)}, f32[264,512]{1,0:T(8,128)S(1)}, u32[]{:S(2)}, u32[]{:S(2)}) collective-permute-start(f32[264,512]{1,0:T(8,128)S(1)} %collective-permute-done.29.refs_16_), channel_id=1, source_target_pairs={{0,4},{4,0},{8,12},{12,8},{16,20},{20,16},{24,28},{28,24},{1,5},{5... | collective-permute-start | bytes 1622024 | tf_op jit(solution)/shard_map/ppermute | solution.py:21
  291.2 10.7 %collective-permute-start.35 = (f32[264,512]{1,0:T(8,128)S(1)}, f32[264,512]{1,0:T(8,128)S(1)}, u32[]{:S(2)}, u32[]{:S(2)}) collective-permute-start(f32[264,512]{1,0:T(8,128)S(1)} %collective-permute-done.30.refs_18_), channel_id=1, source_target_pairs={{0,4},{4,0},{8,12},{12,8},{16,20},{20,16},{24,28},{28,24},{1,5},{5... | collective-permute-start | bytes 1622024 | tf_op jit(solution)/shard_map/ppermute | solution.py:21
  291.5 10.4 %collective-permute-start.33 = (f32[136,512]{1,0:T(8,128)S(1)}, f32[136,512]{1,0:T(8,128)}, u32[]{:S(2)}, u32[]{:S(2)}) collective-permute-start(f32[136,512]{1,0:T(8,128)S(1)} %slice.53), channel_id=1, source_target_pairs={{0,8},{4,12},{8,0},{12,4},{16,24},{20,28},{24,16},{28,20},{1,9},{5... | collective-permute-start | bytes 835592 | tf_op jit(solution)/shard_map/ppermute | solution.py:21
  292.0 9.9 %collective-permute-start.32 = (f32[128,512]{1,0:T(8,128)S(1)}, f32[128,512]{1,0:T(8,128)}, u32[]{:S(2)}, u32[]{:S(2)}) collective-permute-start(f32[128,512]{1,0:T(8,128)S(1)} %slice.52), channel_id=1, source_target_pairs={{0,16},{4,20},{8,24},{12,28},{16,0},{20,4},{24,8},{28,12},{1,17},{... | collective-permute-start | bytes 786440 | tf_op jit(solution)/shard_map/ppermute | solution.py:21
  302.7 2.7 collective-permute-start.37
  303.6 1.9 collective-permute-start.36
  308.3 20.9 %collective-permute-start.39 = (f32[128,2048]{1,0:T(8,128)}, f32[128,2048]{1,0:T(8,128)S(1)}, u32[]{:S(2)}, u32[]{:S(2)}) collective-permute-start(f32[128,2048]{1,0:T(8,128)} %collective-permute-done.25.refs_2_), channel_id=1, source_target_pairs={{0,4},{4,0},{8,12},{12,8},{16,20},{20,16},{24,28},{28,24},{1,5},{5... | collective-permute-start | bytes 3145736 | tf_op jit(solution)/shard_map/ppermute | solution.py:21
  308.5 20.7 %collective-permute-start.40 = (f32[128,2048]{1,0:T(8,128)}, f32[128,2048]{1,0:T(8,128)S(1)}, u32[]{:S(2)}, u32[]{:S(2)}) collective-permute-start(f32[128,2048]{1,0:T(8,128)} %collective-permute-done.26.refs_3_), channel_id=1, source_target_pairs={{0,4},{4,0},{8,12},{12,8},{16,20},{20,16},{24,28},{28,24},{1,5},{5... | collective-permute-start | bytes 3145736 | tf_op jit(solution)/shard_map/ppermute | solution.py:21
  308.8 27.7 %collective-permute-start.41 = (f32[128,2048]{1,0:T(8,128)}, f32[128,2048]{1,0:T(8,128)}, u32[]{:S(2)}, u32[]{:S(2)}) collective-permute-start(f32[128,2048]{1,0:T(8,128)} %get-tuple-element.275), channel_id=1, source_target_pairs={{0,1},{3,2},{4,5},{7,6},{8,9},{11,10},{12,13},{15,14},{16,17},{19,... | collective-permute-start | bytes 3145736 | tf_op jit(solution)/shard_map/ppermute | solution.py:21
  311.0 25.5 %collective-permute-start.42 = (f32[128,2048]{1,0:T(8,128)}, f32[128,2048]{1,0:T(8,128)}, u32[]{:S(2)}, u32[]{:S(2)}) collective-permute-start(f32[128,2048]{1,0:T(8,128)} %get-tuple-element.276), channel_id=1, source_target_pairs={{1,2},{2,1},{5,6},{6,5},{9,10},{10,9},{13,14},{14,13},{17,18},{18,... | collective-permute-start | bytes 3145736 | tf_op jit(solution)/shard_map/ppermute | solution.py:21
  340.7 29.4 %collective-permute-start.45 = (f32[128,2048]{1,0:T(8,128)S(1)}, f32[128,2048]{1,0:T(8,128)}, u32[]{:S(2)}, u32[]{:S(2)}) collective-permute-start(f32[128,2048]{1,0:T(8,128)S(1)} %slice_add_fusion.2), channel_id=1, source_target_pairs={{1,2},{2,1},{5,6},{6,5},{9,10},{10,9},{13,14},{14,13},{17,18},{18,... | collective-permute-start | bytes 3145736 | tf_op jit(solution)/shard_map/ppermute | solution.py:21
  342.4 27.7 %collective-permute-start.46 = (f32[128,2048]{1,0:T(8,128)}, f32[128,2048]{1,0:T(8,128)}, u32[]{:S(2)}, u32[]{:S(2)}) collective-permute-start(f32[128,2048]{1,0:T(8,128)} %add.226), channel_id=1, source_target_pairs={{1,0},{2,3},{5,4},{6,7},{9,8},{10,11},{13,12},{14,15},{17,16},{18,... | collective-permute-start | bytes 3145736 | tf_op jit(solution)/shard_map/ppermute | solution.py:21
  343.6 26.5 %collective-permute-start.44 = (f32[2,2048]{1,0:T(2,128)S(1)}, f32[2,2048]{1,0:T(2,128)S(1)}, u32[]{:S(2)}, u32[]{:S(2)}) collective-permute-start(f32[2,2048]{1,0:T(2,128)S(1)} %pad_maximum_fusion.3), channel_id=1, source_target_pairs={{0,1},{1,0},{2,3},{3,2},{4,5},{5,4},{6,7},{7,6},{8,9},{9,8},{10,11... | collective-permute-start | bytes 49160 | tf_op jit(solution)/shard_map/ppermute | solution.py:21
  347.3 24.7 %collective-permute-start.43 = (f32[128,2048]{1,0:T(8,128)}, f32[128,2048]{1,0:T(8,128)}, u32[]{:S(2)}, u32[]{:S(2)}) collective-permute-start(f32[128,2048]{1,0:T(8,128)} %split.18), channel_id=1, source_target_pairs={{0,1},{3,2},{4,5},{7,6},{8,9},{11,10},{12,13},{15,14},{16,17},{19,... | collective-permute-start | bytes 3145736 | tf_op jit(solution)/shard_map/ppermute | solution.py:21
  350.6 34.7 %slice-start.4 = ((s8[5636096]{0:T(1024)(128)(4,1)}), s8[1441792]{0:T(1024)(128)(4,1)S(1)}, s32[]{:S(2)}) async-start(s8[5636096]{0:T(1024)(128)(4,1)} %bitcast.75), calls=%async_computation.7 | async-start | bytes 2883584
  375.2 35.2 %collective-permute-start.50 = (f32[128,2048]{1,0:T(8,128)S(1)}, f32[128,2048]{1,0:T(8,128)}, u32[]{:S(2)}, u32[]{:S(2)}) collective-permute-start(f32[128,2048]{1,0:T(8,128)S(1)} %add.229), channel_id=1, source_target_pairs={{1,0},{2,3},{5,4},{6,7},{9,8},{10,11},{13,12},{14,15},{17,16},{18,... | collective-permute-start | bytes 3145736 | tf_op jit(solution)/shard_map/ppermute | solution.py:21
  376.8 33.7 %collective-permute-start.47 = (f32[128,2048]{1,0:T(8,128)S(1)}, f32[128,2048]{1,0:T(8,128)S(1)}, u32[]{:S(2)}, u32[]{:S(2)}) collective-permute-start(f32[128,2048]{1,0:T(8,128)S(1)} %get-tuple-element.313), channel_id=1, source_target_pairs={{0,1},{3,2},{4,5},{7,6},{8,9},{11,10},{12,13},{15,14},{16,17},{19,... | collective-permute-start | bytes 3145736 | tf_op jit(solution)/shard_map/ppermute | solution.py:21
  382.5 28.0 %collective-permute-start.48 = (f32[128,2048]{1,0:T(8,128)S(1)}, f32[128,2048]{1,0:T(8,128)S(1)}, u32[]{:S(2)}, u32[]{:S(2)}) collective-permute-start(f32[128,2048]{1,0:T(8,128)S(1)} %get-tuple-element.314), channel_id=1, source_target_pairs={{1,2},{2,1},{5,6},{6,5},{9,10},{10,9},{13,14},{14,13},{17,18},{18,... | collective-permute-start | bytes 3145736 | tf_op jit(solution)/shard_map/ppermute | solution.py:21
  383.3 27.2 %collective-permute-start.49 = (f32[2,2048]{1,0:T(2,128)S(1)}, f32[2,2048]{1,0:T(2,128)S(1)}, u32[]{:S(2)}, u32[]{:S(2)}) collective-permute-start(f32[2,2048]{1,0:T(2,128)S(1)} %fusion.19), channel_id=1, source_target_pairs={{0,2},{1,3},{2,0},{3,1},{4,6},{5,7},{6,4},{7,5},{8,10},{9,11},{10,... | collective-permute-start | bytes 49160 | tf_op jit(solution)/shard_map/ppermute | solution.py:21
  410.8 15.5 %collective-permute-start.53 = (f32[2,2048]{1,0:T(2,128)S(1)}, f32[2,2048]{1,0:T(2,128)S(1)}, u32[]{:S(2)}, u32[]{:S(2)}) collective-permute-start(f32[2,2048]{1,0:T(2,128)S(1)} %fusion.102), channel_id=1, source_target_pairs={{0,4},{4,0},{8,12},{12,8},{16,20},{20,16},{24,28},{28,24},{1,5},{5... | collective-permute-start | bytes 49160 | tf_op jit(solution)/shard_map/ppermute | solution.py:21
  410.9 15.4 %collective-permute-start.51 = (f32[128,2048]{1,0:T(8,128)S(1)}, f32[128,2048]{1,0:T(8,128)S(1)}, u32[]{:S(2)}, u32[]{:S(2)}) collective-permute-start(f32[128,2048]{1,0:T(8,128)S(1)} %slice_add_fusion), channel_id=1, source_target_pairs={{1,2},{2,1},{5,6},{6,5},{9,10},{10,9},{13,14},{14,13},{17,18},{18,... | collective-permute-start | bytes 3145736 | tf_op jit(solution)/shard_map/ppermute | solution.py:21
  411.7 27.4 %collective-permute-start.52 = (f32[128,2048]{1,0:T(8,128)S(1)}, f32[128,2048]{1,0:T(8,128)S(1)}, u32[]{:S(2)}, u32[]{:S(2)}) collective-permute-start(f32[128,2048]{1,0:T(8,128)S(1)} %add.233), channel_id=1, source_target_pairs={{1,0},{2,3},{5,4},{6,7},{9,8},{10,11},{13,12},{14,15},{17,16},{18,... | collective-permute-start | bytes 3145736 | tf_op jit(solution)/shard_map/ppermute | solution.py:21
  439.3 30.1 %collective-permute-start.54 = (f32[128,2048]{1,0:T(8,128)S(1)}, f32[128,2048]{1,0:T(8,128)S(1)}, u32[]{:S(2)}, u32[]{:S(2)}) collective-permute-start(f32[128,2048]{1,0:T(8,128)S(1)} %add.236), channel_id=1, source_target_pairs={{1,0},{2,3},{5,4},{6,7},{9,8},{10,11},{13,12},{14,15},{17,16},{18,... | collective-permute-start | bytes 3145736 | tf_op jit(solution)/shard_map/ppermute | solution.py:21
  440.9 28.5 %collective-permute-start.55 = (f32[2,2048]{1,0:T(2,128)S(1)}, f32[2,2048]{1,0:T(2,128)S(1)}, u32[]{:S(2)}, u32[]{:S(2)}) collective-permute-start(f32[2,2048]{1,0:T(2,128)S(1)} %add.237), channel_id=1, source_target_pairs={{0,8},{4,12},{8,0},{12,4},{16,24},{20,28},{24,16},{28,20},{1,9},{5... | collective-permute-start | bytes 49160 | tf_op jit(solution)/shard_map/ppermute | solution.py:21
  441.8 27.6 %collective-permute-start.56 = (f32[2,2048]{1,0:T(2,128)S(1)}, f32[2,2048]{1,0:T(2,128)S(1)}, u32[]{:S(2)}, u32[]{:S(2)}) collective-permute-start(f32[2,2048]{1,0:T(2,128)S(1)} %add.237), channel_id=1, source_target_pairs={{0,16},{4,20},{8,24},{12,28},{16,0},{20,4},{24,8},{28,12},{1,17},{... | collective-permute-start | bytes 49160 | tf_op jit(solution)/shard_map/ppermute | solution.py:21
  443.3 26.1 %collective-permute-start.57 = (f32[2,2048]{1,0:T(2,128)S(1)}, f32[2,2048]{1,0:T(2,128)S(1)}, u32[]{:S(2)}, u32[]{:S(2)}) collective-permute-start(f32[2,2048]{1,0:T(2,128)S(1)} %add.237), channel_id=1, source_target_pairs={{0,24},{4,28},{8,16},{12,20},{16,8},{20,12},{24,0},{28,4},{1,25},{... | collective-permute-start | bytes 49160 | tf_op jit(solution)/shard_map/ppermute | solution.py:21
  (75 other events, 579.6 us)
Sparse Core Ops, SparseCore 0:
  67.6 87.4 all-reduce.5
  178.6 83.7 all-reduce.7
  350.7 138.7 all-reduce.9

commit v5 on v4

--- a/solution.py
+++ b/solution.py
@@ -4,6 +4,7 @@
 import jax.numpy as jnp
 from jax import lax
 from jax.experimental import pallas as pl
+from jax.experimental.layout import Layout, with_layout_constraint
 from jax.experimental.pallas import tpu as pltpu
 from jax.sharding import PartitionSpec as P
 
@@ -23,26 +24,6 @@
 
 def after(value, *others):
     return lax.optimization_barrier((value, others))[0]
-
-
-def gather_blk(value):
-    count = lax.axis_size("blk")
-    if count != 8:
-        slots, bit = [value], 1
-        while bit < count:
-            slots = slots + [hop(slot, "blk", bit) for slot in slots]
-            bit *= 2
-        return [[slot] for slot in slots]
-    half = value.shape[0] // 16 * 8
-    low, high = value[:half], value[half:]
-    x_low, y_high = hop(low, "blk", 2), hop(high, "blk", 4)
-    x_high, y_low = hop(high, "blk", 2), hop(low, "blk", 4)
-    own_pair = hop(value, "blk", 1)
-    far_low, far_high = hop(x_low, "blk", 4), hop(y_high, "blk", 2)
-    slots = [[value], [own_pair]]
-    for slot in ([x_low, x_high], [y_low, y_high], [far_low, far_high]):
-        slots += [slot, [hop(part, "blk", 1) for part in slot]]
-    return slots
 
 
 class Chain:
@@ -431,7 +412,10 @@
     qkv_own = jnp.concatenate(
         [mm(normed_in, w_query), mm(normed_in, w_key), mm(normed_in, w_value)], axis=1
     )
-    qkv = gather_blk(qkv_own)
+    convoy = Convoy()
+    qkv_slots = {}
+    convoy.finish(Chain(gather_steps(qkv_own, qkv_slots)))
+    qkv = [qkv_slots[slot] for slot in range(blk_count)]
     shape = tuple(len(slot) for slot in qkv)
     qkv_parts = [part for slot in qkv for part in slot]
 
@@ -453,7 +437,6 @@
     order = [0, 1, 2, 4, 3, 5, 6, 7] if blk_count == 8 else list(range(blk_count))
     early, late = order[: blk_count // 2], order[blk_count // 2 :]
     ones = jnp.ones_like(gain_two)
-    convoy = Convoy()
 
     def ready(chain, slots, wanted):
         while not all(slot in slots for slot in wanted):
@@ -472,7 +455,7 @@
         return gated(gate, mm(rows_of, w_up), hidden_grad)
 
     cot_slots = {}
-    cot = Chain(gather_steps(after(cot_wide, qkv[-2]), cot_slots))
+    cot = Chain(gather_steps(cot_wide, cot_slots))
     own_hidden_grad = convoy.wave(
         [cot], lambda left, _: mm_t(left, w_down), cotangent, attn_part
     )
@@ -563,27 +546,26 @@
             *grad_parts,
             flops=2 * cost,
         )
+        lin_grads = (query_lin_grad, key_lin_grad, value_grad)
+        parts = [t_mm(normed_in, grad) for grad in lin_grads]
+        parts[2] = with_layout_constraint(parts[2], Layout(major_to_minor=(0, 1)))
+        query_lin_grad, key_lin_grad, value_grad = after(lin_grads, parts)
         in_part = mm_t(query_lin_grad, w_query) + mm_t(key_lin_grad, w_key)
-        in_part = in_part + mm_t(value_grad, w_value)
-        return in_part, query_lin_grad, key_lin_grad, value_grad
+        return in_part + mm_t(value_grad, w_value), parts
 
     grad_parts = [part for slot in grad_slots for part in slot]
     convoy.launch(mid, mlp)
-    in_part, *lin_grads = convoy.work(key_work, query_lin_grad, grad_parts)
+    in_part, parts = convoy.work(key_work, query_lin_grad, grad_parts)
+    *qkv_w_grads, out_w_grad = lax.psum((*parts, out_part), "blk")
     convoy.land(mid)
     mid_late = ready(mid, mid_slots, late)
 
     in_sum = Chain(line_steps(in_part, 2))
     convoy.launch(in_sum)
 
-    def parts_work(normed_in, *lin_grads):
-        return [t_mm(normed_in, grad) for grad in lin_grads]
-
-    parts = convoy.work(parts_work, normed_in, *lin_grads)
-    *qkv_w_grads, out_w_grad = lax.psum((*parts, out_part), "blk")
     gain_parts = jnp.stack(
         [
-            jnp.sum(after(in_part, parts) * token_wide * inv_in, axis=0),
+            jnp.sum(after(in_part, convoy.sent) * token_wide * inv_in, axis=0),
             jnp.sum(mid_part * scaled_mid, axis=0),
         ]
     )
@@ -619,7 +601,7 @@
     while any(chain.due for chain in chains):
         convoy.wave(chains)
     in_grad, gain_grads = (chain.result for chain in chains)
-    in_grad = after(in_grad, qkv_w_grads, out_w_grad)
+    gain_grads = after(gain_grads, qkv_w_grads, out_w_grad)
     input_grad = resid_grad + norm_back(in_grad, token_wide, inv_in, gain_one)
     return (
         output,

time: 520 us -> 502 us (0.965)
  other arithmetic: 45.4 us -> 34.2 us
  waiting for transfers between devices: 123 us -> 116 us
  starting transfers between devices: 62.2 us -> 55.6 us
  local copies, waits for them, and re-layouts: 34.9 us -> 40.2 us
    ppermute x58 -> x54, waiting for transfers between devices: 57.5 us -> 72.3 us  [hop(): return lax.ppermute(value, axis, way)]
    psum x1, waiting for transfers between devices: 17.9 us -> 3.39 us  [per_device(): *qkv_w_grads, out_w_grad = lax.psum((*parts, out_part), 'blk')]
    psum x2, waiting for transfers between devices: 47.7 us -> 40.4 us  [sum_head(): return lax.psum(value, 'head')]
    unnamed x161 -> x151, local copies, waits for them, and re-layouts: 18.9 us -> 25.6 us
    ppermute x58 -> x54, starting transfers between devices: 62.1 us -> 55.5 us  [hop(): return lax.ppermute(value, axis, way)]
  transfers between devices with their start and end apart: 61 -> 57, of which waited for: 16 -> 15; matrix products, arithmetic and copies ran while one was open for 42% -> 44% of each run, Pallas kernels for 11% -> 11%
where the time goes in v5:
time: 502 us; the launch traced here: 493 us
  matrix products  175 us (35%)
  waiting for transfers between devices  116 us (23%)
  starting transfers between devices  55.6 us (11%)
  Pallas kernels  53.8 us (11%)
  local copies, waits for them, and re-layouts  40.2 us (8%)
  other arithmetic  34.2 us (7%)
  between operations  17.7 us (4%)
    dot_general x10, matrix products, t_mm(): return jnp.einsum('ca,cb->ab', left, right, preferred_element_type=f32)  72.4 us
    ppermute x54, waiting for transfers between devices, hop(): return lax.ppermute(value, axis, way)  72.3 us
    dot_general x11, matrix products, mm(): return jnp.dot(left, right, preferred_element_type=f32)  67.9 us
    ppermute x54, starting transfers between devices, hop(): return lax.ppermute(value, axis, way)  55.5 us
    psum x2, waiting for transfers between devices, sum_head(): return lax.psum(value, 'head')  40.4 us
    dot_general x9, matrix products, mm_t(): return jnp.einsum('ac,bc->ab', left, right, preferred_element_type=f32)  35.2 us
    pallas_call x3, Pallas kernels, whole_call(): pl.pallas_call(body, out_shape=outs, in_specs=[pl.BlockSpec(memory_space=...  28.6 us
    unnamed x151, local copies, waits for them, and re-layouts  25.6 us
  transfers between devices with their start and end apart: 57, of which 15 were waited for; matrix products, arithmetic and copies ran while one was open for 44% of the time, Pallas kernels for 11%

profile of v5, /device:TPU:0, one launch (start us, length us, event | category | flops | bytes accessed | tf_op | source)
XLA Modules:
  0.0 493.1 jit_solution(17493267420412761618)
XLA Ops:
  8.1 1.6 multiply_reduce_fusion.5
  13.3 3.0 collective-permute-start
  17.8 13.2 %collective-permute-done.refs_2_ = f32[256,640]{1,0:T(8,128)S(1)} collective-permute-done((f32[256,640]{1,0:T(8,128)S(1)}, f32[256,640]{1,0:T(8,128)S(1)}, u32[]{:S(2)}, u32[]{:S(2)}) %collective-permute-start) | collective-permute-done | bytes 655392 | tf_op jit(solution)/shard_map/ppermute | solution.py:22
  35.1 7.6 %collective-permute-done.3.refs_6_ = f32[128,640]{1,0:T(8,128)S(1)} collective-permute-done((f32[128,640]{1,0:T(8,128)S(1)}, f32[128,640]{1,0:T(8,128)S(1)}, u32[]{:S(2)}, u32[]{:S(2)}) %collective-permute-start.3) | collective-permute-done | bytes 327712 | tf_op jit(solution)/shard_map/ppermute | solution.py:22
  45.2 1.6 convert_element_type.115.refs_0_
  56.8 7.9 %shard_map.203 = (bf16[256,512]{1,0:T(8,128)(2,1)}, f32[256,512]{1,0:T(8,128)}, f32[256,512]{1,0:T(8,128)}) custom-call(s32[256,4]{1,0:T(8,128)} %copy.28.col_ref, s32[24,256]{1,0:T(8,128)} %pad_add_fusion.row_ref, f32[256,640]{1,0:T(8,128)} %copy-done.32, f32[256,640]{1,0:T(8,128)} %copy-done.51, f32[256,640]{1,0:T(8,128)} %copy-done.41, ...), custom_call_target="tpu_custom_call" | custom-call | flops 2147483648 | bytes 6582272 | tf_op jit(solution)/shard_map/pallas_call | solution.py:299
  64.8 3.0 fusion.29
  67.8 5.7 %fusion.30 = f32[256,1376]{0,1:T(8,128)} fusion(bf16[256,2048]{1,0:T(8,128)(2,1)} %param.23, bf16[1376,2048]{1,0:T(8,128)(2,1)} %param.21), kind=kOutput, calls=%fused_computation.92 | convolution fusion | flops 1442840576 | bytes 8093696 | tf_op jit(solution)/shard_map/ac,bc->ab/dot_general | solution.py:355
  73.5 22.3 %collective-permute-done.10.refs_3_ = f32[256,2048]{1,0:T(8,128)} collective-permute-done((f32[256,2048]{1,0:T(8,128)}, f32[256,2048]{1,0:T(8,128)}, u32[]{:S(2)}, u32[]{:S(2)}) %collective-permute-start.10) | collective-permute-done | bytes 2097184 | tf_op jit(solution)/shard_map/ppermute | solution.py:22
  96.6 2.3 slice.48
  98.9 2.3 slice.49
  104.1 6.2 %shard_map.204 = bf16[1024,2048]{1,0:T(8,128)(2,1)} custom-call(f32[1,2048]{1,0:T(1,128)} %broadcast_12_scale_ref.2.scale_ref, f32[256,2048]{1,0:T(8,128)} %convert_element_type.115.refs_0_, f32[256,2048]{1,0:T(8,128)} %collective-permute-done.11.refs_1_, f32[256,2048]{1,0:T(8,128)} %collective-permute-done.9.refs_2_, ...), custom_call_target="tpu_custom_call" | custom-call | bytes 12582912 | tf_op jit(solution)/shard_map/pallas_call | solution.py:326
  110.4 10.9 %fusion.31 = f32[1024,1376]{0,1:T(8,128)} fusion(bf16[1024,2048]{1,0:T(8,128)(2,1)} %shard_map.204, bf16[1376,2048]{1,0:T(8,128)(2,1)} %param.21), kind=kOutput, calls=%fused_computation.93 | convolution fusion | flops 5771362304 | bytes 15466496 | tf_op jit(solution)/shard_map/ac,bc->ab/dot_general | solution.py:355
  121.2 34.0 %all-reduce.6.cloned.1.call-done = f32[256,2048]{1,0:T(8,128)} async-done(((f32[256,2048]{1,0:T(8,128)}), f32[256,2048]{1,0:T(8,128)}) %all-reduce.6.cloned.1.call-update) | async-done | bytes 2097168 | tf_op jit(solution)/shard_map/psum | solution.py:160
  155.2 2.5 multiply_reduce_fusion.4
  163.4 5.1 %fusion.8 = f32[256,1376]{0,1:T(8,128)S(1)} fusion(bf16[2048,1376]{0,1:T(8,128)(2,1)} %param.19, f32[256,2048]{1,0:T(8,128)} %broadcast_multiply_fusion.refs_0_, f32[2048]{0:T(1024)S(1)} %convert_element_type.125), kind=kOutput, calls=%fused_computation.49 | convolution fusion | flops 1443889152 | bytes 9150464 | tf_op jit(solution)/shard_map/dot_general | solution.py:351
  168.6 4.5 multiply_convert_fusion.10
  173.1 2.2 fusion.3
  175.3 3.2 convolution_add_fusion.5
  178.6 4.7 fusion.32
  185.7 6.4 %shard_map.205 = bf16[1024,2048]{1,0:T(8,128)(2,1)} custom-call(f32[1,2048]{1,0:T(1,128)} %broadcast_12_scale_ref.2.scale_ref, f32[256,2048]{1,0:T(8,128)} %collective-permute-done.14.refs_0_, f32[256,2048]{1,0:T(8,128)} %collective-permute-done.15.refs_1_, f32[128,2048]{1,0:T(8,128)} %collective-permute-done.12.refs_2_, ...), custom_call_target="tpu_custom_call" | custom-call | bytes 12582912 | tf_op jit(solution)/shard_map/pallas_call | solution.py:326
  192.1 10.9 %fusion.33 = f32[1024,1376]{0,1:T(8,128)} fusion(bf16[1024,2048]{1,0:T(8,128)(2,1)} %shard_map.205, bf16[1376,2048]{1,0:T(8,128)(2,1)} %param.21), kind=kOutput, calls=%fused_computation.95 | convolution fusion | flops 5771362304 | bytes 15466496 | tf_op jit(solution)/shard_map/ac,bc->ab/dot_general | solution.py:355
  203.0 5.4 %collective-permute-done.16.refs_2_ = f32[256,2048]{1,0:T(8,128)} collective-permute-done((f32[256,2048]{1,0:T(8,128)}, f32[256,2048]{1,0:T(8,128)}, u32[]{:S(2)}, u32[]{:S(2)}) %collective-permute-start.16) | collective-permute-done | bytes 2097184 | tf_op jit(solution)/shard_map/ppermute | solution.py:22
  209.6 2.3 slice.50
  211.9 2.3 slice.51
  216.8 6.3 %shard_map.206 = bf16[1024,2048]{1,0:T(8,128)(2,1)} custom-call(f32[1,2048]{1,0:T(1,128)} %bitcast.81, f32[256,2048]{1,0:T(8,128)} %broadcast_multiply_fusion.refs_0_, f32[256,2048]{1,0:T(8,128)} %collective-permute-done.18.refs_1_, f32[256,2048]{1,0:T(8,128)} %collective-permute-done.16.refs_2_, f32[256,2048]{1,0:T(8,128)} %collective-permute-done.17.refs_3_), custom_call_target="tpu_custom_call" | custom-call | bytes 12582912 | tf_op jit(solution)/shard_map/pallas_call | solution.py:326
  223.0 11.3 %fusion.34 = f32[1024,1376]{0,1:T(8,128)} fusion(bf16[1024,2048]{1,0:T(8,128)(2,1)} %shard_map.206, bf16[2048,1376]{0,1:T(8,128)(2,1)} %param.19), kind=kOutput, calls=%fused_computation.96 | convolution fusion | flops 5771362304 | bytes 15466496 | tf_op jit(solution)/shard_map/dot_general | solution.py:351
  234.4 12.7 %multiply_convert_fusion.3 = (bf16[1024,1376]{0,1:T(8,128)(2,1)}, bf16[1024,1376]{0,1:T(8,128)(2,1)}, bf16[1024,1376]{0,1:T(8,128)(2,1)S(1)}) fusion(f32[1024,1376]{0,1:T(8,128)} %fusion.31, f32[1024,1376]{0,1:T(8,128)} %fusion.34, bf16[1024,2048]{1,0:T(8,128)(2,1)S(1)} %copy-done.17, bf16[2048,1376]{0,1:T(8,128)(2,1)S(1)} %bitcast.74), kind=kOutput, calls=%fused_computation.8 | convolution fusion | flops 5792497664 | bytes 29556736 | tf_op jit(solution)/shard_map/dot_general | solution.py:351
  247.1 8.9 %fusion.35 = f32[1376,2048]{1,0:T(8,128)} fusion(bf16[1024,1376]{0,1:T(8,128)(2,1)S(1)} %get-tuple-element.271, bf16[1024,2048]{1,0:T(8,128)(2,1)S(1)} %copy-done.21), kind=kOutput, calls=%fused_computation.97 | convolution fusion | flops 5771362304 | bytes 18284544 | tf_op jit(solution)/shard_map/ca,cb->ab/dot_general | solution.py:359
  256.0 6.4 %all-reduce.8.cloned.1.call-done = f32[256,2048]{1,0:T(8,128)} async-done(((f32[256,2048]{1,0:T(8,128)}), f32[256,2048]{1,0:T(8,128)}) %all-reduce.8.cloned.1.call-update) | async-done | bytes 2097168 | tf_op jit(solution)/shard_map/psum | solution.py:160
  262.4 2.7 multiply_reduce_fusion.3
  265.9 2.8 multiply_reduce_fusion.1
  274.3 2.9 collective-permute-start.34
  278.4 9.4 %shard_map.207 = bf16[256,64]{1,0:T(8,128)(2,1)} custom-call(s32[256,4]{1,0:T(8,128)} %copy.28.col_ref, s32[24,256]{1,0:T(8,128)} %pad_add_fusion.row_ref, f32[256,512]{1,0:T(8,128)} %copy-done.26, f32[256,512]{1,0:T(8,128)} %bitcast.80, f32[256,640]{1,0:T(8,128)} %copy-done.32, f32[256,640]{1,0:T(8,128)} %copy-done.51, f32[256,640]{1,0:T(8,128)} %copy-done.41, ...), custom_call_target="tpu_custom_call" | custom-call | flops 2147483648 | bytes 6352896 | tf_op jit(solution)/shard_map/pallas_call | solution.py:299
  287.9 2.9 fusion.37
  293.0 8.8 %fusion.43 = f32[2048,1376]{0,1:T(8,128)} fusion(bf16[1024,1376]{0,1:T(8,128)(2,1)S(1)} %copy-done.61, bf16[1024,2048]{1,0:T(8,128)(2,1)S(1)} %copy-done.18), kind=kOutput, calls=%fused_computation.105 | convolution fusion | flops 5771362304 | bytes 18284544 | tf_op jit(solution)/shard_map/ca,cb->ab/dot_general | solution.py:359
  303.7 1.6 collective-permute-done.32.refs_18_
  305.4 2.8 slice_add_fusion.3
  308.7 2.2 collective-permute-start.37
  310.9 1.8 collective-permute-start.38
  312.7 11.3 %shard_map.208 = (bf16[256,64]{1,0:T(8,128)(2,1)}, bf16[256,512]{1,0:T(8,128)(2,1)}) custom-call(s32[256,4]{1,0:T(8,128)} %copy.28.col_ref, s32[24,256]{1,0:T(8,128)} %pad_add_fusion.row_ref, f32[256,640]{1,0:T(8,128)} %copy-done.32, f32[256,640]{1,0:T(8,128)} %copy-done.51, f32[256,640]{1,0:T(8,128)} %copy-done.41, f32[256,640]{1,0:T(8,128)} %copy-done.52, ...), custom_call_target="tpu_custom_call" | custom-call | flops 4294967296 | bytes 9891840 | tf_op jit(solution)/shard_map/pallas_call | solution.py:299
  324.1 3.7 fusion.40
  336.1 1.8 add.226
  341.6 3.6 collective-permute-start.40
  345.2 3.3 collective-permute-start.39
  348.5 6.3 %shard_map.209 = bf16[1024,2048]{1,0:T(8,128)(2,1)} custom-call(f32[1,2048]{1,0:T(1,128)} %bitcast.82, f32[256,2048]{1,0:T(8,128)} %collective-permute-done.23.refs_0_, f32[256,2048]{1,0:T(8,128)} %collective-permute-done.24.refs_1_, f32[128,2048]{1,0:T(8,128)} %collective-permute-done.21.refs_2_, f32[128,2048]{1,0:T(8,128)} %collective-permute-done.22.refs_3_, ...), custom_call_target="tpu_custom_call" | custom-call | bytes 12582912 | tf_op jit(solution)/shard_map/pallas_call | solution.py:326
  354.8 11.0 %fusion.42 = f32[1024,1376]{0,1:T(8,128)} fusion(bf16[1024,2048]{1,0:T(8,128)(2,1)} %shard_map.209, bf16[2048,1376]{0,1:T(8,128)(2,1)} %param.19), kind=kOutput, calls=%fused_computation.104 | convolution fusion | flops 5771362304 | bytes 15466496 | tf_op jit(solution)/shard_map/dot_general | solution.py:351
  365.8 2.0 collective-permute-done.40
  367.9 2.1 collective-permute-done.39
  373.1 4.8 collective-permute-start.43
  378.7 2.0 collective-permute-start.45
  380.7 14.0 %multiply_convert_fusion = (bf16[1024,1376]{0,1:T(8,128)(2,1)}, bf16[1024,1376]{0,1:T(8,128)(2,1)}, bf16[1024,1376]{0,1:T(8,128)(2,1)}) fusion(f32[1024,1376]{0,1:T(8,128)} %fusion.33, f32[1024,1376]{0,1:T(8,128)} %fusion.42, bf16[1024,2048]{1,0:T(8,128)(2,1)} %shard_map.209, bf16[2048,1376]{0,1:T(8,128)(2,1)S(1)} %bitcast.76), kind=kOutput, calls=%fused_computation.3 | convolution fusion | flops 5792497664 | bytes 29556736 | tf_op jit(solution)/shard_map/dot_general | solution.py:351
  394.7 10.5 %fusion.44 = f32[2048,1376]{0,1:T(8,128)} fusion(bf16[1024,1376]{0,1:T(8,128)(2,1)} %get-tuple-element.352, bf16[1024,2048]{1,0:T(8,128)(2,1)S(1)} %copy-done.19), kind=kOutput, calls=%fused_computation.106 | convolution fusion | flops 5771362304 | bytes 18284544 | tf_op jit(solution)/shard_map/ca,cb->ab/dot_general | solution.py:359
  408.0 1.6 collective-permute-start.48
  409.7 12.1 %convolution_add_fusion.2 = f32[1376,2048]{1,0:T(8,128)} fusion(f32[1376,2048]{1,0:T(8,128)} %fusion.35, bf16[1024,1376]{0,1:T(8,128)(2,1)S(1)} %copy-done.64, bf16[1024,2048]{1,0:T(8,128)(2,1)S(1)} %copy-done.16), kind=kOutput, calls=%fused_computation.2 | convolution fusion | flops 5774180352 | bytes 29556736 | tf_op jit(solution)/shard_map/ca,cb->ab/dot_general | solution.py:359
  422.0 13.3 %collective-permute-done.48 = f32[128,2048]{1,0:T(8,128)S(1)} collective-permute-done((f32[128,2048]{1,0:T(8,128)S(1)}, f32[128,2048]{1,0:T(8,128)S(1)}, u32[]{:S(2)}, u32[]{:S(2)}) %collective-permute-start.48) | collective-permute-done | bytes 1048608 | tf_op jit(solution)/shard_map/ppermute | solution.py:22
  441.9 11.7 %convolution_add_fusion.1 = f32[2048,1376]{0,1:T(8,128)} fusion(f32[2048,1376]{0,1:T(8,128)} %fusion.43, bf16[1024,1376]{0,1:T(8,128)(2,1)S(1)} %copy-done.63, bf16[1024,2048]{1,0:T(8,128)(2,1)S(1)} %copy-done.20), kind=kOutput, calls=%fused_computation.1 | convolution fusion | flops 5774180352 | bytes 29556736 | tf_op jit(solution)/shard_map/ca,cb->ab/dot_general | solution.py:359
  453.6 11.6 %convolution_add_fusion = f32[2048,1376]{0,1:T(8,128)} fusion(f32[2048,1376]{0,1:T(8,128)} %fusion.44, bf16[1024,1376]{0,1:T(8,128)(2,1)S(1)} %copy-done.62, bf16[1024,2048]{1,0:T(8,128)(2,1)S(1)} %copy-done.20), kind=kOutput, calls=%fused_computation | convolution fusion | flops 5774180352 | bytes 29556736 | tf_op jit(solution)/shard_map/ca,cb->ab/dot_general | solution.py:359
  468.0 2.7 multiply_add_fusion.2
  470.7 3.4 all-reduce.10.cloned.1.call-done
  474.7 1.9 copy.43
  476.6 1.9 copy.44
  478.5 4.8 copy.45
  483.3 2.1 copy.46
  (310 shorter events, 77.2 us)
Async XLA Ops:
  7.2 57.6 %copy-start = (bf16[512,2048]{1,0:T(8,128)(2,1)S(1)}, bf16[512,2048]{1,0:T(8,128)(2,1)}, u32[]{:S(2)}) copy-start(bf16[512,2048]{1,0:T(8,128)(2,1)} %param.17) | copy-start | bytes 6291460
  7.2 148.0 %all-reduce.6.cloned.1.call-start = ((), (), s32[]{:S(2)}) async-start(), calls=%async_computation | async-start | bytes 4194304 | tf_op jit(solution)/shard_map/psum | solution.py:160
  12.7 32.5 %copy-start.12 = (bf16[256,2048]{1,0:T(8,128)(2,1)S(1)}, bf16[256,2048]{1,0:T(8,128)(2,1)}, u32[]{:S(2)}) copy-start(bf16[256,2048]{1,0:T(8,128)(2,1)} %param.23) | copy-start | bytes 3145732
  13.2 36.0 %copy-start.5 = (bf16[256,2048]{1,0:T(8,128)(2,1)S(1)}, bf16[256,2048]{1,0:T(8,128)(2,1)}, u32[]{:S(2)}) copy-start(bf16[256,2048]{1,0:T(8,128)(2,1)} %param.12) | copy-start | bytes 3145732
  13.3 17.7 %collective-permute-start = (f32[256,640]{1,0:T(8,128)S(1)}, f32[256,640]{1,0:T(8,128)S(1)}, u32[]{:S(2)}, u32[]{:S(2)}) collective-permute-start(f32[256,640]{1,0:T(8,128)S(1)} %pad_maximum_fusion.1.refs_0_), channel_id=1, source_target_pairs={{0,8},{4,12},{8,0},{12,4},{16,24},{20,28},{24,16},{28,20},{1,9},{5... | collective-permute-start | bytes 1966088 | tf_op jit(solution)/shard_map/ppermute | solution.py:22
  16.3 16.2 %collective-permute-start.1 = (f32[256,640]{1,0:T(8,128)S(1)}, f32[256,640]{1,0:T(8,128)S(1)}, u32[]{:S(2)}, u32[]{:S(2)}) collective-permute-start(f32[256,640]{1,0:T(8,128)S(1)} %pad_maximum_fusion.1.refs_0_), channel_id=1, source_target_pairs={{0,16},{4,20},{8,24},{12,28},{16,0},{20,4},{24,8},{28,12},{1,17},{... | collective-permute-start | bytes 1966088 | tf_op jit(solution)/shard_map/ppermute | solution.py:22
  17.8 14.7 %collective-permute-start.2 = (f32[256,640]{1,0:T(8,128)S(1)}, f32[256,640]{1,0:T(8,128)S(1)}, u32[]{:S(2)}, u32[]{:S(2)}) collective-permute-start(f32[256,640]{1,0:T(8,128)S(1)} %pad_maximum_fusion.1.refs_0_), channel_id=1, source_target_pairs={{0,4},{4,0},{8,12},{12,8},{16,20},{20,16},{24,28},{28,24},{1,5},{5... | collective-permute-start | bytes 1966088 | tf_op jit(solution)/shard_map/ppermute | solution.py:22
  32.5 11.5 %collective-permute-start.5 = (f32[256,640]{1,0:T(8,128)S(1)}, f32[256,640]{1,0:T(8,128)S(1)}, u32[]{:S(2)}, u32[]{:S(2)}) collective-permute-start(f32[256,640]{1,0:T(8,128)S(1)} %collective-permute-done.refs_2_), channel_id=1, source_target_pairs={{0,4},{4,0},{8,12},{12,8},{16,20},{20,16},{24,28},{28,24},{1,5},{5... | collective-permute-start | bytes 1966088 | tf_op jit(solution)/shard_map/ppermute | solution.py:22
  32.6 11.5 %collective-permute-start.6 = (f32[256,640]{1,0:T(8,128)S(1)}, f32[256,640]{1,0:T(8,128)S(1)}, u32[]{:S(2)}, u32[]{:S(2)}) collective-permute-start(f32[256,640]{1,0:T(8,128)S(1)} %collective-permute-done.1.refs_4_), channel_id=1, source_target_pairs={{0,4},{4,0},{8,12},{12,8},{16,20},{20,16},{24,28},{28,24},{1,5},{5... | collective-permute-start | bytes 1966088 | tf_op jit(solution)/shard_map/ppermute | solution.py:22
  33.1 9.7 %collective-permute-start.3 = (f32[128,640]{1,0:T(8,128)S(1)}, f32[128,640]{1,0:T(8,128)S(1)}, u32[]{:S(2)}, u32[]{:S(2)}) collective-permute-start(f32[128,640]{1,0:T(8,128)S(1)} %slice.42), channel_id=1, source_target_pairs={{0,16},{4,20},{8,24},{12,28},{16,0},{20,4},{24,8},{28,12},{1,17},{... | collective-permute-start | bytes 983048 | tf_op jit(solution)/shard_map/ppermute | solution.py:22
  34.6 9.4 %collective-permute-start.4 = (f32[128,640]{1,0:T(8,128)S(1)}, f32[128,640]{1,0:T(8,128)S(1)}, u32[]{:S(2)}, u32[]{:S(2)}) collective-permute-start(f32[128,640]{1,0:T(8,128)S(1)} %slice.43), channel_id=1, source_target_pairs={{0,8},{4,12},{8,0},{12,4},{16,24},{20,28},{24,16},{28,20},{1,9},{5... | collective-permute-start | bytes 983048 | tf_op jit(solution)/shard_map/ppermute | solution.py:22
  44.1 2.7 collective-permute-start.7
  45.2 1.6 collective-permute-start.8
  47.5 48.4 %collective-permute-start.10 = (f32[256,2048]{1,0:T(8,128)}, f32[256,2048]{1,0:T(8,128)}, u32[]{:S(2)}, u32[]{:S(2)}) collective-permute-start(f32[256,2048]{1,0:T(8,128)} %convert_element_type.115.refs_0_), channel_id=1, source_target_pairs={{0,16},{4,20},{8,24},{12,28},{16,0},{20,4},{24,8},{28,12},{1,17},{... | collective-permute-start | bytes 6291464 | tf_op jit(solution)/shard_map/ppermute | solution.py:22
  48.2 47.6 %collective-permute-start.11 = (f32[256,2048]{1,0:T(8,128)}, f32[256,2048]{1,0:T(8,128)}, u32[]{:S(2)}, u32[]{:S(2)}) collective-permute-start(f32[256,2048]{1,0:T(8,128)} %convert_element_type.115.refs_0_), channel_id=1, source_target_pairs={{0,4},{4,0},{8,12},{12,8},{16,20},{20,16},{24,28},{28,24},{1,5},{5... | collective-permute-start | bytes 6291464 | tf_op jit(solution)/shard_map/ppermute | solution.py:22
  48.7 47.9 %collective-permute-start.9 = (f32[256,2048]{1,0:T(8,128)}, f32[256,2048]{1,0:T(8,128)}, u32[]{:S(2)}, u32[]{:S(2)}) collective-permute-start(f32[256,2048]{1,0:T(8,128)} %convert_element_type.115.refs_0_), channel_id=1, source_target_pairs={{0,8},{4,12},{8,0},{12,4},{16,24},{20,28},{24,16},{28,20},{1,9},{5... | collective-permute-start | bytes 6291464 | tf_op jit(solution)/shard_map/ppermute | solution.py:22
  55.5 113.0 %copy-start.36 = (f32[2048]{0:T(1024)}, f32[2048]{0:T(1024)S(1)}, u32[]{:S(2)}) copy-start(f32[2048]{0:T(1024)S(1)} %convert_element_type.125) | copy-start | bytes 24580
  67.8 194.7 %all-reduce.8.cloned.1.call-start = ((), (), s32[]{:S(2)}) async-start(), calls=%async_computation.1 | async-start | bytes 4194304 | tf_op jit(solution)/shard_map/psum | solution.py:160
  101.2 58.8 %collective-permute-start.14 = (f32[256,2048]{1,0:T(8,128)}, f32[256,2048]{1,0:T(8,128)}, u32[]{:S(2)}, u32[]{:S(2)}) collective-permute-start(f32[256,2048]{1,0:T(8,128)} %collective-permute-done.9.refs_2_), channel_id=1, source_target_pairs={{0,4},{4,0},{8,12},{12,8},{16,20},{20,16},{24,28},{28,24},{1,5},{5... | collective-permute-start | bytes 6291464 | tf_op jit(solution)/shard_map/ppermute | solution.py:22
  101.2 58.8 %collective-permute-start.15 = (f32[256,2048]{1,0:T(8,128)}, f32[256,2048]{1,0:T(8,128)}, u32[]{:S(2)}, u32[]{:S(2)}) collective-permute-start(f32[256,2048]{1,0:T(8,128)} %collective-permute-done.10.refs_3_), channel_id=1, source_target_pairs={{0,4},{4,0},{8,12},{12,8},{16,20},{20,16},{24,28},{28,24},{1,5},{5... | collective-permute-start | bytes 6291464 | tf_op jit(solution)/shard_map/ppermute | solution.py:22
  101.7 58.2 %collective-permute-start.12 = (f32[128,2048]{1,0:T(8,128)}, f32[128,2048]{1,0:T(8,128)}, u32[]{:S(2)}, u32[]{:S(2)}) collective-permute-start(f32[128,2048]{1,0:T(8,128)} %slice.48), channel_id=1, source_target_pairs={{0,16},{4,20},{8,24},{12,28},{16,0},{20,4},{24,8},{28,12},{1,17},{... | collective-permute-start | bytes 3145736 | tf_op jit(solution)/shard_map/ppermute | solution.py:22
  103.0 56.9 %collective-permute-start.13 = (f32[128,2048]{1,0:T(8,128)}, f32[128,2048]{1,0:T(8,128)}, u32[]{:S(2)}, u32[]{:S(2)}) collective-permute-start(f32[128,2048]{1,0:T(8,128)} %slice.49), channel_id=1, source_target_pairs={{0,8},{4,12},{8,0},{12,4},{16,24},{20,28},{24,16},{28,20},{1,9},{5... | collective-permute-start | bytes 3145736 | tf_op jit(solution)/shard_map/ppermute | solution.py:22
  159.9 18.7 %collective-permute-start.19 = (f32[128,2048]{1,0:T(8,128)}, f32[128,2048]{1,0:T(8,128)}, u32[]{:S(2)}, u32[]{:S(2)}) collective-permute-start(f32[128,2048]{1,0:T(8,128)} %collective-permute-done.12.refs_2_), channel_id=1, source_target_pairs={{0,4},{4,0},{8,12},{12,8},{16,20},{20,16},{24,28},{28,24},{1,5},{5... | collective-permute-start | bytes 3145736 | tf_op jit(solution)/shard_map/ppermute | solution.py:22
  160.0 18.6 %collective-permute-start.20 = (f32[128,2048]{1,0:T(8,128)}, f32[128,2048]{1,0:T(8,128)}, u32[]{:S(2)}, u32[]{:S(2)}) collective-permute-start(f32[128,2048]{1,0:T(8,128)} %collective-permute-done.13.refs_3_), channel_id=1, source_target_pairs={{0,4},{4,0},{8,12},{12,8},{16,20},{20,16},{24,28},{28,24},{1,5},{5... | collective-permute-start | bytes 3145736 | tf_op jit(solution)/shard_map/ppermute | solution.py:22
  160.5 47.9 %collective-permute-start.16 = (f32[256,2048]{1,0:T(8,128)}, f32[256,2048]{1,0:T(8,128)}, u32[]{:S(2)}, u32[]{:S(2)}) collective-permute-start(f32[256,2048]{1,0:T(8,128)} %broadcast_multiply_fusion.refs_0_), channel_id=1, source_target_pairs={{0,8},{4,12},{8,0},{12,4},{16,24},{20,28},{24,16},{28,20},{1,9},{5... | collective-permute-start | bytes 6291464 | tf_op jit(solution)/shard_map/ppermute | solution.py:22
  161.9 47.6 %collective-permute-start.17 = (f32[256,2048]{1,0:T(8,128)}, f32[256,2048]{1,0:T(8,128)}, u32[]{:S(2)}, u32[]{:S(2)}) collective-permute-start(f32[256,2048]{1,0:T(8,128)} %broadcast_multiply_fusion.refs_0_), channel_id=1, source_target_pairs={{0,16},{4,20},{8,24},{12,28},{16,0},{20,4},{24,8},{28,12},{1,17},{... | collective-permute-start | bytes 6291464 | tf_op jit(solution)/shard_map/ppermute | solution.py:22
  163.4 46.2 %collective-permute-start.18 = (f32[256,2048]{1,0:T(8,128)}, f32[256,2048]{1,0:T(8,128)}, u32[]{:S(2)}, u32[]{:S(2)}) collective-permute-start(f32[256,2048]{1,0:T(8,128)} %broadcast_multiply_fusion.refs_0_), channel_id=1, source_target_pairs={{0,4},{4,0},{8,12},{12,8},{16,20},{20,16},{24,28},{28,24},{1,5},{5... | collective-permute-start | bytes 6291464 | tf_op jit(solution)/shard_map/ppermute | solution.py:22
  178.5 295.6 %all-reduce.10.cloned.1.call-start = ((), (), s32[]{:S(2)}) async-start(), calls=%async_computation.2 | async-start | bytes 18874368 | tf_op jit(solution)/shard_map/psum | solution.py:559
  214.2 57.1 %collective-permute-start.23 = (f32[256,2048]{1,0:T(8,128)}, f32[256,2048]{1,0:T(8,128)}, u32[]{:S(2)}, u32[]{:S(2)}) collective-permute-start(f32[256,2048]{1,0:T(8,128)} %collective-permute-done.16.refs_2_), channel_id=1, source_target_pairs={{0,4},{4,0},{8,12},{12,8},{16,20},{20,16},{24,28},{28,24},{1,5},{5... | collective-permute-start | bytes 6291464 | tf_op jit(solution)/shard_map/ppermute | solution.py:22
  214.2 57.1 %collective-permute-start.24 = (f32[256,2048]{1,0:T(8,128)}, f32[256,2048]{1,0:T(8,128)}, u32[]{:S(2)}, u32[]{:S(2)}) collective-permute-start(f32[256,2048]{1,0:T(8,128)} %collective-permute-done.17.refs_3_), channel_id=1, source_target_pairs={{0,4},{4,0},{8,12},{12,8},{16,20},{20,16},{24,28},{28,24},{1,5},{5... | collective-permute-start | bytes 6291464 | tf_op jit(solution)/shard_map/ppermute | solution.py:22
  214.7 56.6 %collective-permute-start.21 = (f32[128,2048]{1,0:T(8,128)}, f32[128,2048]{1,0:T(8,128)}, u32[]{:S(2)}, u32[]{:S(2)}) collective-permute-start(f32[128,2048]{1,0:T(8,128)} %slice.50), channel_id=1, source_target_pairs={{0,16},{4,20},{8,24},{12,28},{16,0},{20,4},{24,8},{28,12},{1,17},{... | collective-permute-start | bytes 3145736 | tf_op jit(solution)/shard_map/ppermute | solution.py:22
  216.2 55.1 %collective-permute-start.22 = (f32[128,2048]{1,0:T(8,128)}, f32[128,2048]{1,0:T(8,128)}, u32[]{:S(2)}, u32[]{:S(2)}) collective-permute-start(f32[128,2048]{1,0:T(8,128)} %slice.51), channel_id=1, source_target_pairs={{0,8},{4,12},{8,0},{12,4},{16,24},{20,28},{24,16},{28,20},{1,9},{5... | collective-permute-start | bytes 3145736 | tf_op jit(solution)/shard_map/ppermute | solution.py:22
  271.3 19.4 %collective-permute-start.25 = (f32[264,512]{1,0:T(8,128)S(1)}, f32[264,512]{1,0:T(8,128)S(1)}, u32[]{:S(2)}, u32[]{:S(2)}) collective-permute-start(f32[264,512]{1,0:T(8,128)S(1)} %select_maximum_fusion.refs_10_), channel_id=1, source_target_pairs={{0,8},{4,12},{8,0},{12,4},{16,24},{20,28},{24,16},{28,20},{1,9},{5... | collective-permute-start | bytes 1622024 | tf_op jit(solution)/shard_map/ppermute | solution.py:22
  272.8 17.9 %collective-permute-start.26 = (f32[264,512]{1,0:T(8,128)S(1)}, f32[264,512]{1,0:T(8,128)S(1)}, u32[]{:S(2)}, u32[]{:S(2)}) collective-permute-start(f32[264,512]{1,0:T(8,128)S(1)} %select_maximum_fusion.refs_10_), channel_id=1, source_target_pairs={{0,16},{4,20},{8,24},{12,28},{16,0},{20,4},{24,8},{28,12},{1,17},{... | collective-permute-start | bytes 1622024 | tf_op jit(solution)/shard_map/ppermute | solution.py:22
  274.3 16.4 %collective-permute-start.27 = (f32[264,512]{1,0:T(8,128)S(1)}, f32[264,512]{1,0:T(8,128)S(1)}, u32[]{:S(2)}, u32[]{:S(2)}) collective-permute-start(f32[264,512]{1,0:T(8,128)S(1)} %select_maximum_fusion.refs_10_), channel_id=1, source_target_pairs={{0,4},{4,0},{8,12},{12,8},{16,20},{20,16},{24,28},{28,24},{1,5},{5... | collective-permute-start | bytes 1622024 | tf_op jit(solution)/shard_map/ppermute | solution.py:22
  274.3 29.4 %collective-permute-start.34 = (f32[128,2048]{1,0:T(8,128)}, f32[128,2048]{1,0:T(8,128)}, u32[]{:S(2)}, u32[]{:S(2)}) collective-permute-start(f32[128,2048]{1,0:T(8,128)} %split.16), channel_id=1, source_target_pairs={{0,1},{3,2},{4,5},{7,6},{8,9},{11,10},{12,13},{15,14},{16,17},{19,... | collective-permute-start | bytes 3145736 | tf_op jit(solution)/shard_map/ppermute | solution.py:22
  290.8 11.0 %collective-permute-start.30 = (f32[264,512]{1,0:T(8,128)S(1)}, f32[264,512]{1,0:T(8,128)S(1)}, u32[]{:S(2)}, u32[]{:S(2)}) collective-permute-start(f32[264,512]{1,0:T(8,128)S(1)} %collective-permute-done.25.refs_12_), channel_id=1, source_target_pairs={{0,4},{4,0},{8,12},{12,8},{16,20},{20,16},{24,28},{28,24},{1,5},{5... | collective-permute-start | bytes 1622024 | tf_op jit(solution)/shard_map/ppermute | solution.py:22
  291.1 10.7 %collective-permute-start.31 = (f32[264,512]{1,0:T(8,128)S(1)}, f32[264,512]{1,0:T(8,128)S(1)}, u32[]{:S(2)}, u32[]{:S(2)}) collective-permute-start(f32[264,512]{1,0:T(8,128)S(1)} %collective-permute-done.26.refs_14_), channel_id=1, source_target_pairs={{0,4},{4,0},{8,12},{12,8},{16,20},{20,16},{24,28},{28,24},{1,5},{5... | collective-permute-start | bytes 1622024 | tf_op jit(solution)/shard_map/ppermute | solution.py:22
  291.4 10.4 %collective-permute-start.29 = (f32[136,512]{1,0:T(8,128)S(1)}, f32[136,512]{1,0:T(8,128)}, u32[]{:S(2)}, u32[]{:S(2)}) collective-permute-start(f32[136,512]{1,0:T(8,128)S(1)} %slice.53), channel_id=1, source_target_pairs={{0,8},{4,12},{8,0},{12,4},{16,24},{20,28},{24,16},{28,20},{1,9},{5... | collective-permute-start | bytes 835592 | tf_op jit(solution)/shard_map/ppermute | solution.py:22
  292.0 9.8 %collective-permute-start.28 = (f32[128,512]{1,0:T(8,128)S(1)}, f32[128,512]{1,0:T(8,128)}, u32[]{:S(2)}, u32[]{:S(2)}) collective-permute-start(f32[128,512]{1,0:T(8,128)S(1)} %slice.52), channel_id=1, source_target_pairs={{0,16},{4,20},{8,24},{12,28},{16,0},{20,4},{24,8},{28,12},{1,17},{... | collective-permute-start | bytes 786440 | tf_op jit(solution)/shard_map/ppermute | solution.py:22
  302.7 2.7 collective-permute-start.33
  303.5 1.9 collective-permute-start.32
  308.2 26.3 %collective-permute-start.35 = (f32[128,2048]{1,0:T(8,128)}, f32[128,2048]{1,0:T(8,128)}, u32[]{:S(2)}, u32[]{:S(2)}) collective-permute-start(f32[128,2048]{1,0:T(8,128)} %collective-permute-done.21.refs_2_), channel_id=1, source_target_pairs={{0,4},{4,0},{8,12},{12,8},{16,20},{20,16},{24,28},{28,24},{1,5},{5... | collective-permute-start | bytes 3145736 | tf_op jit(solution)/shard_map/ppermute | solution.py:22
  308.4 26.1 %collective-permute-start.36 = (f32[128,2048]{1,0:T(8,128)}, f32[128,2048]{1,0:T(8,128)}, u32[]{:S(2)}, u32[]{:S(2)}) collective-permute-start(f32[128,2048]{1,0:T(8,128)} %collective-permute-done.22.refs_3_), channel_id=1, source_target_pairs={{0,4},{4,0},{8,12},{12,8},{16,20},{20,16},{24,28},{28,24},{1,5},{5... | collective-permute-start | bytes 3145736 | tf_op jit(solution)/shard_map/ppermute | solution.py:22
  308.7 27.4 %collective-permute-start.37 = (f32[128,2048]{1,0:T(8,128)}, f32[128,2048]{1,0:T(8,128)}, u32[]{:S(2)}, u32[]{:S(2)}) collective-permute-start(f32[128,2048]{1,0:T(8,128)} %get-tuple-element.308), channel_id=1, source_target_pairs={{0,1},{3,2},{4,5},{7,6},{8,9},{11,10},{12,13},{15,14},{16,17},{19,... | collective-permute-start | bytes 3145736 | tf_op jit(solution)/shard_map/ppermute | solution.py:22
  310.9 25.1 %collective-permute-start.38 = (f32[128,2048]{1,0:T(8,128)}, f32[128,2048]{1,0:T(8,128)}, u32[]{:S(2)}, u32[]{:S(2)}) collective-permute-start(f32[128,2048]{1,0:T(8,128)} %get-tuple-element.309), channel_id=1, source_target_pairs={{1,2},{2,1},{5,6},{6,5},{9,10},{10,9},{13,14},{14,13},{17,18},{18,... | collective-permute-start | bytes 3145736 | tf_op jit(solution)/shard_map/ppermute | solution.py:22
  339.6 28.3 %collective-permute-start.41 = (f32[128,2048]{1,0:T(8,128)S(1)}, f32[128,2048]{1,0:T(8,128)S(1)}, u32[]{:S(2)}, u32[]{:S(2)}) collective-permute-start(f32[128,2048]{1,0:T(8,128)S(1)} %slice_add_fusion.2), channel_id=1, source_target_pairs={{1,2},{2,1},{5,6},{6,5},{9,10},{10,9},{13,14},{14,13},{17,18},{18,... | collective-permute-start | bytes 3145736 | tf_op jit(solution)/shard_map/ppermute | solution.py:22
  340.3 27.5 %collective-permute-start.42 = (f32[128,2048]{1,0:T(8,128)S(1)}, f32[128,2048]{1,0:T(8,128)}, u32[]{:S(2)}, u32[]{:S(2)}) collective-permute-start(f32[128,2048]{1,0:T(8,128)S(1)} %add.226), channel_id=1, source_target_pairs={{1,0},{2,3},{5,4},{6,7},{9,8},{10,11},{13,12},{14,15},{17,16},{18,... | collective-permute-start | bytes 3145736 | tf_op jit(solution)/shard_map/ppermute | solution.py:22
  341.6 26.2 %collective-permute-start.40 = (f32[2,2048]{1,0:T(2,128)S(1)}, f32[2,2048]{1,0:T(2,128)S(1)}, u32[]{:S(2)}, u32[]{:S(2)}) collective-permute-start(f32[2,2048]{1,0:T(2,128)S(1)} %pad_maximum_fusion.2), channel_id=1, source_target_pairs={{0,1},{1,0},{2,3},{3,2},{4,5},{5,4},{6,7},{7,6},{8,9},{9,8},{10,11... | collective-permute-start | bytes 49160 | tf_op jit(solution)/shard_map/ppermute | solution.py:22
  345.2 24.7 %collective-permute-start.39 = (f32[128,2048]{1,0:T(8,128)}, f32[128,2048]{1,0:T(8,128)}, u32[]{:S(2)}, u32[]{:S(2)}) collective-permute-start(f32[128,2048]{1,0:T(8,128)} %split.18), channel_id=1, source_target_pairs={{0,1},{3,2},{4,5},{7,6},{8,9},{11,10},{12,13},{15,14},{16,17},{19,... | collective-permute-start | bytes 3145736 | tf_op jit(solution)/shard_map/ppermute | solution.py:22
  348.5 32.2 %slice-start.4 = ((s8[5636096]{0:T(1024)(128)(4,1)}), s8[1441792]{0:T(1024)(128)(4,1)S(1)}, s32[]{:S(2)}) async-start(s8[5636096]{0:T(1024)(128)(4,1)} %bitcast.75), calls=%async_computation.7 | async-start | bytes 2883584
  354.8 25.9 %slice-start.5 = ((s8[5636096]{0:T(1024)(128)(4,1)}), s8[4194304]{0:T(1024)(128)(4,1)S(1)}, s32[]{:S(2)}) async-start(s8[5636096]{0:T(1024)(128)(4,1)} %bitcast.75), calls=%async_computation.8 | async-start | bytes 8388608
  371.5 23.2 %copy-start.19 = (bf16[1024,2048]{1,0:T(8,128)(2,1)S(1)}, bf16[1024,2048]{1,0:T(8,128)(2,1)}, u32[]{:S(2)}) copy-start(bf16[1024,2048]{1,0:T(8,128)(2,1)} %shard_map.206) | copy-start | bytes 12582916
  371.5 35.2 %collective-permute-start.46 = (f32[128,2048]{1,0:T(8,128)S(1)}, f32[128,2048]{1,0:T(8,128)S(1)}, u32[]{:S(2)}, u32[]{:S(2)}) collective-permute-start(f32[128,2048]{1,0:T(8,128)S(1)} %add.229), channel_id=1, source_target_pairs={{1,0},{2,3},{5,4},{6,7},{9,8},{10,11},{13,12},{14,15},{17,16},{18,... | collective-permute-start | bytes 3145736 | tf_op jit(solution)/shard_map/ppermute | solution.py:22
  373.1 33.7 %collective-permute-start.43 = (f32[128,2048]{1,0:T(8,128)S(1)}, f32[128,2048]{1,0:T(8,128)S(1)}, u32[]{:S(2)}, u32[]{:S(2)}) collective-permute-start(f32[128,2048]{1,0:T(8,128)S(1)} %get-tuple-element.345), channel_id=1, source_target_pairs={{0,1},{3,2},{4,5},{7,6},{8,9},{11,10},{12,13},{15,14},{16,17},{19,... | collective-permute-start | bytes 3145736 | tf_op jit(solution)/shard_map/ppermute | solution.py:22
  377.9 28.8 %collective-permute-start.44 = (f32[128,2048]{1,0:T(8,128)S(1)}, f32[128,2048]{1,0:T(8,128)S(1)}, u32[]{:S(2)}, u32[]{:S(2)}) collective-permute-start(f32[128,2048]{1,0:T(8,128)S(1)} %get-tuple-element.346), channel_id=1, source_target_pairs={{1,2},{2,1},{5,6},{6,5},{9,10},{10,9},{13,14},{14,13},{17,18},{18,... | collective-permute-start | bytes 3145736 | tf_op jit(solution)/shard_map/ppermute | solution.py:22
  378.7 28.1 %collective-permute-start.45 = (f32[2,2048]{1,0:T(2,128)S(1)}, f32[2,2048]{1,0:T(2,128)S(1)}, u32[]{:S(2)}, u32[]{:S(2)}) collective-permute-start(f32[2,2048]{1,0:T(2,128)S(1)} %fusion.19), channel_id=1, source_target_pairs={{0,2},{1,3},{2,0},{3,1},{4,6},{5,7},{6,4},{7,5},{8,10},{9,11},{10,... | collective-permute-start | bytes 49160 | tf_op jit(solution)/shard_map/ppermute | solution.py:22
  407.1 14.9 %collective-permute-start.49 = (f32[2,2048]{1,0:T(2,128)S(1)}, f32[2,2048]{1,0:T(2,128)S(1)}, u32[]{:S(2)}, u32[]{:S(2)}) collective-permute-start(f32[2,2048]{1,0:T(2,128)S(1)} %fusion.101), channel_id=1, source_target_pairs={{0,4},{4,0},{8,12},{12,8},{16,20},{20,16},{24,28},{28,24},{1,5},{5... | collective-permute-start | bytes 49160 | tf_op jit(solution)/shard_map/ppermute | solution.py:22
  407.2 14.9 %collective-permute-start.47 = (f32[128,2048]{1,0:T(8,128)S(1)}, f32[128,2048]{1,0:T(8,128)S(1)}, u32[]{:S(2)}, u32[]{:S(2)}) collective-permute-start(f32[128,2048]{1,0:T(8,128)S(1)} %slice_add_fusion), channel_id=1, source_target_pairs={{1,2},{2,1},{5,6},{6,5},{9,10},{10,9},{13,14},{14,13},{17,18},{18,... | collective-permute-start | bytes 3145736 | tf_op jit(solution)/shard_map/ppermute | solution.py:22
  408.0 27.3 %collective-permute-start.48 = (f32[128,2048]{1,0:T(8,128)S(1)}, f32[128,2048]{1,0:T(8,128)S(1)}, u32[]{:S(2)}, u32[]{:S(2)}) collective-permute-start(f32[128,2048]{1,0:T(8,128)S(1)} %add.233), channel_id=1, source_target_pairs={{1,0},{2,3},{5,4},{6,7},{9,8},{10,11},{13,12},{14,15},{17,16},{18,... | collective-permute-start | bytes 3145736 | tf_op jit(solution)/shard_map/ppermute | solution.py:22
  435.5 29.9 %collective-permute-start.50 = (f32[128,2048]{1,0:T(8,128)S(1)}, f32[128,2048]{1,0:T(8,128)S(1)}, u32[]{:S(2)}, u32[]{:S(2)}) collective-permute-start(f32[128,2048]{1,0:T(8,128)S(1)} %add.236), channel_id=1, source_target_pairs={{1,0},{2,3},{5,4},{6,7},{9,8},{10,11},{13,12},{14,15},{17,16},{18,... | collective-permute-start | bytes 3145736 | tf_op jit(solution)/shard_map/ppermute | solution.py:22
  437.1 28.3 %collective-permute-start.51 = (f32[2,2048]{1,0:T(2,128)S(1)}, f32[2,2048]{1,0:T(2,128)S(1)}, u32[]{:S(2)}, u32[]{:S(2)}) collective-permute-start(f32[2,2048]{1,0:T(2,128)S(1)} %add.237), channel_id=1, source_target_pairs={{0,8},{4,12},{8,0},{12,4},{16,24},{20,28},{24,16},{28,20},{1,9},{5... | collective-permute-start | bytes 49160 | tf_op jit(solution)/shard_map/ppermute | solution.py:22
  438.1 27.3 %collective-permute-start.52 = (f32[2,2048]{1,0:T(2,128)S(1)}, f32[2,2048]{1,0:T(2,128)S(1)}, u32[]{:S(2)}, u32[]{:S(2)}) collective-permute-start(f32[2,2048]{1,0:T(2,128)S(1)} %add.237), channel_id=1, source_target_pairs={{0,16},{4,20},{8,24},{12,28},{16,0},{20,4},{24,8},{28,12},{1,17},{... | collective-permute-start | bytes 49160 | tf_op jit(solution)/shard_map/ppermute | solution.py:22
  439.5 25.9 %collective-permute-start.53 = (f32[2,2048]{1,0:T(2,128)S(1)}, f32[2,2048]{1,0:T(2,128)S(1)}, u32[]{:S(2)}, u32[]{:S(2)}) collective-permute-start(f32[2,2048]{1,0:T(2,128)S(1)} %add.237), channel_id=1, source_target_pairs={{0,24},{4,28},{8,16},{12,20},{16,8},{20,12},{24,0},{28,4},{1,25},{... | collective-permute-start | bytes 49160 | tf_op jit(solution)/shard_map/ppermute | solution.py:22
  (66 other events, 396.7 us)
Sparse Core Ops, SparseCore 0:
  67.9 87.2 all-reduce.5
  178.7 83.7 all-reduce.7
  334.6 139.4 all-reduce.9

commit v6 on v5

--- a/solution.py
+++ b/solution.py
@@ -4,7 +4,6 @@
 import jax.numpy as jnp
 from jax import lax
 from jax.experimental import pallas as pl
-from jax.experimental.layout import Layout, with_layout_constraint
 from jax.experimental.pallas import tpu as pltpu
 from jax.sharding import PartitionSpec as P
 
@@ -246,7 +245,7 @@
             first = 2 * qk + head * DV
             value = read(slots[slot], None, slice(first, first + DV)).astype(bf16)
             grad = dot_t(numer_ref[:, head * DV : (head + 1) * DV].astype(bf16), value)
-            grad = grad + denom_ref[:, head * DV : head * DV + 1]
+            grad = grad + denom_ref[:, head : head + 1]
             grad = jnp.where(allowed, grad * near, 0.0).astype(bf16)
             sums[head] = sums[head] + dot_n(grad, keys)
     total = jnp.zeros((rows, 2 * qk), f32)
@@ -388,25 +387,27 @@
     qk, vw = heads * FEAT, heads * DV
     blk_index, blk_count = lax.axis_index("blk"), lax.axis_size("blk")
 
-    ends = [doc_lengths[0]]
-    for doc in range(1, doc_lengths.shape[0]):
-        ends.append(ends[-1] + doc_lengths[doc])
-
-    def layout(positions):
-        docs = sum((positions >= end).astype(jnp.int32) for end in ends[:-1])
-        valid = positions < ends[-1]
-        return docs, valid, jnp.where(valid, docs, -1)
-
-    own_pos = blk_index * rows + jnp.arange(rows, dtype=jnp.int32)
-    own_docs, own_valid, own_key_docs = layout(own_pos)
-    columns = jnp.stack([own_pos, own_docs, own_valid.astype(jnp.int32), own_key_docs], axis=1)
-    slot_blocks = blk_index ^ jnp.arange(blk_count, dtype=jnp.int32)
-    slot_pos = slot_blocks[:, None] * rows + jnp.arange(rows, dtype=jnp.int32)[None, :]
-    slot_docs, _, slot_key_docs = layout(slot_pos)
-    lines = jnp.concatenate([slot_pos, slot_key_docs, slot_docs])
+    def layout(doc_lengths, cotangent):
+        ends = [doc_lengths[0]]
+        for doc in range(1, doc_lengths.shape[0]):
+            ends.append(ends[-1] + doc_lengths[doc])
+
+        def documents(positions):
+            docs = sum((positions >= end).astype(jnp.int32) for end in ends[:-1])
+            valid = positions < ends[-1]
+            return docs, valid, jnp.where(valid, docs, -1)
+
+        own_pos = blk_index * rows + jnp.arange(rows, dtype=jnp.int32)
+        own_docs, own_valid, own_key_docs = documents(own_pos)
+        columns = [own_pos, own_docs, own_valid.astype(jnp.int32), own_key_docs]
+        slot_blocks = blk_index ^ jnp.arange(blk_count, dtype=jnp.int32)
+        slot_pos = slot_blocks[:, None] * rows + jnp.arange(rows, dtype=jnp.int32)[None, :]
+        slot_docs, _, slot_key_docs = documents(slot_pos)
+        lines = jnp.concatenate([slot_pos, slot_key_docs, slot_docs])
+        return jnp.stack(columns, axis=1), lines, cotangent.astype(f32)
 
     gain_one, gain_two = gain_attn.astype(f32), gain_mlp.astype(f32)
-    token_wide, cot_wide = tokens.astype(f32), cotangent.astype(f32)
+    token_wide = tokens.astype(f32)
     inv_in = lax.rsqrt(jnp.mean(token_wide * token_wide, axis=-1, keepdims=True) + epsilon)
     normed_in = (token_wide * inv_in * gain_one).astype(bf16)
     qkv_own = jnp.concatenate(
@@ -414,7 +415,9 @@
     )
     convoy = Convoy()
     qkv_slots = {}
-    convoy.finish(Chain(gather_steps(qkv_own, qkv_slots)))
+    qkv_chain = Chain(gather_steps(qkv_own, qkv_slots))
+    columns, lines, cot_wide = convoy.wave([qkv_chain], layout, doc_lengths, cotangent)
+    convoy.finish(qkv_chain)
     qkv = [qkv_slots[slot] for slot in range(blk_count)]
     shape = tuple(len(slot) for slot in qkv)
     qkv_parts = [part for slot in qkv for part in slot]
@@ -513,23 +516,23 @@
     grad_slots = {}
     grads = Chain(gather_steps(sent, grad_slots))
 
-    def query_work(numer_grad, denom_grad, out_lin_grad):
+    def query_work(numer_grad, denom_grad):
         (query_lin_grad,) = whole_call(
             functools.partial(query_kernel, heads, shape),
             (jax.ShapeDtypeStruct((rows, qk), bf16),),
             columns,
             lines,
             numer_grad,
-            jnp.repeat(denom_grad, DV, axis=1),
+            denom_grad,
             *qkv_parts,
             flops=cost,
         )
-        return query_lin_grad, t_mm(attended, after(out_lin_grad, query_lin_grad))
+        return query_lin_grad
 
     convoy.launch(grads, mlp)
-    query_lin_grad, out_part = convoy.work(query_work, numer_grad, denom_grad, out_lin_grad)
+    query_lin_grad = convoy.work(query_work, numer_grad, denom_grad)
     convoy.land(grads)
-    gate_part = convoy.wave([grads], t_mm, mid_a, gate_grad_a)
+    out_part = convoy.wave([grads], t_mm, attended, out_lin_grad)
     convoy.launch(grads)
     convoy.land(grads, mlp)
     convoy.finish(grads)
@@ -548,7 +551,6 @@
         )
         lin_grads = (query_lin_grad, key_lin_grad, value_grad)
         parts = [t_mm(normed_in, grad) for grad in lin_grads]
-        parts[2] = with_layout_constraint(parts[2], Layout(major_to_minor=(0, 1)))
         query_lin_grad, key_lin_grad, value_grad = after(lin_grads, parts)
         in_part = mm_t(query_lin_grad, w_query) + mm_t(key_lin_grad, w_key)
         return in_part + mm_t(value_grad, w_value), parts
@@ -584,7 +586,12 @@
     hidden_b, gate_grad_b, up_grad_b, up_part = convoy.wave(
         chains, second_work, mid_b, gate_b, hidden_grad_b
     )
-    down_w_grad = convoy.wave(chains, lambda x, y: down_a + t_mm(x, y), hidden_b, cot_b)
+
+    def third_work(hidden_b, gate_grad_a):
+        down_w_grad = down_a + t_mm(hidden_b, cot_b)
+        return down_w_grad, t_mm(mid_a, after(gate_grad_a, down_w_grad))
+
+    down_w_grad, gate_part = convoy.wave(chains, third_work, hidden_b, gate_grad_a)
     convoy.finish(mlp)
 
     def gate_last(gate_grad_b, mlp_sum):

time: 502 us -> 506 us (level)
  waiting for transfers between devices: 116 us -> 103 us
  other arithmetic: 34.2 us -> 45.6 us
    ppermute x54, waiting for transfers between devices: 72.3 us -> 66.8 us  [hop(): return lax.ppermute(value, axis, way)]
    unnamed x151 -> x142, local copies, waits for them, and re-layouts: 25.6 us -> 23.6 us
  transfers between devices with their start and end apart: 57 -> 57, of which waited for: 15 -> 19; matrix products, arithmetic and copies ran while one was open for 44% -> 46% of each run, Pallas kernels for 11% -> 11%
where the time goes in v6:
time: 506 us; the launch traced here: 497 us
  matrix products  177 us (35%)
  waiting for transfers between devices  103 us (20%)
  starting transfers between devices  58.4 us (12%)
  Pallas kernels  53.7 us (11%)
  other arithmetic  45.6 us (9%)
  local copies, waits for them, and re-layouts  41.9 us (8%)
  between operations  17.6 us (3%)
    dot_general x10, matrix products, t_mm(): return jnp.einsum('ca,cb->ab', left, right, preferred_element_type=f32)  71.9 us
    dot_general x11, matrix products, mm(): return jnp.dot(left, right, preferred_element_type=f32)  69.6 us
    ppermute x54, waiting for transfers between devices, hop(): return lax.ppermute(value, axis, way)  66.8 us
    ppermute x54, starting transfers between devices, hop(): return lax.ppermute(value, axis, way)  58.3 us
    psum x2, waiting for transfers between devices, sum_head(): return lax.psum(value, 'head')  36.1 us
    dot_general x9, matrix products, mm_t(): return jnp.einsum('ac,bc->ab', left, right, preferred_element_type=f32)  35.2 us
    pallas_call x3, Pallas kernels, whole_call(): pl.pallas_call(body, out_shape=outs, in_specs=[pl.BlockSpec(memory_space=...  28.6 us
    pallas_call x4, Pallas kernels, join_rounded(): pl.pallas_call(functools.partial(join_kernel, tuple((len(slot) for slot i...  25.2 us
  transfers between devices with their start and end apart: 57, of which 19 were waited for; matrix products, arithmetic and copies ran while one was open for 46% of the time, Pallas kernels for 11%

profile of v6, /device:TPU:0, one launch (start us, length us, event | category | flops | bytes accessed | tf_op | source)
XLA Modules:
  0.0 496.9 jit_solution(17344115852852425325)
XLA Ops:
  14.1 2.9 collective-permute-start
  21.8 2.8 convert_element_type.117.refs_0_
  26.6 5.5 %collective-permute-done.refs_2_ = f32[256,640]{1,0:T(8,128)} collective-permute-done((f32[256,640]{1,0:T(8,128)}, f32[256,640]{1,0:T(8,128)}, u32[]{:S(2)}, u32[]{:S(2)}) %collective-permute-start) | collective-permute-done | bytes 655392 | tf_op jit(solution)/shard_map/ppermute | solution.py:21
  38.2 7.6 %collective-permute-done.3.refs_6_ = f32[128,640]{1,0:T(8,128)S(1)} collective-permute-done((f32[128,640]{1,0:T(8,128)S(1)}, f32[128,640]{1,0:T(8,128)S(1)}, u32[]{:S(2)}, u32[]{:S(2)}) %collective-permute-start.3) | collective-permute-done | bytes 327712 | tf_op jit(solution)/shard_map/ppermute | solution.py:21
  51.8 2.8 convert_element_type.114
  54.6 7.9 %shard_map.203 = (bf16[256,512]{1,0:T(8,128)(2,1)}, f32[256,512]{1,0:T(8,128)}, f32[256,512]{1,0:T(8,128)}) custom-call(s32[256,4]{1,0:T(8,128)} %copy.28.col_ref, s32[24,256]{1,0:T(8,128)} %pad_add_fusion.row_ref, f32[256,640]{1,0:T(8,128)} %pad_maximum_fusion.1.refs_0_, f32[256,640]{1,0:T(8,128)} %collective-permute-done.2.refs_1_, ...), custom_call_target="tpu_custom_call" | custom-call | flops 2147483648 | bytes 6582272 | tf_op jit(solution)/shard_map/pallas_call | solution.py:298
  62.5 3.0 fusion.29
  65.6 5.7 %fusion.30 = f32[256,1376]{0,1:T(8,128)} fusion(bf16[256,2048]{1,0:T(8,128)(2,1)} %param.23, bf16[1376,2048]{1,0:T(8,128)(2,1)} %param.21), kind=kOutput, calls=%fused_computation.91 | convolution fusion | flops 1442840576 | bytes 8093696 | tf_op jit(solution)/shard_map/ac,bc->ab/dot_general | solution.py:354
  71.3 26.2 %collective-permute-done.10.refs_3_ = f32[256,2048]{1,0:T(8,128)} collective-permute-done((f32[256,2048]{1,0:T(8,128)}, f32[256,2048]{1,0:T(8,128)}, u32[]{:S(2)}, u32[]{:S(2)}) %collective-permute-start.10) | collective-permute-done | bytes 2097184 | tf_op jit(solution)/shard_map/ppermute | solution.py:21
  98.9 2.3 slice.48
  101.1 2.3 slice.49
  106.2 6.3 %shard_map.204 = bf16[1024,2048]{1,0:T(8,128)(2,1)} custom-call(f32[1,2048]{1,0:T(1,128)} %broadcast_12_scale_ref.2.scale_ref, f32[256,2048]{1,0:T(8,128)} %convert_element_type.117.refs_0_, f32[256,2048]{1,0:T(8,128)} %collective-permute-done.11.refs_1_, f32[256,2048]{1,0:T(8,128)} %collective-permute-done.9.refs_2_, ...), custom_call_target="tpu_custom_call" | custom-call | bytes 12582912 | tf_op jit(solution)/shard_map/pallas_call | solution.py:325
  112.4 11.0 %fusion.31 = f32[1024,1376]{0,1:T(8,128)} fusion(bf16[1024,2048]{1,0:T(8,128)(2,1)} %shard_map.204, bf16[1376,2048]{1,0:T(8,128)(2,1)} %param.21), kind=kOutput, calls=%fused_computation.92 | convolution fusion | flops 5771362304 | bytes 15466496 | tf_op jit(solution)/shard_map/ac,bc->ab/dot_general | solution.py:354
  123.4 29.6 %all-reduce.6.cloned.1.call-done = f32[256,2048]{1,0:T(8,128)} async-done(((f32[256,2048]{1,0:T(8,128)}), f32[256,2048]{1,0:T(8,128)}) %all-reduce.6.cloned.1.call-update) | async-done | bytes 2097168 | tf_op jit(solution)/shard_map/psum | solution.py:159
  153.0 2.5 multiply_reduce_fusion.4
  161.2 5.1 %fusion.8 = f32[256,1376]{0,1:T(8,128)S(1)} fusion(bf16[2048,1376]{0,1:T(8,128)(2,1)} %param.19, f32[256,2048]{1,0:T(8,128)} %broadcast_multiply_fusion.refs_0_, f32[2048]{0:T(1024)S(1)} %convert_element_type.125), kind=kOutput, calls=%fused_computation.48 | convolution fusion | flops 1443889152 | bytes 9150464 | tf_op jit(solution)/shard_map/dot_general | solution.py:350
  166.4 4.5 multiply_convert_fusion.10
  170.9 2.2 fusion.3
  173.1 3.2 convolution_add_fusion.5
  176.4 6.0 %fusion.32 = f32[256,2048]{1,0:T(8,128)} fusion(bf16[256,1376]{0,1:T(8,128)(2,1)} %get-tuple-element.245, bf16[1376,2048]{1,0:T(8,128)(2,1)} %param.21), kind=kOutput, calls=%fused_computation.93 | convolution fusion | flops 1442840576 | bytes 8437760 | tf_op jit(solution)/shard_map/dot_general | solution.py:350
  182.4 6.4 %shard_map.205 = bf16[1024,2048]{1,0:T(8,128)(2,1)} custom-call(f32[1,2048]{1,0:T(1,128)} %broadcast_12_scale_ref.2.scale_ref, f32[256,2048]{1,0:T(8,128)} %collective-permute-done.14.refs_0_, f32[256,2048]{1,0:T(8,128)} %collective-permute-done.15.refs_1_, f32[128,2048]{1,0:T(8,128)} %collective-permute-done.12.refs_2_, ...), custom_call_target="tpu_custom_call" | custom-call | bytes 12582912 | tf_op jit(solution)/shard_map/pallas_call | solution.py:325
  188.7 10.9 %fusion.33 = f32[1024,1376]{0,1:T(8,128)} fusion(bf16[1024,2048]{1,0:T(8,128)(2,1)} %shard_map.205, bf16[1376,2048]{1,0:T(8,128)(2,1)} %param.21), kind=kOutput, calls=%fused_computation.94 | convolution fusion | flops 5771362304 | bytes 15466496 | tf_op jit(solution)/shard_map/ac,bc->ab/dot_general | solution.py:354
  199.6 6.6 %collective-permute-done.16.refs_2_ = f32[256,2048]{1,0:T(8,128)} collective-permute-done((f32[256,2048]{1,0:T(8,128)}, f32[256,2048]{1,0:T(8,128)}, u32[]{:S(2)}, u32[]{:S(2)}) %collective-permute-start.16) | collective-permute-done | bytes 2097184 | tf_op jit(solution)/shard_map/ppermute | solution.py:21
  207.4 2.3 slice.50
  209.7 2.3 slice.51
  214.6 6.2 %shard_map.206 = bf16[1024,2048]{1,0:T(8,128)(2,1)} custom-call(f32[1,2048]{1,0:T(1,128)} %bitcast.75, f32[256,2048]{1,0:T(8,128)} %broadcast_multiply_fusion.refs_0_, f32[256,2048]{1,0:T(8,128)} %collective-permute-done.18.refs_1_, f32[256,2048]{1,0:T(8,128)} %collective-permute-done.16.refs_2_, f32[256,2048]{1,0:T(8,128)} %collective-permute-done.17.refs_3_), custom_call_target="tpu_custom_call" | custom-call | bytes 12582912 | tf_op jit(solution)/shard_map/pallas_call | solution.py:325
  220.8 11.3 %fusion.34 = f32[1024,1376]{0,1:T(8,128)} fusion(bf16[1024,2048]{1,0:T(8,128)(2,1)} %shard_map.206, bf16[2048,1376]{0,1:T(8,128)(2,1)} %param.19), kind=kOutput, calls=%fused_computation.95 | convolution fusion | flops 5771362304 | bytes 15466496 | tf_op jit(solution)/shard_map/dot_general | solution.py:350
  232.1 12.8 %multiply_convert_fusion.3 = (bf16[1024,1376]{0,1:T(8,128)(2,1)}, bf16[1024,1376]{0,1:T(8,128)(2,1)}, bf16[1024,1376]{0,1:T(8,128)(2,1)S(1)}) fusion(f32[1024,1376]{0,1:T(8,128)} %fusion.31, f32[1024,1376]{0,1:T(8,128)} %fusion.34, bf16[1024,2048]{1,0:T(8,128)(2,1)S(1)} %copy-done.14, bf16[2048,1376]{0,1:T(8,128)(2,1)S(1)} %bitcast.70), kind=kOutput, calls=%fused_computation.8 | convolution fusion | flops 5792497664 | bytes 29556736 | tf_op jit(solution)/shard_map/dot_general | solution.py:350
  244.9 8.9 %fusion.35 = f32[1376,2048]{1,0:T(8,128)} fusion(bf16[1024,1376]{0,1:T(8,128)(2,1)S(1)} %get-tuple-element.274, bf16[1024,2048]{1,0:T(8,128)(2,1)S(1)} %copy-done.17), kind=kOutput, calls=%fused_computation.96 | convolution fusion | flops 5771362304 | bytes 18284544 | tf_op jit(solution)/shard_map/ca,cb->ab/dot_general | solution.py:358
  253.8 6.5 %all-reduce.8.cloned.1.call-done = f32[256,2048]{1,0:T(8,128)} async-done(((f32[256,2048]{1,0:T(8,128)}), f32[256,2048]{1,0:T(8,128)}) %all-reduce.8.cloned.1.call-update) | async-done | bytes 2097168 | tf_op jit(solution)/shard_map/psum | solution.py:159
  260.3 2.7 multiply_reduce_fusion.3
  263.8 2.8 multiply_reduce_fusion.1
  269.4 2.2 reshape.103
  271.5 2.0 reduce_sum.66
  280.5 3.1 collective-permute-start.34
  283.6 9.3 %shard_map.207 = bf16[256,64]{1,0:T(8,128)(2,1)} custom-call(s32[256,4]{1,0:T(8,128)} %copy.28.col_ref, s32[24,256]{1,0:T(8,128)} %pad_add_fusion.row_ref, f32[256,512]{1,0:T(8,128)} %get-tuple-element.287.numer_ref, f32[256,4]{1,0:T(8,128)} %get-tuple-element.288.denom_ref, f32[256,640]{1,0:T(8,128)} %pad_maximum_fusion.1.refs_0_, ...), custom_call_target="tpu_custom_call" | custom-call | flops 2147483648 | bytes 5832704 | tf_op jit(solution)/shard_map/pallas_call | solution.py:298
  294.7 2.7 fusion.37
  297.5 5.0 collective-permute-done.28.refs_16_
  304.2 1.7 collective-permute-done.34
  306.0 2.8 slice_add_fusion.3
  309.4 5.2 %collective-permute-start.37 = (f32[128,2048]{1,0:T(8,128)}, f32[128,2048]{1,0:T(8,128)}, u32[]{:S(2)}, u32[]{:S(2)}) collective-permute-start(f32[128,2048]{1,0:T(8,128)} %get-tuple-element.309), channel_id=1, source_target_pairs={{0,1},{3,2},{4,5},{7,6},{8,9},{11,10},{12,13},{15,14},{16,17},{19,... | collective-permute-start | bytes 3145736 | tf_op jit(solution)/shard_map/ppermute | solution.py:21
  314.5 1.9 collective-permute-start.38
  316.4 11.4 %shard_map.208 = (bf16[256,64]{1,0:T(8,128)(2,1)}, bf16[256,512]{1,0:T(8,128)(2,1)}) custom-call(s32[256,4]{1,0:T(8,128)} %copy.28.col_ref, s32[24,256]{1,0:T(8,128)} %pad_add_fusion.row_ref, f32[256,640]{1,0:T(8,128)} %pad_maximum_fusion.1.refs_0_, f32[256,640]{1,0:T(8,128)} %collective-permute-done.2.refs_1_, f32[256,640]{1,0:T(8,128)} %collective-permute-done.refs_2_, ...), custom_call_target="tpu_custom_call" | custom-call | flops 4294967296 | bytes 9891840 | tf_op jit(solution)/shard_map/pallas_call | solution.py:298
  327.8 3.7 fusion.40
  339.8 1.8 add.226
  345.6 3.6 collective-permute-start.40
  349.2 3.3 collective-permute-start.39
  352.5 6.4 %shard_map.209 = bf16[1024,2048]{1,0:T(8,128)(2,1)} custom-call(f32[1,2048]{1,0:T(1,128)} %bitcast.76, f32[256,2048]{1,0:T(8,128)} %collective-permute-done.23.refs_0_, f32[256,2048]{1,0:T(8,128)} %collective-permute-done.24.refs_1_, f32[128,2048]{1,0:T(8,128)} %collective-permute-done.21.refs_2_, f32[128,2048]{1,0:T(8,128)} %collective-permute-done.22.refs_3_, ...), custom_call_target="tpu_custom_call" | custom-call | bytes 12582912 | tf_op jit(solution)/shard_map/pallas_call | solution.py:325
  358.9 11.3 %fusion.42 = f32[1024,1376]{0,1:T(8,128)} fusion(bf16[1024,2048]{1,0:T(8,128)(2,1)} %shard_map.209, bf16[2048,1376]{0,1:T(8,128)(2,1)} %param.19), kind=kOutput, calls=%fused_computation.103 | convolution fusion | flops 5771362304 | bytes 15466496 | tf_op jit(solution)/shard_map/dot_general | solution.py:350
  377.9 4.8 collective-permute-start.43
  383.5 2.0 collective-permute-start.45
  385.5 14.2 %multiply_convert_fusion = (bf16[1024,1376]{0,1:T(8,128)(2,1)}, bf16[1024,1376]{0,1:T(8,128)(2,1)}, bf16[1024,1376]{0,1:T(8,128)(2,1)}) fusion(f32[1024,1376]{0,1:T(8,128)} %fusion.33, f32[1024,1376]{0,1:T(8,128)} %fusion.42, bf16[1024,2048]{1,0:T(8,128)(2,1)} %shard_map.209, bf16[2048,1376]{0,1:T(8,128)(2,1)S(1)} %bitcast.72), kind=kOutput, calls=%fused_computation.3 | convolution fusion | flops 5792497664 | bytes 29556736 | tf_op jit(solution)/shard_map/dot_general | solution.py:350
  399.7 10.5 %fusion.43 = f32[2048,1376]{0,1:T(8,128)} fusion(bf16[1024,1376]{0,1:T(8,128)(2,1)} %get-tuple-element.353, bf16[1024,2048]{1,0:T(8,128)(2,1)S(1)} %copy-done.15), kind=kOutput, calls=%fused_computation.104 | convolution fusion | flops 5771362304 | bytes 18284544 | tf_op jit(solution)/shard_map/ca,cb->ab/dot_general | solution.py:358
  417.7 12.2 %convolution_add_fusion.2 = f32[1376,2048]{1,0:T(8,128)} fusion(f32[1376,2048]{1,0:T(8,128)} %fusion.35, bf16[1024,1376]{0,1:T(8,128)(2,1)} %get-tuple-element.361, bf16[1024,2048]{1,0:T(8,128)(2,1)S(1)} %copy-done.13), kind=kOutput, calls=%fused_computation.2 | convolution fusion | flops 5774180352 | bytes 29556736 | tf_op jit(solution)/shard_map/ca,cb->ab/dot_general | solution.py:358
  429.9 8.7 %fusion.44 = f32[2048,1376]{0,1:T(8,128)} fusion(bf16[1024,1376]{0,1:T(8,128)(2,1)S(1)} %copy-done.58, bf16[1024,2048]{1,0:T(8,128)(2,1)S(1)} %copy-done.15), kind=kOutput, calls=%fused_computation.105 | convolution fusion | flops 5771362304 | bytes 18284544 | tf_op jit(solution)/shard_map/ca,cb->ab/dot_general | solution.py:358
  438.9 4.6 collective-permute-done.48
  446.0 2.8 collective-permute-start.53
  450.1 11.5 %convolution_add_fusion.1 = f32[2048,1376]{0,1:T(8,128)} fusion(f32[2048,1376]{0,1:T(8,128)} %fusion.44, bf16[1024,1376]{0,1:T(8,128)(2,1)S(1)} %copy-done.60, bf16[1024,2048]{1,0:T(8,128)(2,1)S(1)} %copy-done.16), kind=kOutput, calls=%fused_computation.1 | convolution fusion | flops 5774180352 | bytes 29556736 | tf_op jit(solution)/shard_map/ca,cb->ab/dot_general | solution.py:358
  461.6 11.4 %convolution_add_fusion = f32[2048,1376]{0,1:T(8,128)} fusion(f32[2048,1376]{0,1:T(8,128)} %fusion.43, bf16[1024,1376]{0,1:T(8,128)(2,1)S(1)} %copy-done.59, bf16[1024,2048]{1,0:T(8,128)(2,1)S(1)} %copy-done.16), kind=kOutput, calls=%fused_computation | convolution fusion | flops 5774180352 | bytes 29556736 | tf_op jit(solution)/shard_map/ca,cb->ab/dot_general | solution.py:358
  475.2 2.7 multiply_add_fusion.2
  478.5 1.9 copy.40
  480.4 1.9 copy.41
  482.3 4.8 copy.42
  487.1 2.1 copy.43
  (300 shorter events, 86.7 us)
Async XLA Ops:
  7.2 55.4 %copy-start = (bf16[512,2048]{1,0:T(8,128)(2,1)S(1)}, bf16[512,2048]{1,0:T(8,128)(2,1)}, u32[]{:S(2)}) copy-start(bf16[512,2048]{1,0:T(8,128)(2,1)} %param.17) | copy-start | bytes 6291460
  7.2 145.8 %all-reduce.6.cloned.1.call-start = ((), (), s32[]{:S(2)}) async-start(), calls=%async_computation | async-start | bytes 4194304 | tf_op jit(solution)/shard_map/psum | solution.py:159
  14.1 18.0 %collective-permute-start = (f32[256,640]{1,0:T(8,128)}, f32[256,640]{1,0:T(8,128)}, u32[]{:S(2)}, u32[]{:S(2)}) collective-permute-start(f32[256,640]{1,0:T(8,128)} %pad_maximum_fusion.1.refs_0_), channel_id=1, source_target_pairs={{0,8},{4,12},{8,0},{12,4},{16,24},{20,28},{24,16},{28,20},{1,9},{5... | collective-permute-start | bytes 1966088 | tf_op jit(solution)/shard_map/ppermute | solution.py:21
  17.0 16.5 %collective-permute-start.1 = (f32[256,640]{1,0:T(8,128)}, f32[256,640]{1,0:T(8,128)}, u32[]{:S(2)}, u32[]{:S(2)}) collective-permute-start(f32[256,640]{1,0:T(8,128)} %pad_maximum_fusion.1.refs_0_), channel_id=1, source_target_pairs={{0,16},{4,20},{8,24},{12,28},{16,0},{20,4},{24,8},{28,12},{1,17},{... | collective-permute-start | bytes 1966088 | tf_op jit(solution)/shard_map/ppermute | solution.py:21
  18.6 15.0 %collective-permute-start.2 = (f32[256,640]{1,0:T(8,128)}, f32[256,640]{1,0:T(8,128)}, u32[]{:S(2)}, u32[]{:S(2)}) collective-permute-start(f32[256,640]{1,0:T(8,128)} %pad_maximum_fusion.1.refs_0_), channel_id=1, source_target_pairs={{0,4},{4,0},{8,12},{12,8},{16,20},{20,16},{24,28},{28,24},{1,5},{5... | collective-permute-start | bytes 1966088 | tf_op jit(solution)/shard_map/ppermute | solution.py:21
  34.6 20.1 %copy-start.50 = (bf16[2048]{0:T(1024)(128)(2,1)S(1)}, bf16[2048]{0:T(1024)(128)(2,1)}, u32[]{:S(2)}) copy-start(bf16[2048]{0:T(1024)(128)(2,1)} %param.18) | copy-start | bytes 12292
  35.6 11.5 %collective-permute-start.5 = (f32[256,640]{1,0:T(8,128)}, f32[256,640]{1,0:T(8,128)}, u32[]{:S(2)}, u32[]{:S(2)}) collective-permute-start(f32[256,640]{1,0:T(8,128)} %collective-permute-done.refs_2_), channel_id=1, source_target_pairs={{0,4},{4,0},{8,12},{12,8},{16,20},{20,16},{24,28},{28,24},{1,5},{5... | collective-permute-start | bytes 1966088 | tf_op jit(solution)/shard_map/ppermute | solution.py:21
  35.7 11.4 %collective-permute-start.6 = (f32[256,640]{1,0:T(8,128)}, f32[256,640]{1,0:T(8,128)}, u32[]{:S(2)}, u32[]{:S(2)}) collective-permute-start(f32[256,640]{1,0:T(8,128)} %collective-permute-done.1.refs_4_), channel_id=1, source_target_pairs={{0,4},{4,0},{8,12},{12,8},{16,20},{20,16},{24,28},{28,24},{1,5},{5... | collective-permute-start | bytes 1966088 | tf_op jit(solution)/shard_map/ppermute | solution.py:21
  36.2 9.7 %collective-permute-start.3 = (f32[128,640]{1,0:T(8,128)S(1)}, f32[128,640]{1,0:T(8,128)S(1)}, u32[]{:S(2)}, u32[]{:S(2)}) collective-permute-start(f32[128,640]{1,0:T(8,128)S(1)} %slice.46), channel_id=1, source_target_pairs={{0,16},{4,20},{8,24},{12,28},{16,0},{20,4},{24,8},{28,12},{1,17},{... | collective-permute-start | bytes 983048 | tf_op jit(solution)/shard_map/ppermute | solution.py:21
  37.7 9.4 %collective-permute-start.4 = (f32[128,640]{1,0:T(8,128)S(1)}, f32[128,640]{1,0:T(8,128)S(1)}, u32[]{:S(2)}, u32[]{:S(2)}) collective-permute-start(f32[128,640]{1,0:T(8,128)S(1)} %slice.47), channel_id=1, source_target_pairs={{0,8},{4,12},{8,0},{12,4},{16,24},{20,28},{24,16},{28,20},{1,9},{5... | collective-permute-start | bytes 983048 | tf_op jit(solution)/shard_map/ppermute | solution.py:21
  47.1 1.7 collective-permute-start.7
  47.2 2.1 collective-permute-start.8
  49.5 48.0 %collective-permute-start.10 = (f32[256,2048]{1,0:T(8,128)}, f32[256,2048]{1,0:T(8,128)}, u32[]{:S(2)}, u32[]{:S(2)}) collective-permute-start(f32[256,2048]{1,0:T(8,128)} %convert_element_type.117.refs_0_), channel_id=1, source_target_pairs={{0,16},{4,20},{8,24},{12,28},{16,0},{20,4},{24,8},{28,12},{1,17},{... | collective-permute-start | bytes 6291464 | tf_op jit(solution)/shard_map/ppermute | solution.py:21
  50.5 47.0 %collective-permute-start.11 = (f32[256,2048]{1,0:T(8,128)}, f32[256,2048]{1,0:T(8,128)}, u32[]{:S(2)}, u32[]{:S(2)}) collective-permute-start(f32[256,2048]{1,0:T(8,128)} %convert_element_type.117.refs_0_), channel_id=1, source_target_pairs={{0,4},{4,0},{8,12},{12,8},{16,20},{20,16},{24,28},{28,24},{1,5},{5... | collective-permute-start | bytes 6291464 | tf_op jit(solution)/shard_map/ppermute | solution.py:21
  50.5 48.4 %collective-permute-start.9 = (f32[256,2048]{1,0:T(8,128)}, f32[256,2048]{1,0:T(8,128)}, u32[]{:S(2)}, u32[]{:S(2)}) collective-permute-start(f32[256,2048]{1,0:T(8,128)} %convert_element_type.117.refs_0_), channel_id=1, source_target_pairs={{0,8},{4,12},{8,0},{12,4},{16,24},{20,28},{24,16},{28,20},{1,9},{5... | collective-permute-start | bytes 6291464 | tf_op jit(solution)/shard_map/ppermute | solution.py:21
  54.6 111.7 %copy-start.34 = (f32[2048]{0:T(1024)}, f32[2048]{0:T(1024)S(1)}, u32[]{:S(2)}) copy-start(f32[2048]{0:T(1024)S(1)} %convert_element_type.125) | copy-start | bytes 24580
  65.5 194.8 %all-reduce.8.cloned.1.call-start = ((), (), s32[]{:S(2)}) async-start(), calls=%async_computation.1 | async-start | bytes 4194304 | tf_op jit(solution)/shard_map/psum | solution.py:159
  103.5 54.2 %collective-permute-start.14 = (f32[256,2048]{1,0:T(8,128)}, f32[256,2048]{1,0:T(8,128)}, u32[]{:S(2)}, u32[]{:S(2)}) collective-permute-start(f32[256,2048]{1,0:T(8,128)} %collective-permute-done.9.refs_2_), channel_id=1, source_target_pairs={{0,4},{4,0},{8,12},{12,8},{16,20},{20,16},{24,28},{28,24},{1,5},{5... | collective-permute-start | bytes 6291464 | tf_op jit(solution)/shard_map/ppermute | solution.py:21
  103.5 54.2 %collective-permute-start.15 = (f32[256,2048]{1,0:T(8,128)}, f32[256,2048]{1,0:T(8,128)}, u32[]{:S(2)}, u32[]{:S(2)}) collective-permute-start(f32[256,2048]{1,0:T(8,128)} %collective-permute-done.10.refs_3_), channel_id=1, source_target_pairs={{0,4},{4,0},{8,12},{12,8},{16,20},{20,16},{24,28},{28,24},{1,5},{5... | collective-permute-start | bytes 6291464 | tf_op jit(solution)/shard_map/ppermute | solution.py:21
  104.0 53.7 %collective-permute-start.12 = (f32[128,2048]{1,0:T(8,128)}, f32[128,2048]{1,0:T(8,128)}, u32[]{:S(2)}, u32[]{:S(2)}) collective-permute-start(f32[128,2048]{1,0:T(8,128)} %slice.48), channel_id=1, source_target_pairs={{0,16},{4,20},{8,24},{12,28},{16,0},{20,4},{24,8},{28,12},{1,17},{... | collective-permute-start | bytes 3145736 | tf_op jit(solution)/shard_map/ppermute | solution.py:21
  105.0 52.6 %collective-permute-start.13 = (f32[128,2048]{1,0:T(8,128)}, f32[128,2048]{1,0:T(8,128)}, u32[]{:S(2)}, u32[]{:S(2)}) collective-permute-start(f32[128,2048]{1,0:T(8,128)} %slice.49), channel_id=1, source_target_pairs={{0,8},{4,12},{8,0},{12,4},{16,24},{20,28},{24,16},{28,20},{1,9},{5... | collective-permute-start | bytes 3145736 | tf_op jit(solution)/shard_map/ppermute | solution.py:21
  155.6 107.4 %copy-start.45 = (f32[256]{0:T(256)}, f32[256]{0:T(256)S(1)}, u32[]{:S(2)}) copy-start(f32[256]{0:T(256)S(1)} %add_rsqrt_fusion) | copy-start | bytes 3076
  157.7 18.7 %collective-permute-start.19 = (f32[128,2048]{1,0:T(8,128)}, f32[128,2048]{1,0:T(8,128)}, u32[]{:S(2)}, u32[]{:S(2)}) collective-permute-start(f32[128,2048]{1,0:T(8,128)} %collective-permute-done.12.refs_2_), channel_id=1, source_target_pairs={{0,4},{4,0},{8,12},{12,8},{16,20},{20,16},{24,28},{28,24},{1,5},{5... | collective-permute-start | bytes 3145736 | tf_op jit(solution)/shard_map/ppermute | solution.py:21
  157.8 18.6 %collective-permute-start.20 = (f32[128,2048]{1,0:T(8,128)}, f32[128,2048]{1,0:T(8,128)}, u32[]{:S(2)}, u32[]{:S(2)}) collective-permute-start(f32[128,2048]{1,0:T(8,128)} %collective-permute-done.13.refs_3_), channel_id=1, source_target_pairs={{0,4},{4,0},{8,12},{12,8},{16,20},{20,16},{24,28},{28,24},{1,5},{5... | collective-permute-start | bytes 3145736 | tf_op jit(solution)/shard_map/ppermute | solution.py:21
  158.3 47.9 %collective-permute-start.16 = (f32[256,2048]{1,0:T(8,128)}, f32[256,2048]{1,0:T(8,128)}, u32[]{:S(2)}, u32[]{:S(2)}) collective-permute-start(f32[256,2048]{1,0:T(8,128)} %broadcast_multiply_fusion.refs_0_), channel_id=1, source_target_pairs={{0,8},{4,12},{8,0},{12,4},{16,24},{20,28},{24,16},{28,20},{1,9},{5... | collective-permute-start | bytes 6291464 | tf_op jit(solution)/shard_map/ppermute | solution.py:21
  159.8 47.6 %collective-permute-start.17 = (f32[256,2048]{1,0:T(8,128)}, f32[256,2048]{1,0:T(8,128)}, u32[]{:S(2)}, u32[]{:S(2)}) collective-permute-start(f32[256,2048]{1,0:T(8,128)} %broadcast_multiply_fusion.refs_0_), channel_id=1, source_target_pairs={{0,16},{4,20},{8,24},{12,28},{16,0},{20,4},{24,8},{28,12},{1,17},{... | collective-permute-start | bytes 6291464 | tf_op jit(solution)/shard_map/ppermute | solution.py:21
  161.2 46.2 %collective-permute-start.18 = (f32[256,2048]{1,0:T(8,128)}, f32[256,2048]{1,0:T(8,128)}, u32[]{:S(2)}, u32[]{:S(2)}) collective-permute-start(f32[256,2048]{1,0:T(8,128)} %broadcast_multiply_fusion.refs_0_), channel_id=1, source_target_pairs={{0,4},{4,0},{8,12},{12,8},{16,20},{20,16},{24,28},{28,24},{1,5},{5... | collective-permute-start | bytes 6291464 | tf_op jit(solution)/shard_map/ppermute | solution.py:21
  176.3 301.6 %all-reduce.10.cloned.1.call-start = ((), (), s32[]{:S(2)}) async-start(), calls=%async_computation.2 | async-start | bytes 18874368 | tf_op jit(solution)/shard_map/psum | solution.py:561
  212.0 64.3 %collective-permute-start.23 = (f32[256,2048]{1,0:T(8,128)}, f32[256,2048]{1,0:T(8,128)}, u32[]{:S(2)}, u32[]{:S(2)}) collective-permute-start(f32[256,2048]{1,0:T(8,128)} %collective-permute-done.16.refs_2_), channel_id=1, source_target_pairs={{0,4},{4,0},{8,12},{12,8},{16,20},{20,16},{24,28},{28,24},{1,5},{5... | collective-permute-start | bytes 6291464 | tf_op jit(solution)/shard_map/ppermute | solution.py:21
  212.0 64.4 %collective-permute-start.24 = (f32[256,2048]{1,0:T(8,128)}, f32[256,2048]{1,0:T(8,128)}, u32[]{:S(2)}, u32[]{:S(2)}) collective-permute-start(f32[256,2048]{1,0:T(8,128)} %collective-permute-done.17.refs_3_), channel_id=1, source_target_pairs={{0,4},{4,0},{8,12},{12,8},{16,20},{20,16},{24,28},{28,24},{1,5},{5... | collective-permute-start | bytes 6291464 | tf_op jit(solution)/shard_map/ppermute | solution.py:21
  212.5 63.8 %collective-permute-start.21 = (f32[128,2048]{1,0:T(8,128)}, f32[128,2048]{1,0:T(8,128)}, u32[]{:S(2)}, u32[]{:S(2)}) collective-permute-start(f32[128,2048]{1,0:T(8,128)} %slice.50), channel_id=1, source_target_pairs={{0,16},{4,20},{8,24},{12,28},{16,0},{20,4},{24,8},{28,12},{1,17},{... | collective-permute-start | bytes 3145736 | tf_op jit(solution)/shard_map/ppermute | solution.py:21
  214.0 62.4 %collective-permute-start.22 = (f32[128,2048]{1,0:T(8,128)}, f32[128,2048]{1,0:T(8,128)}, u32[]{:S(2)}, u32[]{:S(2)}) collective-permute-start(f32[128,2048]{1,0:T(8,128)} %slice.51), channel_id=1, source_target_pairs={{0,8},{4,12},{8,0},{12,4},{16,24},{20,28},{24,16},{28,20},{1,9},{5... | collective-permute-start | bytes 3145736 | tf_op jit(solution)/shard_map/ppermute | solution.py:21
  276.4 16.6 %collective-permute-start.25 = (f32[264,512]{1,0:T(8,128)S(1)}, f32[264,512]{1,0:T(8,128)S(1)}, u32[]{:S(2)}, u32[]{:S(2)}) collective-permute-start(f32[264,512]{1,0:T(8,128)S(1)} %select_maximum_fusion.refs_10_), channel_id=1, source_target_pairs={{0,8},{4,12},{8,0},{12,4},{16,24},{20,28},{24,16},{28,20},{1,9},{5... | collective-permute-start | bytes 1622024 | tf_op jit(solution)/shard_map/ppermute | solution.py:21
  277.9 15.1 %collective-permute-start.26 = (f32[264,512]{1,0:T(8,128)S(1)}, f32[264,512]{1,0:T(8,128)S(1)}, u32[]{:S(2)}, u32[]{:S(2)}) collective-permute-start(f32[264,512]{1,0:T(8,128)S(1)} %select_maximum_fusion.refs_10_), channel_id=1, source_target_pairs={{0,16},{4,20},{8,24},{12,28},{16,0},{20,4},{24,8},{28,12},{1,17},{... | collective-permute-start | bytes 1622024 | tf_op jit(solution)/shard_map/ppermute | solution.py:21
  279.4 13.6 %collective-permute-start.27 = (f32[264,512]{1,0:T(8,128)S(1)}, f32[264,512]{1,0:T(8,128)S(1)}, u32[]{:S(2)}, u32[]{:S(2)}) collective-permute-start(f32[264,512]{1,0:T(8,128)S(1)} %select_maximum_fusion.refs_10_), channel_id=1, source_target_pairs={{0,4},{4,0},{8,12},{12,8},{16,20},{20,16},{24,28},{28,24},{1,5},{5... | collective-permute-start | bytes 1622024 | tf_op jit(solution)/shard_map/ppermute | solution.py:21
  280.5 25.4 %collective-permute-start.34 = (f32[128,2048]{1,0:T(8,128)}, f32[128,2048]{1,0:T(8,128)}, u32[]{:S(2)}, u32[]{:S(2)}) collective-permute-start(f32[128,2048]{1,0:T(8,128)} %split.16), channel_id=1, source_target_pairs={{0,1},{3,2},{4,5},{7,6},{8,9},{11,10},{12,13},{15,14},{16,17},{19,... | collective-permute-start | bytes 3145736 | tf_op jit(solution)/shard_map/ppermute | solution.py:21
  293.1 9.5 %collective-permute-start.30 = (f32[264,512]{1,0:T(8,128)S(1)}, f32[264,512]{1,0:T(8,128)S(1)}, u32[]{:S(2)}, u32[]{:S(2)}) collective-permute-start(f32[264,512]{1,0:T(8,128)S(1)} %collective-permute-done.25.refs_12_), channel_id=1, source_target_pairs={{0,4},{4,0},{8,12},{12,8},{16,20},{20,16},{24,28},{28,24},{1,5},{5... | collective-permute-start | bytes 1622024 | tf_op jit(solution)/shard_map/ppermute | solution.py:21
  293.4 9.2 %collective-permute-start.31 = (f32[264,512]{1,0:T(8,128)S(1)}, f32[264,512]{1,0:T(8,128)S(1)}, u32[]{:S(2)}, u32[]{:S(2)}) collective-permute-start(f32[264,512]{1,0:T(8,128)S(1)} %collective-permute-done.26.refs_14_), channel_id=1, source_target_pairs={{0,4},{4,0},{8,12},{12,8},{16,20},{20,16},{24,28},{28,24},{1,5},{5... | collective-permute-start | bytes 1622024 | tf_op jit(solution)/shard_map/ppermute | solution.py:21
  293.6 8.9 %collective-permute-start.29 = (f32[136,512]{1,0:T(8,128)S(1)}, f32[136,512]{1,0:T(8,128)}, u32[]{:S(2)}, u32[]{:S(2)}) collective-permute-start(f32[136,512]{1,0:T(8,128)S(1)} %slice.53), channel_id=1, source_target_pairs={{0,8},{4,12},{8,0},{12,4},{16,24},{20,28},{24,16},{28,20},{1,9},{5... | collective-permute-start | bytes 835592 | tf_op jit(solution)/shard_map/ppermute | solution.py:21
  294.2 8.3 %collective-permute-start.28 = (f32[128,512]{1,0:T(8,128)S(1)}, f32[128,512]{1,0:T(8,128)}, u32[]{:S(2)}, u32[]{:S(2)}) collective-permute-start(f32[128,512]{1,0:T(8,128)S(1)} %slice.52), channel_id=1, source_target_pairs={{0,16},{4,20},{8,24},{12,28},{16,0},{20,4},{24,8},{28,12},{1,17},{... | collective-permute-start | bytes 786440 | tf_op jit(solution)/shard_map/ppermute | solution.py:21
  303.3 2.7 collective-permute-start.33
  304.2 1.9 collective-permute-start.32
  308.8 29.3 %collective-permute-start.35 = (f32[128,2048]{1,0:T(8,128)}, f32[128,2048]{1,0:T(8,128)}, u32[]{:S(2)}, u32[]{:S(2)}) collective-permute-start(f32[128,2048]{1,0:T(8,128)} %collective-permute-done.21.refs_2_), channel_id=1, source_target_pairs={{0,4},{4,0},{8,12},{12,8},{16,20},{20,16},{24,28},{28,24},{1,5},{5... | collective-permute-start | bytes 3145736 | tf_op jit(solution)/shard_map/ppermute | solution.py:21
  309.0 29.2 %collective-permute-start.36 = (f32[128,2048]{1,0:T(8,128)}, f32[128,2048]{1,0:T(8,128)}, u32[]{:S(2)}, u32[]{:S(2)}) collective-permute-start(f32[128,2048]{1,0:T(8,128)} %collective-permute-done.22.refs_3_), channel_id=1, source_target_pairs={{0,4},{4,0},{8,12},{12,8},{16,20},{20,16},{24,28},{28,24},{1,5},{5... | collective-permute-start | bytes 3145736 | tf_op jit(solution)/shard_map/ppermute | solution.py:21
  309.4 30.4 %collective-permute-start.37 = (f32[128,2048]{1,0:T(8,128)}, f32[128,2048]{1,0:T(8,128)}, u32[]{:S(2)}, u32[]{:S(2)}) collective-permute-start(f32[128,2048]{1,0:T(8,128)} %get-tuple-element.309), channel_id=1, source_target_pairs={{0,1},{3,2},{4,5},{7,6},{8,9},{11,10},{12,13},{15,14},{16,17},{19,... | collective-permute-start | bytes 3145736 | tf_op jit(solution)/shard_map/ppermute | solution.py:21
  314.5 25.3 %collective-permute-start.38 = (f32[128,2048]{1,0:T(8,128)}, f32[128,2048]{1,0:T(8,128)}, u32[]{:S(2)}, u32[]{:S(2)}) collective-permute-start(f32[128,2048]{1,0:T(8,128)} %get-tuple-element.310), channel_id=1, source_target_pairs={{1,2},{2,1},{5,6},{6,5},{9,10},{10,9},{13,14},{14,13},{17,18},{18,... | collective-permute-start | bytes 3145736 | tf_op jit(solution)/shard_map/ppermute | solution.py:21
  343.5 27.8 %collective-permute-start.41 = (f32[128,2048]{1,0:T(8,128)S(1)}, f32[128,2048]{1,0:T(8,128)S(1)}, u32[]{:S(2)}, u32[]{:S(2)}) collective-permute-start(f32[128,2048]{1,0:T(8,128)S(1)} %slice_add_fusion.2), channel_id=1, source_target_pairs={{1,2},{2,1},{5,6},{6,5},{9,10},{10,9},{13,14},{14,13},{17,18},{18,... | collective-permute-start | bytes 3145736 | tf_op jit(solution)/shard_map/ppermute | solution.py:21
  344.3 27.1 %collective-permute-start.42 = (f32[128,2048]{1,0:T(8,128)S(1)}, f32[128,2048]{1,0:T(8,128)}, u32[]{:S(2)}, u32[]{:S(2)}) collective-permute-start(f32[128,2048]{1,0:T(8,128)S(1)} %add.226), channel_id=1, source_target_pairs={{1,0},{2,3},{5,4},{6,7},{9,8},{10,11},{13,12},{14,15},{17,16},{18,... | collective-permute-start | bytes 3145736 | tf_op jit(solution)/shard_map/ppermute | solution.py:21
  345.6 25.8 %collective-permute-start.40 = (f32[2,2048]{1,0:T(2,128)S(1)}, f32[2,2048]{1,0:T(2,128)S(1)}, u32[]{:S(2)}, u32[]{:S(2)}) collective-permute-start(f32[2,2048]{1,0:T(2,128)S(1)} %pad_maximum_fusion.2), channel_id=1, source_target_pairs={{0,1},{1,0},{2,3},{3,2},{4,5},{5,4},{6,7},{7,6},{8,9},{9,8},{10,11... | collective-permute-start | bytes 49160 | tf_op jit(solution)/shard_map/ppermute | solution.py:21
  349.2 24.3 %collective-permute-start.39 = (f32[128,2048]{1,0:T(8,128)}, f32[128,2048]{1,0:T(8,128)}, u32[]{:S(2)}, u32[]{:S(2)}) collective-permute-start(f32[128,2048]{1,0:T(8,128)} %split.18), channel_id=1, source_target_pairs={{0,1},{3,2},{4,5},{7,6},{8,9},{11,10},{12,13},{15,14},{16,17},{19,... | collective-permute-start | bytes 3145736 | tf_op jit(solution)/shard_map/ppermute | solution.py:21
  352.5 33.0 %slice-start.4 = ((s8[5636096]{0:T(1024)(128)(4,1)}), s8[1441792]{0:T(1024)(128)(4,1)S(1)}, s32[]{:S(2)}) async-start(s8[5636096]{0:T(1024)(128)(4,1)} %bitcast.71), calls=%async_computation.7 | async-start | bytes 2883584
  358.9 26.6 %slice-start.5 = ((s8[5636096]{0:T(1024)(128)(4,1)}), s8[4194304]{0:T(1024)(128)(4,1)S(1)}, s32[]{:S(2)}) async-start(s8[5636096]{0:T(1024)(128)(4,1)} %bitcast.71), calls=%async_computation.8 | async-start | bytes 8388608
  376.3 23.3 %copy-start.15 = (bf16[1024,2048]{1,0:T(8,128)(2,1)S(1)}, bf16[1024,2048]{1,0:T(8,128)(2,1)}, u32[]{:S(2)}) copy-start(bf16[1024,2048]{1,0:T(8,128)(2,1)} %shard_map.206) | copy-start | bytes 12582916
  376.4 35.2 %collective-permute-start.46 = (f32[128,2048]{1,0:T(8,128)S(1)}, f32[128,2048]{1,0:T(8,128)S(1)}, u32[]{:S(2)}, u32[]{:S(2)}) collective-permute-start(f32[128,2048]{1,0:T(8,128)S(1)} %add.229), channel_id=1, source_target_pairs={{1,0},{2,3},{5,4},{6,7},{9,8},{10,11},{13,12},{14,15},{17,16},{18,... | collective-permute-start | bytes 3145736 | tf_op jit(solution)/shard_map/ppermute | solution.py:21
  377.9 33.7 %collective-permute-start.43 = (f32[128,2048]{1,0:T(8,128)S(1)}, f32[128,2048]{1,0:T(8,128)S(1)}, u32[]{:S(2)}, u32[]{:S(2)}) collective-permute-start(f32[128,2048]{1,0:T(8,128)S(1)} %get-tuple-element.346), channel_id=1, source_target_pairs={{0,1},{3,2},{4,5},{7,6},{8,9},{11,10},{12,13},{15,14},{16,17},{19,... | collective-permute-start | bytes 3145736 | tf_op jit(solution)/shard_map/ppermute | solution.py:21
  382.7 28.9 %collective-permute-start.44 = (f32[128,2048]{1,0:T(8,128)S(1)}, f32[128,2048]{1,0:T(8,128)S(1)}, u32[]{:S(2)}, u32[]{:S(2)}) collective-permute-start(f32[128,2048]{1,0:T(8,128)S(1)} %get-tuple-element.347), channel_id=1, source_target_pairs={{1,2},{2,1},{5,6},{6,5},{9,10},{10,9},{13,14},{14,13},{17,18},{18,... | collective-permute-start | bytes 3145736 | tf_op jit(solution)/shard_map/ppermute | solution.py:21
  383.5 28.1 %collective-permute-start.45 = (f32[2,2048]{1,0:T(2,128)S(1)}, f32[2,2048]{1,0:T(2,128)S(1)}, u32[]{:S(2)}, u32[]{:S(2)}) collective-permute-start(f32[2,2048]{1,0:T(2,128)S(1)} %fusion.19), channel_id=1, source_target_pairs={{0,2},{1,3},{2,0},{3,1},{4,6},{5,7},{6,4},{7,5},{8,10},{9,11},{10,... | collective-permute-start | bytes 49160 | tf_op jit(solution)/shard_map/ppermute | solution.py:21
  415.3 23.6 %collective-permute-start.49 = (f32[2,2048]{1,0:T(2,128)S(1)}, f32[2,2048]{1,0:T(2,128)S(1)}, u32[]{:S(2)}, u32[]{:S(2)}) collective-permute-start(f32[2,2048]{1,0:T(2,128)S(1)} %fusion.101), channel_id=1, source_target_pairs={{0,4},{4,0},{8,12},{12,8},{16,20},{20,16},{24,28},{28,24},{1,5},{5... | collective-permute-start | bytes 49160 | tf_op jit(solution)/shard_map/ppermute | solution.py:21
  415.4 23.5 %collective-permute-start.47 = (f32[128,2048]{1,0:T(8,128)S(1)}, f32[128,2048]{1,0:T(8,128)S(1)}, u32[]{:S(2)}, u32[]{:S(2)}) collective-permute-start(f32[128,2048]{1,0:T(8,128)S(1)} %slice_add_fusion), channel_id=1, source_target_pairs={{1,2},{2,1},{5,6},{6,5},{9,10},{10,9},{13,14},{14,13},{17,18},{18,... | collective-permute-start | bytes 3145736 | tf_op jit(solution)/shard_map/ppermute | solution.py:21
  416.2 27.3 %collective-permute-start.48 = (f32[128,2048]{1,0:T(8,128)S(1)}, f32[128,2048]{1,0:T(8,128)S(1)}, u32[]{:S(2)}, u32[]{:S(2)}) collective-permute-start(f32[128,2048]{1,0:T(8,128)S(1)} %add.233), channel_id=1, source_target_pairs={{1,0},{2,3},{5,4},{6,7},{9,8},{10,11},{13,12},{14,15},{17,16},{18,... | collective-permute-start | bytes 3145736 | tf_op jit(solution)/shard_map/ppermute | solution.py:21
  443.7 29.3 %collective-permute-start.50 = (f32[128,2048]{1,0:T(8,128)S(1)}, f32[128,2048]{1,0:T(8,128)S(1)}, u32[]{:S(2)}, u32[]{:S(2)}) collective-permute-start(f32[128,2048]{1,0:T(8,128)S(1)} %add.236), channel_id=1, source_target_pairs={{1,0},{2,3},{5,4},{6,7},{9,8},{10,11},{13,12},{14,15},{17,16},{18,... | collective-permute-start | bytes 3145736 | tf_op jit(solution)/shard_map/ppermute | solution.py:21
  445.3 27.7 %collective-permute-start.51 = (f32[2,2048]{1,0:T(2,128)S(1)}, f32[2,2048]{1,0:T(2,128)S(1)}, u32[]{:S(2)}, u32[]{:S(2)}) collective-permute-start(f32[2,2048]{1,0:T(2,128)S(1)} %add.237), channel_id=1, source_target_pairs={{0,8},{4,12},{8,0},{12,4},{16,24},{20,28},{24,16},{28,20},{1,9},{5... | collective-permute-start | bytes 49160 | tf_op jit(solution)/shard_map/ppermute | solution.py:21
  445.5 27.5 %collective-permute-start.52 = (f32[2,2048]{1,0:T(2,128)S(1)}, f32[2,2048]{1,0:T(2,128)S(1)}, u32[]{:S(2)}, u32[]{:S(2)}) collective-permute-start(f32[2,2048]{1,0:T(2,128)S(1)} %add.237), channel_id=1, source_target_pairs={{0,16},{4,20},{8,24},{12,28},{16,0},{20,4},{24,8},{28,12},{1,17},{... | collective-permute-start | bytes 49160 | tf_op jit(solution)/shard_map/ppermute | solution.py:21
  446.0 27.0 %collective-permute-start.53 = (f32[2,2048]{1,0:T(2,128)S(1)}, f32[2,2048]{1,0:T(2,128)S(1)}, u32[]{:S(2)}, u32[]{:S(2)}) collective-permute-start(f32[2,2048]{1,0:T(2,128)S(1)} %add.237), channel_id=1, source_target_pairs={{0,24},{4,28},{8,16},{12,20},{16,8},{20,12},{24,0},{28,4},{1,25},{... | collective-permute-start | bytes 49160 | tf_op jit(solution)/shard_map/ppermute | solution.py:21
  (62 other events, 315.8 us)
Sparse Core Ops, SparseCore 0:
  65.7 87.3 all-reduce.5
  176.4 83.8 all-reduce.7
  338.3 138.0 all-reduce.9

commit v7 on v6

--- a/solution.py
+++ b/solution.py
@@ -245,7 +245,7 @@
             first = 2 * qk + head * DV
             value = read(slots[slot], None, slice(first, first + DV)).astype(bf16)
             grad = dot_t(numer_ref[:, head * DV : (head + 1) * DV].astype(bf16), value)
-            grad = grad + denom_ref[:, head : head + 1]
+            grad = grad + denom_ref[:, head * DV : head * DV + 1]
             grad = jnp.where(allowed, grad * near, 0.0).astype(bf16)
             sums[head] = sums[head] + dot_n(grad, keys)
     total = jnp.zeros((rows, 2 * qk), f32)
@@ -465,6 +465,7 @@
     cot_early = ready(cot, cot_slots, early)
     convoy.launch(cot)
     cot_a, hidden_grad_a = convoy.work(cot_work, *cot_early)
+    token_wide = after(tokens, attn_part).astype(f32)
     resid_mid = after(token_wide, convoy.done) + attn_sum
     inv_mid = lax.rsqrt(jnp.mean(resid_mid * resid_mid, axis=-1, keepdims=True) + epsilon)
     scaled_mid = resid_mid * inv_mid
@@ -523,7 +524,7 @@
             columns,
             lines,
             numer_grad,
-            denom_grad,
+            jnp.repeat(denom_grad, DV, axis=1),
             *qkv_parts,
             flops=cost,
         )

time: 506 us -> 507 us (level)
    unnamed x142 -> x143, local copies, waits for them, and re-layouts: 23.6 us -> 24.5 us
where the time goes in v7:
time: 507 us; the launch traced here: 498 us
  matrix products  177 us (35%)
  waiting for transfers between devices  103 us (20%)
  starting transfers between devices  57.1 us (11%)
  Pallas kernels  53.8 us (11%)
  other arithmetic  45.6 us (9%)
  local copies, waits for them, and re-layouts  43.9 us (9%)
  between operations  17.6 us (3%)
    dot_general x10, matrix products, t_mm(): return jnp.einsum('ca,cb->ab', left, right, preferred_element_type=f32)  71.9 us
    dot_general x11, matrix products, mm(): return jnp.dot(left, right, preferred_element_type=f32)  69.7 us
    ppermute x54, waiting for transfers between devices, hop(): return lax.ppermute(value, axis, way)  66.7 us
    ppermute x54, starting transfers between devices, hop(): return lax.ppermute(value, axis, way)  57 us
    psum x2, waiting for transfers between devices, sum_head(): return lax.psum(value, 'head')  36.1 us
    dot_general x9, matrix products, mm_t(): return jnp.einsum('ac,bc->ab', left, right, preferred_element_type=f32)  35.2 us
    pallas_call x3, Pallas kernels, whole_call(): pl.pallas_call(body, out_shape=outs, in_specs=[pl.BlockSpec(memory_space=...  28.7 us
    pallas_call x4, Pallas kernels, join_rounded(): pl.pallas_call(functools.partial(join_kernel, tuple((len(slot) for slot i...  25.2 us
  transfers between devices with their start and end apart: 57, of which 19 were waited for; matrix products, arithmetic and copies ran while one was open for 46% of the time, Pallas kernels for 11%

profile of v7, /device:TPU:0, one launch (start us, length us, event | category | flops | bytes accessed | tf_op | source)
XLA Modules:
  0.0 497.7 jit_solution(7633524418473860589)
XLA Ops:
  8.1 1.6 fusion.2
  14.1 2.9 collective-permute-start
  21.8 2.8 convert_element_type.127.refs_0_
  26.6 5.5 %collective-permute-done.refs_2_ = f32[256,640]{1,0:T(8,128)} collective-permute-done((f32[256,640]{1,0:T(8,128)}, f32[256,640]{1,0:T(8,128)}, u32[]{:S(2)}, u32[]{:S(2)}) %collective-permute-start) | collective-permute-done | bytes 655392 | tf_op jit(solution)/shard_map/ppermute | solution.py:21
  38.2 7.6 %collective-permute-done.3.refs_6_ = f32[128,640]{1,0:T(8,128)S(1)} collective-permute-done((f32[128,640]{1,0:T(8,128)S(1)}, f32[128,640]{1,0:T(8,128)S(1)}, u32[]{:S(2)}, u32[]{:S(2)}) %collective-permute-start.3) | collective-permute-done | bytes 327712 | tf_op jit(solution)/shard_map/ppermute | solution.py:21
  51.8 7.9 %shard_map.203 = (bf16[256,512]{1,0:T(8,128)(2,1)}, f32[256,512]{1,0:T(8,128)}, f32[256,512]{1,0:T(8,128)}) custom-call(s32[256,4]{1,0:T(8,128)} %copy.28.col_ref, s32[24,256]{1,0:T(8,128)} %pad_add_fusion.row_ref, f32[256,640]{1,0:T(8,128)} %pad_maximum_fusion.1.refs_0_, f32[256,640]{1,0:T(8,128)} %collective-permute-done.2.refs_1_, ...), custom_call_target="tpu_custom_call" | custom-call | flops 2147483648 | bytes 6582272 | tf_op jit(solution)/shard_map/pallas_call | solution.py:298
  59.7 3.0 fusion.32
  62.7 2.8 convert_element_type.128
  65.6 5.7 %fusion.33 = f32[256,1376]{0,1:T(8,128)} fusion(bf16[256,2048]{1,0:T(8,128)(2,1)} %param.23, bf16[1376,2048]{1,0:T(8,128)(2,1)} %param.21), kind=kOutput, calls=%fused_computation.94 | convolution fusion | flops 1442840576 | bytes 8093696 | tf_op jit(solution)/shard_map/ac,bc->ab/dot_general | solution.py:354
  71.3 26.2 %collective-permute-done.10.refs_3_ = f32[256,2048]{1,0:T(8,128)} collective-permute-done((f32[256,2048]{1,0:T(8,128)}, f32[256,2048]{1,0:T(8,128)}, u32[]{:S(2)}, u32[]{:S(2)}) %collective-permute-start.10) | collective-permute-done | bytes 2097184 | tf_op jit(solution)/shard_map/ppermute | solution.py:21
  98.8 2.3 slice.48
  101.1 2.3 slice.49
  106.1 6.3 %shard_map.204 = bf16[1024,2048]{1,0:T(8,128)(2,1)} custom-call(f32[1,2048]{1,0:T(1,128)} %broadcast_12_scale_ref.2.scale_ref, f32[256,2048]{1,0:T(8,128)} %convert_element_type.127.refs_0_, f32[256,2048]{1,0:T(8,128)} %collective-permute-done.11.refs_1_, f32[256,2048]{1,0:T(8,128)} %collective-permute-done.9.refs_2_, ...), custom_call_target="tpu_custom_call" | custom-call | bytes 12582912 | tf_op jit(solution)/shard_map/pallas_call | solution.py:325
  112.4 11.0 %fusion.34 = f32[1024,1376]{0,1:T(8,128)} fusion(bf16[1024,2048]{1,0:T(8,128)(2,1)} %shard_map.204, bf16[1376,2048]{1,0:T(8,128)(2,1)} %param.21), kind=kOutput, calls=%fused_computation.95 | convolution fusion | flops 5771362304 | bytes 15466496 | tf_op jit(solution)/shard_map/ac,bc->ab/dot_general | solution.py:354
  123.4 29.7 %all-reduce.6.cloned.1.call-done = f32[256,2048]{1,0:T(8,128)} async-done(((f32[256,2048]{1,0:T(8,128)}), f32[256,2048]{1,0:T(8,128)}) %all-reduce.6.cloned.1.call-update) | async-done | bytes 2097168 | tf_op jit(solution)/shard_map/psum | solution.py:159
  153.0 2.5 multiply_reduce_fusion.4
  161.2 5.1 %fusion.11 = f32[256,1376]{0,1:T(8,128)S(1)} fusion(bf16[2048,1376]{0,1:T(8,128)(2,1)} %param.19, f32[256,2048]{1,0:T(8,128)} %broadcast_multiply_fusion.refs_0_, f32[2048]{0:T(1024)S(1)} %convert_element_type.129), kind=kOutput, calls=%fused_computation.51 | convolution fusion | flops 1443889152 | bytes 9150464 | tf_op jit(solution)/shard_map/dot_general | solution.py:350
  166.4 4.5 multiply_convert_fusion.9
  170.9 2.2 fusion.6
  173.1 3.2 convolution_add_fusion.5
  176.4 6.0 %fusion.35 = f32[256,2048]{1,0:T(8,128)} fusion(bf16[256,1376]{0,1:T(8,128)(2,1)} %get-tuple-element.247, bf16[1376,2048]{1,0:T(8,128)(2,1)} %param.21), kind=kOutput, calls=%fused_computation.96 | convolution fusion | flops 1442840576 | bytes 8437760 | tf_op jit(solution)/shard_map/dot_general | solution.py:350
  182.4 6.4 %shard_map.205 = bf16[1024,2048]{1,0:T(8,128)(2,1)} custom-call(f32[1,2048]{1,0:T(1,128)} %broadcast_12_scale_ref.2.scale_ref, f32[256,2048]{1,0:T(8,128)} %collective-permute-done.14.refs_0_, f32[256,2048]{1,0:T(8,128)} %collective-permute-done.15.refs_1_, f32[128,2048]{1,0:T(8,128)} %collective-permute-done.12.refs_2_, ...), custom_call_target="tpu_custom_call" | custom-call | bytes 12582912 | tf_op jit(solution)/shard_map/pallas_call | solution.py:325
  188.8 10.9 %fusion.36 = f32[1024,1376]{0,1:T(8,128)} fusion(bf16[1024,2048]{1,0:T(8,128)(2,1)} %shard_map.205, bf16[1376,2048]{1,0:T(8,128)(2,1)} %param.21), kind=kOutput, calls=%fused_computation.97 | convolution fusion | flops 5771362304 | bytes 15466496 | tf_op jit(solution)/shard_map/ac,bc->ab/dot_general | solution.py:354
  199.6 6.6 %collective-permute-done.16.refs_2_ = f32[256,2048]{1,0:T(8,128)} collective-permute-done((f32[256,2048]{1,0:T(8,128)}, f32[256,2048]{1,0:T(8,128)}, u32[]{:S(2)}, u32[]{:S(2)}) %collective-permute-start.16) | collective-permute-done | bytes 2097184 | tf_op jit(solution)/shard_map/ppermute | solution.py:21
  207.4 2.3 slice.50
  209.7 2.3 slice.51
  214.5 6.2 %shard_map.206 = bf16[1024,2048]{1,0:T(8,128)(2,1)} custom-call(f32[1,2048]{1,0:T(1,128)} %bitcast.81, f32[256,2048]{1,0:T(8,128)} %broadcast_multiply_fusion.refs_0_, f32[256,2048]{1,0:T(8,128)} %collective-permute-done.18.refs_1_, f32[256,2048]{1,0:T(8,128)} %collective-permute-done.16.refs_2_, f32[256,2048]{1,0:T(8,128)} %collective-permute-done.17.refs_3_), custom_call_target="tpu_custom_call" | custom-call | bytes 12582912 | tf_op jit(solution)/shard_map/pallas_call | solution.py:325
  220.7 11.3 %fusion.37 = f32[1024,1376]{0,1:T(8,128)} fusion(bf16[1024,2048]{1,0:T(8,128)(2,1)} %shard_map.206, bf16[2048,1376]{0,1:T(8,128)(2,1)} %param.19), kind=kOutput, calls=%fused_computation.98 | convolution fusion | flops 5771362304 | bytes 15466496 | tf_op jit(solution)/shard_map/dot_general | solution.py:350
  232.1 12.8 %multiply_convert_fusion.3 = (bf16[1024,1376]{0,1:T(8,128)(2,1)}, bf16[1024,1376]{0,1:T(8,128)(2,1)}, bf16[1024,1376]{0,1:T(8,128)(2,1)S(1)}) fusion(f32[1024,1376]{0,1:T(8,128)} %fusion.34, f32[1024,1376]{0,1:T(8,128)} %fusion.37, bf16[1024,2048]{1,0:T(8,128)(2,1)S(1)} %copy-done.14, bf16[2048,1376]{0,1:T(8,128)(2,1)S(1)} %bitcast.74), kind=kOutput, calls=%fused_computation.8 | convolution fusion | flops 5792497664 | bytes 29556736 | tf_op jit(solution)/shard_map/dot_general | solution.py:350
  244.9 8.9 %fusion.38 = f32[1376,2048]{1,0:T(8,128)} fusion(bf16[1024,1376]{0,1:T(8,128)(2,1)S(1)} %get-tuple-element.276, bf16[1024,2048]{1,0:T(8,128)(2,1)S(1)} %copy-done.17), kind=kOutput, calls=%fused_computation.99 | convolution fusion | flops 5771362304 | bytes 18284544 | tf_op jit(solution)/shard_map/ca,cb->ab/dot_general | solution.py:358
  253.8 6.4 %all-reduce.8.cloned.1.call-done = f32[256,2048]{1,0:T(8,128)} async-done(((f32[256,2048]{1,0:T(8,128)}), f32[256,2048]{1,0:T(8,128)}) %all-reduce.8.cloned.1.call-update) | async-done | bytes 2097168 | tf_op jit(solution)/shard_map/psum | solution.py:159
  260.2 2.7 multiply_reduce_fusion.3
  263.7 2.8 multiply_reduce_fusion.1
  269.3 2.2 reshape.106
  271.4 2.0 reduce_sum.66
  281.3 3.1 collective-permute-start.34
  285.6 9.4 %shard_map.207 = bf16[256,64]{1,0:T(8,128)(2,1)} custom-call(s32[256,4]{1,0:T(8,128)} %copy.28.col_ref, s32[24,256]{1,0:T(8,128)} %pad_add_fusion.row_ref, f32[256,512]{1,0:T(8,128)} %get-tuple-element.289.numer_ref, f32[256,512]{1,0:T(8,128)} %bitcast.80, f32[256,640]{1,0:T(8,128)} %pad_maximum_fusion.1.refs_0_, f32[256,640]{1,0:T(8,128)} %collective-permute-done.2.refs_1_, ...), custom_call_target="tpu_custom_call" | custom-call | flops 2147483648 | bytes 6352896 | tf_op jit(solution)/shard_map/pallas_call | solution.py:298
  296.8 2.7 fusion.40
  299.6 5.0 collective-permute-done.28.refs_16_
  308.1 2.8 slice_add_fusion.3
  311.4 3.9 collective-permute-start.37
  315.3 1.9 collective-permute-start.38
  317.3 11.4 %shard_map.208 = (bf16[256,64]{1,0:T(8,128)(2,1)}, bf16[256,512]{1,0:T(8,128)(2,1)}) custom-call(s32[256,4]{1,0:T(8,128)} %copy.28.col_ref, s32[24,256]{1,0:T(8,128)} %pad_add_fusion.row_ref, f32[256,640]{1,0:T(8,128)} %pad_maximum_fusion.1.refs_0_, f32[256,640]{1,0:T(8,128)} %collective-permute-done.2.refs_1_, f32[256,640]{1,0:T(8,128)} %collective-permute-done.refs_2_, ...), custom_call_target="tpu_custom_call" | custom-call | flops 4294967296 | bytes 9891840 | tf_op jit(solution)/shard_map/pallas_call | solution.py:298
  328.6 3.7 fusion.43
  340.6 1.8 add.226
  346.4 3.6 collective-permute-start.40
  350.1 3.3 collective-permute-start.39
  353.4 6.3 %shard_map.209 = bf16[1024,2048]{1,0:T(8,128)(2,1)} custom-call(f32[1,2048]{1,0:T(1,128)} %bitcast.82, f32[256,2048]{1,0:T(8,128)} %collective-permute-done.23.refs_0_, f32[256,2048]{1,0:T(8,128)} %collective-permute-done.24.refs_1_, f32[128,2048]{1,0:T(8,128)} %collective-permute-done.21.refs_2_, f32[128,2048]{1,0:T(8,128)} %collective-permute-done.22.refs_3_, ...), custom_call_target="tpu_custom_call" | custom-call | bytes 12582912 | tf_op jit(solution)/shard_map/pallas_call | solution.py:325
  359.7 11.3 %fusion.45 = f32[1024,1376]{0,1:T(8,128)} fusion(bf16[1024,2048]{1,0:T(8,128)(2,1)} %shard_map.209, bf16[2048,1376]{0,1:T(8,128)(2,1)} %param.19), kind=kOutput, calls=%fused_computation.106 | convolution fusion | flops 5771362304 | bytes 15466496 | tf_op jit(solution)/shard_map/dot_general | solution.py:350
  378.8 4.8 collective-permute-start.43
  384.3 2.0 collective-permute-start.45
  386.4 14.1 %multiply_convert_fusion = (bf16[1024,1376]{0,1:T(8,128)(2,1)}, bf16[1024,1376]{0,1:T(8,128)(2,1)}, bf16[1024,1376]{0,1:T(8,128)(2,1)}) fusion(f32[1024,1376]{0,1:T(8,128)} %fusion.36, f32[1024,1376]{0,1:T(8,128)} %fusion.45, bf16[1024,2048]{1,0:T(8,128)(2,1)} %shard_map.209, bf16[2048,1376]{0,1:T(8,128)(2,1)S(1)} %bitcast.76), kind=kOutput, calls=%fused_computation.3 | convolution fusion | flops 5792497664 | bytes 29556736 | tf_op jit(solution)/shard_map/dot_general | solution.py:350
  400.5 10.5 %fusion.46 = f32[2048,1376]{0,1:T(8,128)} fusion(bf16[1024,1376]{0,1:T(8,128)(2,1)} %get-tuple-element.355, bf16[1024,2048]{1,0:T(8,128)(2,1)S(1)} %copy-done.15), kind=kOutput, calls=%fused_computation.107 | convolution fusion | flops 5771362304 | bytes 18284544 | tf_op jit(solution)/shard_map/ca,cb->ab/dot_general | solution.py:358
  418.5 12.2 %convolution_add_fusion.2 = f32[1376,2048]{1,0:T(8,128)} fusion(f32[1376,2048]{1,0:T(8,128)} %fusion.38, bf16[1024,1376]{0,1:T(8,128)(2,1)} %get-tuple-element.363, bf16[1024,2048]{1,0:T(8,128)(2,1)S(1)} %copy-done.13), kind=kOutput, calls=%fused_computation.2 | convolution fusion | flops 5774180352 | bytes 29556736 | tf_op jit(solution)/shard_map/ca,cb->ab/dot_general | solution.py:358
  430.7 8.7 %fusion.47 = f32[2048,1376]{0,1:T(8,128)} fusion(bf16[1024,1376]{0,1:T(8,128)(2,1)S(1)} %copy-done.58, bf16[1024,2048]{1,0:T(8,128)(2,1)S(1)} %copy-done.15), kind=kOutput, calls=%fused_computation.108 | convolution fusion | flops 5771362304 | bytes 18284544 | tf_op jit(solution)/shard_map/ca,cb->ab/dot_general | solution.py:358
  439.7 4.6 collective-permute-done.48
  446.9 2.8 collective-permute-start.53
  450.9 11.5 %convolution_add_fusion.1 = f32[2048,1376]{0,1:T(8,128)} fusion(f32[2048,1376]{0,1:T(8,128)} %fusion.47, bf16[1024,1376]{0,1:T(8,128)(2,1)S(1)} %copy-done.60, bf16[1024,2048]{1,0:T(8,128)(2,1)S(1)} %copy-done.16), kind=kOutput, calls=%fused_computation.1 | convolution fusion | flops 5774180352 | bytes 29556736 | tf_op jit(solution)/shard_map/ca,cb->ab/dot_general | solution.py:358
  462.4 11.4 %convolution_add_fusion = f32[2048,1376]{0,1:T(8,128)} fusion(f32[2048,1376]{0,1:T(8,128)} %fusion.46, bf16[1024,1376]{0,1:T(8,128)(2,1)S(1)} %copy-done.59, bf16[1024,2048]{1,0:T(8,128)(2,1)S(1)} %copy-done.16), kind=kOutput, calls=%fused_computation | convolution fusion | flops 5774180352 | bytes 29556736 | tf_op jit(solution)/shard_map/ca,cb->ab/dot_general | solution.py:358
  476.0 2.7 multiply_add_fusion.2
  479.4 1.9 copy.43
  481.2 1.9 copy.44
  483.1 4.8 copy.45
  487.9 2.1 copy.46
  (302 shorter events, 88.8 us)
Async XLA Ops:
  7.2 52.6 %copy-start = (bf16[512,2048]{1,0:T(8,128)(2,1)S(1)}, bf16[512,2048]{1,0:T(8,128)(2,1)}, u32[]{:S(2)}) copy-start(bf16[512,2048]{1,0:T(8,128)(2,1)} %param.17) | copy-start | bytes 6291460
  7.2 145.8 %all-reduce.6.cloned.1.call-start = ((), (), s32[]{:S(2)}) async-start(), calls=%async_computation | async-start | bytes 4194304 | tf_op jit(solution)/shard_map/psum | solution.py:159
  14.1 18.0 %collective-permute-start = (f32[256,640]{1,0:T(8,128)}, f32[256,640]{1,0:T(8,128)}, u32[]{:S(2)}, u32[]{:S(2)}) collective-permute-start(f32[256,640]{1,0:T(8,128)} %pad_maximum_fusion.1.refs_0_), channel_id=1, source_target_pairs={{0,8},{4,12},{8,0},{12,4},{16,24},{20,28},{24,16},{28,20},{1,9},{5... | collective-permute-start | bytes 1966088 | tf_op jit(solution)/shard_map/ppermute | solution.py:21
  17.0 16.5 %collective-permute-start.1 = (f32[256,640]{1,0:T(8,128)}, f32[256,640]{1,0:T(8,128)}, u32[]{:S(2)}, u32[]{:S(2)}) collective-permute-start(f32[256,640]{1,0:T(8,128)} %pad_maximum_fusion.1.refs_0_), channel_id=1, source_target_pairs={{0,16},{4,20},{8,24},{12,28},{16,0},{20,4},{24,8},{28,12},{1,17},{... | collective-permute-start | bytes 1966088 | tf_op jit(solution)/shard_map/ppermute | solution.py:21
  18.6 15.0 %collective-permute-start.2 = (f32[256,640]{1,0:T(8,128)}, f32[256,640]{1,0:T(8,128)}, u32[]{:S(2)}, u32[]{:S(2)}) collective-permute-start(f32[256,640]{1,0:T(8,128)} %pad_maximum_fusion.1.refs_0_), channel_id=1, source_target_pairs={{0,4},{4,0},{8,12},{12,8},{16,20},{20,16},{24,28},{28,24},{1,5},{5... | collective-permute-start | bytes 1966088 | tf_op jit(solution)/shard_map/ppermute | solution.py:21
  21.8 30.0 %copy-start.50 = (bf16[2048]{0:T(1024)(128)(2,1)S(1)}, bf16[2048]{0:T(1024)(128)(2,1)}, u32[]{:S(2)}) copy-start(bf16[2048]{0:T(1024)(128)(2,1)} %param.18) | copy-start | bytes 12292
  35.6 11.5 %collective-permute-start.5 = (f32[256,640]{1,0:T(8,128)}, f32[256,640]{1,0:T(8,128)}, u32[]{:S(2)}, u32[]{:S(2)}) collective-permute-start(f32[256,640]{1,0:T(8,128)} %collective-permute-done.refs_2_), channel_id=1, source_target_pairs={{0,4},{4,0},{8,12},{12,8},{16,20},{20,16},{24,28},{28,24},{1,5},{5... | collective-permute-start | bytes 1966088 | tf_op jit(solution)/shard_map/ppermute | solution.py:21
  35.6 11.4 %collective-permute-start.6 = (f32[256,640]{1,0:T(8,128)}, f32[256,640]{1,0:T(8,128)}, u32[]{:S(2)}, u32[]{:S(2)}) collective-permute-start(f32[256,640]{1,0:T(8,128)} %collective-permute-done.1.refs_4_), channel_id=1, source_target_pairs={{0,4},{4,0},{8,12},{12,8},{16,20},{20,16},{24,28},{28,24},{1,5},{5... | collective-permute-start | bytes 1966088 | tf_op jit(solution)/shard_map/ppermute | solution.py:21
  36.1 9.7 %collective-permute-start.3 = (f32[128,640]{1,0:T(8,128)S(1)}, f32[128,640]{1,0:T(8,128)S(1)}, u32[]{:S(2)}, u32[]{:S(2)}) collective-permute-start(f32[128,640]{1,0:T(8,128)S(1)} %slice.46), channel_id=1, source_target_pairs={{0,16},{4,20},{8,24},{12,28},{16,0},{20,4},{24,8},{28,12},{1,17},{... | collective-permute-start | bytes 983048 | tf_op jit(solution)/shard_map/ppermute | solution.py:21
  37.7 9.4 %collective-permute-start.4 = (f32[128,640]{1,0:T(8,128)S(1)}, f32[128,640]{1,0:T(8,128)S(1)}, u32[]{:S(2)}, u32[]{:S(2)}) collective-permute-start(f32[128,640]{1,0:T(8,128)S(1)} %slice.47), channel_id=1, source_target_pairs={{0,8},{4,12},{8,0},{12,4},{16,24},{20,28},{24,16},{28,20},{1,9},{5... | collective-permute-start | bytes 983048 | tf_op jit(solution)/shard_map/ppermute | solution.py:21
  47.1 1.7 collective-permute-start.7
  47.2 2.1 collective-permute-start.8
  49.5 48.0 %collective-permute-start.10 = (f32[256,2048]{1,0:T(8,128)}, f32[256,2048]{1,0:T(8,128)}, u32[]{:S(2)}, u32[]{:S(2)}) collective-permute-start(f32[256,2048]{1,0:T(8,128)} %convert_element_type.127.refs_0_), channel_id=1, source_target_pairs={{0,16},{4,20},{8,24},{12,28},{16,0},{20,4},{24,8},{28,12},{1,17},{... | collective-permute-start | bytes 6291464 | tf_op jit(solution)/shard_map/ppermute | solution.py:21
  50.5 47.0 %collective-permute-start.11 = (f32[256,2048]{1,0:T(8,128)}, f32[256,2048]{1,0:T(8,128)}, u32[]{:S(2)}, u32[]{:S(2)}) collective-permute-start(f32[256,2048]{1,0:T(8,128)} %convert_element_type.127.refs_0_), channel_id=1, source_target_pairs={{0,4},{4,0},{8,12},{12,8},{16,20},{20,16},{24,28},{28,24},{1,5},{5... | collective-permute-start | bytes 6291464 | tf_op jit(solution)/shard_map/ppermute | solution.py:21
  50.5 48.4 %collective-permute-start.9 = (f32[256,2048]{1,0:T(8,128)}, f32[256,2048]{1,0:T(8,128)}, u32[]{:S(2)}, u32[]{:S(2)}) collective-permute-start(f32[256,2048]{1,0:T(8,128)} %convert_element_type.127.refs_0_), channel_id=1, source_target_pairs={{0,8},{4,12},{8,0},{12,4},{16,24},{20,28},{24,16},{28,20},{1,9},{5... | collective-permute-start | bytes 6291464 | tf_op jit(solution)/shard_map/ppermute | solution.py:21
  51.8 114.5 %copy-start.34 = (f32[2048]{0:T(1024)}, f32[2048]{0:T(1024)S(1)}, u32[]{:S(2)}) copy-start(f32[2048]{0:T(1024)S(1)} %convert_element_type.129) | copy-start | bytes 24580
  65.5 194.7 %all-reduce.8.cloned.1.call-start = ((), (), s32[]{:S(2)}) async-start(), calls=%async_computation.1 | async-start | bytes 4194304 | tf_op jit(solution)/shard_map/psum | solution.py:159
  103.4 54.3 %collective-permute-start.14 = (f32[256,2048]{1,0:T(8,128)}, f32[256,2048]{1,0:T(8,128)}, u32[]{:S(2)}, u32[]{:S(2)}) collective-permute-start(f32[256,2048]{1,0:T(8,128)} %collective-permute-done.9.refs_2_), channel_id=1, source_target_pairs={{0,4},{4,0},{8,12},{12,8},{16,20},{20,16},{24,28},{28,24},{1,5},{5... | collective-permute-start | bytes 6291464 | tf_op jit(solution)/shard_map/ppermute | solution.py:21
  103.4 54.3 %collective-permute-start.15 = (f32[256,2048]{1,0:T(8,128)}, f32[256,2048]{1,0:T(8,128)}, u32[]{:S(2)}, u32[]{:S(2)}) collective-permute-start(f32[256,2048]{1,0:T(8,128)} %collective-permute-done.10.refs_3_), channel_id=1, source_target_pairs={{0,4},{4,0},{8,12},{12,8},{16,20},{20,16},{24,28},{28,24},{1,5},{5... | collective-permute-start | bytes 6291464 | tf_op jit(solution)/shard_map/ppermute | solution.py:21
  104.0 53.7 %collective-permute-start.12 = (f32[128,2048]{1,0:T(8,128)}, f32[128,2048]{1,0:T(8,128)}, u32[]{:S(2)}, u32[]{:S(2)}) collective-permute-start(f32[128,2048]{1,0:T(8,128)} %slice.48), channel_id=1, source_target_pairs={{0,16},{4,20},{8,24},{12,28},{16,0},{20,4},{24,8},{28,12},{1,17},{... | collective-permute-start | bytes 3145736 | tf_op jit(solution)/shard_map/ppermute | solution.py:21
  105.0 52.7 %collective-permute-start.13 = (f32[128,2048]{1,0:T(8,128)}, f32[128,2048]{1,0:T(8,128)}, u32[]{:S(2)}, u32[]{:S(2)}) collective-permute-start(f32[128,2048]{1,0:T(8,128)} %slice.49), channel_id=1, source_target_pairs={{0,8},{4,12},{8,0},{12,4},{16,24},{20,28},{24,16},{28,20},{1,9},{5... | collective-permute-start | bytes 3145736 | tf_op jit(solution)/shard_map/ppermute | solution.py:21
  155.6 107.3 %copy-start.45 = (f32[256]{0:T(256)}, f32[256]{0:T(256)S(1)}, u32[]{:S(2)}) copy-start(f32[256]{0:T(256)S(1)} %add_rsqrt_fusion) | copy-start | bytes 3076
  157.7 18.6 %collective-permute-start.19 = (f32[128,2048]{1,0:T(8,128)}, f32[128,2048]{1,0:T(8,128)}, u32[]{:S(2)}, u32[]{:S(2)}) collective-permute-start(f32[128,2048]{1,0:T(8,128)} %collective-permute-done.12.refs_2_), channel_id=1, source_target_pairs={{0,4},{4,0},{8,12},{12,8},{16,20},{20,16},{24,28},{28,24},{1,5},{5... | collective-permute-start | bytes 3145736 | tf_op jit(solution)/shard_map/ppermute | solution.py:21
  157.8 18.6 %collective-permute-start.20 = (f32[128,2048]{1,0:T(8,128)}, f32[128,2048]{1,0:T(8,128)}, u32[]{:S(2)}, u32[]{:S(2)}) collective-permute-start(f32[128,2048]{1,0:T(8,128)} %collective-permute-done.13.refs_3_), channel_id=1, source_target_pairs={{0,4},{4,0},{8,12},{12,8},{16,20},{20,16},{24,28},{28,24},{1,5},{5... | collective-permute-start | bytes 3145736 | tf_op jit(solution)/shard_map/ppermute | solution.py:21
  158.3 47.9 %collective-permute-start.16 = (f32[256,2048]{1,0:T(8,128)}, f32[256,2048]{1,0:T(8,128)}, u32[]{:S(2)}, u32[]{:S(2)}) collective-permute-start(f32[256,2048]{1,0:T(8,128)} %broadcast_multiply_fusion.refs_0_), channel_id=1, source_target_pairs={{0,8},{4,12},{8,0},{12,4},{16,24},{20,28},{24,16},{28,20},{1,9},{5... | collective-permute-start | bytes 6291464 | tf_op jit(solution)/shard_map/ppermute | solution.py:21
  159.8 47.6 %collective-permute-start.17 = (f32[256,2048]{1,0:T(8,128)}, f32[256,2048]{1,0:T(8,128)}, u32[]{:S(2)}, u32[]{:S(2)}) collective-permute-start(f32[256,2048]{1,0:T(8,128)} %broadcast_multiply_fusion.refs_0_), channel_id=1, source_target_pairs={{0,16},{4,20},{8,24},{12,28},{16,0},{20,4},{24,8},{28,12},{1,17},{... | collective-permute-start | bytes 6291464 | tf_op jit(solution)/shard_map/ppermute | solution.py:21
  161.2 46.2 %collective-permute-start.18 = (f32[256,2048]{1,0:T(8,128)}, f32[256,2048]{1,0:T(8,128)}, u32[]{:S(2)}, u32[]{:S(2)}) collective-permute-start(f32[256,2048]{1,0:T(8,128)} %broadcast_multiply_fusion.refs_0_), channel_id=1, source_target_pairs={{0,4},{4,0},{8,12},{12,8},{16,20},{20,16},{24,28},{28,24},{1,5},{5... | collective-permute-start | bytes 6291464 | tf_op jit(solution)/shard_map/ppermute | solution.py:21
  176.3 302.4 %all-reduce.10.cloned.1.call-start = ((), (), s32[]{:S(2)}) async-start(), calls=%async_computation.2 | async-start | bytes 18874368 | tf_op jit(solution)/shard_map/psum | solution.py:562
  212.0 65.2 %collective-permute-start.23 = (f32[256,2048]{1,0:T(8,128)}, f32[256,2048]{1,0:T(8,128)}, u32[]{:S(2)}, u32[]{:S(2)}) collective-permute-start(f32[256,2048]{1,0:T(8,128)} %collective-permute-done.16.refs_2_), channel_id=1, source_target_pairs={{0,4},{4,0},{8,12},{12,8},{16,20},{20,16},{24,28},{28,24},{1,5},{5... | collective-permute-start | bytes 6291464 | tf_op jit(solution)/shard_map/ppermute | solution.py:21
  212.0 65.2 %collective-permute-start.24 = (f32[256,2048]{1,0:T(8,128)}, f32[256,2048]{1,0:T(8,128)}, u32[]{:S(2)}, u32[]{:S(2)}) collective-permute-start(f32[256,2048]{1,0:T(8,128)} %collective-permute-done.17.refs_3_), channel_id=1, source_target_pairs={{0,4},{4,0},{8,12},{12,8},{16,20},{20,16},{24,28},{28,24},{1,5},{5... | collective-permute-start | bytes 6291464 | tf_op jit(solution)/shard_map/ppermute | solution.py:21
  212.5 64.7 %collective-permute-start.21 = (f32[128,2048]{1,0:T(8,128)}, f32[128,2048]{1,0:T(8,128)}, u32[]{:S(2)}, u32[]{:S(2)}) collective-permute-start(f32[128,2048]{1,0:T(8,128)} %slice.50), channel_id=1, source_target_pairs={{0,16},{4,20},{8,24},{12,28},{16,0},{20,4},{24,8},{28,12},{1,17},{... | collective-permute-start | bytes 3145736 | tf_op jit(solution)/shard_map/ppermute | solution.py:21
  214.0 63.2 %collective-permute-start.22 = (f32[128,2048]{1,0:T(8,128)}, f32[128,2048]{1,0:T(8,128)}, u32[]{:S(2)}, u32[]{:S(2)}) collective-permute-start(f32[128,2048]{1,0:T(8,128)} %slice.51), channel_id=1, source_target_pairs={{0,8},{4,12},{8,0},{12,4},{16,24},{20,28},{24,16},{28,20},{1,9},{5... | collective-permute-start | bytes 3145736 | tf_op jit(solution)/shard_map/ppermute | solution.py:21
  277.2 17.8 %collective-permute-start.25 = (f32[264,512]{1,0:T(8,128)S(1)}, f32[264,512]{1,0:T(8,128)S(1)}, u32[]{:S(2)}, u32[]{:S(2)}) collective-permute-start(f32[264,512]{1,0:T(8,128)S(1)} %select_maximum_fusion.refs_10_), channel_id=1, source_target_pairs={{0,8},{4,12},{8,0},{12,4},{16,24},{20,28},{24,16},{28,20},{1,9},{5... | collective-permute-start | bytes 1622024 | tf_op jit(solution)/shard_map/ppermute | solution.py:21
  278.7 16.3 %collective-permute-start.26 = (f32[264,512]{1,0:T(8,128)S(1)}, f32[264,512]{1,0:T(8,128)S(1)}, u32[]{:S(2)}, u32[]{:S(2)}) collective-permute-start(f32[264,512]{1,0:T(8,128)S(1)} %select_maximum_fusion.refs_10_), channel_id=1, source_target_pairs={{0,16},{4,20},{8,24},{12,28},{16,0},{20,4},{24,8},{28,12},{1,17},{... | collective-permute-start | bytes 1622024 | tf_op jit(solution)/shard_map/ppermute | solution.py:21
  280.2 14.8 %collective-permute-start.27 = (f32[264,512]{1,0:T(8,128)S(1)}, f32[264,512]{1,0:T(8,128)S(1)}, u32[]{:S(2)}, u32[]{:S(2)}) collective-permute-start(f32[264,512]{1,0:T(8,128)S(1)} %select_maximum_fusion.refs_10_), channel_id=1, source_target_pairs={{0,4},{4,0},{8,12},{12,8},{16,20},{20,16},{24,28},{28,24},{1,5},{5... | collective-permute-start | bytes 1622024 | tf_op jit(solution)/shard_map/ppermute | solution.py:21
  281.3 25.4 %collective-permute-start.34 = (f32[128,2048]{1,0:T(8,128)}, f32[128,2048]{1,0:T(8,128)}, u32[]{:S(2)}, u32[]{:S(2)}) collective-permute-start(f32[128,2048]{1,0:T(8,128)} %split.16), channel_id=1, source_target_pairs={{0,1},{3,2},{4,5},{7,6},{8,9},{11,10},{12,13},{15,14},{16,17},{19,... | collective-permute-start | bytes 3145736 | tf_op jit(solution)/shard_map/ppermute | solution.py:21
  295.1 9.5 %collective-permute-start.30 = (f32[264,512]{1,0:T(8,128)S(1)}, f32[264,512]{1,0:T(8,128)S(1)}, u32[]{:S(2)}, u32[]{:S(2)}) collective-permute-start(f32[264,512]{1,0:T(8,128)S(1)} %collective-permute-done.25.refs_12_), channel_id=1, source_target_pairs={{0,4},{4,0},{8,12},{12,8},{16,20},{20,16},{24,28},{28,24},{1,5},{5... | collective-permute-start | bytes 1622024 | tf_op jit(solution)/shard_map/ppermute | solution.py:21
  295.4 9.2 %collective-permute-start.31 = (f32[264,512]{1,0:T(8,128)S(1)}, f32[264,512]{1,0:T(8,128)S(1)}, u32[]{:S(2)}, u32[]{:S(2)}) collective-permute-start(f32[264,512]{1,0:T(8,128)S(1)} %collective-permute-done.26.refs_14_), channel_id=1, source_target_pairs={{0,4},{4,0},{8,12},{12,8},{16,20},{20,16},{24,28},{28,24},{1,5},{5... | collective-permute-start | bytes 1622024 | tf_op jit(solution)/shard_map/ppermute | solution.py:21
  295.7 8.9 %collective-permute-start.29 = (f32[136,512]{1,0:T(8,128)S(1)}, f32[136,512]{1,0:T(8,128)}, u32[]{:S(2)}, u32[]{:S(2)}) collective-permute-start(f32[136,512]{1,0:T(8,128)S(1)} %slice.53), channel_id=1, source_target_pairs={{0,8},{4,12},{8,0},{12,4},{16,24},{20,28},{24,16},{28,20},{1,9},{5... | collective-permute-start | bytes 835592 | tf_op jit(solution)/shard_map/ppermute | solution.py:21
  296.3 8.3 %collective-permute-start.28 = (f32[128,512]{1,0:T(8,128)S(1)}, f32[128,512]{1,0:T(8,128)}, u32[]{:S(2)}, u32[]{:S(2)}) collective-permute-start(f32[128,512]{1,0:T(8,128)S(1)} %slice.52), channel_id=1, source_target_pairs={{0,16},{4,20},{8,24},{12,28},{16,0},{20,4},{24,8},{28,12},{1,17},{... | collective-permute-start | bytes 786440 | tf_op jit(solution)/shard_map/ppermute | solution.py:21
  305.4 2.7 collective-permute-start.33
  306.2 1.9 collective-permute-start.32
  310.9 28.1 %collective-permute-start.35 = (f32[128,2048]{1,0:T(8,128)}, f32[128,2048]{1,0:T(8,128)}, u32[]{:S(2)}, u32[]{:S(2)}) collective-permute-start(f32[128,2048]{1,0:T(8,128)} %collective-permute-done.21.refs_2_), channel_id=1, source_target_pairs={{0,4},{4,0},{8,12},{12,8},{16,20},{20,16},{24,28},{28,24},{1,5},{5... | collective-permute-start | bytes 3145736 | tf_op jit(solution)/shard_map/ppermute | solution.py:21
  311.1 28.0 %collective-permute-start.36 = (f32[128,2048]{1,0:T(8,128)}, f32[128,2048]{1,0:T(8,128)}, u32[]{:S(2)}, u32[]{:S(2)}) collective-permute-start(f32[128,2048]{1,0:T(8,128)} %collective-permute-done.22.refs_3_), channel_id=1, source_target_pairs={{0,4},{4,0},{8,12},{12,8},{16,20},{20,16},{24,28},{28,24},{1,5},{5... | collective-permute-start | bytes 3145736 | tf_op jit(solution)/shard_map/ppermute | solution.py:21
  311.4 29.2 %collective-permute-start.37 = (f32[128,2048]{1,0:T(8,128)}, f32[128,2048]{1,0:T(8,128)}, u32[]{:S(2)}, u32[]{:S(2)}) collective-permute-start(f32[128,2048]{1,0:T(8,128)} %get-tuple-element.311), channel_id=1, source_target_pairs={{0,1},{3,2},{4,5},{7,6},{8,9},{11,10},{12,13},{15,14},{16,17},{19,... | collective-permute-start | bytes 3145736 | tf_op jit(solution)/shard_map/ppermute | solution.py:21
  315.3 25.3 %collective-permute-start.38 = (f32[128,2048]{1,0:T(8,128)}, f32[128,2048]{1,0:T(8,128)}, u32[]{:S(2)}, u32[]{:S(2)}) collective-permute-start(f32[128,2048]{1,0:T(8,128)} %get-tuple-element.312), channel_id=1, source_target_pairs={{1,2},{2,1},{5,6},{6,5},{9,10},{10,9},{13,14},{14,13},{17,18},{18,... | collective-permute-start | bytes 3145736 | tf_op jit(solution)/shard_map/ppermute | solution.py:21
  344.4 27.8 %collective-permute-start.41 = (f32[128,2048]{1,0:T(8,128)S(1)}, f32[128,2048]{1,0:T(8,128)S(1)}, u32[]{:S(2)}, u32[]{:S(2)}) collective-permute-start(f32[128,2048]{1,0:T(8,128)S(1)} %slice_add_fusion.2), channel_id=1, source_target_pairs={{1,2},{2,1},{5,6},{6,5},{9,10},{10,9},{13,14},{14,13},{17,18},{18,... | collective-permute-start | bytes 3145736 | tf_op jit(solution)/shard_map/ppermute | solution.py:21
  345.1 27.1 %collective-permute-start.42 = (f32[128,2048]{1,0:T(8,128)S(1)}, f32[128,2048]{1,0:T(8,128)}, u32[]{:S(2)}, u32[]{:S(2)}) collective-permute-start(f32[128,2048]{1,0:T(8,128)S(1)} %add.226), channel_id=1, source_target_pairs={{1,0},{2,3},{5,4},{6,7},{9,8},{10,11},{13,12},{14,15},{17,16},{18,... | collective-permute-start | bytes 3145736 | tf_op jit(solution)/shard_map/ppermute | solution.py:21
  346.4 25.8 %collective-permute-start.40 = (f32[2,2048]{1,0:T(2,128)S(1)}, f32[2,2048]{1,0:T(2,128)S(1)}, u32[]{:S(2)}, u32[]{:S(2)}) collective-permute-start(f32[2,2048]{1,0:T(2,128)S(1)} %pad_maximum_fusion.2), channel_id=1, source_target_pairs={{0,1},{1,0},{2,3},{3,2},{4,5},{5,4},{6,7},{7,6},{8,9},{9,8},{10,11... | collective-permute-start | bytes 49160 | tf_op jit(solution)/shard_map/ppermute | solution.py:21
  350.1 24.3 %collective-permute-start.39 = (f32[128,2048]{1,0:T(8,128)}, f32[128,2048]{1,0:T(8,128)}, u32[]{:S(2)}, u32[]{:S(2)}) collective-permute-start(f32[128,2048]{1,0:T(8,128)} %split.18), channel_id=1, source_target_pairs={{0,1},{3,2},{4,5},{7,6},{8,9},{11,10},{12,13},{15,14},{16,17},{19,... | collective-permute-start | bytes 3145736 | tf_op jit(solution)/shard_map/ppermute | solution.py:21
  353.4 33.0 %slice-start.4 = ((s8[5636096]{0:T(1024)(128)(4,1)}), s8[1441792]{0:T(1024)(128)(4,1)S(1)}, s32[]{:S(2)}) async-start(s8[5636096]{0:T(1024)(128)(4,1)} %bitcast.75), calls=%async_computation.7 | async-start | bytes 2883584
  359.7 26.6 %slice-start.5 = ((s8[5636096]{0:T(1024)(128)(4,1)}), s8[4194304]{0:T(1024)(128)(4,1)S(1)}, s32[]{:S(2)}) async-start(s8[5636096]{0:T(1024)(128)(4,1)} %bitcast.75), calls=%async_computation.8 | async-start | bytes 8388608
  377.2 23.3 %copy-start.15 = (bf16[1024,2048]{1,0:T(8,128)(2,1)S(1)}, bf16[1024,2048]{1,0:T(8,128)(2,1)}, u32[]{:S(2)}) copy-start(bf16[1024,2048]{1,0:T(8,128)(2,1)} %shard_map.206) | copy-start | bytes 12582916
  377.2 35.2 %collective-permute-start.46 = (f32[128,2048]{1,0:T(8,128)S(1)}, f32[128,2048]{1,0:T(8,128)S(1)}, u32[]{:S(2)}, u32[]{:S(2)}) collective-permute-start(f32[128,2048]{1,0:T(8,128)S(1)} %add.229), channel_id=1, source_target_pairs={{1,0},{2,3},{5,4},{6,7},{9,8},{10,11},{13,12},{14,15},{17,16},{18,... | collective-permute-start | bytes 3145736 | tf_op jit(solution)/shard_map/ppermute | solution.py:21
  378.8 33.6 %collective-permute-start.43 = (f32[128,2048]{1,0:T(8,128)S(1)}, f32[128,2048]{1,0:T(8,128)S(1)}, u32[]{:S(2)}, u32[]{:S(2)}) collective-permute-start(f32[128,2048]{1,0:T(8,128)S(1)} %get-tuple-element.348), channel_id=1, source_target_pairs={{0,1},{3,2},{4,5},{7,6},{8,9},{11,10},{12,13},{15,14},{16,17},{19,... | collective-permute-start | bytes 3145736 | tf_op jit(solution)/shard_map/ppermute | solution.py:21
  383.6 28.8 %collective-permute-start.44 = (f32[128,2048]{1,0:T(8,128)S(1)}, f32[128,2048]{1,0:T(8,128)S(1)}, u32[]{:S(2)}, u32[]{:S(2)}) collective-permute-start(f32[128,2048]{1,0:T(8,128)S(1)} %get-tuple-element.349), channel_id=1, source_target_pairs={{1,2},{2,1},{5,6},{6,5},{9,10},{10,9},{13,14},{14,13},{17,18},{18,... | collective-permute-start | bytes 3145736 | tf_op jit(solution)/shard_map/ppermute | solution.py:21
  384.3 28.1 %collective-permute-start.45 = (f32[2,2048]{1,0:T(2,128)S(1)}, f32[2,2048]{1,0:T(2,128)S(1)}, u32[]{:S(2)}, u32[]{:S(2)}) collective-permute-start(f32[2,2048]{1,0:T(2,128)S(1)} %fusion.22), channel_id=1, source_target_pairs={{0,2},{1,3},{2,0},{3,1},{4,6},{5,7},{6,4},{7,5},{8,10},{9,11},{10,... | collective-permute-start | bytes 49160 | tf_op jit(solution)/shard_map/ppermute | solution.py:21
  416.1 23.6 %collective-permute-start.49 = (f32[2,2048]{1,0:T(2,128)S(1)}, f32[2,2048]{1,0:T(2,128)S(1)}, u32[]{:S(2)}, u32[]{:S(2)}) collective-permute-start(f32[2,2048]{1,0:T(2,128)S(1)} %fusion.104), channel_id=1, source_target_pairs={{0,4},{4,0},{8,12},{12,8},{16,20},{20,16},{24,28},{28,24},{1,5},{5... | collective-permute-start | bytes 49160 | tf_op jit(solution)/shard_map/ppermute | solution.py:21
  416.2 23.5 %collective-permute-start.47 = (f32[128,2048]{1,0:T(8,128)S(1)}, f32[128,2048]{1,0:T(8,128)S(1)}, u32[]{:S(2)}, u32[]{:S(2)}) collective-permute-start(f32[128,2048]{1,0:T(8,128)S(1)} %slice_add_fusion), channel_id=1, source_target_pairs={{1,2},{2,1},{5,6},{6,5},{9,10},{10,9},{13,14},{14,13},{17,18},{18,... | collective-permute-start | bytes 3145736 | tf_op jit(solution)/shard_map/ppermute | solution.py:21
  417.1 27.3 %collective-permute-start.48 = (f32[128,2048]{1,0:T(8,128)S(1)}, f32[128,2048]{1,0:T(8,128)S(1)}, u32[]{:S(2)}, u32[]{:S(2)}) collective-permute-start(f32[128,2048]{1,0:T(8,128)S(1)} %add.233), channel_id=1, source_target_pairs={{1,0},{2,3},{5,4},{6,7},{9,8},{10,11},{13,12},{14,15},{17,16},{18,... | collective-permute-start | bytes 3145736 | tf_op jit(solution)/shard_map/ppermute | solution.py:21
  444.5 29.3 %collective-permute-start.50 = (f32[128,2048]{1,0:T(8,128)S(1)}, f32[128,2048]{1,0:T(8,128)S(1)}, u32[]{:S(2)}, u32[]{:S(2)}) collective-permute-start(f32[128,2048]{1,0:T(8,128)S(1)} %add.236), channel_id=1, source_target_pairs={{1,0},{2,3},{5,4},{6,7},{9,8},{10,11},{13,12},{14,15},{17,16},{18,... | collective-permute-start | bytes 3145736 | tf_op jit(solution)/shard_map/ppermute | solution.py:21
  446.1 27.7 %collective-permute-start.51 = (f32[2,2048]{1,0:T(2,128)S(1)}, f32[2,2048]{1,0:T(2,128)S(1)}, u32[]{:S(2)}, u32[]{:S(2)}) collective-permute-start(f32[2,2048]{1,0:T(2,128)S(1)} %add.237), channel_id=1, source_target_pairs={{0,8},{4,12},{8,0},{12,4},{16,24},{20,28},{24,16},{28,20},{1,9},{5... | collective-permute-start | bytes 49160 | tf_op jit(solution)/shard_map/ppermute | solution.py:21
  446.4 27.5 %collective-permute-start.52 = (f32[2,2048]{1,0:T(2,128)S(1)}, f32[2,2048]{1,0:T(2,128)S(1)}, u32[]{:S(2)}, u32[]{:S(2)}) collective-permute-start(f32[2,2048]{1,0:T(2,128)S(1)} %add.237), channel_id=1, source_target_pairs={{0,16},{4,20},{8,24},{12,28},{16,0},{20,4},{24,8},{28,12},{1,17},{... | collective-permute-start | bytes 49160 | tf_op jit(solution)/shard_map/ppermute | solution.py:21
  446.9 27.0 %collective-permute-start.53 = (f32[2,2048]{1,0:T(2,128)S(1)}, f32[2,2048]{1,0:T(2,128)S(1)}, u32[]{:S(2)}, u32[]{:S(2)}) collective-permute-start(f32[2,2048]{1,0:T(2,128)S(1)} %add.237), channel_id=1, source_target_pairs={{0,24},{4,28},{8,16},{12,20},{16,8},{20,12},{24,0},{28,4},{1,25},{... | collective-permute-start | bytes 49160 | tf_op jit(solution)/shard_map/ppermute | solution.py:21
  (62 other events, 318.0 us)
Sparse Core Ops, SparseCore 0:
  65.6 87.3 all-reduce.5
  176.5 83.7 all-reduce.7
  339.2 138.1 all-reduce.9

commit v8 on v7

--- a/solution.py
+++ b/solution.py
@@ -227,6 +227,22 @@
         inverse_ref[:, span] = jnp.broadcast_to(valid / denom[head], (rows, DV))
 
 
+def share_kernel(heads, grad_ref, inverse_ref, mean_ref, sent_ref, denom_ref):
+    rows = grad_ref.shape[0]
+    vw = heads * DV
+    sent_ref[rows:, :] = jnp.zeros((sent_ref.shape[0] - rows, vw), f32)
+    for head in range(heads):
+        span = slice(head * DV, (head + 1) * DV)
+        numer = grad_ref[:, span] * inverse_ref[:, span]
+        sent_ref[:rows, span] = numer
+        product = numer * mean_ref[:, span]
+        denom_ref[:, span] = jnp.broadcast_to(
+            -jnp.sum(product, axis=1, keepdims=True), (rows, DV)
+        )
+        line, lane = rows + (head * rows) // vw, (head * rows) % vw
+        sent_ref[line : line + 1, lane : lane + rows] = -jnp.sum(product.T, axis=0, keepdims=True)
+
+
 def query_kernel(heads, shape, col_ref, row_ref, numer_ref, denom_ref, *refs):
     slots, (out_ref,) = split_refs(refs, shape)
     count = len(slots)
@@ -244,7 +260,7 @@
             near = 1.0 + dot_t(queries[head], keys)
             first = 2 * qk + head * DV
             value = read(slots[slot], None, slice(first, first + DV)).astype(bf16)
-            grad = dot_t(numer_ref[:, head * DV : (head + 1) * DV].astype(bf16), value)
+            grad = dot_t(numer_ref[:rows, head * DV : (head + 1) * DV].astype(bf16), value)
             grad = grad + denom_ref[:, head * DV : head * DV + 1]
             grad = jnp.where(allowed, grad * near, 0.0).astype(bf16)
             sums[head] = sums[head] + dot_n(grad, keys)
@@ -507,31 +523,37 @@
     resid_grad = cot_wide + norm_back(mid_grad, resid_mid, inv_mid, gain_two)
     out_lin_grad = resid_grad.astype(bf16)
     attended_grad = mm_t(out_lin_grad, w_out)
-    numer_grad = attended_grad * inverse
-    denom_grad = -jnp.sum((numer_grad * mean).reshape(rows, heads, DV), axis=-1)
-    denom_lines = denom_grad.T.reshape(rows // DV, vw)
-    denom_lines = jnp.pad(denom_lines, ((0, -denom_lines.shape[0] % 8), (0, 0)))
-    sent = jnp.concatenate([numer_grad, denom_lines])
+    extra = -(-rows // DV // 8) * 8
+    sent, denom_grad = whole_call(
+        functools.partial(share_kernel, heads),
+        (
+            jax.ShapeDtypeStruct((rows + extra, vw), f32),
+            jax.ShapeDtypeStruct((rows, vw), f32),
+        ),
+        attended_grad,
+        inverse,
+        mean,
+    )
     convoy.done = sent
     convoy.land(mid)
     grad_slots = {}
     grads = Chain(gather_steps(sent, grad_slots))
 
-    def query_work(numer_grad, denom_grad):
+    def query_work(sent, denom_grad):
         (query_lin_grad,) = whole_call(
             functools.partial(query_kernel, heads, shape),
             (jax.ShapeDtypeStruct((rows, qk), bf16),),
             columns,
             lines,
-            numer_grad,
-            jnp.repeat(denom_grad, DV, axis=1),
+            sent,
+            denom_grad,
             *qkv_parts,
             flops=cost,
         )
         return query_lin_grad
 
     convoy.launch(grads, mlp)
-    query_lin_grad = convoy.work(query_work, numer_grad, denom_grad)
+    query_lin_grad = convoy.work(query_work, sent, denom_grad)
     convoy.land(grads)
     out_part = convoy.wave([grads], t_mm, attended, out_lin_grad)
     convoy.launch(grads)

time: 507 us -> 500 us (0.986)
  other arithmetic: 45.6 us -> 39.7 us
    pallas_call x3 -> x4, Pallas kernels: 28.7 us -> 31.3 us  [whole_call(): pl.pallas_call(body, out_shape=outs, in_specs=[pl.BlockSpec(memory_space=...]
    unnamed x143 -> x124, local copies, waits for them, and re-layouts: 24.5 us -> 23.6 us
  transfers between devices with their start and end apart: 57 -> 57, of which waited for: 19 -> 19; matrix products, arithmetic and copies ran while one was open for 46% -> 45% of each run, Pallas kernels for 11% -> 11%
where the time goes in v8:
time: 500 us; the launch traced here: 491 us
  matrix products  178 us (36%)
  waiting for transfers between devices  103 us (21%)
  starting transfers between devices  57.6 us (12%)
  Pallas kernels  56.4 us (11%)
  other arithmetic  39.7 us (8%)
  local copies, waits for them, and re-layouts  39.6 us (8%)
  between operations  17.5 us (4%)
    dot_general x10, matrix products, t_mm(): return jnp.einsum('ca,cb->ab', left, right, preferred_element_type=f32)  71.9 us
    dot_general x11, matrix products, mm(): return jnp.dot(left, right, preferred_element_type=f32)  69.6 us
    ppermute x54, waiting for transfers between devices, hop(): return lax.ppermute(value, axis, way)  66.6 us
    ppermute x54, starting transfers between devices, hop(): return lax.ppermute(value, axis, way)  57.5 us
    psum x2, waiting for transfers between devices, sum_head(): return lax.psum(value, 'head')  36.1 us
    dot_general x9, matrix products, mm_t(): return jnp.einsum('ac,bc->ab', left, right, preferred_element_type=f32)  36.1 us
    pallas_call x4, Pallas kernels, whole_call(): pl.pallas_call(body, out_shape=outs, in_specs=[pl.BlockSpec(memory_space=...  31.3 us
    pallas_call x4, Pallas kernels, join_rounded(): pl.pallas_call(functools.partial(join_kernel, tuple((len(slot) for slot i...  25.1 us
  transfers between devices with their start and end apart: 57, of which 19 were waited for; matrix products, arithmetic and copies ran while one was open for 45% of the time, Pallas kernels for 11%

profile of v8, /device:TPU:0, one launch (start us, length us, event | category | flops | bytes accessed | tf_op | source)
XLA Modules:
  0.0 491.2 jit_solution(17691412995295190082)
XLA Ops:
  8.1 1.6 fusion.2
  14.1 2.9 collective-permute-start
  21.8 2.8 convert_element_type.125.refs_0_
  26.6 5.5 %collective-permute-done.refs_2_ = f32[256,640]{1,0:T(8,128)} collective-permute-done((f32[256,640]{1,0:T(8,128)}, f32[256,640]{1,0:T(8,128)}, u32[]{:S(2)}, u32[]{:S(2)}) %collective-permute-start) | collective-permute-done | bytes 655392 | tf_op jit(solution)/shard_map/ppermute | solution.py:21
  38.2 7.6 %collective-permute-done.3.refs_6_ = f32[128,640]{1,0:T(8,128)S(1)} collective-permute-done((f32[128,640]{1,0:T(8,128)S(1)}, f32[128,640]{1,0:T(8,128)S(1)}, u32[]{:S(2)}, u32[]{:S(2)}) %collective-permute-start.3) | collective-permute-done | bytes 327712 | tf_op jit(solution)/shard_map/ppermute | solution.py:21
  51.8 7.9 %shard_map.203 = (bf16[256,512]{1,0:T(8,128)(2,1)}, f32[256,512]{1,0:T(8,128)}, f32[256,512]{1,0:T(8,128)}) custom-call(s32[256,4]{1,0:T(8,128)} %copy.27.col_ref, s32[24,256]{1,0:T(8,128)} %pad_add_fusion.row_ref, f32[256,640]{1,0:T(8,128)} %pad_maximum_fusion.1.refs_0_, f32[256,640]{1,0:T(8,128)} %collective-permute-done.2.refs_1_, ...), custom_call_target="tpu_custom_call" | custom-call | flops 2147483648 | bytes 6582272 | tf_op jit(solution)/shard_map/pallas_call | solution.py:314
  59.7 3.0 fusion.30
  62.7 2.8 convert_element_type.126
  65.5 5.7 %fusion.31 = f32[256,1376]{0,1:T(8,128)} fusion(bf16[256,2048]{1,0:T(8,128)(2,1)} %param.23, bf16[1376,2048]{1,0:T(8,128)(2,1)} %param.21), kind=kOutput, calls=%fused_computation.88 | convolution fusion | flops 1442840576 | bytes 8093696 | tf_op jit(solution)/shard_map/ac,bc->ab/dot_general | solution.py:370
  71.2 26.3 %collective-permute-done.10.refs_3_ = f32[256,2048]{1,0:T(8,128)} collective-permute-done((f32[256,2048]{1,0:T(8,128)}, f32[256,2048]{1,0:T(8,128)}, u32[]{:S(2)}, u32[]{:S(2)}) %collective-permute-start.10) | collective-permute-done | bytes 2097184 | tf_op jit(solution)/shard_map/ppermute | solution.py:21
  98.8 2.3 slice.48
  101.1 2.3 slice.49
  106.1 6.3 %shard_map.204 = bf16[1024,2048]{1,0:T(8,128)(2,1)} custom-call(f32[1,2048]{1,0:T(1,128)} %broadcast_12_scale_ref.2.scale_ref, f32[256,2048]{1,0:T(8,128)} %convert_element_type.125.refs_0_, f32[256,2048]{1,0:T(8,128)} %collective-permute-done.11.refs_1_, f32[256,2048]{1,0:T(8,128)} %collective-permute-done.9.refs_2_, ...), custom_call_target="tpu_custom_call" | custom-call | bytes 12582912 | tf_op jit(solution)/shard_map/pallas_call | solution.py:341
  112.4 11.0 %fusion.32 = f32[1024,1376]{0,1:T(8,128)} fusion(bf16[1024,2048]{1,0:T(8,128)(2,1)} %shard_map.204, bf16[1376,2048]{1,0:T(8,128)(2,1)} %param.21), kind=kOutput, calls=%fused_computation.89 | convolution fusion | flops 5771362304 | bytes 15466496 | tf_op jit(solution)/shard_map/ac,bc->ab/dot_general | solution.py:370
  123.4 29.6 %all-reduce.5.cloned.1.call-done = f32[256,2048]{1,0:T(8,128)} async-done(((f32[256,2048]{1,0:T(8,128)}), f32[256,2048]{1,0:T(8,128)}) %all-reduce.5.cloned.1.call-update) | async-done | bytes 2097168 | tf_op jit(solution)/shard_map/psum | solution.py:159
  153.0 2.5 multiply_reduce_fusion.4
  161.2 5.1 %fusion.11 = f32[256,1376]{0,1:T(8,128)S(1)} fusion(bf16[2048,1376]{0,1:T(8,128)(2,1)} %param.19, f32[256,2048]{1,0:T(8,128)} %broadcast_multiply_fusion.refs_0_, f32[2048]{0:T(1024)S(1)} %convert_element_type.127), kind=kOutput, calls=%fused_computation.48 | convolution fusion | flops 1443889152 | bytes 9150464 | tf_op jit(solution)/shard_map/dot_general | solution.py:366
  166.3 4.5 multiply_convert_fusion.9
  170.9 2.2 fusion.6
  173.1 3.2 convolution_add_fusion.5
  176.4 6.1 %fusion.33 = f32[256,2048]{1,0:T(8,128)} fusion(bf16[256,1376]{0,1:T(8,128)(2,1)} %get-tuple-element.249, bf16[1376,2048]{1,0:T(8,128)(2,1)} %param.21), kind=kOutput, calls=%fused_computation.90 | convolution fusion | flops 1442840576 | bytes 8437760 | tf_op jit(solution)/shard_map/dot_general | solution.py:366
  182.4 6.4 %shard_map.205 = bf16[1024,2048]{1,0:T(8,128)(2,1)} custom-call(f32[1,2048]{1,0:T(1,128)} %broadcast_12_scale_ref.2.scale_ref, f32[256,2048]{1,0:T(8,128)} %collective-permute-done.14.refs_0_, f32[256,2048]{1,0:T(8,128)} %collective-permute-done.15.refs_1_, f32[128,2048]{1,0:T(8,128)} %collective-permute-done.12.refs_2_, ...), custom_call_target="tpu_custom_call" | custom-call | bytes 12582912 | tf_op jit(solution)/shard_map/pallas_call | solution.py:341
  188.8 10.9 %fusion.34 = f32[1024,1376]{0,1:T(8,128)} fusion(bf16[1024,2048]{1,0:T(8,128)(2,1)} %shard_map.205, bf16[1376,2048]{1,0:T(8,128)(2,1)} %param.21), kind=kOutput, calls=%fused_computation.91 | convolution fusion | flops 5771362304 | bytes 15466496 | tf_op jit(solution)/shard_map/ac,bc->ab/dot_general | solution.py:370
  199.7 6.5 %collective-permute-done.16.refs_2_ = f32[256,2048]{1,0:T(8,128)} collective-permute-done((f32[256,2048]{1,0:T(8,128)}, f32[256,2048]{1,0:T(8,128)}, u32[]{:S(2)}, u32[]{:S(2)}) %collective-permute-start.16) | collective-permute-done | bytes 2097184 | tf_op jit(solution)/shard_map/ppermute | solution.py:21
  207.4 2.3 slice.50
  209.7 2.3 slice.51
  214.6 6.2 %shard_map.206 = bf16[1024,2048]{1,0:T(8,128)(2,1)} custom-call(f32[1,2048]{1,0:T(1,128)} %bitcast.73, f32[256,2048]{1,0:T(8,128)} %broadcast_multiply_fusion.refs_0_, f32[256,2048]{1,0:T(8,128)} %collective-permute-done.18.refs_1_, f32[256,2048]{1,0:T(8,128)} %collective-permute-done.16.refs_2_, f32[256,2048]{1,0:T(8,128)} %collective-permute-done.17.refs_3_), custom_call_target="tpu_custom_call" | custom-call | bytes 12582912 | tf_op jit(solution)/shard_map/pallas_call | solution.py:341
  220.7 11.3 %fusion.35 = f32[1024,1376]{0,1:T(8,128)} fusion(bf16[1024,2048]{1,0:T(8,128)(2,1)} %shard_map.206, bf16[2048,1376]{0,1:T(8,128)(2,1)} %param.19), kind=kOutput, calls=%fused_computation.92 | convolution fusion | flops 5771362304 | bytes 15466496 | tf_op jit(solution)/shard_map/dot_general | solution.py:366
  232.1 12.7 %multiply_convert_fusion.3 = (bf16[1024,1376]{0,1:T(8,128)(2,1)}, bf16[1024,1376]{0,1:T(8,128)(2,1)}, bf16[1024,1376]{0,1:T(8,128)(2,1)S(1)}) fusion(f32[1024,1376]{0,1:T(8,128)} %fusion.32, f32[1024,1376]{0,1:T(8,128)} %fusion.35, bf16[1024,2048]{1,0:T(8,128)(2,1)S(1)} %copy-done.15, bf16[2048,1376]{0,1:T(8,128)(2,1)S(1)} %bitcast.68), kind=kOutput, calls=%fused_computation.8 | convolution fusion | flops 5792497664 | bytes 29556736 | tf_op jit(solution)/shard_map/dot_general | solution.py:366
  244.8 8.9 %fusion.36 = f32[1376,2048]{1,0:T(8,128)} fusion(bf16[1024,1376]{0,1:T(8,128)(2,1)S(1)} %get-tuple-element.278, bf16[1024,2048]{1,0:T(8,128)(2,1)S(1)} %copy-done.18), kind=kOutput, calls=%fused_computation.93 | convolution fusion | flops 5771362304 | bytes 18284544 | tf_op jit(solution)/shard_map/ca,cb->ab/dot_general | solution.py:374
  253.7 6.5 %all-reduce.7.cloned.1.call-done = f32[256,2048]{1,0:T(8,128)} async-done(((f32[256,2048]{1,0:T(8,128)}), f32[256,2048]{1,0:T(8,128)}) %all-reduce.7.cloned.1.call-update) | async-done | bytes 2097168 | tf_op jit(solution)/shard_map/psum | solution.py:159
  260.3 2.7 multiply_reduce_fusion.3
  263.8 2.8 multiply_reduce_fusion.1
  268.2 2.7 shard_map.207
  275.0 2.9 collective-permute-start.34
  278.0 9.4 %shard_map.208 = bf16[256,64]{1,0:T(8,128)(2,1)} custom-call(s32[256,4]{1,0:T(8,128)} %copy.27.col_ref, s32[24,256]{1,0:T(8,128)} %pad_add_fusion.row_ref, f32[264,512]{1,0:T(8,128)} %get-tuple-element.318.numer_ref.refs_10_, f32[256,512]{1,0:T(8,128)} %get-tuple-element.294.denom_ref, f32[256,640]{1,0:T(8,128)} %pad_maximum_fusion.1.refs_0_, ...), custom_call_target="tpu_custom_call" | custom-call | flops 2147483648 | bytes 6369280 | tf_op jit(solution)/shard_map/pallas_call | solution.py:314
  289.9 2.7 fusion.38
  292.6 5.0 %collective-permute-done.28.refs_16_ = f32[128,512]{1,0:T(8,128)} collective-permute-done((f32[128,512]{1,0:T(8,128)S(1)}, f32[128,512]{1,0:T(8,128)}, u32[]{:S(2)}, u32[]{:S(2)}) %collective-permute-start.28) | collective-permute-done | bytes 262176 | tf_op jit(solution)/shard_map/ppermute | solution.py:21
  301.2 2.8 slice_add_fusion.3
  304.5 4.6 collective-permute-start.37
  309.1 1.9 collective-permute-start.38
  310.9 11.3 %shard_map.209 = (bf16[256,64]{1,0:T(8,128)(2,1)}, bf16[256,512]{1,0:T(8,128)(2,1)}) custom-call(s32[256,4]{1,0:T(8,128)} %copy.27.col_ref, s32[24,256]{1,0:T(8,128)} %pad_add_fusion.row_ref, f32[256,640]{1,0:T(8,128)} %pad_maximum_fusion.1.refs_0_, f32[256,640]{1,0:T(8,128)} %collective-permute-done.2.refs_1_, f32[256,640]{1,0:T(8,128)} %collective-permute-done.refs_2_, ...), custom_call_target="tpu_custom_call" | custom-call | flops 4294967296 | bytes 9891840 | tf_op jit(solution)/shard_map/pallas_call | solution.py:314
  322.3 3.7 fusion.41
  334.3 1.8 add.224
  340.0 3.6 collective-permute-start.40
  343.7 3.2 collective-permute-start.39
  347.0 6.3 %shard_map.210 = bf16[1024,2048]{1,0:T(8,128)(2,1)} custom-call(f32[1,2048]{1,0:T(1,128)} %bitcast.74, f32[256,2048]{1,0:T(8,128)} %collective-permute-done.23.refs_0_, f32[256,2048]{1,0:T(8,128)} %collective-permute-done.24.refs_1_, f32[128,2048]{1,0:T(8,128)} %collective-permute-done.21.refs_2_, f32[128,2048]{1,0:T(8,128)} %collective-permute-done.22.refs_3_, ...), custom_call_target="tpu_custom_call" | custom-call | bytes 12582912 | tf_op jit(solution)/shard_map/pallas_call | solution.py:341
  353.3 11.3 %fusion.43 = f32[1024,1376]{0,1:T(8,128)} fusion(bf16[1024,2048]{1,0:T(8,128)(2,1)} %shard_map.210, bf16[2048,1376]{0,1:T(8,128)(2,1)} %param.19), kind=kOutput, calls=%fused_computation.100 | convolution fusion | flops 5771362304 | bytes 15466496 | tf_op jit(solution)/shard_map/dot_general | solution.py:366
  372.3 4.8 collective-permute-start.43
  377.9 2.0 collective-permute-start.45
  379.9 14.0 %multiply_convert_fusion = (bf16[1024,1376]{0,1:T(8,128)(2,1)}, bf16[1024,1376]{0,1:T(8,128)(2,1)}, bf16[1024,1376]{0,1:T(8,128)(2,1)}) fusion(f32[1024,1376]{0,1:T(8,128)} %fusion.34, f32[1024,1376]{0,1:T(8,128)} %fusion.43, bf16[1024,2048]{1,0:T(8,128)(2,1)} %shard_map.210, bf16[2048,1376]{0,1:T(8,128)(2,1)S(1)} %bitcast.70), kind=kOutput, calls=%fused_computation.3 | convolution fusion | flops 5792497664 | bytes 29556736 | tf_op jit(solution)/shard_map/dot_general | solution.py:366
  394.0 10.4 %fusion.44 = f32[2048,1376]{0,1:T(8,128)} fusion(bf16[1024,1376]{0,1:T(8,128)(2,1)} %get-tuple-element.359, bf16[1024,2048]{1,0:T(8,128)(2,1)S(1)} %copy-done.16), kind=kOutput, calls=%fused_computation.101 | convolution fusion | flops 5771362304 | bytes 18284544 | tf_op jit(solution)/shard_map/ca,cb->ab/dot_general | solution.py:374
  410.5 1.6 collective-permute-start.48
  412.1 12.2 %convolution_add_fusion.2 = f32[1376,2048]{1,0:T(8,128)} fusion(f32[1376,2048]{1,0:T(8,128)} %fusion.36, bf16[1024,1376]{0,1:T(8,128)(2,1)} %get-tuple-element.367, bf16[1024,2048]{1,0:T(8,128)(2,1)S(1)} %copy-done.14), kind=kOutput, calls=%fused_computation.2 | convolution fusion | flops 5774180352 | bytes 29556736 | tf_op jit(solution)/shard_map/ca,cb->ab/dot_general | solution.py:374
  424.3 8.7 %fusion.45 = f32[2048,1376]{0,1:T(8,128)} fusion(bf16[1024,1376]{0,1:T(8,128)(2,1)S(1)} %copy-done.49, bf16[1024,2048]{1,0:T(8,128)(2,1)S(1)} %copy-done.16), kind=kOutput, calls=%fused_computation.102 | convolution fusion | flops 5771362304 | bytes 18284544 | tf_op jit(solution)/shard_map/ca,cb->ab/dot_general | solution.py:374
  433.3 4.5 collective-permute-done.48
  440.4 2.7 collective-permute-start.53
  444.3 11.5 %convolution_add_fusion.1 = f32[2048,1376]{0,1:T(8,128)} fusion(f32[2048,1376]{0,1:T(8,128)} %fusion.45, bf16[1024,1376]{0,1:T(8,128)(2,1)S(1)} %copy-done.51, bf16[1024,2048]{1,0:T(8,128)(2,1)S(1)} %copy-done.17), kind=kOutput, calls=%fused_computation.1 | convolution fusion | flops 5774180352 | bytes 29556736 | tf_op jit(solution)/shard_map/ca,cb->ab/dot_general | solution.py:374
  455.9 11.4 %convolution_add_fusion = f32[2048,1376]{0,1:T(8,128)} fusion(f32[2048,1376]{0,1:T(8,128)} %fusion.44, bf16[1024,1376]{0,1:T(8,128)(2,1)S(1)} %copy-done.50, bf16[1024,2048]{1,0:T(8,128)(2,1)S(1)} %copy-done.17), kind=kOutput, calls=%fused_computation | convolution fusion | flops 5774180352 | bytes 29556736 | tf_op jit(solution)/shard_map/ca,cb->ab/dot_general | solution.py:374
  469.4 2.7 multiply_add_fusion.2
  472.8 1.9 copy.38
  474.6 1.9 copy.39
  476.5 4.8 copy.40
  481.3 2.1 copy.41
  (276 shorter events, 82.4 us)
Async XLA Ops:
  7.2 52.5 %copy-start = (bf16[512,2048]{1,0:T(8,128)(2,1)S(1)}, bf16[512,2048]{1,0:T(8,128)(2,1)}, u32[]{:S(2)}) copy-start(bf16[512,2048]{1,0:T(8,128)(2,1)} %param.17) | copy-start | bytes 6291460
  7.2 145.8 %all-reduce.5.cloned.1.call-start = ((), (), s32[]{:S(2)}) async-start(), calls=%async_computation | async-start | bytes 4194304 | tf_op jit(solution)/shard_map/psum | solution.py:159
  14.1 18.0 %collective-permute-start = (f32[256,640]{1,0:T(8,128)}, f32[256,640]{1,0:T(8,128)}, u32[]{:S(2)}, u32[]{:S(2)}) collective-permute-start(f32[256,640]{1,0:T(8,128)} %pad_maximum_fusion.1.refs_0_), channel_id=1, source_target_pairs={{0,8},{4,12},{8,0},{12,4},{16,24},{20,28},{24,16},{28,20},{1,9},{5... | collective-permute-start | bytes 1966088 | tf_op jit(solution)/shard_map/ppermute | solution.py:21
  17.0 16.5 %collective-permute-start.1 = (f32[256,640]{1,0:T(8,128)}, f32[256,640]{1,0:T(8,128)}, u32[]{:S(2)}, u32[]{:S(2)}) collective-permute-start(f32[256,640]{1,0:T(8,128)} %pad_maximum_fusion.1.refs_0_), channel_id=1, source_target_pairs={{0,16},{4,20},{8,24},{12,28},{16,0},{20,4},{24,8},{28,12},{1,17},{... | collective-permute-start | bytes 1966088 | tf_op jit(solution)/shard_map/ppermute | solution.py:21
  18.6 15.0 %collective-permute-start.2 = (f32[256,640]{1,0:T(8,128)}, f32[256,640]{1,0:T(8,128)}, u32[]{:S(2)}, u32[]{:S(2)}) collective-permute-start(f32[256,640]{1,0:T(8,128)} %pad_maximum_fusion.1.refs_0_), channel_id=1, source_target_pairs={{0,4},{4,0},{8,12},{12,8},{16,20},{20,16},{24,28},{28,24},{1,5},{5... | collective-permute-start | bytes 1966088 | tf_op jit(solution)/shard_map/ppermute | solution.py:21
  21.8 30.0 %copy-start.42 = (bf16[2048]{0:T(1024)(128)(2,1)S(1)}, bf16[2048]{0:T(1024)(128)(2,1)}, u32[]{:S(2)}) copy-start(bf16[2048]{0:T(1024)(128)(2,1)} %param.18) | copy-start | bytes 12292
  35.5 11.5 %collective-permute-start.5 = (f32[256,640]{1,0:T(8,128)}, f32[256,640]{1,0:T(8,128)}, u32[]{:S(2)}, u32[]{:S(2)}) collective-permute-start(f32[256,640]{1,0:T(8,128)} %collective-permute-done.refs_2_), channel_id=1, source_target_pairs={{0,4},{4,0},{8,12},{12,8},{16,20},{20,16},{24,28},{28,24},{1,5},{5... | collective-permute-start | bytes 1966088 | tf_op jit(solution)/shard_map/ppermute | solution.py:21
  35.6 11.4 %collective-permute-start.6 = (f32[256,640]{1,0:T(8,128)}, f32[256,640]{1,0:T(8,128)}, u32[]{:S(2)}, u32[]{:S(2)}) collective-permute-start(f32[256,640]{1,0:T(8,128)} %collective-permute-done.1.refs_4_), channel_id=1, source_target_pairs={{0,4},{4,0},{8,12},{12,8},{16,20},{20,16},{24,28},{28,24},{1,5},{5... | collective-permute-start | bytes 1966088 | tf_op jit(solution)/shard_map/ppermute | solution.py:21
  36.1 9.7 %collective-permute-start.3 = (f32[128,640]{1,0:T(8,128)S(1)}, f32[128,640]{1,0:T(8,128)S(1)}, u32[]{:S(2)}, u32[]{:S(2)}) collective-permute-start(f32[128,640]{1,0:T(8,128)S(1)} %slice.46), channel_id=1, source_target_pairs={{0,16},{4,20},{8,24},{12,28},{16,0},{20,4},{24,8},{28,12},{1,17},{... | collective-permute-start | bytes 983048 | tf_op jit(solution)/shard_map/ppermute | solution.py:21
  37.6 9.4 %collective-permute-start.4 = (f32[128,640]{1,0:T(8,128)S(1)}, f32[128,640]{1,0:T(8,128)S(1)}, u32[]{:S(2)}, u32[]{:S(2)}) collective-permute-start(f32[128,640]{1,0:T(8,128)S(1)} %slice.47), channel_id=1, source_target_pairs={{0,8},{4,12},{8,0},{12,4},{16,24},{20,28},{24,16},{28,20},{1,9},{5... | collective-permute-start | bytes 983048 | tf_op jit(solution)/shard_map/ppermute | solution.py:21
  47.1 1.7 collective-permute-start.7
  47.2 2.1 collective-permute-start.8
  49.5 48.0 %collective-permute-start.10 = (f32[256,2048]{1,0:T(8,128)}, f32[256,2048]{1,0:T(8,128)}, u32[]{:S(2)}, u32[]{:S(2)}) collective-permute-start(f32[256,2048]{1,0:T(8,128)} %convert_element_type.125.refs_0_), channel_id=1, source_target_pairs={{0,16},{4,20},{8,24},{12,28},{16,0},{20,4},{24,8},{28,12},{1,17},{... | collective-permute-start | bytes 6291464 | tf_op jit(solution)/shard_map/ppermute | solution.py:21
  50.4 47.1 %collective-permute-start.11 = (f32[256,2048]{1,0:T(8,128)}, f32[256,2048]{1,0:T(8,128)}, u32[]{:S(2)}, u32[]{:S(2)}) collective-permute-start(f32[256,2048]{1,0:T(8,128)} %convert_element_type.125.refs_0_), channel_id=1, source_target_pairs={{0,4},{4,0},{8,12},{12,8},{16,20},{20,16},{24,28},{28,24},{1,5},{5... | collective-permute-start | bytes 6291464 | tf_op jit(solution)/shard_map/ppermute | solution.py:21
  50.4 48.4 %collective-permute-start.9 = (f32[256,2048]{1,0:T(8,128)}, f32[256,2048]{1,0:T(8,128)}, u32[]{:S(2)}, u32[]{:S(2)}) collective-permute-start(f32[256,2048]{1,0:T(8,128)} %convert_element_type.125.refs_0_), channel_id=1, source_target_pairs={{0,8},{4,12},{8,0},{12,4},{16,24},{20,28},{24,16},{28,20},{1,9},{5... | collective-permute-start | bytes 6291464 | tf_op jit(solution)/shard_map/ppermute | solution.py:21
  51.8 114.5 %copy-start.30 = (f32[2048]{0:T(1024)}, f32[2048]{0:T(1024)S(1)}, u32[]{:S(2)}) copy-start(f32[2048]{0:T(1024)S(1)} %convert_element_type.127) | copy-start | bytes 24580
  65.5 194.8 %all-reduce.7.cloned.1.call-start = ((), (), s32[]{:S(2)}) async-start(), calls=%async_computation.1 | async-start | bytes 4194304 | tf_op jit(solution)/shard_map/psum | solution.py:159
  103.4 54.2 %collective-permute-start.14 = (f32[256,2048]{1,0:T(8,128)}, f32[256,2048]{1,0:T(8,128)}, u32[]{:S(2)}, u32[]{:S(2)}) collective-permute-start(f32[256,2048]{1,0:T(8,128)} %collective-permute-done.9.refs_2_), channel_id=1, source_target_pairs={{0,4},{4,0},{8,12},{12,8},{16,20},{20,16},{24,28},{28,24},{1,5},{5... | collective-permute-start | bytes 6291464 | tf_op jit(solution)/shard_map/ppermute | solution.py:21
  103.4 54.3 %collective-permute-start.15 = (f32[256,2048]{1,0:T(8,128)}, f32[256,2048]{1,0:T(8,128)}, u32[]{:S(2)}, u32[]{:S(2)}) collective-permute-start(f32[256,2048]{1,0:T(8,128)} %collective-permute-done.10.refs_3_), channel_id=1, source_target_pairs={{0,4},{4,0},{8,12},{12,8},{16,20},{20,16},{24,28},{28,24},{1,5},{5... | collective-permute-start | bytes 6291464 | tf_op jit(solution)/shard_map/ppermute | solution.py:21
  103.9 53.7 %collective-permute-start.12 = (f32[128,2048]{1,0:T(8,128)}, f32[128,2048]{1,0:T(8,128)}, u32[]{:S(2)}, u32[]{:S(2)}) collective-permute-start(f32[128,2048]{1,0:T(8,128)} %slice.48), channel_id=1, source_target_pairs={{0,16},{4,20},{8,24},{12,28},{16,0},{20,4},{24,8},{28,12},{1,17},{... | collective-permute-start | bytes 3145736 | tf_op jit(solution)/shard_map/ppermute | solution.py:21
  105.0 52.6 %collective-permute-start.13 = (f32[128,2048]{1,0:T(8,128)}, f32[128,2048]{1,0:T(8,128)}, u32[]{:S(2)}, u32[]{:S(2)}) collective-permute-start(f32[128,2048]{1,0:T(8,128)} %slice.49), channel_id=1, source_target_pairs={{0,8},{4,12},{8,0},{12,4},{16,24},{20,28},{24,16},{28,20},{1,9},{5... | collective-permute-start | bytes 3145736 | tf_op jit(solution)/shard_map/ppermute | solution.py:21
  157.7 18.7 %collective-permute-start.19 = (f32[128,2048]{1,0:T(8,128)}, f32[128,2048]{1,0:T(8,128)}, u32[]{:S(2)}, u32[]{:S(2)}) collective-permute-start(f32[128,2048]{1,0:T(8,128)} %collective-permute-done.12.refs_2_), channel_id=1, source_target_pairs={{0,4},{4,0},{8,12},{12,8},{16,20},{20,16},{24,28},{28,24},{1,5},{5... | collective-permute-start | bytes 3145736 | tf_op jit(solution)/shard_map/ppermute | solution.py:21
  157.8 18.6 %collective-permute-start.20 = (f32[128,2048]{1,0:T(8,128)}, f32[128,2048]{1,0:T(8,128)}, u32[]{:S(2)}, u32[]{:S(2)}) collective-permute-start(f32[128,2048]{1,0:T(8,128)} %collective-permute-done.13.refs_3_), channel_id=1, source_target_pairs={{0,4},{4,0},{8,12},{12,8},{16,20},{20,16},{24,28},{28,24},{1,5},{5... | collective-permute-start | bytes 3145736 | tf_op jit(solution)/shard_map/ppermute | solution.py:21
  158.3 47.9 %collective-permute-start.16 = (f32[256,2048]{1,0:T(8,128)}, f32[256,2048]{1,0:T(8,128)}, u32[]{:S(2)}, u32[]{:S(2)}) collective-permute-start(f32[256,2048]{1,0:T(8,128)} %broadcast_multiply_fusion.refs_0_), channel_id=1, source_target_pairs={{0,8},{4,12},{8,0},{12,4},{16,24},{20,28},{24,16},{28,20},{1,9},{5... | collective-permute-start | bytes 6291464 | tf_op jit(solution)/shard_map/ppermute | solution.py:21
  159.7 47.6 %collective-permute-start.17 = (f32[256,2048]{1,0:T(8,128)}, f32[256,2048]{1,0:T(8,128)}, u32[]{:S(2)}, u32[]{:S(2)}) collective-permute-start(f32[256,2048]{1,0:T(8,128)} %broadcast_multiply_fusion.refs_0_), channel_id=1, source_target_pairs={{0,16},{4,20},{8,24},{12,28},{16,0},{20,4},{24,8},{28,12},{1,17},{... | collective-permute-start | bytes 6291464 | tf_op jit(solution)/shard_map/ppermute | solution.py:21
  161.2 46.2 %collective-permute-start.18 = (f32[256,2048]{1,0:T(8,128)}, f32[256,2048]{1,0:T(8,128)}, u32[]{:S(2)}, u32[]{:S(2)}) collective-permute-start(f32[256,2048]{1,0:T(8,128)} %broadcast_multiply_fusion.refs_0_), channel_id=1, source_target_pairs={{0,4},{4,0},{8,12},{12,8},{16,20},{20,16},{24,28},{28,24},{1,5},{5... | collective-permute-start | bytes 6291464 | tf_op jit(solution)/shard_map/ppermute | solution.py:21
  176.3 295.8 %all-reduce.9.cloned.1.call-start = ((), (), s32[]{:S(2)}) async-start(), calls=%async_computation.2 | async-start | bytes 18874368 | tf_op jit(solution)/shard_map/psum | solution.py:584
  212.0 58.9 %collective-permute-start.23 = (f32[256,2048]{1,0:T(8,128)}, f32[256,2048]{1,0:T(8,128)}, u32[]{:S(2)}, u32[]{:S(2)}) collective-permute-start(f32[256,2048]{1,0:T(8,128)} %collective-permute-done.16.refs_2_), channel_id=1, source_target_pairs={{0,4},{4,0},{8,12},{12,8},{16,20},{20,16},{24,28},{28,24},{1,5},{5... | collective-permute-start | bytes 6291464 | tf_op jit(solution)/shard_map/ppermute | solution.py:21
  212.0 58.9 %collective-permute-start.24 = (f32[256,2048]{1,0:T(8,128)}, f32[256,2048]{1,0:T(8,128)}, u32[]{:S(2)}, u32[]{:S(2)}) collective-permute-start(f32[256,2048]{1,0:T(8,128)} %collective-permute-done.17.refs_3_), channel_id=1, source_target_pairs={{0,4},{4,0},{8,12},{12,8},{16,20},{20,16},{24,28},{28,24},{1,5},{5... | collective-permute-start | bytes 6291464 | tf_op jit(solution)/shard_map/ppermute | solution.py:21
  212.5 58.4 %collective-permute-start.21 = (f32[128,2048]{1,0:T(8,128)}, f32[128,2048]{1,0:T(8,128)}, u32[]{:S(2)}, u32[]{:S(2)}) collective-permute-start(f32[128,2048]{1,0:T(8,128)} %slice.50), channel_id=1, source_target_pairs={{0,16},{4,20},{8,24},{12,28},{16,0},{20,4},{24,8},{28,12},{1,17},{... | collective-permute-start | bytes 3145736 | tf_op jit(solution)/shard_map/ppermute | solution.py:21
  214.0 56.9 %collective-permute-start.22 = (f32[128,2048]{1,0:T(8,128)}, f32[128,2048]{1,0:T(8,128)}, u32[]{:S(2)}, u32[]{:S(2)}) collective-permute-start(f32[128,2048]{1,0:T(8,128)} %slice.51), channel_id=1, source_target_pairs={{0,8},{4,12},{8,0},{12,4},{16,24},{20,28},{24,16},{28,20},{1,9},{5... | collective-permute-start | bytes 3145736 | tf_op jit(solution)/shard_map/ppermute | solution.py:21
  214.6 17.5 %slice-start.2 = ((s8[5636096]{0:T(1024)(128)(4,1)}), s8[1441792]{0:T(1024)(128)(4,1)S(1)}, s32[]{:S(2)}) async-start(s8[5636096]{0:T(1024)(128)(4,1)} %bitcast.67), calls=%async_computation.5 | async-start | bytes 2883584
  270.9 16.4 %collective-permute-start.25 = (f32[264,512]{1,0:T(8,128)}, f32[264,512]{1,0:T(8,128)S(1)}, u32[]{:S(2)}, u32[]{:S(2)}) collective-permute-start(f32[264,512]{1,0:T(8,128)} %get-tuple-element.318.numer_ref.refs_10_), channel_id=1, source_target_pairs={{0,8},{4,12},{8,0},{12,4},{16,24},{20,28},{24,16},{28,20},{1,9},{5... | collective-permute-start | bytes 1622024 | tf_op jit(solution)/shard_map/ppermute | solution.py:21
  272.5 14.8 %collective-permute-start.26 = (f32[264,512]{1,0:T(8,128)}, f32[264,512]{1,0:T(8,128)S(1)}, u32[]{:S(2)}, u32[]{:S(2)}) collective-permute-start(f32[264,512]{1,0:T(8,128)} %get-tuple-element.318.numer_ref.refs_10_), channel_id=1, source_target_pairs={{0,16},{4,20},{8,24},{12,28},{16,0},{20,4},{24,8},{28,12},{1,17},{... | collective-permute-start | bytes 1622024 | tf_op jit(solution)/shard_map/ppermute | solution.py:21
  273.9 13.4 %collective-permute-start.27 = (f32[264,512]{1,0:T(8,128)}, f32[264,512]{1,0:T(8,128)}, u32[]{:S(2)}, u32[]{:S(2)}) collective-permute-start(f32[264,512]{1,0:T(8,128)} %get-tuple-element.318.numer_ref.refs_10_), channel_id=1, source_target_pairs={{0,4},{4,0},{8,12},{12,8},{16,20},{20,16},{24,28},{28,24},{1,5},{5... | collective-permute-start | bytes 1622024 | tf_op jit(solution)/shard_map/ppermute | solution.py:21
  275.0 25.4 %collective-permute-start.34 = (f32[128,2048]{1,0:T(8,128)}, f32[128,2048]{1,0:T(8,128)}, u32[]{:S(2)}, u32[]{:S(2)}) collective-permute-start(f32[128,2048]{1,0:T(8,128)} %split.16), channel_id=1, source_target_pairs={{0,1},{3,2},{4,5},{7,6},{8,9},{11,10},{12,13},{15,14},{16,17},{19,... | collective-permute-start | bytes 3145736 | tf_op jit(solution)/shard_map/ppermute | solution.py:21
  288.2 9.5 %collective-permute-start.30 = (f32[264,512]{1,0:T(8,128)}, f32[264,512]{1,0:T(8,128)S(1)}, u32[]{:S(2)}, u32[]{:S(2)}) collective-permute-start(f32[264,512]{1,0:T(8,128)} %copy-done.38), channel_id=1, source_target_pairs={{0,4},{4,0},{8,12},{12,8},{16,20},{20,16},{24,28},{28,24},{1,5},{5... | collective-permute-start | bytes 1622024 | tf_op jit(solution)/shard_map/ppermute | solution.py:21
  288.5 9.2 %collective-permute-start.31 = (f32[264,512]{1,0:T(8,128)S(1)}, f32[264,512]{1,0:T(8,128)S(1)}, u32[]{:S(2)}, u32[]{:S(2)}) collective-permute-start(f32[264,512]{1,0:T(8,128)S(1)} %collective-permute-done.26.refs_14_), channel_id=1, source_target_pairs={{0,4},{4,0},{8,12},{12,8},{16,20},{20,16},{24,28},{28,24},{1,5},{5... | collective-permute-start | bytes 1622024 | tf_op jit(solution)/shard_map/ppermute | solution.py:21
  288.7 8.9 %collective-permute-start.29 = (f32[136,512]{1,0:T(8,128)S(1)}, f32[136,512]{1,0:T(8,128)}, u32[]{:S(2)}, u32[]{:S(2)}) collective-permute-start(f32[136,512]{1,0:T(8,128)S(1)} %slice.53), channel_id=1, source_target_pairs={{0,8},{4,12},{8,0},{12,4},{16,24},{20,28},{24,16},{28,20},{1,9},{5... | collective-permute-start | bytes 835592 | tf_op jit(solution)/shard_map/ppermute | solution.py:21
  289.3 8.3 %collective-permute-start.28 = (f32[128,512]{1,0:T(8,128)S(1)}, f32[128,512]{1,0:T(8,128)}, u32[]{:S(2)}, u32[]{:S(2)}) collective-permute-start(f32[128,512]{1,0:T(8,128)S(1)} %slice.52), channel_id=1, source_target_pairs={{0,16},{4,20},{8,24},{12,28},{16,0},{20,4},{24,8},{28,12},{1,17},{... | collective-permute-start | bytes 786440 | tf_op jit(solution)/shard_map/ppermute | solution.py:21
  298.5 2.7 collective-permute-start.33
  299.3 1.9 collective-permute-start.32
  304.0 28.7 %collective-permute-start.35 = (f32[128,2048]{1,0:T(8,128)}, f32[128,2048]{1,0:T(8,128)}, u32[]{:S(2)}, u32[]{:S(2)}) collective-permute-start(f32[128,2048]{1,0:T(8,128)} %collective-permute-done.21.refs_2_), channel_id=1, source_target_pairs={{0,4},{4,0},{8,12},{12,8},{16,20},{20,16},{24,28},{28,24},{1,5},{5... | collective-permute-start | bytes 3145736 | tf_op jit(solution)/shard_map/ppermute | solution.py:21
  304.1 28.5 %collective-permute-start.36 = (f32[128,2048]{1,0:T(8,128)}, f32[128,2048]{1,0:T(8,128)}, u32[]{:S(2)}, u32[]{:S(2)}) collective-permute-start(f32[128,2048]{1,0:T(8,128)} %collective-permute-done.22.refs_3_), channel_id=1, source_target_pairs={{0,4},{4,0},{8,12},{12,8},{16,20},{20,16},{24,28},{28,24},{1,5},{5... | collective-permute-start | bytes 3145736 | tf_op jit(solution)/shard_map/ppermute | solution.py:21
  304.5 29.8 %collective-permute-start.37 = (f32[128,2048]{1,0:T(8,128)}, f32[128,2048]{1,0:T(8,128)}, u32[]{:S(2)}, u32[]{:S(2)}) collective-permute-start(f32[128,2048]{1,0:T(8,128)} %get-tuple-element.315), channel_id=1, source_target_pairs={{0,1},{3,2},{4,5},{7,6},{8,9},{11,10},{12,13},{15,14},{16,17},{19,... | collective-permute-start | bytes 3145736 | tf_op jit(solution)/shard_map/ppermute | solution.py:21
  309.1 25.2 %collective-permute-start.38 = (f32[128,2048]{1,0:T(8,128)}, f32[128,2048]{1,0:T(8,128)}, u32[]{:S(2)}, u32[]{:S(2)}) collective-permute-start(f32[128,2048]{1,0:T(8,128)} %get-tuple-element.316), channel_id=1, source_target_pairs={{1,2},{2,1},{5,6},{6,5},{9,10},{10,9},{13,14},{14,13},{17,18},{18,... | collective-permute-start | bytes 3145736 | tf_op jit(solution)/shard_map/ppermute | solution.py:21
  338.0 27.8 %collective-permute-start.41 = (f32[128,2048]{1,0:T(8,128)S(1)}, f32[128,2048]{1,0:T(8,128)S(1)}, u32[]{:S(2)}, u32[]{:S(2)}) collective-permute-start(f32[128,2048]{1,0:T(8,128)S(1)} %slice_add_fusion.2), channel_id=1, source_target_pairs={{1,2},{2,1},{5,6},{6,5},{9,10},{10,9},{13,14},{14,13},{17,18},{18,... | collective-permute-start | bytes 3145736 | tf_op jit(solution)/shard_map/ppermute | solution.py:21
  338.7 27.1 %collective-permute-start.42 = (f32[128,2048]{1,0:T(8,128)S(1)}, f32[128,2048]{1,0:T(8,128)}, u32[]{:S(2)}, u32[]{:S(2)}) collective-permute-start(f32[128,2048]{1,0:T(8,128)S(1)} %add.224), channel_id=1, source_target_pairs={{1,0},{2,3},{5,4},{6,7},{9,8},{10,11},{13,12},{14,15},{17,16},{18,... | collective-permute-start | bytes 3145736 | tf_op jit(solution)/shard_map/ppermute | solution.py:21
  340.0 25.8 %collective-permute-start.40 = (f32[2,2048]{1,0:T(2,128)S(1)}, f32[2,2048]{1,0:T(2,128)S(1)}, u32[]{:S(2)}, u32[]{:S(2)}) collective-permute-start(f32[2,2048]{1,0:T(2,128)S(1)} %pad_maximum_fusion.2), channel_id=1, source_target_pairs={{0,1},{1,0},{2,3},{3,2},{4,5},{5,4},{6,7},{7,6},{8,9},{9,8},{10,11... | collective-permute-start | bytes 49160 | tf_op jit(solution)/shard_map/ppermute | solution.py:21
  343.7 24.2 %collective-permute-start.39 = (f32[128,2048]{1,0:T(8,128)}, f32[128,2048]{1,0:T(8,128)}, u32[]{:S(2)}, u32[]{:S(2)}) collective-permute-start(f32[128,2048]{1,0:T(8,128)} %split.18), channel_id=1, source_target_pairs={{0,1},{3,2},{4,5},{7,6},{8,9},{11,10},{12,13},{15,14},{16,17},{19,... | collective-permute-start | bytes 3145736 | tf_op jit(solution)/shard_map/ppermute | solution.py:21
  346.9 33.0 %slice-start.4 = ((s8[5636096]{0:T(1024)(128)(4,1)}), s8[1441792]{0:T(1024)(128)(4,1)S(1)}, s32[]{:S(2)}) async-start(s8[5636096]{0:T(1024)(128)(4,1)} %bitcast.69), calls=%async_computation.7 | async-start | bytes 2883584
  353.3 26.6 %slice-start.5 = ((s8[5636096]{0:T(1024)(128)(4,1)}), s8[4194304]{0:T(1024)(128)(4,1)S(1)}, s32[]{:S(2)}) async-start(s8[5636096]{0:T(1024)(128)(4,1)} %bitcast.69), calls=%async_computation.8 | async-start | bytes 8388608
  370.8 23.2 %copy-start.16 = (bf16[1024,2048]{1,0:T(8,128)(2,1)S(1)}, bf16[1024,2048]{1,0:T(8,128)(2,1)}, u32[]{:S(2)}) copy-start(bf16[1024,2048]{1,0:T(8,128)(2,1)} %shard_map.206) | copy-start | bytes 12582916
  370.8 35.0 %collective-permute-start.46 = (f32[128,2048]{1,0:T(8,128)S(1)}, f32[128,2048]{1,0:T(8,128)S(1)}, u32[]{:S(2)}, u32[]{:S(2)}) collective-permute-start(f32[128,2048]{1,0:T(8,128)S(1)} %add.227), channel_id=1, source_target_pairs={{1,0},{2,3},{5,4},{6,7},{9,8},{10,11},{13,12},{14,15},{17,16},{18,... | collective-permute-start | bytes 3145736 | tf_op jit(solution)/shard_map/ppermute | solution.py:21
  372.3 33.5 %collective-permute-start.43 = (f32[128,2048]{1,0:T(8,128)S(1)}, f32[128,2048]{1,0:T(8,128)S(1)}, u32[]{:S(2)}, u32[]{:S(2)}) collective-permute-start(f32[128,2048]{1,0:T(8,128)S(1)} %get-tuple-element.352), channel_id=1, source_target_pairs={{0,1},{3,2},{4,5},{7,6},{8,9},{11,10},{12,13},{15,14},{16,17},{19,... | collective-permute-start | bytes 3145736 | tf_op jit(solution)/shard_map/ppermute | solution.py:21
  377.2 28.7 %collective-permute-start.44 = (f32[128,2048]{1,0:T(8,128)S(1)}, f32[128,2048]{1,0:T(8,128)S(1)}, u32[]{:S(2)}, u32[]{:S(2)}) collective-permute-start(f32[128,2048]{1,0:T(8,128)S(1)} %get-tuple-element.353), channel_id=1, source_target_pairs={{1,2},{2,1},{5,6},{6,5},{9,10},{10,9},{13,14},{14,13},{17,18},{18,... | collective-permute-start | bytes 3145736 | tf_op jit(solution)/shard_map/ppermute | solution.py:21
  377.9 27.9 %collective-permute-start.45 = (f32[2,2048]{1,0:T(2,128)S(1)}, f32[2,2048]{1,0:T(2,128)S(1)}, u32[]{:S(2)}, u32[]{:S(2)}) collective-permute-start(f32[2,2048]{1,0:T(2,128)S(1)} %fusion.22), channel_id=1, source_target_pairs={{0,2},{1,3},{2,0},{3,1},{4,6},{5,7},{6,4},{7,5},{8,10},{9,11},{10,... | collective-permute-start | bytes 49160 | tf_op jit(solution)/shard_map/ppermute | solution.py:21
  409.5 23.7 %collective-permute-start.49 = (f32[2,2048]{1,0:T(2,128)S(1)}, f32[2,2048]{1,0:T(2,128)S(1)}, u32[]{:S(2)}, u32[]{:S(2)}) collective-permute-start(f32[2,2048]{1,0:T(2,128)S(1)} %fusion.102), channel_id=1, source_target_pairs={{0,4},{4,0},{8,12},{12,8},{16,20},{20,16},{24,28},{28,24},{1,5},{5... | collective-permute-start | bytes 49160 | tf_op jit(solution)/shard_map/ppermute | solution.py:21
  409.6 23.7 %collective-permute-start.47 = (f32[128,2048]{1,0:T(8,128)S(1)}, f32[128,2048]{1,0:T(8,128)S(1)}, u32[]{:S(2)}, u32[]{:S(2)}) collective-permute-start(f32[128,2048]{1,0:T(8,128)S(1)} %slice_add_fusion), channel_id=1, source_target_pairs={{1,2},{2,1},{5,6},{6,5},{9,10},{10,9},{13,14},{14,13},{17,18},{18,... | collective-permute-start | bytes 3145736 | tf_op jit(solution)/shard_map/ppermute | solution.py:21
  410.5 27.3 %collective-permute-start.48 = (f32[128,2048]{1,0:T(8,128)S(1)}, f32[128,2048]{1,0:T(8,128)S(1)}, u32[]{:S(2)}, u32[]{:S(2)}) collective-permute-start(f32[128,2048]{1,0:T(8,128)S(1)} %add.231), channel_id=1, source_target_pairs={{1,0},{2,3},{5,4},{6,7},{9,8},{10,11},{13,12},{14,15},{17,16},{18,... | collective-permute-start | bytes 3145736 | tf_op jit(solution)/shard_map/ppermute | solution.py:21
  438.0 29.3 %collective-permute-start.50 = (f32[128,2048]{1,0:T(8,128)S(1)}, f32[128,2048]{1,0:T(8,128)S(1)}, u32[]{:S(2)}, u32[]{:S(2)}) collective-permute-start(f32[128,2048]{1,0:T(8,128)S(1)} %add.234), channel_id=1, source_target_pairs={{1,0},{2,3},{5,4},{6,7},{9,8},{10,11},{13,12},{14,15},{17,16},{18,... | collective-permute-start | bytes 3145736 | tf_op jit(solution)/shard_map/ppermute | solution.py:21
  439.5 27.7 %collective-permute-start.51 = (f32[2,2048]{1,0:T(2,128)S(1)}, f32[2,2048]{1,0:T(2,128)S(1)}, u32[]{:S(2)}, u32[]{:S(2)}) collective-permute-start(f32[2,2048]{1,0:T(2,128)S(1)} %add.235), channel_id=1, source_target_pairs={{0,8},{4,12},{8,0},{12,4},{16,24},{20,28},{24,16},{28,20},{1,9},{5... | collective-permute-start | bytes 49160 | tf_op jit(solution)/shard_map/ppermute | solution.py:21
  439.9 27.3 %collective-permute-start.52 = (f32[2,2048]{1,0:T(2,128)S(1)}, f32[2,2048]{1,0:T(2,128)S(1)}, u32[]{:S(2)}, u32[]{:S(2)}) collective-permute-start(f32[2,2048]{1,0:T(2,128)S(1)} %add.235), channel_id=1, source_target_pairs={{0,16},{4,20},{8,24},{12,28},{16,0},{20,4},{24,8},{28,12},{1,17},{... | collective-permute-start | bytes 49160 | tf_op jit(solution)/shard_map/ppermute | solution.py:21
  440.4 26.9 %collective-permute-start.53 = (f32[2,2048]{1,0:T(2,128)S(1)}, f32[2,2048]{1,0:T(2,128)S(1)}, u32[]{:S(2)}, u32[]{:S(2)}) collective-permute-start(f32[2,2048]{1,0:T(2,128)S(1)} %add.235), channel_id=1, source_target_pairs={{0,24},{4,28},{8,16},{12,20},{16,8},{20,12},{24,0},{28,4},{1,25},{... | collective-permute-start | bytes 49160 | tf_op jit(solution)/shard_map/ppermute | solution.py:21
  (53 other events, 263.1 us)
Sparse Core Ops, SparseCore 0:
  65.6 87.3 all-reduce.4
  176.4 83.7 all-reduce.6
  332.8 138.1 all-reduce.8
